TPU v7x, 128 devices: a whole 4x4x4 slice. The times are simulated.
128 devices in a mesh: sub: 32 (over y, z, core), grp: 4 (over x).
Axes of the slice: x: 4, y: 4, z: 4, core: 2. Of those that a mesh axis runs over, the one named last changes fastest.
Arguments:
- flex: float32 [64, 4, 1024, 1024], P('sub', 'grp'), may hold values from -4 to 29, as said below
- coupling: float32 [64, 4, 64, 1024], P('sub', 'grp'), may hold values from -0.375 to 0.375
- weight: float32 [64, 4, 1024], P('sub', 'grp'), may hold values from 1 to 18, as said below
- iface_size: int32 [64, 4], P('sub', 'grp'), may hold values from 128 to 1024, as said below
- partner: int32 [64, 4, 1024], P('sub', 'grp'), may hold values from 0 to 65535, as said below
- corner_map: int32 [64, 4, 64], P('sub', 'grp'), may hold values from 0 to 255
- coarse_factor: float32 [32, 256, 256], P('sub', 'grp'), may hold values from -1 to 2.5, as said below
- lam: float32 [64, 4, 1024, 256], P('sub', 'grp'), may hold values from -8 to 8, as said below
- resid: float32 [64, 4, 1024, 256], P('sub', 'grp'), may hold values from -8 to 8, as said below
- direc: float32 [64, 4, 1024, 256], P('sub', 'grp'), may hold values from -8 to 8, as said below
Outputs:
- lam_next: float32 [64, 4, 1024, 256], P('sub', 'grp')
- resid_next: float32 [64, 4, 1024, 256], P('sub', 'grp')
- direc_next: float32 [64, 4, 1024, 256], P('sub', 'grp')
- ratio: float32 [256], replicated
Inputs may be any that keep to these rules, and one draw needn't show every extreme that they name: `iface_size`: every subdomain has at least 128 and at most 1024 live interface dofs, and some subdomain has exactly 1024 in every draw. `partner`: each live dof is matched with exactly one live dof of the subdomain just before or just after it along the chain, in the same cycle position; matching is mutual; a dof that is not live names itself. Two neighbouring subdomains share at most 512 matched pairs, reached between two devices' subdomains in every draw. `weight`: equal at the two dofs of every matched pair. `flex`: each block is symmetric. `coarse_factor`: each cluster's block is lower triangular with a positive diagonal. `lam`: equal and opposite at the two dofs of every matched pair; zero at dofs that are not live. `resid`: equal and opposite at the two dofs of every matched pair; zero at dofs that are not live. `direc`: equal and opposite at the two dofs of every matched pair; zero at dofs that are not live.
All inputs are finite; a program needn't handle non-finite values.
Results may differ from a plain program's by a relative error of at most 0.000094.
Values sent between devices are 32-bit elements; how exact they have to be, the bound alone decides.
No kernel may reach another device: no remote copies, remote signals or barrier semaphores. Data moves between devices by JAX's collectives and lax.ppermute only.
A program may use at most 128 MiB of HBM per device.

v0:
```python
import jax
import jax.numpy as jnp
from jax import lax
from jax.sharding import PartitionSpec as P


def extended(x, sides, width):
    for axis, dim in sides:
        size, length = (lax.axis_size(axis), x.shape[dim])
        up = [(i, (i + 1) % size) for i in range(size - 1)]
        down = [(j, i) for i, j in up]
        last = lax.slice_in_dim(x, length - width, length, axis=dim)
        first = lax.slice_in_dim(x, 0, width, axis=dim)
        before = lax.ppermute(last, axis, up)
        after = lax.ppermute(first, axis, down)
        x = jnp.concatenate([before, x, after], axis=dim)
    return x


def per_device(
    flex, coupling, weight, iface_size, partner, corner_map, coarse_factor, lam, resid, direc
):
    highest = lax.Precision.HIGHEST
    member_count = flex.shape[0]
    dof_count = flex.shape[2]
    load_count = direc.shape[3]
    blocks = flex[:, 0]
    links = coupling[:, 0]
    residual = resid[:, 0]
    direction = direc[:, 0]
    scaling = weight[:, 0][..., None]
    live_mask = (jnp.arange(dof_count, dtype=jnp.int32)[None, :] < iface_size)[..., None]
    masked = jnp.where(live_mask, direction, 0.0)
    local = jnp.einsum(
        "sij,sjl->sil", blocks, masked, precision=highest, preferred_element_type=jnp.float32
    )
    primal = jnp.einsum(
        "scj,sjl->scl", links, masked, precision=highest, preferred_element_type=jnp.float32
    )
    coarse_size = coarse_factor.shape[2]
    selector = (
        corner_map[:, 0, :, None] == jnp.arange(coarse_size, dtype=jnp.int32)[None, None, :]
    ).astype(jnp.float32)
    partial_rhs = jnp.einsum(
        "scm,scl->ml", selector, primal, precision=highest, preferred_element_type=jnp.float32
    )
    coarse_rhs = lax.psum(partial_rhs, "grp")
    factor_rows = coarse_factor[0]
    coarse_mid = jnp.dot(
        factor_rows, coarse_rhs, precision=highest, preferred_element_type=jnp.float32
    )
    share = jnp.einsum(
        "rm,rl->ml", factor_rows, coarse_mid, precision=highest, preferred_element_type=jnp.float32
    )
    coarse_sol = lax.psum(share, "grp")
    picked = jnp.einsum(
        "scm,ml->scl", selector, coarse_sol, precision=highest, preferred_element_type=jnp.float32
    )
    image = local + jnp.einsum(
        "scj,scl->sjl", links, picked, precision=highest, preferred_element_type=jnp.float32
    )
    chain_start = lax.axis_index("sub") * member_count
    partner_local = partner[:, 0, :]
    window = extended(image, (("sub", 0),), 1)
    offset = partner_local - (chain_start - 1) * dof_count
    opposite = jnp.take(window.reshape(-1, load_count), offset.reshape(-1), axis=0)
    opposite = opposite.reshape(member_count, dof_count, load_count)
    jump = jnp.where(live_mask, image - opposite, 0.0)
    precond = jnp.where(live_mask, scaling * residual, 0.0)
    rz_old, curvature = lax.psum(
        (jnp.sum(residual * precond, axis=(0, 1)), jnp.sum(direction * jump, axis=(0, 1))),
        ("sub", "grp"),
    )
    alpha = rz_old / curvature
    resid_next = residual - alpha * jump
    precond_next = jnp.where(live_mask, scaling * resid_next, 0.0)
    rz_new = lax.psum(jnp.sum(resid_next * precond_next, axis=(0, 1)), ("sub", "grp"))
    lam_next = lam[:, 0] + alpha * direction
    ratio = rz_new / rz_old
    direc_next = precond_next + ratio * direction
    return (lam_next[:, None], resid_next[:, None], direc_next[:, None], ratio)


def solution(mesh):
    placed = (
        P("sub", "grp", None, None),
        P("sub", "grp", None, None),
        P("sub", "grp", None),
        P("sub", "grp"),
        P("sub", "grp", None),
        P("sub", "grp", None),
        P("sub", "grp", None),
        P("sub", "grp", None, None),
        P("sub", "grp", None, None),
        P("sub", "grp", None, None),
    )
    return jax.shard_map(
        per_device,
        mesh=mesh,
        in_specs=placed,
        out_specs=(
            P("sub", "grp", None, None),
            P("sub", "grp", None, None),
            P("sub", "grp", None, None),
            P(),
        ),
        check_vma=False,
    )
```

profile of v0, /device:TPU:0, one launch (start us, length us, event | category | flops | bytes accessed | tf_op | source)
XLA Modules:
  0.0 305.1 jit_solution(11546244064647247971)
XLA Ops:
  7.2 0.0 copy-start
  7.2 0.0 all-reduce.4.cloned.1.call-start
  7.2 0.8 iota_compare_fusion.2
  8.0 1.9 copy.19
  9.9 0.0 copy-done
  9.9 0.0 copy-start.6
  10.0 0.0 copy-start.3
  10.0 1.9 fusion.8
  11.9 0.0 copy-done.6
  11.9 1.1 convolution_bitcast_fusion
  13.0 0.0 all-reduce.4.cloned.1.call-update
  13.1 0.0 all-reduce.6.cloned.1.call-start
  13.1 44.2 %all-reduce.4.cloned.1.call-done = f32[256,256]{1,0:T(8,128)} async-done(((f32[256,256]{1,0:T(8,128)}), f32[256,256]{1,0:T(8,128)}) %all-reduce.4.cloned.1.call-update) | async-done | bytes 262160 | tf_op jit(solution)/shard_map/psum | solution.py:47
  57.3 0.0 copy-done.3
  57.3 1.5 fusion.20
  58.8 1.1 convolution_bitcast_fusion.1
  59.9 0.0 all-reduce.6.cloned.1.call-update
  59.9 0.0 copy-start.4
  59.9 10.6 %fusion = f32[2,256,1024]{2,1,0:T(8,128)} fusion(f32[2,1,1024,1024]{3,2,1,0:T(8,128)} %param.10, f32[2,1,1024,256]{2,3,0,1:T(8,128)S(1)} %copy.19, pred[2,1024]{1,0:T(4,128)(4,1)S(1)} %iota_compare_fusion.2), kind=kOutput, calls=%fused_computation.1 | convolution fusion | flops 6442975232 | bytes 12584960 | tf_op jit(solution)/shard_map/sij,sjl->sil/dot_general | solution.py:34
  70.5 0.0 copy-done.4
  70.5 3.0 copy.18
  73.5 28.9 %all-reduce.6.cloned.1.call-done = f32[256,256]{0,1:T(8,128)} async-done(((f32[256,256]{0,1:T(8,128)}), f32[256,256]{0,1:T(8,128)}) %all-reduce.6.cloned.1.call-update) | async-done | bytes 262160 | tf_op jit(solution)/shard_map/psum | solution.py:55
  102.4 1.2 fusion.15
  103.7 3.4 %add_bitcast_fusion = f32[2,1024,256]{1,2,0:T(8,128)S(1)} fusion(f32[2,256,1024]{2,1,0:T(8,128)} %fusion, f32[2,64,256]{2,1,0:T(8,128)S(1)} %fusion.15, f32[2,1,64,1024]{3,2,1,0:T(8,128)S(1)} %copy-done), kind=kOutput, calls=%fused_computation.19 | convolution fusion | flops 403177472 | bytes 4849664 | tf_op jit(solution)/shard_map/scj,scl->sjl/dot_general | solution.py:59
  107.1 0.0 copy-start.1
  107.1 0.0 copy-start.5
  107.2 0.1 fusion.26
  107.3 1.4 collective-permute-start
  108.7 1.5 collective-permute-start.1
  110.1 0.0 copy-done.5
  110.2 0.6 collective-permute-done
  110.9 4.1 %collective-permute-done.1 = f32[1,1024,256]{1,2,0:T(8,128)S(1)} collective-permute-done((f32[1,1024,256]{1,2,0:T(8,128)S(1)}, f32[1,1024,256]{1,2,0:T(8,128)S(1)}, u32[]{:S(2)}, u32[]{:S(2)}) %collective-permute-start.1) | collective-permute-done | bytes 1048608 | tf_op jit(solution)/shard_map/ppermute | solution.py:15
  114.9 0.0 copy-done.1
  114.9 2.5 pad_maximum_fusion
  117.5 5.4 %copy.20 = f32[4,1024,256]{2,1,0:T(8,128)} copy(f32[4,1024,256]{1,2,0:T(8,128)} %pad_maximum_fusion) | data formatting | bytes 8388608 | tf_op jit(solution)/shard_map/concatenate | solution.py:16
  122.8 10.8 %gather_fusion = f32[2048,256]{1,0:T(8,128)} fusion(f32[4096,256]{1,0:T(8,128)} %bitcast.67, s32[2048]{0:T(1024)S(1)} %broadcast_clamp_fusion), kind=kCustom, calls=%fused_computation | custom fusion | bytes 4202496 | tf_op jit(solution)/shard_map/jit(_take)/gather | solution.py:66
  133.6 2.9 copy.21
  136.5 3.6 %fusion.2 = (f32[256]{0:T(256)S(1)}, f32[256]{0:T(256)S(1)}) fusion(f32[2,1,1024,256]{2,3,0,1:T(8,128)S(1)} %copy.19, f32[2,1024,256]{1,2,0:T(8,128)} %copy-done.1, f32[2,1024,256]{1,2,0:T(8,128)} %copy.21, pred[2,1024]{1,0:T(4,128)(4,1)S(1)} %compare_and_fusion, pred[2,1024]{1,0:T(4,128)(4,1)S(1)} %iota_compare_fusion.2, f32[2,1024]{1,0:T(2,128)S(1)} %bitcast.70, ...), kind=kLoop, calls=%fused_computation.7 | loop fusion | flops 4718080 | bytes 8402944 | tf_op jit(solution)/shard_map/reduce_sum | solution.py:71
  140.1 78.3 %all-reduce = (f32[256]{0:T(256)S(1)}, f32[256]{0:T(256)S(1)}) all-reduce(f32[256]{0:T(256)S(1)} %get-tuple-element.13, f32[256]{0:T(256)S(1)} %get-tuple-element.12), channel_id=1, replica_groups=mesh['sub'=32,'grp'=4] {'sub','grp'}, use_global_device_ids=true, to_apply=%region_1.2 | all-reduce | flops 512 | bytes 4096 | tf_op jit(solution)/shard_map/psum | solution.py:70
  218.4 4.9 %multiply_reduce_fusion = (f32[256]{0:T(256)S(1)}, f32[2,1024,256]{1,2,0:T(8,128)}) fusion(f32[2,1024]{1,0:T(2,128)S(1)} %bitcast.71, pred[2,1024]{1,0:T(4,128)(4,1)S(1)} %iota_compare_fusion.2, f32[2,1024,256]{1,2,0:T(8,128)} %copy-done.1, f32[2,1024,256]{1,2,0:T(8,128)} %copy.21, pred[2,1024]{1,0:T(4,128)(4,1)S(1)} %compare_and_fusion, f32[256]{0:T(256)S(1)} %div.6, ...), kind=kLoop, calls=%fused_computation.15 | loop fusion | flops 4718336 | bytes 8402944 | tf_op jit(solution)/shard_map/reduce_sum | solution.py:77
  223.4 63.0 %psum.39 = f32[256]{0:T(256)S(1)} all-reduce(f32[256]{0:T(256)S(1)} %get-tuple-element.16), channel_id=1, replica_groups=mesh['sub'=32,'grp'=4] {'sub','grp'}, use_global_device_ids=true, to_apply=%region_7.8 | all-reduce | flops 256 | bytes 2048 | tf_op jit(solution)/shard_map/psum | solution.py:77
  286.4 0.0 copy-start.7
  286.4 3.2 %fusion.4 = f32[2,1,1024,256]{2,3,0,1:T(8,128)} fusion(f32[2,1,1024,256]{2,3,0,1:T(8,128)S(1)} %copy.19, f32[2,1024,256]{1,2,0:T(8,128)} %get-tuple-element.17, f32[256]{0:T(256)S(1)} %div.7, f32[2,1024]{1,0:T(2,128)S(1)} %bitcast.72, pred[2,1024]{1,0:T(4,128)(4,1)S(1)} %iota_compare_fusion.2), kind=kLoop, calls=%fused_computation.9 | loop fusion | flops 2097152 | bytes 6302720 | tf_op jit(solution)/shard_map/broadcast_in_dim | solution.py:81
  289.6 0.0 copy-done.7
  289.7 3.0 copy.23
  292.7 0.0 copy-done.2
  292.7 1.8 copy.22
  294.5 3.8 %multiply_add_fusion = f32[2,1,1024,256]{3,2,1,0:T(8,128)} fusion(f32[2,1,1024,256]{3,2,1,0:T(8,128)} %param.17, f32[2,1,1024,256]{3,2,1,0:T(8,128)} %param.19, f32[256]{0:T(256)S(1)} %div.6), kind=kLoop, calls=%fused_computation.17 | loop fusion | flops 1048576 | bytes 6292480 | tf_op jit(solution)/shard_map/add | solution.py:78
  (8 shorter events, 0.1 us)
Async XLA Ops:
  7.2 2.8 copy-start
  7.2 50.1 %all-reduce.4.cloned.1.call-start = ((), (), s32[]{:S(2)}) async-start(), calls=%async_computation | async-start | bytes 524288 | tf_op jit(solution)/shard_map/psum | solution.py:47
  9.9 2.0 copy-start.6
  10.0 47.3 %copy-start.3 = (f32[1,64,256]{2,1,0:T(8,128)S(1)}, f32[1,64,256]{2,1,0:T(8,128)}, u32[]{:S(2)}) copy-start(f32[1,64,256]{2,1,0:T(8,128)} %param.16) | copy-start | bytes 196612
  13.1 89.4 %all-reduce.6.cloned.1.call-start = ((), (), s32[]{:S(2)}) async-start(), calls=%async_computation.1 | async-start | bytes 524288 | tf_op jit(solution)/shard_map/psum | solution.py:55
  59.9 10.6 %copy-start.4 = (f32[2,1,1024]{2,1,0:T(1,128)S(1)}, f32[2,1,1024]{2,1,0:T(1,128)}, u32[]{:S(2)}) copy-start(f32[2,1,1024]{2,1,0:T(1,128)} %param.12) | copy-start | bytes 24580
  107.1 7.8 %copy-start.1 = (f32[2,1024,256]{1,2,0:T(8,128)}, f32[2,1024,256]{1,2,0:T(8,128)S(1)}, u32[]{:S(2)}) copy-start(f32[2,1024,256]{1,2,0:T(8,128)S(1)} %add_bitcast_fusion) | copy-start | bytes 6291460
  107.1 3.0 copy-start.5
  107.3 3.6 %collective-permute-start = (f32[1,1024,256]{1,2,0:T(8,128)S(1)}, f32[1,1024,256]{1,2,0:T(8,128)S(1)}, u32[]{:S(2)}, u32[]{:S(2)}) collective-permute-start(f32[1,1024,256]{1,2,0:T(8,128)S(1)} %get-tuple-element.18), channel_id=1, source_target_pairs={{0,4},{4,8},{8,12},{12,16},{16,20},{20,24},{24,28},{28,32},{32,36}... | collective-permute-start | bytes 3145736 | tf_op jit(solution)/shard_map/ppermute | solution.py:14
  108.7 6.3 %collective-permute-start.1 = (f32[1,1024,256]{1,2,0:T(8,128)S(1)}, f32[1,1024,256]{1,2,0:T(8,128)S(1)}, u32[]{:S(2)}, u32[]{:S(2)}) collective-permute-start(f32[1,1024,256]{1,2,0:T(8,128)S(1)} %get-tuple-element.19), channel_id=1, source_target_pairs={{4,0},{8,4},{12,8},{16,12},{20,16},{24,20},{28,24},{32,28},{36,32}... | collective-permute-start | bytes 3145736 | tf_op jit(solution)/shard_map/ppermute | solution.py:15
  286.4 3.3 %copy-start.7 = (f32[256]{0:T(256)}, f32[256]{0:T(256)S(1)}, u32[]{:S(2)}) copy-start(f32[256]{0:T(256)S(1)} %div.7) | copy-start | bytes 3076
  289.7 3.0 copy-start.2
Sparse Core Ops, SparseCore 0:
  13.2 44.0 all-reduce.3
  60.3 42.0 all-reduce.5
where the time goes:
time: 307 us; the launch traced here: 305 us
  blocking collectives  141 us (46%)
  waiting for transfers between devices  77.9 us (25%)
  local copies, waits for them, and re-layouts  28.9 us (9%)
  matrix products  20.9 us (7%)
  other arithmetic  19 us (6%)
  between operations  14.2 us (5%)
    psum x1, blocking collectives, per_device(): lax.psum((jnp.sum(residual * precond, axis=(0, 1)), jnp.sum(direction * j...  78.3 us
    psum x1, blocking collectives, per_device(): lax.psum(jnp.sum(resid_next * precond_next, axis=(0, 1)), ('sub', 'grp'))  63 us
    psum x1, waiting for transfers between devices, per_device(): coarse_rhs = lax.psum(partial_rhs, 'grp')  44.2 us
    psum x1, waiting for transfers between devices, per_device(): coarse_sol = lax.psum(share, 'grp')  28.9 us
    gather x2, local copies, waits for them, and re-layouts, per_device(): jnp.take(window.reshape(-1, load_count), offset.reshape(-1), axis=0)  13.7 us
    dot_general x1, matrix products, per_device(): jnp.einsum('sij,sjl->sil', blocks, masked, precision=highest, preferred_e...  10.6 us
    unnamed x21, local copies, waits for them, and re-layouts  9.77 us
  transfers between devices with their start and end apart: 4, of which 4 were waited for; matrix products, arithmetic and copies ran while one was open for 4% of the time, Pallas kernels for 0%

commit v1 on v0

v1 whole, which is shorter than its diff:
```python
import functools

import jax
import jax.numpy as jnp
from jax import lax
from jax.experimental import pallas as pl
from jax.experimental.pallas import tpu as pltpu
from jax.sharding import PartitionSpec as P

F32 = jnp.float32
BF16 = jnp.bfloat16
N = 1024
L = 256
C = 64
HALF = 512
MIB = 1 << 20


def dot(a, b):
    return lax.dot_general(a, b, (((1,), (0,)), ((), ())), preferred_element_type=F32)


def dot_t(a, b):
    return lax.dot_general(a, b, (((0,), (0,)), ((), ())), preferred_element_type=F32)


def split(x):
    high = x.astype(BF16)
    low = (x - high.astype(F32)).astype(BF16)
    return high, low


def iota(shape, dim):
    return lax.broadcasted_iota(jnp.int32, shape, dim)


def one_hot(test):
    return jnp.where(test, 1.0, 0.0).astype(BF16)


def fold(x):
    return jnp.sum(x.reshape(-1, 8, x.shape[-1]), axis=0)


def column(row):
    tall = jnp.transpose(jnp.broadcast_to(row, (128, row.shape[1])))
    return jnp.concatenate([tall, tall], axis=1)


def primal_kernel(direc_ref, coup_ref, map_ref, factor_ref, pay_ref):
    for s in range(2):
        dh, dl = split(direc_ref[s])
        ch, cl = split(coup_ref[s])
        pay_ref[s * C : (s + 1) * C] = dot(ch, dh) + dot(ch, dl) + dot(cl, dh)
    pay_ref[2 * C : 3 * C] = factor_ref[...]
    pay_ref[3 * C :] = jnp.zeros((8, L), F32)
    for s in range(2):
        pay_ref[3 * C + s : 3 * C + s + 1, 0:C] = map_ref[s].astype(F32)


def local_kernel(flex_ref, direc_ref, out_ref, high, low):
    @pl.when(pl.program_id(1) == 0)
    def _():
        dh, dl = split(direc_ref[0])
        high[...] = dh
        low[...] = dl

    ah, al = split(flex_ref[0])
    out_ref[0] = dot(ah, high[...]) + dot(ah, low[...]) + dot(al, high[...])


def running_count(mask):
    total = mask.astype(jnp.int32)
    lane = iota(total.shape, 1)
    step = 1
    while step < total.shape[1]:
        total = total + jnp.where(lane >= step, pltpu.roll(total, step, 1), 0)
        step *= 2
    return total


def selector(pay_ref):
    first = pay_ref[3 * C : 3 * C + 1, 0:C]
    second = pay_ref[3 * C + 1 : 3 * C + 2, 0:C]
    both = jnp.concatenate([first, second], axis=1).astype(jnp.int32)
    return one_hot(iota((L, 2 * C), 0) == both)


def image_kernel(
    place_ref, local_ref, pay_ref, one_ref, two_ref, three_ref, coup_ref, partner_ref,
    image_ref, cross_ref, near_ref, high, low,
):
    me = place_ref[0]
    odd = lax.rem(me, 2)
    members = (pay_ref, one_ref, two_ref, three_ref)
    rhs = jnp.zeros((L, L), F32)
    for member in members:
        sel = selector(member)
        ph, pl_ = split(member[0 : 2 * C])
        rhs = rhs + dot(sel, ph) + dot(sel, pl_)
    factor = jnp.concatenate([m[2 * C : 3 * C] for m in members], axis=0)
    fh, fl = split(factor)
    rh, rl = split(rhs)
    mid = dot(fh, rh) + dot(fh, rl) + dot(fl, rh)
    mh, ml = split(mid)
    sol = dot_t(fh, mh) + dot_t(fh, ml) + dot_t(fl, mh)
    sh, sl = split(sol)
    own = selector(pay_ref)
    picked = dot_t(own, sh) + dot_t(own, sl)
    for s in range(2):
        ch, cl = split(coup_ref[s])
        qh, ql = split(picked[s * C : (s + 1) * C])
        left = jnp.concatenate([ch, ch, cl], axis=0)
        right = jnp.concatenate([qh, ql, qh], axis=0)
        for r in range(0, N, L):
            image = local_ref[s, r : r + L] + dot_t(left[:, r : r + L], right)
            image_ref[s, r : r + L] = image
            ih, il = split(image)
            high[r : r + L] = ih
            low[r : r + L] = il
        target = partner_ref[s] - (2 * me - 1) * N
        match = (target >= 3 * N) if s else (target < N)
        key = jnp.where(match, running_count(match) - 1, -1)
        name = jnp.where(match, jnp.bitwise_and(target, N - 1) + 1, 0)
        coarse = lax.shift_right_logical(name, 5)
        fine = jnp.bitwise_and(name, 31)
        digits = jnp.concatenate(
            [coarse, fine, jnp.zeros((6, N), jnp.int32)], axis=0
        ).astype(F32).astype(BF16)

        def pack(ref):
            ref[HALF:] = jnp.zeros((8, L), F32)
            for c in range(2):
                place = one_hot(iota((L, N), 0) + c * L == key)
                ref[c * L : (c + 1) * L] = dot(place, high[...]) + dot(place, low[...])
                names = lax.dot_general(
                    digits, place, (((1,), (1,)), ((), ())), preferred_element_type=F32
                )
                ref[HALF + c : HALF + c + 1] = names[0:1] * 32.0 + names[1:2]

        pl.when(odd == s)(functools.partial(pack, cross_ref))
        pl.when(odd != s)(functools.partial(pack, near_ref))


def inner_kernel(place_ref, image_ref, direc_ref, resid_ref, weight_ref, partner_ref, jump_ref, sums_ref, high, low):
    me = place_ref[0]
    old = jnp.zeros((8, L), F32)
    curve = jnp.zeros((8, L), F32)
    mixed = jnp.zeros((8, L), F32)
    for s in range(2):
        other = 1 - s
        for r in range(0, N, L):
            ih, il = split(image_ref[other, r : r + L])
            high[r : r + L] = ih
            low[r : r + L] = il
        theirs = partner_ref[other] - (2 * me - 1 + 1 + s) * N
        mine = partner_ref[s]
        awake = jnp.where(lax.shift_right_arithmetic(mine, 10) != 2 * me + s, 1.0, 0.0)
        for r in range(0, N, L):
            rows = slice(r, r + L)
            place = one_hot(iota((L, N), 0) + r == theirs)
            opposite = dot(place, high[...]) + dot(place, low[...])
            image = image_ref[s, rows]
            jump_ref[s, rows] = column(awake[:, rows]) * image - opposite
            scaled = column(weight_ref[s][:, rows]) * resid_ref[s, rows]
            old = old + fold(scaled * resid_ref[s, rows])
            curve = curve + fold(direc_ref[s, rows] * image)
            mixed = mixed + fold(scaled * image)
    sums_ref[0] = old
    sums_ref[1] = curve
    sums_ref[2] = mixed


def outer_kernel(place_ref, part_ref, cross_ref, near_ref, weight_ref, sums_ref, jump_ref, total_ref):
    odd = lax.rem(place_ref[0], 2)
    square = jnp.zeros((8, L), F32)
    for ref, s in ((cross_ref, odd), (near_ref, 1 - odd)):
        pieces = [split(ref[c * L : (c + 1) * L]) for c in range(2)]
        for r in range(0, N, L):
            opposite = jnp.zeros((L, L), F32)
            for c in range(2):
                name = ref[HALF + c : HALF + c + 1].astype(jnp.int32)
                place = one_hot(iota((L, L), 0) + (r + 1) == name)
                opposite = opposite + dot(place, pieces[c][0]) + dot(place, pieces[c][1])
            jump = part_ref[s, r : r + L] - opposite
            jump_ref[s, r : r + L] = jump
            square = square + fold(column(weight_ref[s][:, r : r + L]) * jump * jump)
    rows = [jnp.sum(x, axis=0, keepdims=True) for x in (sums_ref[0], sums_ref[1], sums_ref[2], square)]
    total_ref[...] = jnp.concatenate(rows + [jnp.zeros((4, L), F32)], axis=0)


def final_kernel(total_ref, weight_ref, lam_ref, resid_ref, direc_ref, jump_ref, lam_out, resid_out, direc_out, ratio_out):
    old = total_ref[0:1]
    alpha = old / (2.0 * total_ref[1:2])
    new = old + alpha * (alpha * total_ref[3:4] - 4.0 * total_ref[2:3])
    ratio = new / old
    ratio_out[...] = ratio
    direc = direc_ref[0]
    resid = resid_ref[0] - alpha * jump_ref[0]
    lam_out[0] = lam_ref[0] + alpha * direc
    resid_out[0] = resid
    direc_out[0] = column(weight_ref[0]) * resid + ratio * direc


def vmem():
    return pl.BlockSpec(memory_space=pltpu.VMEM)


def smem():
    return pl.BlockSpec(memory_space=pltpu.SMEM)


def exchange(x, axes, size, route):
    pairs = []
    for i in range(size):
        j = route(i)
        if j is not None:
            pairs.append((i, j))
    return lax.ppermute(x, axes, pairs)


def per_device(
    flex, coupling, weight, iface_size, partner, corner_map, coarse_factor, lam, resid, direc
):
    del iface_size
    blocks, links, scale = flex[:, 0], coupling[:, 0], weight
    lam2, resid2, direc2 = lam[:, 0], resid[:, 0], direc[:, 0]
    chain = lax.axis_size("sub")
    place = lax.axis_index("sub").astype(jnp.int32).reshape(1)

    pay = pl.pallas_call(
        primal_kernel,
        out_shape=jax.ShapeDtypeStruct((3 * C + 8, L), F32),
        in_specs=[vmem()] * 4,
        out_specs=vmem(),
        name="primal",
        compiler_params=pltpu.CompilerParams(vmem_limit_bytes=16 * MIB),
        cost_estimate=pl.CostEstimate(flops=200_000_000, bytes_accessed=3 * MIB, transcendentals=0),
    )(direc2, links, corner_map, coarse_factor[0])
    others = [exchange(pay, "grp", 4, lambda i, m=m: i ^ m) for m in (1, 3, 2)]

    local = pl.pallas_call(
        local_kernel,
        grid=(2, 4),
        out_shape=jax.ShapeDtypeStruct((2, N, L), F32),
        in_specs=[
            pl.BlockSpec((1, L, N), lambda s, r: (s, r, 0)),
            pl.BlockSpec((1, N, L), lambda s, r: (s, 0, 0)),
        ],
        out_specs=pl.BlockSpec((1, L, L), lambda s, r: (s, r, 0)),
        scratch_shapes=[pltpu.VMEM((N, L), BF16)] * 2,
        name="local",
        compiler_params=pltpu.CompilerParams(vmem_limit_bytes=24 * MIB),
        cost_estimate=pl.CostEstimate(flops=3_300_000_000, bytes_accessed=12 * MIB, transcendentals=0),
    )(blocks, direc2)

    packed = jax.ShapeDtypeStruct((HALF + 8, L), F32)
    image, cross, near = pl.pallas_call(
        image_kernel,
        out_shape=(jax.ShapeDtypeStruct((2, N, L), F32), packed, packed),
        in_specs=[smem()] + [vmem()] * 7,
        out_specs=(vmem(), vmem(), vmem()),
        scratch_shapes=[pltpu.VMEM((N, L), BF16)] * 2,
        name="image",
        compiler_params=pltpu.CompilerParams(vmem_limit_bytes=24 * MIB),
    )(place, local, pay, *others, links, partner)

    def across(i):
        j = i + 1 if i % 2 else i - 1
        return j if 0 <= j < chain else None

    got_cross = exchange(cross, "sub", chain, across)
    got_near = exchange(near, "sub", chain, lambda i: i ^ 1)

    part, sums = pl.pallas_call(
        inner_kernel,
        out_shape=(jax.ShapeDtypeStruct((2, N, L), F32), jax.ShapeDtypeStruct((3, 8, L), F32)),
        in_specs=[smem()] + [vmem()] * 5,
        out_specs=(vmem(), vmem()),
        scratch_shapes=[pltpu.VMEM((N, L), BF16)] * 2,
        name="inner",
        compiler_params=pltpu.CompilerParams(vmem_limit_bytes=24 * MIB),
        cost_estimate=pl.CostEstimate(flops=2_200_000_000, bytes_accessed=8 * MIB, transcendentals=0),
    )(place, image, direc2, resid2, scale, partner)

    jump, total = pl.pallas_call(
        outer_kernel,
        out_shape=(jax.ShapeDtypeStruct((2, N, L), F32), jax.ShapeDtypeStruct((8, L), F32)),
        in_specs=[smem()] + [vmem()] * 5,
        out_specs=(vmem(), vmem()),
        name="outer",
        compiler_params=pltpu.CompilerParams(vmem_limit_bytes=24 * MIB),
    )(place, part, got_cross, got_near, scale, sums)

    total = total + exchange(total, "sub", chain, lambda i: i ^ 1)
    for m in (1, 3):
        total = total + exchange(total, "grp", 4, lambda i, m=m: i ^ m)
    for bit in (2, 8):
        for m in (1, 3):
            total = total + exchange(total, "sub", chain, lambda i, m=m, bit=bit: i ^ (m * bit))

    def rows(s, r):
        return (s, r, 0)

    spec = pl.BlockSpec((1, L, L), rows)
    whole = jax.ShapeDtypeStruct((2, N, L), F32)
    lam_next, resid_next, direc_next, ratio = pl.pallas_call(
        final_kernel,
        grid=(2, 4),
        out_shape=(whole, whole, whole, jax.ShapeDtypeStruct((1, L), F32)),
        in_specs=[
            pl.BlockSpec((8, L), lambda s, r: (0, 0)),
            pl.BlockSpec((1, 1, L), lambda s, r: (s, 0, r)),
            spec, spec, spec, spec,
        ],
        out_specs=(spec, spec, spec, pl.BlockSpec((1, L), lambda s, r: (0, 0))),
        name="final",
        compiler_params=pltpu.CompilerParams(vmem_limit_bytes=16 * MIB),
    )(total, scale, lam2, resid2, direc2, jump)
    return (lam_next[:, None], resid_next[:, None], direc_next[:, None], ratio[0])


def solution(mesh):
    placed = (
        P("sub", "grp", None, None),
        P("sub", "grp", None, None),
        P("sub", "grp", None),
        P("sub", "grp"),
        P("sub", "grp", None),
        P("sub", "grp", None),
        P("sub", "grp", None),
        P("sub", "grp", None, None),
        P("sub", "grp", None, None),
        P("sub", "grp", None, None),
    )
    return jax.shard_map(
        per_device,
        mesh=mesh,
        in_specs=placed,
        out_specs=(
            P("sub", "grp", None, None),
            P("sub", "grp", None, None),
            P("sub", "grp", None, None),
            P(),
        ),
        check_vma=False,
    )
```

time: 307 us -> 68.7 us (0.22)
  blocking collectives: 141 us -> 0 us
  waiting for transfers between devices: 77.9 us -> 12.7 us
  starting transfers between devices: 2.91 us -> 28.9 us
  local copies, waits for them, and re-layouts: 28.9 us -> 7.55 us
  matrix products: 20.9 us -> 0 us
  other arithmetic: 19 us -> 0.02 us
  Pallas kernels: 0 us -> 18.4 us
  between operations: 14.2 us -> 0.76 us
    psum x2 -> x0, blocking collectives: 141 us -> none  [the longest x1 78.3 us: per_device(): lax.psum((jnp.sum(residual * precond, axis=(0, 1)), jnp.sum(direction * j...]
    psum x2 -> x0, waiting for transfers between devices: 73.1 us -> none  [the longest x1 44.2 us: per_device(): coarse_rhs = lax.psum(partial_rhs, 'grp')]
    ppermute x2 -> x12, starting transfers between devices: 2.83 us -> 28.9 us  [exchange(): return lax.ppermute(x, axes, pairs)]
    dot_general x7 -> x0, matrix products: 20.9 us -> none  [the longest x1 10.6 us: per_device(): jnp.einsum('sij,sjl->sil', blocks, masked, precision=highest, preferred_e...]
    pallas_call x0 -> x6, Pallas kernels: none -> 18.4 us  [the longest x1 4.99 us: per_device(): pl.pallas_call(local_kernel, grid=(2, 4), out_shape=jax.ShapeDtypeStruct(...]
    gather x2 -> x0, local copies, waits for them, and re-layouts: 13.7 us -> none  [per_device(): jnp.take(window.reshape(-1, load_count), offset.reshape(-1), axis=0)]
    reduce_sum x2 -> x0, other arithmetic: 8.57 us -> none  [the longest x1 4.94 us: per_device(): jnp.sum(resid_next * precond_next, axis=(0, 1))]
    ppermute x2 -> x12, waiting for transfers between devices: 4.72 us -> 12.7 us  [exchange(): return lax.ppermute(x, axes, pairs)]
  transfers between devices with their start and end apart: 4 -> 12, of which waited for: 4 -> 8; matrix products, arithmetic and copies ran while one was open for 4% -> 0% of each run, Pallas kernels for 0% -> 11%
where the time goes in v1:
time: 68.7 us; the launch traced here: 68.4 us
  starting transfers between devices  28.9 us (42%)
  Pallas kernels  18.4 us (27%)
  waiting for transfers between devices  12.7 us (18%)
  local copies, waits for them, and re-layouts  7.55 us (11%)
  between operations  0.76 us (1%)
    ppermute x12, starting transfers between devices, exchange(): return lax.ppermute(x, axes, pairs)  28.9 us
    ppermute x12, waiting for transfers between devices, exchange(): return lax.ppermute(x, axes, pairs)  12.7 us
    unnamed x22, local copies, waits for them, and re-layouts  7.55 us
    pallas_call x1, Pallas kernels, per_device(): pl.pallas_call(local_kernel, grid=(2, 4), out_shape=jax.ShapeDtypeStruct(...  4.99 us
    pallas_call x1, Pallas kernels, per_device(): pl.pallas_call(image_kernel, out_shape=(jax.ShapeDtypeStruct((2, N, L), F...  4.52 us
    pallas_call x1, Pallas kernels, per_device(): pl.pallas_call(final_kernel, grid=(2, 4), out_shape=(whole, whole, whole,...  4.08 us
    pallas_call x1, Pallas kernels, per_device(): pl.pallas_call(inner_kernel, out_shape=(jax.ShapeDtypeStruct((2, N, L), F...  2.71 us
  transfers between devices with their start and end apart: 12, of which 8 were waited for; matrix products, arithmetic and copies ran while one was open for 0% of the time, Pallas kernels for 11%

profile of v1, /device:TPU:0, one launch (start us, length us, event | category | flops | bytes accessed | tf_op | source)
XLA Modules:
  0.0 68.4 jit_solution(10851180207348178683)
XLA Ops:
  0.6 0.0 copy-start
  0.6 1.6 %copy-done = f32[2,1,1024,256]{3,2,1,0:T(8,128)S(1)} copy-done((f32[2,1,1024,256]{3,2,1,0:T(8,128)S(1)}, f32[2,1,1024,256]{3,2,1,0:T(8,128)}, u32[]{:S(2)}) %copy-start) | copy-done | bytes 2097176
  2.2 0.0 copy-start.5
  2.2 1.0 %copy-done.5 = f32[2,1,64,1024]{3,2,1,0:T(8,128)S(1)} copy-done((f32[2,1,64,1024]{3,2,1,0:T(8,128)S(1)}, f32[2,1,64,1024]{3,2,1,0:T(8,128)}, u32[]{:S(2)}) %copy-start.5) | copy-done | bytes 524312
  3.3 0.0 copy-start.7
  3.3 0.8 %copy-done.7 = f32[1,64,256]{2,1,0:T(8,128)S(1)} copy-done((f32[1,64,256]{2,1,0:T(8,128)S(1)}, f32[1,64,256]{2,1,0:T(8,128)}, u32[]{:S(2)}) %copy-start.7) | copy-done | bytes 65560
  4.1 0.0 copy-start.10
  4.1 0.7 copy-done.10
  4.8 0.7 %primal.1.pay_ref = f32[200,256]{1,0:T(8,128)S(1)} custom-call(f32[2,1024,256]{2,1,0:T(8,128)S(1)} %bitcast.17, f32[2,64,1024]{2,1,0:T(8,128)S(1)} %bitcast.25, s32[2,1,64]{2,1,0:T(1,128)S(1)} %copy-done.10, f32[64,256]{1,0:T(8,128)S(1)} %bitcast.27), custom_call_target="tpu_custom_call" | custom-call | flops 200000000 | bytes 3145728 | tf_op jit(solution)/shard_map/primal/pallas_call | solution.py:231
  5.5 3.2 %collective-permute-start.2 = (f32[200,256]{1,0:T(8,128)S(1)}, f32[200,256]{1,0:T(8,128)S(1)}, u32[]{:S(2)}, u32[]{:S(2)}) collective-permute-start(f32[200,256]{1,0:T(8,128)S(1)} %primal.1.pay_ref), channel_id=1, source_target_pairs={{0,2},{1,3},{2,0},{3,1},{4,6},{5,7},{6,4},{7,5},{8,10},{9,11},{10,... | collective-permute-start | bytes 614408 | tf_op jit(solution)/shard_map/ppermute | solution.py:219
  8.7 1.1 %collective-permute-start.1 = (f32[200,256]{1,0:T(8,128)S(1)}, f32[200,256]{1,0:T(8,128)S(1)}, u32[]{:S(2)}, u32[]{:S(2)}) collective-permute-start(f32[200,256]{1,0:T(8,128)S(1)} %primal.1.pay_ref), channel_id=1, source_target_pairs={{0,3},{1,2},{2,1},{3,0},{4,7},{5,6},{6,5},{7,4},{8,11},{9,10},{10,... | collective-permute-start | bytes 614408 | tf_op jit(solution)/shard_map/ppermute | solution.py:219
  9.8 0.0 collective-permute-start
  9.9 0.0 copy-done.1
  9.9 3.4 %copy-done.2 = f32[2,1,1024,1024]{3,2,1,0:T(8,128)S(1)} copy-done((f32[2,1,1024,1024]{3,2,1,0:T(8,128)S(1)}, f32[2,1,1024,1024]{3,2,1,0:T(8,128)}, u32[]{:S(2)}) %copy-start.2) | copy-done | bytes 8388632
  13.2 5.0 %local.1.local_ref = f32[2,1024,256]{2,1,0:T(8,128)S(1)} custom-call(f32[2,1024,1024]{2,1,0:T(8,128)S(1)} %bitcast.21, f32[2,1024,256]{2,1,0:T(8,128)S(1)} %bitcast.18), custom_call_target="tpu_custom_call" | custom-call | flops 3300000000 | bytes 12582912 | tf_op jit(solution)/shard_map/local/pallas_call | solution.py:242
  18.2 0.0 copy-start.3
  18.2 0.0 copy-start.8
  18.3 0.0 collective-permute-done.2.three_ref
  18.3 0.0 collective-permute-done.1.two_ref
  18.3 0.2 collective-permute-done.one_ref
  18.5 0.0 copy-done.6
  18.5 0.0 copy-done.9
  18.5 4.5 %image.1 = (f32[2,1024,256]{2,1,0:T(8,128)S(1)}, f32[520,256]{1,0:T(8,128)S(1)}, f32[520,256]{1,0:T(8,128)S(1)}) custom-call(s32[1]{0:T(128)} %bitcast.place_ref, f32[2,1024,256]{2,1,0:T(8,128)S(1)} %local.1.local_ref, f32[200,256]{1,0:T(8,128)S(1)} %primal.1.pay_ref, f32[200,256]{1,0:T(8,128)S(1)} %collective-permute-done.one_ref, ...), custom_call_target="tpu_custom_call" | custom-call | tf_op jit(solution)/shard_map/image/pallas_call | solution.py:258
  23.1 0.7 %collective-permute-start.3 = (f32[520,256]{1,0:T(8,128)S(1)}, f32[520,256]{1,0:T(8,128)S(1)}, u32[]{:S(2)}, u32[]{:S(2)}) collective-permute-start(f32[520,256]{1,0:T(8,128)S(1)} %get-tuple-element.17), channel_id=1, source_target_pairs={{4,8},{8,4},{12,16},{16,12},{20,24},{24,20},{28,32},{32,28},{36,40... | collective-permute-start | bytes 1597448 | tf_op jit(solution)/shard_map/ppermute | solution.py:219
  23.8 3.3 %collective-permute-start.4 = (f32[520,256]{1,0:T(8,128)S(1)}, f32[520,256]{1,0:T(8,128)S(1)}, u32[]{:S(2)}, u32[]{:S(2)}) collective-permute-start(f32[520,256]{1,0:T(8,128)S(1)} %get-tuple-element.18), channel_id=1, source_target_pairs={{0,4},{4,0},{8,12},{12,8},{16,20},{20,16},{24,28},{28,24},{32,36},... | collective-permute-start | bytes 1597448 | tf_op jit(solution)/shard_map/ppermute | solution.py:219
  27.1 0.0 copy-done.3
  27.1 0.0 copy-done.8
  27.1 2.7 %inner.1 = (f32[2,1024,256]{2,1,0:T(8,128)S(1)}, f32[3,8,256]{2,1,0:T(8,128)S(1)}) custom-call(s32[1]{0:T(128)} %bitcast.place_ref, f32[2,1024,256]{2,1,0:T(8,128)S(1)} %get-tuple-element.15.image_ref, f32[2,1024,256]{2,1,0:T(8,128)S(1)} %bitcast.19, f32[2,1024,256]{2,1,0:T(8,128)S(1)} %bitcast.22, f32[2,1,1024]{2,1,0:T(1,128)S(1)} %copy-done.8, ...), custom_call_target="tpu_custom_call" | custom-call | flops 2200000000 | bytes 8388608 | tf_op jit(solution)/shard_map/inner/pallas_call | solution.py:275
  29.8 0.0 copy-start.4
  29.8 0.0 collective-permute-done.3.cross_ref
  29.8 0.0 collective-permute-done.4.near_ref
  29.8 1.4 %outer.1 = (f32[2,1024,256]{2,1,0:T(8,128)S(1)}, f32[8,256]{1,0:T(8,128)S(1)}) custom-call(s32[1]{0:T(128)} %bitcast.place_ref, f32[2,1024,256]{2,1,0:T(8,128)S(1)} %get-tuple-element.16.part_ref, f32[520,256]{1,0:T(8,128)S(1)} %collective-permute-done.3.cross_ref, f32[520,256]{1,0:T(8,128)S(1)} %collective-permute-done.4.near_ref, ...), custom_call_target="tpu_custom_call" | custom-call | tf_op jit(solution)/shard_map/outer/pallas_call | solution.py:286
  31.2 4.2 %collective-permute-start.5 = (f32[8,256]{1,0:T(8,128)S(1)}, f32[8,256]{1,0:T(8,128)S(1)}, u32[]{:S(2)}, u32[]{:S(2)}) collective-permute-start(f32[8,256]{1,0:T(8,128)S(1)} %get-tuple-element.20), channel_id=1, source_target_pairs={{0,4},{4,0},{8,12},{12,8},{16,20},{20,16},{24,28},{28,24},{32,36},... | collective-permute-start | bytes 24584 | tf_op jit(solution)/shard_map/ppermute | solution.py:219
  35.4 0.8 %collective-permute-done.5 = f32[8,256]{1,0:T(8,128)S(1)} collective-permute-done((f32[8,256]{1,0:T(8,128)S(1)}, f32[8,256]{1,0:T(8,128)S(1)}, u32[]{:S(2)}, u32[]{:S(2)}) %collective-permute-start.5) | collective-permute-done | bytes 8224 | tf_op jit(solution)/shard_map/ppermute | solution.py:219
  36.2 1.8 %collective-permute-start.6 = (f32[8,256]{1,0:T(8,128)S(1)}, f32[8,256]{1,0:T(8,128)S(1)}, u32[]{:S(2)}, u32[]{:S(2)}) collective-permute-start(f32[8,256]{1,0:T(8,128)S(1)} %add.21), channel_id=1, source_target_pairs={{0,1},{1,0},{2,3},{3,2},{4,5},{5,4},{6,7},{7,6},{8,9},{9,8},{10,11... | collective-permute-start | bytes 24584 | tf_op jit(solution)/shard_map/ppermute | solution.py:219
  38.0 1.8 %collective-permute-done.6 = f32[8,256]{1,0:T(8,128)S(1)} collective-permute-done((f32[8,256]{1,0:T(8,128)S(1)}, f32[8,256]{1,0:T(8,128)S(1)}, u32[]{:S(2)}, u32[]{:S(2)}) %collective-permute-start.6) | collective-permute-done | bytes 8224 | tf_op jit(solution)/shard_map/ppermute | solution.py:219
  39.9 2.6 %collective-permute-start.7 = (f32[8,256]{1,0:T(8,128)S(1)}, f32[8,256]{1,0:T(8,128)S(1)}, u32[]{:S(2)}, u32[]{:S(2)}) collective-permute-start(f32[8,256]{1,0:T(8,128)S(1)} %add.22), channel_id=1, source_target_pairs={{0,3},{1,2},{2,1},{3,0},{4,7},{5,6},{6,5},{7,4},{8,11},{9,10},{10,... | collective-permute-start | bytes 24584 | tf_op jit(solution)/shard_map/ppermute | solution.py:219
  42.5 2.2 %collective-permute-done.7 = f32[8,256]{1,0:T(8,128)S(1)} collective-permute-done((f32[8,256]{1,0:T(8,128)S(1)}, f32[8,256]{1,0:T(8,128)S(1)}, u32[]{:S(2)}, u32[]{:S(2)}) %collective-permute-start.7) | collective-permute-done | bytes 8224 | tf_op jit(solution)/shard_map/ppermute | solution.py:219
  44.7 2.0 %collective-permute-start.8 = (f32[8,256]{1,0:T(8,128)S(1)}, f32[8,256]{1,0:T(8,128)S(1)}, u32[]{:S(2)}, u32[]{:S(2)}) collective-permute-start(f32[8,256]{1,0:T(8,128)S(1)} %add.23), channel_id=1, source_target_pairs={{0,8},{4,12},{8,0},{12,4},{16,24},{20,28},{24,16},{28,20},{32,40},... | collective-permute-start | bytes 24584 | tf_op jit(solution)/shard_map/ppermute | solution.py:219
  46.7 1.7 %collective-permute-done.8 = f32[8,256]{1,0:T(8,128)S(1)} collective-permute-done((f32[8,256]{1,0:T(8,128)S(1)}, f32[8,256]{1,0:T(8,128)S(1)}, u32[]{:S(2)}, u32[]{:S(2)}) %collective-permute-start.8) | collective-permute-done | bytes 8224 | tf_op jit(solution)/shard_map/ppermute | solution.py:219
  48.4 5.7 %collective-permute-start.9 = (f32[8,256]{1,0:T(8,128)S(1)}, f32[8,256]{1,0:T(8,128)S(1)}, u32[]{:S(2)}, u32[]{:S(2)}) collective-permute-start(f32[8,256]{1,0:T(8,128)S(1)} %add.24), channel_id=1, source_target_pairs={{0,24},{4,28},{8,16},{12,20},{16,8},{20,12},{24,0},{28,4},{32,56},... | collective-permute-start | bytes 24584 | tf_op jit(solution)/shard_map/ppermute | solution.py:219
  54.1 1.6 %collective-permute-done.9 = f32[8,256]{1,0:T(8,128)S(1)} collective-permute-done((f32[8,256]{1,0:T(8,128)S(1)}, f32[8,256]{1,0:T(8,128)S(1)}, u32[]{:S(2)}, u32[]{:S(2)}) %collective-permute-start.9) | collective-permute-done | bytes 8224 | tf_op jit(solution)/shard_map/ppermute | solution.py:219
  55.8 1.6 %collective-permute-start.10 = (f32[8,256]{1,0:T(8,128)S(1)}, f32[8,256]{1,0:T(8,128)S(1)}, u32[]{:S(2)}, u32[]{:S(2)}) collective-permute-start(f32[8,256]{1,0:T(8,128)S(1)} %add.25), channel_id=1, source_target_pairs={{0,32},{4,36},{8,40},{12,44},{16,48},{20,52},{24,56},{28,60},{32,0... | collective-permute-start | bytes 24584 | tf_op jit(solution)/shard_map/ppermute | solution.py:219
  57.4 2.1 %collective-permute-done.10 = f32[8,256]{1,0:T(8,128)S(1)} collective-permute-done((f32[8,256]{1,0:T(8,128)S(1)}, f32[8,256]{1,0:T(8,128)S(1)}, u32[]{:S(2)}, u32[]{:S(2)}) %collective-permute-start.10) | collective-permute-done | bytes 8224 | tf_op jit(solution)/shard_map/ppermute | solution.py:219
  59.4 2.7 %collective-permute-start.11 = (f32[8,256]{1,0:T(8,128)S(1)}, f32[8,256]{1,0:T(8,128)S(1)}, u32[]{:S(2)}, u32[]{:S(2)}) collective-permute-start(f32[8,256]{1,0:T(8,128)S(1)} %add.26), channel_id=1, source_target_pairs={{0,96},{4,100},{8,104},{12,108},{16,112},{20,116},{24,120},{28,124... | collective-permute-start | bytes 24584 | tf_op jit(solution)/shard_map/ppermute | solution.py:219
  62.1 2.2 %collective-permute-done.11 = f32[8,256]{1,0:T(8,128)S(1)} collective-permute-done((f32[8,256]{1,0:T(8,128)S(1)}, f32[8,256]{1,0:T(8,128)S(1)}, u32[]{:S(2)}, u32[]{:S(2)}) %collective-permute-start.11) | collective-permute-done | bytes 8224 | tf_op jit(solution)/shard_map/ppermute | solution.py:219
  64.3 0.0 copy-done.4
  64.3 4.1 %final.1 = (f32[2,1024,256]{2,1,0:T(8,128)}, f32[2,1024,256]{2,1,0:T(8,128)}, f32[2,1024,256]{2,1,0:T(8,128)}, f32[1,256]{1,0:T(1,128)}) custom-call(f32[8,256]{1,0:T(8,128)S(1)} %add.27.total_ref, f32[2,1,1024]{2,1,0:T(1,128)S(1)} %copy-done.8, f32[2,1024,256]{2,1,0:T(8,128)S(1)} %bitcast.24, f32[2,1024,256]{2,1,0:T(8,128)S(1)} %bitcast.23, ...), custom_call_target="tpu_custom_call" | custom-call | tf_op jit(solution)/shard_map/final/pallas_call | solution.py:307
  (11 shorter events, 0.0 us)
Async XLA Ops:
  0.6 1.6 %copy-start = (f32[2,1,1024,256]{3,2,1,0:T(8,128)S(1)}, f32[2,1,1024,256]{3,2,1,0:T(8,128)}, u32[]{:S(2)}) copy-start(f32[2,1,1024,256]{3,2,1,0:T(8,128)} %param.18) | copy-start | bytes 6291460
  2.2 1.0 %copy-start.5 = (f32[2,1,64,1024]{3,2,1,0:T(8,128)S(1)}, f32[2,1,64,1024]{3,2,1,0:T(8,128)}, u32[]{:S(2)}) copy-start(f32[2,1,64,1024]{3,2,1,0:T(8,128)} %param.11) | copy-start | bytes 1572868
  3.3 0.8 %copy-start.7 = (f32[1,64,256]{2,1,0:T(8,128)S(1)}, f32[1,64,256]{2,1,0:T(8,128)}, u32[]{:S(2)}) copy-start(f32[1,64,256]{2,1,0:T(8,128)} %param.15) | copy-start | bytes 196612
  4.1 0.7 copy-start.10
  4.8 5.1 %copy-start.1 = (f32[2,1,1024,256]{3,2,1,0:T(8,128)S(1)}, f32[2,1,1024,256]{3,2,1,0:T(8,128)}, u32[]{:S(2)}) copy-start(f32[2,1,1024,256]{3,2,1,0:T(8,128)} %param.18) | copy-start | bytes 6291460
  5.5 12.7 %collective-permute-start.2 = (f32[200,256]{1,0:T(8,128)S(1)}, f32[200,256]{1,0:T(8,128)S(1)}, u32[]{:S(2)}, u32[]{:S(2)}) collective-permute-start(f32[200,256]{1,0:T(8,128)S(1)} %primal.1.pay_ref), channel_id=1, source_target_pairs={{0,2},{1,3},{2,0},{3,1},{4,6},{5,7},{6,4},{7,5},{8,10},{9,11},{10,... | collective-permute-start | bytes 614408 | tf_op jit(solution)/shard_map/ppermute | solution.py:219
  8.7 9.6 %collective-permute-start.1 = (f32[200,256]{1,0:T(8,128)S(1)}, f32[200,256]{1,0:T(8,128)S(1)}, u32[]{:S(2)}, u32[]{:S(2)}) collective-permute-start(f32[200,256]{1,0:T(8,128)S(1)} %primal.1.pay_ref), channel_id=1, source_target_pairs={{0,3},{1,2},{2,1},{3,0},{4,7},{5,6},{6,5},{7,4},{8,11},{9,10},{10,... | collective-permute-start | bytes 614408 | tf_op jit(solution)/shard_map/ppermute | solution.py:219
  9.8 8.7 %collective-permute-start = (f32[200,256]{1,0:T(8,128)S(1)}, f32[200,256]{1,0:T(8,128)S(1)}, u32[]{:S(2)}, u32[]{:S(2)}) collective-permute-start(f32[200,256]{1,0:T(8,128)S(1)} %primal.1.pay_ref), channel_id=1, source_target_pairs={{0,1},{1,0},{2,3},{3,2},{4,5},{5,4},{6,7},{7,6},{8,9},{9,8},{10,11... | collective-permute-start | bytes 614408 | tf_op jit(solution)/shard_map/ppermute | solution.py:219
  9.9 3.4 %copy-start.2 = (f32[2,1,1024,1024]{3,2,1,0:T(8,128)S(1)}, f32[2,1,1024,1024]{3,2,1,0:T(8,128)}, u32[]{:S(2)}) copy-start(f32[2,1,1024,1024]{3,2,1,0:T(8,128)} %param.10) | copy-start | bytes 25165828
  13.2 5.3 %copy-start.6 = (f32[2,1,64,1024]{3,2,1,0:T(8,128)S(1)}, f32[2,1,64,1024]{3,2,1,0:T(8,128)}, u32[]{:S(2)}) copy-start(f32[2,1,64,1024]{3,2,1,0:T(8,128)} %param.11) | copy-start | bytes 1572868
  13.2 5.3 %copy-start.9 = (s32[2,1,1024]{2,1,0:T(1,128)S(1)}, s32[2,1,1024]{2,1,0:T(1,128)}, u32[]{:S(2)}) copy-start(s32[2,1,1024]{2,1,0:T(1,128)} %partner_ref.3) | copy-start | bytes 24580
  18.2 8.8 %copy-start.3 = (f32[2,1,1024,256]{3,2,1,0:T(8,128)S(1)}, f32[2,1,1024,256]{3,2,1,0:T(8,128)}, u32[]{:S(2)}) copy-start(f32[2,1,1024,256]{3,2,1,0:T(8,128)} %param.17) | copy-start | bytes 6291460
  18.2 8.8 %copy-start.8 = (f32[2,1,1024]{2,1,0:T(1,128)S(1)}, f32[2,1,1024]{2,1,0:T(1,128)}, u32[]{:S(2)}) copy-start(f32[2,1,1024]{2,1,0:T(1,128)} %weight_ref.5) | copy-start | bytes 24580
  23.1 6.8 %collective-permute-start.3 = (f32[520,256]{1,0:T(8,128)S(1)}, f32[520,256]{1,0:T(8,128)S(1)}, u32[]{:S(2)}, u32[]{:S(2)}) collective-permute-start(f32[520,256]{1,0:T(8,128)S(1)} %get-tuple-element.17), channel_id=1, source_target_pairs={{4,8},{8,4},{12,16},{16,12},{20,24},{24,20},{28,32},{32,28},{36,40... | collective-permute-start | bytes 1597448 | tf_op jit(solution)/shard_map/ppermute | solution.py:219
  23.8 6.1 %collective-permute-start.4 = (f32[520,256]{1,0:T(8,128)S(1)}, f32[520,256]{1,0:T(8,128)S(1)}, u32[]{:S(2)}, u32[]{:S(2)}) collective-permute-start(f32[520,256]{1,0:T(8,128)S(1)} %get-tuple-element.18), channel_id=1, source_target_pairs={{0,4},{4,0},{8,12},{12,8},{16,20},{20,16},{24,28},{28,24},{32,36},... | collective-permute-start | bytes 1597448 | tf_op jit(solution)/shard_map/ppermute | solution.py:219
  29.8 34.5 %copy-start.4 = (f32[2,1,1024,256]{3,2,1,0:T(8,128)S(1)}, f32[2,1,1024,256]{3,2,1,0:T(8,128)}, u32[]{:S(2)}) copy-start(f32[2,1,1024,256]{3,2,1,0:T(8,128)} %param.16) | copy-start | bytes 6291460
  31.2 5.0 %collective-permute-start.5 = (f32[8,256]{1,0:T(8,128)S(1)}, f32[8,256]{1,0:T(8,128)S(1)}, u32[]{:S(2)}, u32[]{:S(2)}) collective-permute-start(f32[8,256]{1,0:T(8,128)S(1)} %get-tuple-element.20), channel_id=1, source_target_pairs={{0,4},{4,0},{8,12},{12,8},{16,20},{20,16},{24,28},{28,24},{32,36},... | collective-permute-start | bytes 24584 | tf_op jit(solution)/shard_map/ppermute | solution.py:219
  36.2 3.7 %collective-permute-start.6 = (f32[8,256]{1,0:T(8,128)S(1)}, f32[8,256]{1,0:T(8,128)S(1)}, u32[]{:S(2)}, u32[]{:S(2)}) collective-permute-start(f32[8,256]{1,0:T(8,128)S(1)} %add.21), channel_id=1, source_target_pairs={{0,1},{1,0},{2,3},{3,2},{4,5},{5,4},{6,7},{7,6},{8,9},{9,8},{10,11... | collective-permute-start | bytes 24584 | tf_op jit(solution)/shard_map/ppermute | solution.py:219
  39.9 4.9 %collective-permute-start.7 = (f32[8,256]{1,0:T(8,128)S(1)}, f32[8,256]{1,0:T(8,128)S(1)}, u32[]{:S(2)}, u32[]{:S(2)}) collective-permute-start(f32[8,256]{1,0:T(8,128)S(1)} %add.22), channel_id=1, source_target_pairs={{0,3},{1,2},{2,1},{3,0},{4,7},{5,6},{6,5},{7,4},{8,11},{9,10},{10,... | collective-permute-start | bytes 24584 | tf_op jit(solution)/shard_map/ppermute | solution.py:219
  44.7 3.7 %collective-permute-start.8 = (f32[8,256]{1,0:T(8,128)S(1)}, f32[8,256]{1,0:T(8,128)S(1)}, u32[]{:S(2)}, u32[]{:S(2)}) collective-permute-start(f32[8,256]{1,0:T(8,128)S(1)} %add.23), channel_id=1, source_target_pairs={{0,8},{4,12},{8,0},{12,4},{16,24},{20,28},{24,16},{28,20},{32,40},... | collective-permute-start | bytes 24584 | tf_op jit(solution)/shard_map/ppermute | solution.py:219
  48.4 7.4 %collective-permute-start.9 = (f32[8,256]{1,0:T(8,128)S(1)}, f32[8,256]{1,0:T(8,128)S(1)}, u32[]{:S(2)}, u32[]{:S(2)}) collective-permute-start(f32[8,256]{1,0:T(8,128)S(1)} %add.24), channel_id=1, source_target_pairs={{0,24},{4,28},{8,16},{12,20},{16,8},{20,12},{24,0},{28,4},{32,56},... | collective-permute-start | bytes 24584 | tf_op jit(solution)/shard_map/ppermute | solution.py:219
  55.8 3.7 %collective-permute-start.10 = (f32[8,256]{1,0:T(8,128)S(1)}, f32[8,256]{1,0:T(8,128)S(1)}, u32[]{:S(2)}, u32[]{:S(2)}) collective-permute-start(f32[8,256]{1,0:T(8,128)S(1)} %add.25), channel_id=1, source_target_pairs={{0,32},{4,36},{8,40},{12,44},{16,48},{20,52},{24,56},{28,60},{32,0... | collective-permute-start | bytes 24584 | tf_op jit(solution)/shard_map/ppermute | solution.py:219
  59.4 4.9 %collective-permute-start.11 = (f32[8,256]{1,0:T(8,128)S(1)}, f32[8,256]{1,0:T(8,128)S(1)}, u32[]{:S(2)}, u32[]{:S(2)}) collective-permute-start(f32[8,256]{1,0:T(8,128)S(1)} %add.26), channel_id=1, source_target_pairs={{0,96},{4,100},{8,104},{12,108},{16,112},{20,116},{24,120},{28,124... | collective-permute-start | bytes 24584 | tf_op jit(solution)/shard_map/ppermute | solution.py:219

commit v2 on v1

v2 whole, which is shorter than its diff:
```python
import functools

import jax
import jax.numpy as jnp
from jax import lax
from jax.experimental import pallas as pl
from jax.experimental.pallas import tpu as pltpu
from jax.sharding import PartitionSpec as P

F32 = jnp.float32
BF16 = jnp.bfloat16
N = 1024
L = 256
C = 64
HALF = 512
NAMES = HALF + 2 * C
STRIP = 512
ROUNDS = N // STRIP
MIB = 1 << 20


def dot(a, b):
    return lax.dot_general(a, b, (((1,), (0,)), ((), ())), preferred_element_type=F32)


def dot_t(a, b):
    return lax.dot_general(a, b, (((0,), (0,)), ((), ())), preferred_element_type=F32)


def split(x):
    high = x.astype(BF16)
    low = (x - high.astype(F32)).astype(BF16)
    return high, low


def iota(shape, dim):
    return lax.broadcasted_iota(jnp.int32, shape, dim)


def one_hot(test):
    return jnp.where(test, 1.0, 0.0).astype(BF16)


def fold(x):
    return jnp.sum(x.reshape(-1, 8, x.shape[-1]), axis=0)


def column(row):
    tall = jnp.transpose(jnp.broadcast_to(row, (128, row.shape[1])))
    return jnp.concatenate([tall, tall], axis=1)


def primal_kernel(direc_hbm, coup_hbm, map_hbm, factor_hbm, pay_ref, direc, coup, corner, sems):
    copies = [
        pltpu.make_async_copy(coup_hbm, coup, sems.at[0]),
        pltpu.make_async_copy(direc_hbm.at[0], direc.at[0], sems.at[1]),
        pltpu.make_async_copy(direc_hbm.at[1], direc.at[1], sems.at[2]),
        pltpu.make_async_copy(map_hbm, corner, sems.at[3]),
        pltpu.make_async_copy(factor_hbm, pay_ref.at[pl.ds(2 * C, C)], sems.at[4]),
    ]
    for copy in copies:
        copy.start()
    pay_ref[3 * C :] = jnp.zeros((8, L), F32)
    copies[0].wait()
    for s in range(2):
        ch, cl = split(coup[s])
        copies[1 + s].wait()
        dh, dl = split(direc[s])
        pay_ref[s * C : (s + 1) * C] = dot(ch, dh) + dot(ch, dl) + dot(cl, dh)
    copies[3].wait()
    for s in range(2):
        pay_ref[3 * C + s : 3 * C + s + 1, 0:C] = corner[s].astype(F32)
    copies[4].wait()


def running_count(mask):
    total = mask.astype(jnp.int32)
    lane = iota(total.shape, 1)
    step = 1
    while step < total.shape[1]:
        total = total + jnp.where(lane >= step, pltpu.roll(total, step, 1), 0)
        step *= 2
    return total


def local_kernel(
    place_ref, flex_hbm, direc_ref, coup_ref, partner_ref,
    local_ref, cross_ref, near_ref, flex, right, high, low, sems,
):
    copies = []
    for s in range(2):
        for r in range(ROUNDS):
            rows = pl.ds(r * STRIP, STRIP)
            copy = pltpu.make_async_copy(
                flex_hbm.at[s, rows], flex.at[s, rows], sems.at[s * ROUNDS + r]
            )
            copy.start()
            copies.append(copy)
    me = place_ref[0]
    odd = lax.rem(me, 2)
    for s in range(2):
        dh, dl = split(direc_ref[s])
        right[0:N] = dh
        right[N : 2 * N] = dl
        right[2 * N :] = dh
        for r in range(ROUNDS):
            rows = slice(r * STRIP, (r + 1) * STRIP)
            copies[s * ROUNDS + r].wait()
            ah, al = split(flex[s, rows])
            out = dot(jnp.concatenate([ah, ah, al], axis=1), right[...])
            local_ref[s, rows] = out
            oh, ol = split(out)
            high[rows] = oh
            low[rows] = ol
        target = partner_ref[s] - (2 * me - 1) * N
        match = (target >= 3 * N) if s else (target < N)
        key = jnp.where(match, running_count(match) - 1, -1)
        name = jnp.where(match, jnp.bitwise_and(target, N - 1) + 1, 0)
        coarse = lax.shift_right_logical(name, 5)
        fine = jnp.bitwise_and(name, 31)
        digits = jnp.concatenate(
            [coarse, fine, jnp.zeros((14, N), jnp.int32)], axis=0
        ).astype(F32).astype(BF16)
        ch, cl = split(coup_ref[s])
        left = jnp.concatenate([ch, cl, digits], axis=0)

        def pack(ref):
            ref[NAMES:] = jnp.zeros((8, L), F32)
            for c in range(2):
                place = one_hot(iota((L, N), 0) + c * L == key)
                ref[c * L : (c + 1) * L] = dot(place, high[...]) + dot(place, low[...])
                extra = lax.dot_general(
                    left, place, (((1,), (1,)), ((), ())), preferred_element_type=F32
                )
                ref[HALF + c * C : HALF + (c + 1) * C] = extra[0:C] + extra[C : 2 * C]
                ref[NAMES + c : NAMES + c + 1] = extra[2 * C : 2 * C + 1] * 32.0 + extra[2 * C + 1 : 2 * C + 2]

        pl.when(odd == s)(functools.partial(pack, cross_ref))
        pl.when(odd != s)(functools.partial(pack, near_ref))


def selector(pay_ref):
    first = pay_ref[3 * C : 3 * C + 1, 0:C]
    second = pay_ref[3 * C + 1 : 3 * C + 2, 0:C]
    both = jnp.concatenate([first, second], axis=1).astype(jnp.int32)
    return one_hot(iota((L, 2 * C), 0) == both)


def coarse_kernel(place_ref, pay_ref, one_ref, two_ref, three_ref, cross_ref, near_ref):
    odd = lax.rem(place_ref[0], 2)
    members = (pay_ref, one_ref, two_ref, three_ref)
    sels, parts = [], []
    for member in members:
        sel = selector(member)
        ph, pl_ = split(member[0 : 2 * C])
        sels += [sel, sel]
        parts += [ph, pl_]
    rhs = dot(jnp.concatenate(sels, axis=1), jnp.concatenate(parts, axis=0))
    factor = jnp.concatenate([m[2 * C : 3 * C] for m in members], axis=0)
    fh, fl = split(factor)
    rh, rl = split(rhs)
    mid = dot(jnp.concatenate([fh, fh, fl], axis=1), jnp.concatenate([rh, rl, rh], axis=0))
    mh, ml = split(mid)
    sol = dot_t(jnp.concatenate([fh, fh, fl], axis=0), jnp.concatenate([mh, ml, mh], axis=0))
    sh, sl = split(sol)
    own = sels[0]
    picked = dot_t(jnp.concatenate([own, own], axis=0), jnp.concatenate([sh, sl], axis=0))

    @pl.when(odd == 0)
    def _():
        cross_ref[...] = picked[0:C]
        near_ref[...] = picked[C:]

    @pl.when(odd == 1)
    def _():
        near_ref[...] = picked[0:C]
        cross_ref[...] = picked[C:]


def inner_kernel(
    place_ref, local_ref, cross_ref, near_ref, coup_ref, direc_ref, resid_ref, weight_ref, partner_ref,
    jump_ref, sums_ref, image_ref, high, low,
):
    me = place_ref[0]
    odd = lax.rem(me, 2) == 1
    old = jnp.zeros((8, L), F32)
    curve = jnp.zeros((8, L), F32)
    mixed = jnp.zeros((8, L), F32)
    for s in range(2):
        ch, cl = split(coup_ref[s])
        qh, ql = split(jnp.where(odd == (s == 1), cross_ref[...], near_ref[...]))
        left = jnp.concatenate([ch, ch, cl], axis=0)
        right = jnp.concatenate([qh, ql, qh], axis=0)
        for r in range(0, N, L):
            image = local_ref[s, r : r + L] + dot_t(left[:, r : r + L], right)
            image_ref[s, r : r + L] = image
            ih, il = split(image)
            high[s, r : r + L] = ih
            low[s, r : r + L] = il
    for s in range(2):
        other = 1 - s
        theirs = partner_ref[other] - (2 * me + s) * N
        mine = partner_ref[s]
        awake = jnp.where(lax.shift_right_arithmetic(mine, 10) != 2 * me + s, 1.0, 0.0)
        for r in range(0, N, L):
            rows = slice(r, r + L)
            place = one_hot(iota((L, N), 0) + r == theirs)
            opposite = dot(place, high[other]) + dot(place, low[other])
            image = image_ref[s, rows]
            jump_ref[s, rows] = column(awake[:, rows]) * image - opposite
            scaled = column(weight_ref[s][:, rows]) * resid_ref[s, rows]
            old = old + fold(scaled * resid_ref[s, rows])
            curve = curve + fold(direc_ref[s, rows] * image)
            mixed = mixed + fold(scaled * image)
    sums_ref[0] = old
    sums_ref[1] = curve
    sums_ref[2] = mixed


def outer_kernel(
    place_ref, part_ref, cross_ref, near_ref, cross_pick_ref, near_pick_ref, weight_ref, sums_ref,
    jump_ref, total_ref,
):
    odd = lax.rem(place_ref[0], 2)
    square = jnp.zeros((8, L), F32)
    for ref, pick_ref, s in ((cross_ref, cross_pick_ref, odd), (near_ref, near_pick_ref, 1 - odd)):
        qh, ql = split(pick_ref[...])
        right = jnp.concatenate([qh, ql, qh], axis=0)
        highs, lows = [], []
        for c in range(2):
            ch, cl = split(ref[HALF + c * C : HALF + (c + 1) * C])
            left = jnp.concatenate([ch, ch, cl], axis=0)
            image_high, image_low = split(ref[c * L : (c + 1) * L] + dot_t(left, right))
            highs.append(image_high)
            lows.append(image_low)
        stacked = jnp.concatenate(highs + lows, axis=0)
        names = [ref[NAMES + c : NAMES + c + 1].astype(jnp.int32) for c in range(2)]
        for r in range(0, N, L):
            places = [one_hot(iota((L, L), 0) + (r + 1) == name) for name in names]
            opposite = dot(jnp.concatenate(places + places, axis=1), stacked)
            jump = part_ref[s, r : r + L] - opposite
            jump_ref[s, r : r + L] = jump
            square = square + fold(column(weight_ref[s][:, r : r + L]) * jump * jump)
    rows = [jnp.sum(x, axis=0, keepdims=True) for x in (sums_ref[0], sums_ref[1], sums_ref[2], square)]
    total_ref[...] = jnp.concatenate(rows + [jnp.zeros((4, L), F32)], axis=0)


def final_kernel(
    total_ref, weight_ref, lam_ref, resid_ref, direc_ref, jump_ref,
    lam_hbm, resid_hbm, direc_hbm, ratio_ref, lam_out, resid_out, direc_out, sems,
):
    old = total_ref[0:1]
    alpha = old / (2.0 * total_ref[1:2])
    new = old + alpha * (alpha * total_ref[3:4] - 4.0 * total_ref[2:3])
    ratio = new / old
    ratio_ref[...] = ratio
    copies = []
    for s in range(2):
        for r in range(4):
            rows = slice(r * L, (r + 1) * L)
            direc = direc_ref[s, rows]
            resid = resid_ref[s, rows] - alpha * jump_ref[s, rows]
            lam_out[s, rows] = lam_ref[s, rows] + alpha * direc
            resid_out[s, rows] = resid
            direc_out[s, rows] = column(weight_ref[s][:, rows]) * resid + ratio * direc
            piece = pl.ds(r * L, L)
            for k, (here, there) in enumerate(
                ((lam_out, lam_hbm), (resid_out, resid_hbm), (direc_out, direc_hbm))
            ):
                copy = pltpu.make_async_copy(
                    here.at[s, piece], there.at[s, piece], sems.at[(s * 4 + r) * 3 + k]
                )
                copy.start()
                copies.append(copy)
    for copy in copies:
        copy.wait()


def vmem():
    return pl.BlockSpec(memory_space=pltpu.VMEM)


def hbm():
    return pl.BlockSpec(memory_space=pltpu.HBM)


def smem():
    return pl.BlockSpec(memory_space=pltpu.SMEM)


def exchange(x, axes, size, route):
    pairs = []
    for i in range(size):
        j = route(i)
        if j is not None:
            pairs.append((i, j))
    return lax.ppermute(x, axes, pairs)


def per_device(
    flex, coupling, weight, iface_size, partner, corner_map, coarse_factor, lam, resid, direc
):
    del iface_size
    blocks, links, scale = flex[:, 0], coupling[:, 0], weight
    lam2, resid2, direc2 = lam[:, 0], resid[:, 0], direc[:, 0]
    chain = lax.axis_size("sub")
    place = lax.axis_index("sub").astype(jnp.int32).reshape(1)

    pay = pl.pallas_call(
        primal_kernel,
        out_shape=jax.ShapeDtypeStruct((3 * C + 8, L), F32),
        in_specs=[hbm()] * 4,
        out_specs=vmem(),
        scratch_shapes=[
            pltpu.VMEM((2, N, L), F32),
            pltpu.VMEM((2, C, N), F32),
            pltpu.VMEM((2, 1, C), jnp.int32),
            pltpu.SemaphoreType.DMA((5,)),
        ],
        name="primal",
        compiler_params=pltpu.CompilerParams(vmem_limit_bytes=16 * MIB),
        cost_estimate=pl.CostEstimate(flops=200_000_000, bytes_accessed=3 * MIB, transcendentals=0),
    )(direc2, links, corner_map, coarse_factor[0])
    others = [exchange(pay, "grp", 4, lambda i, m=m: i ^ m) for m in (1, 3, 2)]

    packed = jax.ShapeDtypeStruct((NAMES + 8, L), F32)
    local, cross, near = pl.pallas_call(
        local_kernel,
        out_shape=(jax.ShapeDtypeStruct((2, N, L), F32), packed, packed),
        in_specs=[smem(), hbm()] + [vmem()] * 3,
        out_specs=(vmem(), vmem(), vmem()),
        scratch_shapes=[
            pltpu.VMEM((2, N, N), F32),
            pltpu.VMEM((3 * N, L), BF16),
            pltpu.VMEM((N, L), BF16),
            pltpu.VMEM((N, L), BF16),
            pltpu.SemaphoreType.DMA((2 * ROUNDS,)),
        ],
        name="local",
        compiler_params=pltpu.CompilerParams(vmem_limit_bytes=32 * MIB),
        cost_estimate=pl.CostEstimate(flops=4_000_000_000, bytes_accessed=12 * MIB, transcendentals=0),
    )(place, blocks, direc2, links, partner)

    def across(i):
        j = i + 1 if i % 2 else i - 1
        return j if 0 <= j < chain else None

    def beside(i):
        return i ^ 1

    got_cross = exchange(cross, "sub", chain, across)
    got_near = exchange(near, "sub", chain, beside)

    piece = jax.ShapeDtypeStruct((C, L), F32)
    cross_pick, near_pick = pl.pallas_call(
        coarse_kernel,
        out_shape=(piece, piece),
        in_specs=[smem()] + [vmem()] * 4,
        out_specs=(vmem(), vmem()),
        name="coarse",
        compiler_params=pltpu.CompilerParams(vmem_limit_bytes=16 * MIB),
        cost_estimate=pl.CostEstimate(flops=500_000_000, bytes_accessed=MIB, transcendentals=0),
    )(place, pay, *others)
    got_cross_pick = exchange(cross_pick, "sub", chain, across)
    got_near_pick = exchange(near_pick, "sub", chain, beside)

    whole = jax.ShapeDtypeStruct((2, N, L), F32)
    part, sums = pl.pallas_call(
        inner_kernel,
        out_shape=(whole, jax.ShapeDtypeStruct((3, 8, L), F32)),
        in_specs=[smem()] + [vmem()] * 8,
        out_specs=(vmem(), vmem()),
        scratch_shapes=[
            pltpu.VMEM((2, N, L), F32),
            pltpu.VMEM((2, N, L), BF16),
            pltpu.VMEM((2, N, L), BF16),
        ],
        name="inner",
        compiler_params=pltpu.CompilerParams(vmem_limit_bytes=24 * MIB),
        cost_estimate=pl.CostEstimate(flops=2_500_000_000, bytes_accessed=8 * MIB, transcendentals=0),
    )(place, local, cross_pick, near_pick, links, direc2, resid2, scale, partner)

    jump, total = pl.pallas_call(
        outer_kernel,
        out_shape=(whole, jax.ShapeDtypeStruct((8, L), F32)),
        in_specs=[smem()] + [vmem()] * 7,
        out_specs=(vmem(), vmem()),
        name="outer",
        compiler_params=pltpu.CompilerParams(vmem_limit_bytes=24 * MIB),
    )(place, part, got_cross, got_near, got_cross_pick, got_near_pick, scale, sums)

    total = total + exchange(total, "sub", chain, beside)
    for m in (1, 3):
        total = total + exchange(total, "grp", 4, lambda i, m=m: i ^ m)
    for bit in (2, 8):
        for m in (1, 3):
            total = total + exchange(total, "sub", chain, lambda i, m=m, bit=bit: i ^ (m * bit))

    lam_next, resid_next, direc_next, ratio = pl.pallas_call(
        final_kernel,
        out_shape=(whole, whole, whole, jax.ShapeDtypeStruct((1, L), F32)),
        in_specs=[vmem()] * 6,
        out_specs=(hbm(), hbm(), hbm(), vmem()),
        scratch_shapes=[pltpu.VMEM((2, N, L), F32)] * 3 + [pltpu.SemaphoreType.DMA((24,))],
        name="final",
        compiler_params=pltpu.CompilerParams(vmem_limit_bytes=24 * MIB),
    )(total, scale, lam2, resid2, direc2, jump)
    return (lam_next[:, None], resid_next[:, None], direc_next[:, None], ratio[0])


def solution(mesh):
    placed = (
        P("sub", "grp", None, None),
        P("sub", "grp", None, None),
        P("sub", "grp", None),
        P("sub", "grp"),
        P("sub", "grp", None),
        P("sub", "grp", None),
        P("sub", "grp", None),
        P("sub", "grp", None, None),
        P("sub", "grp", None, None),
        P("sub", "grp", None, None),
    )
    return jax.shard_map(
        per_device,
        mesh=mesh,
        in_specs=placed,
        out_specs=(
            P("sub", "grp", None, None),
            P("sub", "grp", None, None),
            P("sub", "grp", None, None),
            P(),
        ),
        check_vma=False,
    )
```

time: 68.7 us -> 79.8 us (1.16)
  waiting for transfers between devices: 12.7 us -> 21.4 us
  Pallas kernels: 18.4 us -> 21.6 us
  local copies, waits for them, and re-layouts: 7.55 us -> 6.72 us
    ppermute x12 -> x14, waiting for transfers between devices: 12.7 us -> 21.4 us  [exchange(): return lax.ppermute(x, axes, pairs)]
    pallas_call x5, Pallas kernels: 17.7 us -> 20 us  [the longest x1 10 us: per_device(): pl.pallas_call(local_kernel, out_shape=(jax.ShapeDtypeStruct((2, N, L), F...]
    unnamed x22 -> x18, local copies, waits for them, and re-layouts: 7.55 us -> 6.72 us
    pallas_call x1, Pallas kernels: 0.73 us -> 1.54 us  [per_device(): pl.pallas_call(primal_kernel, out_shape=jax.ShapeDtypeStruct((3 * C + 8,...]
    ppermute x12 -> x14, starting transfers between devices: 28.9 us -> 28.7 us  [exchange(): return lax.ppermute(x, axes, pairs)]
  transfers between devices with their start and end apart: 12 -> 14, of which waited for: 8 -> 10; matrix products, arithmetic and copies ran while one was open for 0% -> 0% of each run, Pallas kernels for 11% -> 8%
where the time goes in v2:
time: 79.8 us; the launch traced here: 79.3 us
  starting transfers between devices  28.7 us (36%)
  Pallas kernels  21.6 us (27%)
  waiting for transfers between devices  21.4 us (27%)
  local copies, waits for them, and re-layouts  6.72 us (8%)
  between operations  0.93 us (1%)
    ppermute x14, starting transfers between devices, exchange(): return lax.ppermute(x, axes, pairs)  28.7 us
    ppermute x14, waiting for transfers between devices, exchange(): return lax.ppermute(x, axes, pairs)  21.4 us
    pallas_call x1, Pallas kernels, per_device(): pl.pallas_call(local_kernel, out_shape=(jax.ShapeDtypeStruct((2, N, L), F...  10 us
    unnamed x18, local copies, waits for them, and re-layouts  6.72 us
    pallas_call x1, Pallas kernels, per_device(): pl.pallas_call(final_kernel, out_shape=(whole, whole, whole, jax.ShapeDty...  3.48 us
    pallas_call x1, Pallas kernels, per_device(): pl.pallas_call(inner_kernel, out_shape=(whole, jax.ShapeDtypeStruct((3, 8...  3.42 us
    pallas_call x1, Pallas kernels, per_device(): pl.pallas_call(outer_kernel, out_shape=(whole, jax.ShapeDtypeStruct((8, L...  1.82 us
  transfers between devices with their start and end apart: 14, of which 10 were waited for; matrix products, arithmetic and copies ran while one was open for 0% of the time, Pallas kernels for 8%

profile of v2, /device:TPU:0, one launch (start us, length us, event | category | flops | bytes accessed | tf_op | source)
XLA Modules:
  0.0 79.3 jit_solution(9940620052808103833)
XLA Ops:
  0.6 0.0 copy-start
  0.6 1.6 %copy-done = f32[2,1,1024,256]{3,2,1,0:T(8,128)S(1)} copy-done((f32[2,1,1024,256]{3,2,1,0:T(8,128)S(1)}, f32[2,1,1024,256]{3,2,1,0:T(8,128)}, u32[]{:S(2)}) %copy-start) | copy-done | bytes 2097176
  2.2 0.0 copy-start.3
  2.2 1.0 %copy-done.3 = f32[2,1,64,1024]{3,2,1,0:T(8,128)S(1)} copy-done((f32[2,1,64,1024]{3,2,1,0:T(8,128)S(1)}, f32[2,1,64,1024]{3,2,1,0:T(8,128)}, u32[]{:S(2)}) %copy-start.3) | copy-done | bytes 524312
  3.3 0.0 copy-start.7
  3.3 3.4 %copy-done.7 = f32[2,1,1024,1024]{3,2,1,0:T(8,128)S(1)} copy-done((f32[2,1,1024,1024]{3,2,1,0:T(8,128)S(1)}, f32[2,1,1024,1024]{3,2,1,0:T(8,128)}, u32[]{:S(2)}) %copy-start.7) | copy-done | bytes 8388632
  6.7 0.0 copy-start.8
  6.7 0.7 copy-done.8
  7.4 10.0 %local.1 = (f32[2,1024,256]{2,1,0:T(8,128)S(1)}, f32[648,256]{1,0:T(8,128)S(1)}, f32[648,256]{1,0:T(8,128)S(1)}) custom-call(s32[1]{0:T(128)} %bitcast.place_ref, f32[2,1024,1024]{2,1,0:T(8,128)S(1)} %bitcast.28, f32[2,1024,256]{2,1,0:T(8,128)S(1)} %bitcast.17, f32[2,64,1024]{2,1,0:T(8,128)S(1)} %bitcast.24, s32[2,1,1024]{2,1,0:T(1,128)S(1)} %copy-done.8), custom_call_target="tpu_custom_call" | custom-call | flops 4000000000 | bytes 12582912 | tf_op jit(solution)/shard_map/local/pallas_call | solution.py:327
  17.4 0.7 collective-permute-start.3
  18.1 3.4 %collective-permute-start.4 = (f32[648,256]{1,0:T(8,128)S(1)}, f32[648,256]{1,0:T(8,128)S(1)}, u32[]{:S(2)}, u32[]{:S(2)}) collective-permute-start(f32[648,256]{1,0:T(8,128)S(1)} %get-tuple-element.22), channel_id=1, source_target_pairs={{0,4},{4,0},{8,12},{12,8},{16,20},{20,16},{24,28},{28,24},{32,36},... | collective-permute-start | bytes 1990664 | tf_op jit(solution)/shard_map/ppermute | solution.py:297
  21.5 0.0 copy-done.4
  21.5 0.0 copy-done.6
  21.5 1.5 %primal.1.pay_ref = f32[200,256]{1,0:T(8,128)S(1)} custom-call(f32[2,1024,256]{2,1,0:T(8,128)S(1)} %bitcast.18, f32[2,64,1024]{2,1,0:T(8,128)S(1)} %bitcast.25, s32[2,1,64]{2,1,0:T(1,128)S(1)} %copy-done.6, f32[64,256]{1,0:T(8,128)S(1)} %bitcast.27), custom_call_target="tpu_custom_call" | custom-call | flops 200000000 | bytes 3145728 | tf_op jit(solution)/shard_map/primal/pallas_call | solution.py:309
  23.1 3.1 %collective-permute-start.2 = (f32[200,256]{1,0:T(8,128)S(1)}, f32[200,256]{1,0:T(8,128)S(1)}, u32[]{:S(2)}, u32[]{:S(2)}) collective-permute-start(f32[200,256]{1,0:T(8,128)S(1)} %primal.1.pay_ref), channel_id=1, source_target_pairs={{0,2},{1,3},{2,0},{3,1},{4,6},{5,7},{6,4},{7,5},{8,10},{9,11},{10,... | collective-permute-start | bytes 614408 | tf_op jit(solution)/shard_map/ppermute | solution.py:297
  26.2 1.1 %collective-permute-start.1 = (f32[200,256]{1,0:T(8,128)S(1)}, f32[200,256]{1,0:T(8,128)S(1)}, u32[]{:S(2)}, u32[]{:S(2)}) collective-permute-start(f32[200,256]{1,0:T(8,128)S(1)} %primal.1.pay_ref), channel_id=1, source_target_pairs={{0,3},{1,2},{2,1},{3,0},{4,7},{5,6},{6,5},{7,4},{8,11},{9,10},{10,... | collective-permute-start | bytes 614408 | tf_op jit(solution)/shard_map/ppermute | solution.py:297
  27.3 0.0 collective-permute-start
  27.3 5.0 %collective-permute-done.2.three_ref = f32[200,256]{1,0:T(8,128)S(1)} collective-permute-done((f32[200,256]{1,0:T(8,128)S(1)}, f32[200,256]{1,0:T(8,128)S(1)}, u32[]{:S(2)}, u32[]{:S(2)}) %collective-permute-start.2) | collective-permute-done | bytes 204832 | tf_op jit(solution)/shard_map/ppermute | solution.py:297
  32.4 3.7 %collective-permute-done.1.two_ref = f32[200,256]{1,0:T(8,128)S(1)} collective-permute-done((f32[200,256]{1,0:T(8,128)S(1)}, f32[200,256]{1,0:T(8,128)S(1)}, u32[]{:S(2)}, u32[]{:S(2)}) %collective-permute-start.1) | collective-permute-done | bytes 204832 | tf_op jit(solution)/shard_map/ppermute | solution.py:297
  36.1 0.1 collective-permute-done.one_ref
  36.2 1.3 %coarse.1 = (f32[64,256]{1,0:T(8,128)S(1)}, f32[64,256]{1,0:T(8,128)S(1)}) custom-call(s32[1]{0:T(128)} %bitcast.place_ref, f32[200,256]{1,0:T(8,128)S(1)} %primal.1.pay_ref, f32[200,256]{1,0:T(8,128)S(1)} %collective-permute-done.one_ref, f32[200,256]{1,0:T(8,128)S(1)} %collective-permute-done.1.two_ref, f32[200,256]{1,0:T(8,128)S(1)} %collective-permute-done.2.three_ref), custom_call_target="tpu_custom_call" | custom-call | flops 500000000 | bytes 1048576 | tf_op jit(solution)/shard_map/coarse/pallas_call | solution.py:355
  37.5 0.7 collective-permute-start.5
  38.1 3.5 %collective-permute-start.6 = (f32[64,256]{1,0:T(8,128)S(1)}, f32[64,256]{1,0:T(8,128)S(1)}, u32[]{:S(2)}, u32[]{:S(2)}) collective-permute-start(f32[64,256]{1,0:T(8,128)S(1)} %get-tuple-element.19.near_ref), channel_id=1, source_target_pairs={{0,4},{4,0},{8,12},{12,8},{16,20},{20,16},{24,28},{28,24},{32,36},... | collective-permute-start | bytes 196616 | tf_op jit(solution)/shard_map/ppermute | solution.py:297
  41.7 0.0 copy-done.1
  41.7 0.0 copy-done.5
  41.7 3.4 %inner.1 = (f32[2,1024,256]{2,1,0:T(8,128)S(1)}, f32[3,8,256]{2,1,0:T(8,128)S(1)}) custom-call(s32[1]{0:T(128)} %bitcast.place_ref, f32[2,1024,256]{2,1,0:T(8,128)S(1)} %get-tuple-element.17.local_ref, f32[64,256]{1,0:T(8,128)S(1)} %get-tuple-element.18.cross_ref, f32[64,256]{1,0:T(8,128)S(1)} %get-tuple-element.19.near_ref, f32[2,64,1024]{2,1,0:T(8,128)S(1)} %bitcast.26, ...), custom_call_target="tpu_custom_call" | custom-call | flops 2500000000 | bytes 8388608 | tf_op jit(solution)/shard_map/inner/pallas_call | solution.py:368
  45.1 0.0 copy-start.2
  45.1 0.0 collective-permute-done.5.cross_pick_ref
  45.1 0.0 collective-permute-done.6.near_pick_ref
  45.1 0.0 collective-permute-done.3.cross_ref
  45.2 0.0 collective-permute-done.4.near_ref
  45.2 1.8 %outer.1 = (f32[2,1024,256]{2,1,0:T(8,128)S(1)}, f32[8,256]{1,0:T(8,128)S(1)}) custom-call(s32[1]{0:T(128)} %bitcast.place_ref, f32[2,1024,256]{2,1,0:T(8,128)S(1)} %get-tuple-element.20.part_ref, f32[648,256]{1,0:T(8,128)S(1)} %collective-permute-done.3.cross_ref, f32[648,256]{1,0:T(8,128)S(1)} %collective-permute-done.4.near_ref, ...), custom_call_target="tpu_custom_call" | custom-call | tf_op jit(solution)/shard_map/outer/pallas_call | solution.py:383
  47.0 0.1 collective-permute-start.7
  47.1 1.1 %collective-permute-done.7 = f32[8,256]{1,0:T(8,128)S(1)} collective-permute-done((f32[8,256]{1,0:T(8,128)S(1)}, f32[8,256]{1,0:T(8,128)S(1)}, u32[]{:S(2)}, u32[]{:S(2)}) %collective-permute-start.7) | collective-permute-done | bytes 8224 | tf_op jit(solution)/shard_map/ppermute | solution.py:297
  48.2 1.4 %collective-permute-start.8 = (f32[8,256]{1,0:T(8,128)S(1)}, f32[8,256]{1,0:T(8,128)S(1)}, u32[]{:S(2)}, u32[]{:S(2)}) collective-permute-start(f32[8,256]{1,0:T(8,128)S(1)} %add.21), channel_id=1, source_target_pairs={{0,1},{1,0},{2,3},{3,2},{4,5},{5,4},{6,7},{7,6},{8,9},{9,8},{10,11... | collective-permute-start | bytes 24584 | tf_op jit(solution)/shard_map/ppermute | solution.py:297
  49.7 2.2 %collective-permute-done.8 = f32[8,256]{1,0:T(8,128)S(1)} collective-permute-done((f32[8,256]{1,0:T(8,128)S(1)}, f32[8,256]{1,0:T(8,128)S(1)}, u32[]{:S(2)}, u32[]{:S(2)}) %collective-permute-start.8) | collective-permute-done | bytes 8224 | tf_op jit(solution)/shard_map/ppermute | solution.py:297
  51.9 2.6 %collective-permute-start.9 = (f32[8,256]{1,0:T(8,128)S(1)}, f32[8,256]{1,0:T(8,128)S(1)}, u32[]{:S(2)}, u32[]{:S(2)}) collective-permute-start(f32[8,256]{1,0:T(8,128)S(1)} %add.22), channel_id=1, source_target_pairs={{0,3},{1,2},{2,1},{3,0},{4,7},{5,6},{6,5},{7,4},{8,11},{9,10},{10,... | collective-permute-start | bytes 24584 | tf_op jit(solution)/shard_map/ppermute | solution.py:297
  54.5 2.2 %collective-permute-done.9 = f32[8,256]{1,0:T(8,128)S(1)} collective-permute-done((f32[8,256]{1,0:T(8,128)S(1)}, f32[8,256]{1,0:T(8,128)S(1)}, u32[]{:S(2)}, u32[]{:S(2)}) %collective-permute-start.9) | collective-permute-done | bytes 8224 | tf_op jit(solution)/shard_map/ppermute | solution.py:297
  56.8 1.6 %collective-permute-start.10 = (f32[8,256]{1,0:T(8,128)S(1)}, f32[8,256]{1,0:T(8,128)S(1)}, u32[]{:S(2)}, u32[]{:S(2)}) collective-permute-start(f32[8,256]{1,0:T(8,128)S(1)} %add.23), channel_id=1, source_target_pairs={{0,8},{4,12},{8,0},{12,4},{16,24},{20,28},{24,16},{28,20},{32,40},... | collective-permute-start | bytes 24584 | tf_op jit(solution)/shard_map/ppermute | solution.py:297
  58.4 2.0 %collective-permute-done.10 = f32[8,256]{1,0:T(8,128)S(1)} collective-permute-done((f32[8,256]{1,0:T(8,128)S(1)}, f32[8,256]{1,0:T(8,128)S(1)}, u32[]{:S(2)}, u32[]{:S(2)}) %collective-permute-start.10) | collective-permute-done | bytes 8224 | tf_op jit(solution)/shard_map/ppermute | solution.py:297
  60.4 4.1 %collective-permute-start.11 = (f32[8,256]{1,0:T(8,128)S(1)}, f32[8,256]{1,0:T(8,128)S(1)}, u32[]{:S(2)}, u32[]{:S(2)}) collective-permute-start(f32[8,256]{1,0:T(8,128)S(1)} %add.24), channel_id=1, source_target_pairs={{0,24},{4,28},{8,16},{12,20},{16,8},{20,12},{24,0},{28,4},{32,56},... | collective-permute-start | bytes 24584 | tf_op jit(solution)/shard_map/ppermute | solution.py:297
  64.6 1.6 %collective-permute-done.11 = f32[8,256]{1,0:T(8,128)S(1)} collective-permute-done((f32[8,256]{1,0:T(8,128)S(1)}, f32[8,256]{1,0:T(8,128)S(1)}, u32[]{:S(2)}, u32[]{:S(2)}) %collective-permute-start.11) | collective-permute-done | bytes 8224 | tf_op jit(solution)/shard_map/ppermute | solution.py:297
  66.2 2.5 %collective-permute-start.12 = (f32[8,256]{1,0:T(8,128)S(1)}, f32[8,256]{1,0:T(8,128)S(1)}, u32[]{:S(2)}, u32[]{:S(2)}) collective-permute-start(f32[8,256]{1,0:T(8,128)S(1)} %add.25), channel_id=1, source_target_pairs={{0,32},{4,36},{8,40},{12,44},{16,48},{20,52},{24,56},{28,60},{32,0... | collective-permute-start | bytes 24584 | tf_op jit(solution)/shard_map/ppermute | solution.py:297
  68.7 1.6 %collective-permute-done.12 = f32[8,256]{1,0:T(8,128)S(1)} collective-permute-done((f32[8,256]{1,0:T(8,128)S(1)}, f32[8,256]{1,0:T(8,128)S(1)}, u32[]{:S(2)}, u32[]{:S(2)}) %collective-permute-start.12) | collective-permute-done | bytes 8224 | tf_op jit(solution)/shard_map/ppermute | solution.py:297
  70.3 3.8 %collective-permute-start.13 = (f32[8,256]{1,0:T(8,128)S(1)}, f32[8,256]{1,0:T(8,128)S(1)}, u32[]{:S(2)}, u32[]{:S(2)}) collective-permute-start(f32[8,256]{1,0:T(8,128)S(1)} %add.26), channel_id=1, source_target_pairs={{0,96},{4,100},{8,104},{12,108},{16,112},{20,116},{24,120},{28,124... | collective-permute-start | bytes 24584 | tf_op jit(solution)/shard_map/ppermute | solution.py:297
  74.1 1.6 %collective-permute-done.13 = f32[8,256]{1,0:T(8,128)S(1)} collective-permute-done((f32[8,256]{1,0:T(8,128)S(1)}, f32[8,256]{1,0:T(8,128)S(1)}, u32[]{:S(2)}, u32[]{:S(2)}) %collective-permute-start.13) | collective-permute-done | bytes 8224 | tf_op jit(solution)/shard_map/ppermute | solution.py:297
  75.7 0.0 copy-done.2
  75.7 3.5 %final.1 = (f32[2,1024,256]{2,1,0:T(8,128)}, f32[2,1024,256]{2,1,0:T(8,128)}, f32[2,1024,256]{2,1,0:T(8,128)}, f32[1,256]{1,0:T(1,128)}) custom-call(f32[8,256]{1,0:T(8,128)S(1)} %add.27.total_ref, f32[2,1,1024]{2,1,0:T(1,128)S(1)} %copy-done.5, f32[2,1024,256]{2,1,0:T(8,128)S(1)} %bitcast.23, f32[2,1024,256]{2,1,0:T(8,128)S(1)} %bitcast.22, ...), custom_call_target="tpu_custom_call" | custom-call | tf_op jit(solution)/shard_map/final/pallas_call | solution.py:399
  (11 shorter events, 0.0 us)
Async XLA Ops:
  0.6 1.6 %copy-start = (f32[2,1,1024,256]{3,2,1,0:T(8,128)S(1)}, f32[2,1,1024,256]{3,2,1,0:T(8,128)}, u32[]{:S(2)}) copy-start(f32[2,1,1024,256]{3,2,1,0:T(8,128)} %param.18) | copy-start | bytes 6291460
  2.2 1.0 %copy-start.3 = (f32[2,1,64,1024]{3,2,1,0:T(8,128)S(1)}, f32[2,1,64,1024]{3,2,1,0:T(8,128)}, u32[]{:S(2)}) copy-start(f32[2,1,64,1024]{3,2,1,0:T(8,128)} %param.11) | copy-start | bytes 1572868
  3.3 3.4 %copy-start.7 = (f32[2,1,1024,1024]{3,2,1,0:T(8,128)S(1)}, f32[2,1,1024,1024]{3,2,1,0:T(8,128)}, u32[]{:S(2)}) copy-start(f32[2,1,1024,1024]{3,2,1,0:T(8,128)} %param.10) | copy-start | bytes 25165828
  6.7 0.7 copy-start.8
  7.4 14.2 %copy-start.4 = (f32[1,64,256]{2,1,0:T(8,128)S(1)}, f32[1,64,256]{2,1,0:T(8,128)}, u32[]{:S(2)}) copy-start(f32[1,64,256]{2,1,0:T(8,128)} %param.15) | copy-start | bytes 196612
  7.4 14.2 %copy-start.6 = (s32[2,1,64]{2,1,0:T(1,128)S(1)}, s32[2,1,64]{2,1,0:T(1,128)}, u32[]{:S(2)}) copy-start(s32[2,1,64]{2,1,0:T(1,128)} %map_hbm.1) | copy-start | bytes 1540
  17.4 27.8 %collective-permute-start.3 = (f32[648,256]{1,0:T(8,128)S(1)}, f32[648,256]{1,0:T(8,128)S(1)}, u32[]{:S(2)}, u32[]{:S(2)}) collective-permute-start(f32[648,256]{1,0:T(8,128)S(1)} %get-tuple-element.21), channel_id=1, source_target_pairs={{4,8},{8,4},{12,16},{16,12},{20,24},{24,20},{28,32},{32,28},{36,40... | collective-permute-start | bytes 1990664 | tf_op jit(solution)/shard_map/ppermute | solution.py:297
  18.1 27.1 %collective-permute-start.4 = (f32[648,256]{1,0:T(8,128)S(1)}, f32[648,256]{1,0:T(8,128)S(1)}, u32[]{:S(2)}, u32[]{:S(2)}) collective-permute-start(f32[648,256]{1,0:T(8,128)S(1)} %get-tuple-element.22), channel_id=1, source_target_pairs={{0,4},{4,0},{8,12},{12,8},{16,20},{20,16},{24,28},{28,24},{32,36},... | collective-permute-start | bytes 1990664 | tf_op jit(solution)/shard_map/ppermute | solution.py:297
  21.5 20.2 %copy-start.1 = (f32[2,1,1024,256]{3,2,1,0:T(8,128)S(1)}, f32[2,1,1024,256]{3,2,1,0:T(8,128)}, u32[]{:S(2)}) copy-start(f32[2,1,1024,256]{3,2,1,0:T(8,128)} %param.17) | copy-start | bytes 6291460
  21.5 20.2 %copy-start.5 = (f32[2,1,1024]{2,1,0:T(1,128)S(1)}, f32[2,1,1024]{2,1,0:T(1,128)}, u32[]{:S(2)}) copy-start(f32[2,1,1024]{2,1,0:T(1,128)} %weight_ref.5) | copy-start | bytes 24580
  23.1 9.3 %collective-permute-start.2 = (f32[200,256]{1,0:T(8,128)S(1)}, f32[200,256]{1,0:T(8,128)S(1)}, u32[]{:S(2)}, u32[]{:S(2)}) collective-permute-start(f32[200,256]{1,0:T(8,128)S(1)} %primal.1.pay_ref), channel_id=1, source_target_pairs={{0,2},{1,3},{2,0},{3,1},{4,6},{5,7},{6,4},{7,5},{8,10},{9,11},{10,... | collective-permute-start | bytes 614408 | tf_op jit(solution)/shard_map/ppermute | solution.py:297
  26.2 9.9 %collective-permute-start.1 = (f32[200,256]{1,0:T(8,128)S(1)}, f32[200,256]{1,0:T(8,128)S(1)}, u32[]{:S(2)}, u32[]{:S(2)}) collective-permute-start(f32[200,256]{1,0:T(8,128)S(1)} %primal.1.pay_ref), channel_id=1, source_target_pairs={{0,3},{1,2},{2,1},{3,0},{4,7},{5,6},{6,5},{7,4},{8,11},{9,10},{10,... | collective-permute-start | bytes 614408 | tf_op jit(solution)/shard_map/ppermute | solution.py:297
  27.3 8.9 %collective-permute-start = (f32[200,256]{1,0:T(8,128)S(1)}, f32[200,256]{1,0:T(8,128)S(1)}, u32[]{:S(2)}, u32[]{:S(2)}) collective-permute-start(f32[200,256]{1,0:T(8,128)S(1)} %primal.1.pay_ref), channel_id=1, source_target_pairs={{0,1},{1,0},{2,3},{3,2},{4,5},{5,4},{6,7},{7,6},{8,9},{9,8},{10,11... | collective-permute-start | bytes 614408 | tf_op jit(solution)/shard_map/ppermute | solution.py:297
  37.5 7.7 %collective-permute-start.5 = (f32[64,256]{1,0:T(8,128)S(1)}, f32[64,256]{1,0:T(8,128)S(1)}, u32[]{:S(2)}, u32[]{:S(2)}) collective-permute-start(f32[64,256]{1,0:T(8,128)S(1)} %get-tuple-element.18.cross_ref), channel_id=1, source_target_pairs={{4,8},{8,4},{12,16},{16,12},{20,24},{24,20},{28,32},{32,28},{36,40... | collective-permute-start | bytes 196616 | tf_op jit(solution)/shard_map/ppermute | solution.py:297
  38.1 7.0 %collective-permute-start.6 = (f32[64,256]{1,0:T(8,128)S(1)}, f32[64,256]{1,0:T(8,128)S(1)}, u32[]{:S(2)}, u32[]{:S(2)}) collective-permute-start(f32[64,256]{1,0:T(8,128)S(1)} %get-tuple-element.19.near_ref), channel_id=1, source_target_pairs={{0,4},{4,0},{8,12},{12,8},{16,20},{20,16},{24,28},{28,24},{32,36},... | collective-permute-start | bytes 196616 | tf_op jit(solution)/shard_map/ppermute | solution.py:297
  45.1 30.6 %copy-start.2 = (f32[2,1,1024,256]{3,2,1,0:T(8,128)S(1)}, f32[2,1,1024,256]{3,2,1,0:T(8,128)}, u32[]{:S(2)}) copy-start(f32[2,1,1024,256]{3,2,1,0:T(8,128)} %param.16) | copy-start | bytes 6291460
  47.0 1.3 %collective-permute-start.7 = (f32[8,256]{1,0:T(8,128)S(1)}, f32[8,256]{1,0:T(8,128)S(1)}, u32[]{:S(2)}, u32[]{:S(2)}) collective-permute-start(f32[8,256]{1,0:T(8,128)S(1)} %get-tuple-element.24), channel_id=1, source_target_pairs={{0,4},{4,0},{8,12},{12,8},{16,20},{20,16},{24,28},{28,24},{32,36},... | collective-permute-start | bytes 24584 | tf_op jit(solution)/shard_map/ppermute | solution.py:297
  48.2 3.7 %collective-permute-start.8 = (f32[8,256]{1,0:T(8,128)S(1)}, f32[8,256]{1,0:T(8,128)S(1)}, u32[]{:S(2)}, u32[]{:S(2)}) collective-permute-start(f32[8,256]{1,0:T(8,128)S(1)} %add.21), channel_id=1, source_target_pairs={{0,1},{1,0},{2,3},{3,2},{4,5},{5,4},{6,7},{7,6},{8,9},{9,8},{10,11... | collective-permute-start | bytes 24584 | tf_op jit(solution)/shard_map/ppermute | solution.py:297
  51.9 4.9 %collective-permute-start.9 = (f32[8,256]{1,0:T(8,128)S(1)}, f32[8,256]{1,0:T(8,128)S(1)}, u32[]{:S(2)}, u32[]{:S(2)}) collective-permute-start(f32[8,256]{1,0:T(8,128)S(1)} %add.22), channel_id=1, source_target_pairs={{0,3},{1,2},{2,1},{3,0},{4,7},{5,6},{6,5},{7,4},{8,11},{9,10},{10,... | collective-permute-start | bytes 24584 | tf_op jit(solution)/shard_map/ppermute | solution.py:297
  56.8 3.7 %collective-permute-start.10 = (f32[8,256]{1,0:T(8,128)S(1)}, f32[8,256]{1,0:T(8,128)S(1)}, u32[]{:S(2)}, u32[]{:S(2)}) collective-permute-start(f32[8,256]{1,0:T(8,128)S(1)} %add.23), channel_id=1, source_target_pairs={{0,8},{4,12},{8,0},{12,4},{16,24},{20,28},{24,16},{28,20},{32,40},... | collective-permute-start | bytes 24584 | tf_op jit(solution)/shard_map/ppermute | solution.py:297
  60.4 5.8 %collective-permute-start.11 = (f32[8,256]{1,0:T(8,128)S(1)}, f32[8,256]{1,0:T(8,128)S(1)}, u32[]{:S(2)}, u32[]{:S(2)}) collective-permute-start(f32[8,256]{1,0:T(8,128)S(1)} %add.24), channel_id=1, source_target_pairs={{0,24},{4,28},{8,16},{12,20},{16,8},{20,12},{24,0},{28,4},{32,56},... | collective-permute-start | bytes 24584 | tf_op jit(solution)/shard_map/ppermute | solution.py:297
  66.2 4.1 %collective-permute-start.12 = (f32[8,256]{1,0:T(8,128)S(1)}, f32[8,256]{1,0:T(8,128)S(1)}, u32[]{:S(2)}, u32[]{:S(2)}) collective-permute-start(f32[8,256]{1,0:T(8,128)S(1)} %add.25), channel_id=1, source_target_pairs={{0,32},{4,36},{8,40},{12,44},{16,48},{20,52},{24,56},{28,60},{32,0... | collective-permute-start | bytes 24584 | tf_op jit(solution)/shard_map/ppermute | solution.py:297
  70.3 5.4 %collective-permute-start.13 = (f32[8,256]{1,0:T(8,128)S(1)}, f32[8,256]{1,0:T(8,128)S(1)}, u32[]{:S(2)}, u32[]{:S(2)}) collective-permute-start(f32[8,256]{1,0:T(8,128)S(1)} %add.26), channel_id=1, source_target_pairs={{0,96},{4,100},{8,104},{12,108},{16,112},{20,116},{24,120},{28,124... | collective-permute-start | bytes 24584 | tf_op jit(solution)/shard_map/ppermute | solution.py:297

commit v3 on v2

--- a/solution.py
+++ b/solution.py
@@ -14,8 +14,9 @@
 C = 64
 HALF = 512
 NAMES = HALF + 2 * C
-STRIP = 512
+STRIP = 256
 ROUNDS = N // STRIP
+AHEAD = 3
 MIB = 1 << 20
 
 
@@ -84,35 +85,69 @@
 
 
 def local_kernel(
-    place_ref, flex_hbm, direc_ref, coup_ref, partner_ref,
-    local_ref, cross_ref, near_ref, flex, right, high, low, sems,
+    place_ref, pay_hbm, flex_hbm, direc_hbm, coup_hbm, partner_hbm,
+    local_hbm, cross_hbm, near_hbm,
+    flex, direc, coup, partner, local, packed, right, left, high, low, sems, out_sems,
 ):
-    copies = []
-    for s in range(2):
-        for r in range(ROUNDS):
-            rows = pl.ds(r * STRIP, STRIP)
-            copy = pltpu.make_async_copy(
-                flex_hbm.at[s, rows], flex.at[s, rows], sems.at[s * ROUNDS + r]
-            )
-            copy.start()
-            copies.append(copy)
+    del pay_hbm
+    strips = 2 * ROUNDS
+    flex_copies, local_copies = [], []
+    for t in range(strips):
+        s, rows = t // ROUNDS, pl.ds((t % ROUNDS) * STRIP, STRIP)
+        flex_copies.append(
+            pltpu.make_async_copy(flex_hbm.at[s, rows], flex.at[s, rows], sems.at[t])
+        )
+        local_copies.append(
+            pltpu.make_async_copy(local.at[s, rows], local_hbm.at[s, rows], out_sems.at[t])
+        )
+    others = [
+        pltpu.make_async_copy(direc_hbm.at[0], direc.at[0], sems.at[strips]),
+        pltpu.make_async_copy(direc_hbm.at[1], direc.at[1], sems.at[strips + 1]),
+        pltpu.make_async_copy(coup_hbm, coup, sems.at[strips + 2]),
+        pltpu.make_async_copy(partner_hbm, partner, sems.at[strips + 3]),
+    ]
+    others[0].start()
+    flex_copies[0].start()
+    others[1].start()
+    for t in range(1, AHEAD):
+        flex_copies[t].start()
+    others[2].start()
+    others[3].start()
     me = place_ref[0]
     odd = lax.rem(me, 2)
     for s in range(2):
-        dh, dl = split(direc_ref[s])
-        right[0:N] = dh
-        right[N : 2 * N] = dl
-        right[2 * N :] = dh
-        for r in range(ROUNDS):
-            rows = slice(r * STRIP, (r + 1) * STRIP)
-            copies[s * ROUNDS + r].wait()
-            ah, al = split(flex[s, rows])
-            out = dot(jnp.concatenate([ah, ah, al], axis=1), right[...])
-            local_ref[s, rows] = out
-            oh, ol = split(out)
-            high[rows] = oh
-            low[rows] = ol
-        target = partner_ref[s] - (2 * me - 1) * N
+        others[s].wait()
+        dh, dl = split(direc[s])
+        right[s, 0:N] = dh
+        right[s, N:] = dl
+    waited = False
+    for t in range(strips + 1):
+        if t < strips:
+            s, start = t // ROUNDS, (t % ROUNDS) * STRIP
+            flex_copies[t].wait()
+            if t + AHEAD < strips:
+                flex_copies[t + AHEAD].start()
+            ah, al = split(flex[s, start : start + STRIP])
+            left[t % 2, :, 0:N] = ah
+            left[t % 2, :, N:] = al
+        if t == 0:
+            continue
+        u = t - 1
+        s, start = u // ROUNDS, (u % ROUNDS) * STRIP
+        upper = left[u % 2, :, 0:N]
+        out = dot(upper, right[s, 0:N]) + dot(upper, right[s, N:]) + dot(left[u % 2, :, N:], right[s, 0:N])
+        local[s, start : start + STRIP] = out
+        oh, ol = split(out)
+        high[s, start : start + STRIP] = oh
+        low[s, start : start + STRIP] = ol
+        local_copies[u].start()
+        if start + STRIP < N:
+            continue
+        if not waited:
+            others[2].wait()
+            others[3].wait()
+            waited = True
+        target = partner[s] - (2 * me - 1) * N
         match = (target >= 3 * N) if s else (target < N)
         key = jnp.where(match, running_count(match) - 1, -1)
         name = jnp.where(match, jnp.bitwise_and(target, N - 1) + 1, 0)
@@ -121,22 +156,27 @@
         digits = jnp.concatenate(
             [coarse, fine, jnp.zeros((14, N), jnp.int32)], axis=0
         ).astype(F32).astype(BF16)
-        ch, cl = split(coup_ref[s])
-        left = jnp.concatenate([ch, cl, digits], axis=0)
-
-        def pack(ref):
-            ref[NAMES:] = jnp.zeros((8, L), F32)
-            for c in range(2):
-                place = one_hot(iota((L, N), 0) + c * L == key)
-                ref[c * L : (c + 1) * L] = dot(place, high[...]) + dot(place, low[...])
-                extra = lax.dot_general(
-                    left, place, (((1,), (1,)), ((), ())), preferred_element_type=F32
-                )
-                ref[HALF + c * C : HALF + (c + 1) * C] = extra[0:C] + extra[C : 2 * C]
-                ref[NAMES + c : NAMES + c + 1] = extra[2 * C : 2 * C + 1] * 32.0 + extra[2 * C + 1 : 2 * C + 2]
-
-        pl.when(odd == s)(functools.partial(pack, cross_ref))
-        pl.when(odd != s)(functools.partial(pack, near_ref))
+        ch, cl = split(coup[s])
+        stack = jnp.concatenate([ch, cl, digits], axis=0)
+        packed[s, NAMES:] = jnp.zeros((8, L), F32)
+        for c in range(2):
+            place = one_hot(iota((L, N), 0) + c * L == key)
+            packed[s, c * L : (c + 1) * L] = dot(place, high[s]) + dot(place, low[s])
+            extra = lax.dot_general(
+                stack, place, (((1,), (1,)), ((), ())), preferred_element_type=F32
+            )
+            packed[s, HALF + c * C : HALF + (c + 1) * C] = extra[0:C] + extra[C : 2 * C]
+            packed[s, NAMES + c : NAMES + c + 1] = (
+                extra[2 * C : 2 * C + 1] * 32.0 + extra[2 * C + 1 : 2 * C + 2]
+            )
+    cross_copy = pltpu.make_async_copy(packed.at[odd], cross_hbm, out_sems.at[strips])
+    near_copy = pltpu.make_async_copy(packed.at[1 - odd], near_hbm, out_sems.at[strips + 1])
+    cross_copy.start()
+    near_copy.start()
+    for copy in local_copies:
+        copy.wait()
+    cross_copy.wait()
+    near_copy.wait()
 
 
 def selector(pay_ref):
@@ -306,6 +346,7 @@
     chain = lax.axis_size("sub")
     place = lax.axis_index("sub").astype(jnp.int32).reshape(1)
 
+    whole = jax.ShapeDtypeStruct((2, N, L), F32)
     pay = pl.pallas_call(
         primal_kernel,
         out_shape=jax.ShapeDtypeStruct((3 * C + 8, L), F32),
@@ -318,7 +359,7 @@
             pltpu.SemaphoreType.DMA((5,)),
         ],
         name="primal",
-        compiler_params=pltpu.CompilerParams(vmem_limit_bytes=16 * MIB),
+        compiler_params=pltpu.CompilerParams(vmem_limit_bytes=58 * MIB),
         cost_estimate=pl.CostEstimate(flops=200_000_000, bytes_accessed=3 * MIB, transcendentals=0),
     )(direc2, links, corner_map, coarse_factor[0])
     others = [exchange(pay, "grp", 4, lambda i, m=m: i ^ m) for m in (1, 3, 2)]
@@ -327,19 +368,26 @@
     local, cross, near = pl.pallas_call(
         local_kernel,
         out_shape=(jax.ShapeDtypeStruct((2, N, L), F32), packed, packed),
-        in_specs=[smem(), hbm()] + [vmem()] * 3,
-        out_specs=(vmem(), vmem(), vmem()),
+        in_specs=[smem()] + [hbm()] * 5,
+        out_specs=(hbm(), hbm(), hbm()),
         scratch_shapes=[
             pltpu.VMEM((2, N, N), F32),
-            pltpu.VMEM((3 * N, L), BF16),
-            pltpu.VMEM((N, L), BF16),
-            pltpu.VMEM((N, L), BF16),
-            pltpu.SemaphoreType.DMA((2 * ROUNDS,)),
+            pltpu.VMEM((2, N, L), F32),
+            pltpu.VMEM((2, C, N), F32),
+            pltpu.VMEM((2, 1, N), jnp.int32),
+            pltpu.VMEM((2, N, L), F32),
+            pltpu.VMEM((2, NAMES + 8, L), F32),
+            pltpu.VMEM((2, 2 * N, L), BF16),
+            pltpu.VMEM((2, STRIP, 2 * N), BF16),
+            pltpu.VMEM((2, N, L), BF16),
+            pltpu.VMEM((2, N, L), BF16),
+            pltpu.SemaphoreType.DMA((2 * ROUNDS + 4,)),
+            pltpu.SemaphoreType.DMA((2 * ROUNDS + 2,)),
         ],
         name="local",
-        compiler_params=pltpu.CompilerParams(vmem_limit_bytes=32 * MIB),
+        compiler_params=pltpu.CompilerParams(vmem_limit_bytes=58 * MIB),
         cost_estimate=pl.CostEstimate(flops=4_000_000_000, bytes_accessed=12 * MIB, transcendentals=0),
-    )(place, blocks, direc2, links, partner)
+    )(place, pay, blocks, direc2, links, partner)
 
     def across(i):
         j = i + 1 if i % 2 else i - 1
@@ -359,12 +407,11 @@
         out_specs=(vmem(), vmem()),
         name="coarse",
         compiler_params=pltpu.CompilerParams(vmem_limit_bytes=16 * MIB),
-        cost_estimate=pl.CostEstimate(flops=500_000_000, bytes_accessed=MIB, transcendentals=0),
+        cost_estimate=pl.CostEstimate(flops=30_000_000_000, bytes_accessed=MIB, transcendentals=0),
     )(place, pay, *others)
     got_cross_pick = exchange(cross_pick, "sub", chain, across)
     got_near_pick = exchange(near_pick, "sub", chain, beside)
 
-    whole = jax.ShapeDtypeStruct((2, N, L), F32)
     part, sums = pl.pallas_call(
         inner_kernel,
         out_shape=(whole, jax.ShapeDtypeStruct((3, 8, L), F32)),

time: 79.8 us -> 68.9 us (0.86)
  waiting for transfers between devices: 21.4 us -> 12.5 us
  local copies, waits for them, and re-layouts: 6.72 us -> 0.05 us
  Pallas kernels: 21.6 us -> 26.5 us
    ppermute x14, waiting for transfers between devices: 21.4 us -> 12.5 us  [exchange(): return lax.ppermute(x, axes, pairs)]
    unnamed x18 -> x16, local copies, waits for them, and re-layouts: 6.72 us -> 0.05 us
    pallas_call x1, Pallas kernels: 10 us -> 13.2 us  [per_device(): pl.pallas_call(local_kernel, out_shape=(jax.ShapeDtypeStruct((2, N, L), F...]
    pallas_call x1, Pallas kernels: 1.54 us -> 3.3 us  [per_device(): pl.pallas_call(primal_kernel, out_shape=jax.ShapeDtypeStruct((3 * C + 8,...]
  transfers between devices with their start and end apart: 14 -> 14, of which waited for: 10 -> 7; matrix products, arithmetic and copies ran while one was open for 0% -> 0% of each run, Pallas kernels for 8% -> 26%
where the time goes in v3:
time: 68.9 us; the launch traced here: 68.6 us
  starting transfers between devices  28.5 us (41%)
  Pallas kernels  26.5 us (38%)
  waiting for transfers between devices  12.5 us (18%)
  between operations  0.98 us (1%)
    ppermute x14, starting transfers between devices, exchange(): return lax.ppermute(x, axes, pairs)  28.5 us
    pallas_call x1, Pallas kernels, per_device(): pl.pallas_call(local_kernel, out_shape=(jax.ShapeDtypeStruct((2, N, L), F...  13.2 us
    ppermute x14, waiting for transfers between devices, exchange(): return lax.ppermute(x, axes, pairs)  12.5 us
    pallas_call x1, Pallas kernels, per_device(): pl.pallas_call(final_kernel, out_shape=(whole, whole, whole, jax.ShapeDty...  3.48 us
    pallas_call x1, Pallas kernels, per_device(): pl.pallas_call(inner_kernel, out_shape=(whole, jax.ShapeDtypeStruct((3, 8...  3.41 us
    pallas_call x1, Pallas kernels, per_device(): pl.pallas_call(primal_kernel, out_shape=jax.ShapeDtypeStruct((3 * C + 8,...  3.3 us
    pallas_call x1, Pallas kernels, per_device(): pl.pallas_call(outer_kernel, out_shape=(whole, jax.ShapeDtypeStruct((8, L...  1.83 us
  transfers between devices with their start and end apart: 14, of which 7 were waited for; matrix products, arithmetic and copies ran while one was open for 0% of the time, Pallas kernels for 26%

profile of v3, /device:TPU:0, one launch (start us, length us, event | category | flops | bytes accessed | tf_op | source)
XLA Modules:
  0.0 68.6 jit_solution(2063874382439126259)
XLA Ops:
  0.6 3.3 %primal.1.pay_hbm.pay_ref = f32[200,256]{1,0:T(8,128)} custom-call(f32[2,1024,256]{2,1,0:T(8,128)} %bitcast.17, f32[2,64,1024]{2,1,0:T(8,128)} %bitcast.24, s32[2,1,64]{2,1,0:T(1,128)} %map_hbm.1, f32[64,256]{1,0:T(8,128)} %bitcast.27), custom_call_target="tpu_custom_call" | custom-call | flops 200000000 | bytes 3145728 | tf_op jit(solution)/shard_map/primal/pallas_call | solution.py:350
  3.9 3.2 %collective-permute-start.2 = (f32[200,256]{1,0:T(8,128)}, f32[200,256]{1,0:T(8,128)S(1)}, u32[]{:S(2)}, u32[]{:S(2)}) collective-permute-start(f32[200,256]{1,0:T(8,128)} %primal.1.pay_hbm.pay_ref), channel_id=1, source_target_pairs={{0,2},{1,3},{2,0},{3,1},{4,6},{5,7},{6,4},{7,5},{8,10},{9,11},{10,... | collective-permute-start | bytes 614408 | tf_op jit(solution)/shard_map/ppermute | solution.py:337
  7.1 1.1 %collective-permute-start.1 = (f32[200,256]{1,0:T(8,128)}, f32[200,256]{1,0:T(8,128)S(1)}, u32[]{:S(2)}, u32[]{:S(2)}) collective-permute-start(f32[200,256]{1,0:T(8,128)} %primal.1.pay_hbm.pay_ref), channel_id=1, source_target_pairs={{0,3},{1,2},{2,1},{3,0},{4,7},{5,6},{6,5},{7,4},{8,11},{9,10},{10,... | collective-permute-start | bytes 614408 | tf_op jit(solution)/shard_map/ppermute | solution.py:337
  8.3 0.0 collective-permute-start
  8.3 13.2 %local.1 = (f32[2,1024,256]{2,1,0:T(8,128)}, f32[648,256]{1,0:T(8,128)}, f32[648,256]{1,0:T(8,128)}) custom-call(s32[1]{0:T(128)} %bitcast.place_ref, f32[200,256]{1,0:T(8,128)} %primal.1.pay_hbm.pay_ref, f32[2,1024,1024]{2,1,0:T(8,128)} %bitcast.28, f32[2,1024,256]{2,1,0:T(8,128)} %bitcast.18, f32[2,64,1024]{2,1,0:T(8,128)} %bitcast.25, ...), custom_call_target="tpu_custom_call" | custom-call | flops 4000000000 | bytes 12582912 | tf_op jit(solution)/shard_map/local/pallas_call | solution.py:368
  21.5 0.7 %collective-permute-start.3 = (f32[648,256]{1,0:T(8,128)}, f32[648,256]{1,0:T(8,128)S(1)}, u32[]{:S(2)}, u32[]{:S(2)}) collective-permute-start(f32[648,256]{1,0:T(8,128)} %get-tuple-element.21), channel_id=1, source_target_pairs={{4,8},{8,4},{12,16},{16,12},{20,24},{24,20},{28,32},{32,28},{36,40... | collective-permute-start | bytes 1990664 | tf_op jit(solution)/shard_map/ppermute | solution.py:337
  22.2 0.0 copy-start
  22.2 0.0 copy-start.1
  22.2 0.0 copy-start.3
  22.3 0.0 copy-start.5
  22.3 0.0 copy-start.6
  22.3 0.0 copy-start.7
  22.3 3.3 %collective-permute-start.4 = (f32[648,256]{1,0:T(8,128)}, f32[648,256]{1,0:T(8,128)S(1)}, u32[]{:S(2)}, u32[]{:S(2)}) collective-permute-start(f32[648,256]{1,0:T(8,128)} %get-tuple-element.22), channel_id=1, source_target_pairs={{0,4},{4,0},{8,12},{12,8},{16,20},{20,16},{24,28},{28,24},{32,36},... | collective-permute-start | bytes 1990664 | tf_op jit(solution)/shard_map/ppermute | solution.py:337
  25.6 0.0 collective-permute-done.2.three_ref
  25.6 0.0 collective-permute-done.1.two_ref
  25.6 0.0 collective-permute-done.one_ref
  25.6 0.0 copy-done.4
  25.6 1.3 %coarse.1 = (f32[64,256]{1,0:T(8,128)S(1)}, f32[64,256]{1,0:T(8,128)S(1)}) custom-call(s32[1]{0:T(128)} %bitcast.place_ref, f32[200,256]{1,0:T(8,128)S(1)} %copy-done.4, f32[200,256]{1,0:T(8,128)S(1)} %collective-permute-done.one_ref, f32[200,256]{1,0:T(8,128)S(1)} %collective-permute-done.1.two_ref, f32[200,256]{1,0:T(8,128)S(1)} %collective-permute-done.2.three_ref), custom_call_target="tpu_custom_call" | custom-call | flops 30000001024 | bytes 1048576 | tf_op jit(solution)/shard_map/coarse/pallas_call | solution.py:403
  26.9 0.7 collective-permute-start.5
  27.6 3.5 %collective-permute-start.6 = (f32[64,256]{1,0:T(8,128)S(1)}, f32[64,256]{1,0:T(8,128)S(1)}, u32[]{:S(2)}, u32[]{:S(2)}) collective-permute-start(f32[64,256]{1,0:T(8,128)S(1)} %get-tuple-element.19.near_ref), channel_id=1, source_target_pairs={{0,4},{4,0},{8,12},{12,8},{16,20},{20,16},{24,28},{28,24},{32,36},... | collective-permute-start | bytes 196616 | tf_op jit(solution)/shard_map/ppermute | solution.py:337
  31.1 0.0 copy-done
  31.1 0.0 copy-done.1
  31.1 0.0 copy-done.3
  31.1 0.0 copy-done.5
  31.1 0.0 copy-done.6
  31.1 0.0 copy-done.7
  31.2 3.4 %inner.1 = (f32[2,1024,256]{2,1,0:T(8,128)S(1)}, f32[3,8,256]{2,1,0:T(8,128)S(1)}) custom-call(s32[1]{0:T(128)} %bitcast.place_ref, f32[2,1024,256]{2,1,0:T(8,128)S(1)} %copy-done.7, f32[64,256]{1,0:T(8,128)S(1)} %get-tuple-element.18.cross_ref, f32[64,256]{1,0:T(8,128)S(1)} %get-tuple-element.19.near_ref, f32[2,64,1024]{2,1,0:T(8,128)S(1)} %bitcast.26, ...), custom_call_target="tpu_custom_call" | custom-call | flops 2500000000 | bytes 8388608 | tf_op jit(solution)/shard_map/inner/pallas_call | solution.py:415
  34.6 0.0 copy-start.2
  34.6 0.0 collective-permute-done.5.cross_pick_ref
  34.6 0.0 collective-permute-done.6.near_pick_ref
  34.6 0.0 collective-permute-done.3.cross_ref
  34.6 0.0 collective-permute-done.4.near_ref
  34.6 1.8 %outer.1 = (f32[2,1024,256]{2,1,0:T(8,128)S(1)}, f32[8,256]{1,0:T(8,128)S(1)}) custom-call(s32[1]{0:T(128)} %bitcast.place_ref, f32[2,1024,256]{2,1,0:T(8,128)S(1)} %get-tuple-element.20.part_ref, f32[648,256]{1,0:T(8,128)S(1)} %collective-permute-done.3.cross_ref, f32[648,256]{1,0:T(8,128)S(1)} %collective-permute-done.4.near_ref, ...), custom_call_target="tpu_custom_call" | custom-call | tf_op jit(solution)/shard_map/outer/pallas_call | solution.py:430
  36.5 0.2 collective-permute-start.7
  36.6 1.1 %collective-permute-done.7 = f32[8,256]{1,0:T(8,128)S(1)} collective-permute-done((f32[8,256]{1,0:T(8,128)S(1)}, f32[8,256]{1,0:T(8,128)S(1)}, u32[]{:S(2)}, u32[]{:S(2)}) %collective-permute-start.7) | collective-permute-done | bytes 8224 | tf_op jit(solution)/shard_map/ppermute | solution.py:337
  37.7 2.0 %collective-permute-start.8 = (f32[8,256]{1,0:T(8,128)S(1)}, f32[8,256]{1,0:T(8,128)S(1)}, u32[]{:S(2)}, u32[]{:S(2)}) collective-permute-start(f32[8,256]{1,0:T(8,128)S(1)} %add.21), channel_id=1, source_target_pairs={{0,1},{1,0},{2,3},{3,2},{4,5},{5,4},{6,7},{7,6},{8,9},{9,8},{10,11... | collective-permute-start | bytes 24584 | tf_op jit(solution)/shard_map/ppermute | solution.py:337
  39.7 1.6 %collective-permute-done.8 = f32[8,256]{1,0:T(8,128)S(1)} collective-permute-done((f32[8,256]{1,0:T(8,128)S(1)}, f32[8,256]{1,0:T(8,128)S(1)}, u32[]{:S(2)}, u32[]{:S(2)}) %collective-permute-start.8) | collective-permute-done | bytes 8224 | tf_op jit(solution)/shard_map/ppermute | solution.py:337
  41.4 2.1 %collective-permute-start.9 = (f32[8,256]{1,0:T(8,128)S(1)}, f32[8,256]{1,0:T(8,128)S(1)}, u32[]{:S(2)}, u32[]{:S(2)}) collective-permute-start(f32[8,256]{1,0:T(8,128)S(1)} %add.22), channel_id=1, source_target_pairs={{0,3},{1,2},{2,1},{3,0},{4,7},{5,6},{6,5},{7,4},{8,11},{9,10},{10,... | collective-permute-start | bytes 24584 | tf_op jit(solution)/shard_map/ppermute | solution.py:337
  43.5 2.8 %collective-permute-done.9 = f32[8,256]{1,0:T(8,128)S(1)} collective-permute-done((f32[8,256]{1,0:T(8,128)S(1)}, f32[8,256]{1,0:T(8,128)S(1)}, u32[]{:S(2)}, u32[]{:S(2)}) %collective-permute-start.9) | collective-permute-done | bytes 8224 | tf_op jit(solution)/shard_map/ppermute | solution.py:337
  46.2 1.7 %collective-permute-start.10 = (f32[8,256]{1,0:T(8,128)S(1)}, f32[8,256]{1,0:T(8,128)S(1)}, u32[]{:S(2)}, u32[]{:S(2)}) collective-permute-start(f32[8,256]{1,0:T(8,128)S(1)} %add.23), channel_id=1, source_target_pairs={{0,8},{4,12},{8,0},{12,4},{16,24},{20,28},{24,16},{28,20},{32,40},... | collective-permute-start | bytes 24584 | tf_op jit(solution)/shard_map/ppermute | solution.py:337
  48.0 1.9 %collective-permute-done.10 = f32[8,256]{1,0:T(8,128)S(1)} collective-permute-done((f32[8,256]{1,0:T(8,128)S(1)}, f32[8,256]{1,0:T(8,128)S(1)}, u32[]{:S(2)}, u32[]{:S(2)}) %collective-permute-start.10) | collective-permute-done | bytes 8224 | tf_op jit(solution)/shard_map/ppermute | solution.py:337
  49.9 4.9 %collective-permute-start.11 = (f32[8,256]{1,0:T(8,128)S(1)}, f32[8,256]{1,0:T(8,128)S(1)}, u32[]{:S(2)}, u32[]{:S(2)}) collective-permute-start(f32[8,256]{1,0:T(8,128)S(1)} %add.24), channel_id=1, source_target_pairs={{0,24},{4,28},{8,16},{12,20},{16,8},{20,12},{24,0},{28,4},{32,56},... | collective-permute-start | bytes 24584 | tf_op jit(solution)/shard_map/ppermute | solution.py:337
  54.8 1.6 %collective-permute-done.11 = f32[8,256]{1,0:T(8,128)S(1)} collective-permute-done((f32[8,256]{1,0:T(8,128)S(1)}, f32[8,256]{1,0:T(8,128)S(1)}, u32[]{:S(2)}, u32[]{:S(2)}) %collective-permute-start.11) | collective-permute-done | bytes 8224 | tf_op jit(solution)/shard_map/ppermute | solution.py:337
  56.4 1.8 %collective-permute-start.12 = (f32[8,256]{1,0:T(8,128)S(1)}, f32[8,256]{1,0:T(8,128)S(1)}, u32[]{:S(2)}, u32[]{:S(2)}) collective-permute-start(f32[8,256]{1,0:T(8,128)S(1)} %add.25), channel_id=1, source_target_pairs={{0,32},{4,36},{8,40},{12,44},{16,48},{20,52},{24,56},{28,60},{32,0... | collective-permute-start | bytes 24584 | tf_op jit(solution)/shard_map/ppermute | solution.py:337
  58.2 1.8 %collective-permute-done.12 = f32[8,256]{1,0:T(8,128)S(1)} collective-permute-done((f32[8,256]{1,0:T(8,128)S(1)}, f32[8,256]{1,0:T(8,128)S(1)}, u32[]{:S(2)}, u32[]{:S(2)}) %collective-permute-start.12) | collective-permute-done | bytes 8224 | tf_op jit(solution)/shard_map/ppermute | solution.py:337
  60.1 3.3 %collective-permute-start.13 = (f32[8,256]{1,0:T(8,128)S(1)}, f32[8,256]{1,0:T(8,128)S(1)}, u32[]{:S(2)}, u32[]{:S(2)}) collective-permute-start(f32[8,256]{1,0:T(8,128)S(1)} %add.26), channel_id=1, source_target_pairs={{0,96},{4,100},{8,104},{12,108},{16,112},{20,116},{24,120},{28,124... | collective-permute-start | bytes 24584 | tf_op jit(solution)/shard_map/ppermute | solution.py:337
  63.3 1.6 %collective-permute-done.13 = f32[8,256]{1,0:T(8,128)S(1)} collective-permute-done((f32[8,256]{1,0:T(8,128)S(1)}, f32[8,256]{1,0:T(8,128)S(1)}, u32[]{:S(2)}, u32[]{:S(2)}) %collective-permute-start.13) | collective-permute-done | bytes 8224 | tf_op jit(solution)/shard_map/ppermute | solution.py:337
  65.0 3.5 %final.1 = (f32[2,1024,256]{2,1,0:T(8,128)}, f32[2,1024,256]{2,1,0:T(8,128)}, f32[2,1024,256]{2,1,0:T(8,128)}, f32[1,256]{1,0:T(1,128)}) custom-call(f32[8,256]{1,0:T(8,128)S(1)} %add.27.total_ref, f32[2,1,1024]{2,1,0:T(1,128)S(1)} %copy-done.5, f32[2,1024,256]{2,1,0:T(8,128)S(1)} %bitcast.23, f32[2,1024,256]{2,1,0:T(8,128)S(1)} %bitcast.22, ...), custom_call_target="tpu_custom_call" | custom-call | tf_op jit(solution)/shard_map/final/pallas_call | solution.py:446
  (9 shorter events, 0.0 us)
Async XLA Ops:
  3.9 21.7 %collective-permute-start.2 = (f32[200,256]{1,0:T(8,128)}, f32[200,256]{1,0:T(8,128)S(1)}, u32[]{:S(2)}, u32[]{:S(2)}) collective-permute-start(f32[200,256]{1,0:T(8,128)} %primal.1.pay_hbm.pay_ref), channel_id=1, source_target_pairs={{0,2},{1,3},{2,0},{3,1},{4,6},{5,7},{6,4},{7,5},{8,10},{9,11},{10,... | collective-permute-start | bytes 614408 | tf_op jit(solution)/shard_map/ppermute | solution.py:337
  7.1 18.5 %collective-permute-start.1 = (f32[200,256]{1,0:T(8,128)}, f32[200,256]{1,0:T(8,128)S(1)}, u32[]{:S(2)}, u32[]{:S(2)}) collective-permute-start(f32[200,256]{1,0:T(8,128)} %primal.1.pay_hbm.pay_ref), channel_id=1, source_target_pairs={{0,3},{1,2},{2,1},{3,0},{4,7},{5,6},{6,5},{7,4},{8,11},{9,10},{10,... | collective-permute-start | bytes 614408 | tf_op jit(solution)/shard_map/ppermute | solution.py:337
  8.3 17.4 %collective-permute-start = (f32[200,256]{1,0:T(8,128)}, f32[200,256]{1,0:T(8,128)S(1)}, u32[]{:S(2)}, u32[]{:S(2)}) collective-permute-start(f32[200,256]{1,0:T(8,128)} %primal.1.pay_hbm.pay_ref), channel_id=1, source_target_pairs={{0,1},{1,0},{2,3},{3,2},{4,5},{5,4},{6,7},{7,6},{8,9},{9,8},{10,11... | collective-permute-start | bytes 614408 | tf_op jit(solution)/shard_map/ppermute | solution.py:337
  8.3 17.4 %copy-start.4 = (f32[200,256]{1,0:T(8,128)S(1)}, f32[200,256]{1,0:T(8,128)}, u32[]{:S(2)}) copy-start(f32[200,256]{1,0:T(8,128)} %primal.1.pay_hbm.pay_ref) | copy-start | bytes 614404
  21.5 13.1 %collective-permute-start.3 = (f32[648,256]{1,0:T(8,128)}, f32[648,256]{1,0:T(8,128)S(1)}, u32[]{:S(2)}, u32[]{:S(2)}) collective-permute-start(f32[648,256]{1,0:T(8,128)} %get-tuple-element.21), channel_id=1, source_target_pairs={{4,8},{8,4},{12,16},{16,12},{20,24},{24,20},{28,32},{32,28},{36,40... | collective-permute-start | bytes 1990664 | tf_op jit(solution)/shard_map/ppermute | solution.py:337
  22.2 8.9 %copy-start = (f32[2,1,1024,256]{3,2,1,0:T(8,128)S(1)}, f32[2,1,1024,256]{3,2,1,0:T(8,128)}, u32[]{:S(2)}) copy-start(f32[2,1,1024,256]{3,2,1,0:T(8,128)} %param.18) | copy-start | bytes 6291460
  22.2 8.9 %copy-start.1 = (f32[2,1,1024,256]{3,2,1,0:T(8,128)S(1)}, f32[2,1,1024,256]{3,2,1,0:T(8,128)}, u32[]{:S(2)}) copy-start(f32[2,1,1024,256]{3,2,1,0:T(8,128)} %param.17) | copy-start | bytes 6291460
  22.2 8.9 %copy-start.3 = (f32[2,1,64,1024]{3,2,1,0:T(8,128)S(1)}, f32[2,1,64,1024]{3,2,1,0:T(8,128)}, u32[]{:S(2)}) copy-start(f32[2,1,64,1024]{3,2,1,0:T(8,128)} %param.11) | copy-start | bytes 1572868
  22.3 8.9 %copy-start.5 = (f32[2,1,1024]{2,1,0:T(1,128)S(1)}, f32[2,1,1024]{2,1,0:T(1,128)}, u32[]{:S(2)}) copy-start(f32[2,1,1024]{2,1,0:T(1,128)} %weight_ref.5) | copy-start | bytes 24580
  22.3 8.9 %copy-start.6 = (s32[2,1,1024]{2,1,0:T(1,128)S(1)}, s32[2,1,1024]{2,1,0:T(1,128)}, u32[]{:S(2)}) copy-start(s32[2,1,1024]{2,1,0:T(1,128)} %partner_ref.1) | copy-start | bytes 24580
  22.3 8.9 %copy-start.7 = (f32[2,1024,256]{2,1,0:T(8,128)S(1)}, f32[2,1024,256]{2,1,0:T(8,128)}, u32[]{:S(2)}) copy-start(f32[2,1024,256]{2,1,0:T(8,128)} %get-tuple-element.17.local_ref) | copy-start | bytes 6291460
  22.3 12.3 %collective-permute-start.4 = (f32[648,256]{1,0:T(8,128)}, f32[648,256]{1,0:T(8,128)S(1)}, u32[]{:S(2)}, u32[]{:S(2)}) collective-permute-start(f32[648,256]{1,0:T(8,128)} %get-tuple-element.22), channel_id=1, source_target_pairs={{0,4},{4,0},{8,12},{12,8},{16,20},{20,16},{24,28},{28,24},{32,36},... | collective-permute-start | bytes 1990664 | tf_op jit(solution)/shard_map/ppermute | solution.py:337
  26.9 7.7 %collective-permute-start.5 = (f32[64,256]{1,0:T(8,128)S(1)}, f32[64,256]{1,0:T(8,128)S(1)}, u32[]{:S(2)}, u32[]{:S(2)}) collective-permute-start(f32[64,256]{1,0:T(8,128)S(1)} %get-tuple-element.18.cross_ref), channel_id=1, source_target_pairs={{4,8},{8,4},{12,16},{16,12},{20,24},{24,20},{28,32},{32,28},{36,40... | collective-permute-start | bytes 196616 | tf_op jit(solution)/shard_map/ppermute | solution.py:337
  27.6 7.0 %collective-permute-start.6 = (f32[64,256]{1,0:T(8,128)S(1)}, f32[64,256]{1,0:T(8,128)S(1)}, u32[]{:S(2)}, u32[]{:S(2)}) collective-permute-start(f32[64,256]{1,0:T(8,128)S(1)} %get-tuple-element.19.near_ref), channel_id=1, source_target_pairs={{0,4},{4,0},{8,12},{12,8},{16,20},{20,16},{24,28},{28,24},{32,36},... | collective-permute-start | bytes 196616 | tf_op jit(solution)/shard_map/ppermute | solution.py:337
  34.6 30.4 %copy-start.2 = (f32[2,1,1024,256]{3,2,1,0:T(8,128)S(1)}, f32[2,1,1024,256]{3,2,1,0:T(8,128)}, u32[]{:S(2)}) copy-start(f32[2,1,1024,256]{3,2,1,0:T(8,128)} %param.16) | copy-start | bytes 6291460
  36.5 1.3 %collective-permute-start.7 = (f32[8,256]{1,0:T(8,128)S(1)}, f32[8,256]{1,0:T(8,128)S(1)}, u32[]{:S(2)}, u32[]{:S(2)}) collective-permute-start(f32[8,256]{1,0:T(8,128)S(1)} %get-tuple-element.24), channel_id=1, source_target_pairs={{0,4},{4,0},{8,12},{12,8},{16,20},{20,16},{24,28},{28,24},{32,36},... | collective-permute-start | bytes 24584 | tf_op jit(solution)/shard_map/ppermute | solution.py:337
  37.7 3.7 %collective-permute-start.8 = (f32[8,256]{1,0:T(8,128)S(1)}, f32[8,256]{1,0:T(8,128)S(1)}, u32[]{:S(2)}, u32[]{:S(2)}) collective-permute-start(f32[8,256]{1,0:T(8,128)S(1)} %add.21), channel_id=1, source_target_pairs={{0,1},{1,0},{2,3},{3,2},{4,5},{5,4},{6,7},{7,6},{8,9},{9,8},{10,11... | collective-permute-start | bytes 24584 | tf_op jit(solution)/shard_map/ppermute | solution.py:337
  41.4 4.9 %collective-permute-start.9 = (f32[8,256]{1,0:T(8,128)S(1)}, f32[8,256]{1,0:T(8,128)S(1)}, u32[]{:S(2)}, u32[]{:S(2)}) collective-permute-start(f32[8,256]{1,0:T(8,128)S(1)} %add.22), channel_id=1, source_target_pairs={{0,3},{1,2},{2,1},{3,0},{4,7},{5,6},{6,5},{7,4},{8,11},{9,10},{10,... | collective-permute-start | bytes 24584 | tf_op jit(solution)/shard_map/ppermute | solution.py:337
  46.2 3.7 %collective-permute-start.10 = (f32[8,256]{1,0:T(8,128)S(1)}, f32[8,256]{1,0:T(8,128)S(1)}, u32[]{:S(2)}, u32[]{:S(2)}) collective-permute-start(f32[8,256]{1,0:T(8,128)S(1)} %add.23), channel_id=1, source_target_pairs={{0,8},{4,12},{8,0},{12,4},{16,24},{20,28},{24,16},{28,20},{32,40},... | collective-permute-start | bytes 24584 | tf_op jit(solution)/shard_map/ppermute | solution.py:337
  49.9 6.5 %collective-permute-start.11 = (f32[8,256]{1,0:T(8,128)S(1)}, f32[8,256]{1,0:T(8,128)S(1)}, u32[]{:S(2)}, u32[]{:S(2)}) collective-permute-start(f32[8,256]{1,0:T(8,128)S(1)} %add.24), channel_id=1, source_target_pairs={{0,24},{4,28},{8,16},{12,20},{16,8},{20,12},{24,0},{28,4},{32,56},... | collective-permute-start | bytes 24584 | tf_op jit(solution)/shard_map/ppermute | solution.py:337
  56.4 3.7 %collective-permute-start.12 = (f32[8,256]{1,0:T(8,128)S(1)}, f32[8,256]{1,0:T(8,128)S(1)}, u32[]{:S(2)}, u32[]{:S(2)}) collective-permute-start(f32[8,256]{1,0:T(8,128)S(1)} %add.25), channel_id=1, source_target_pairs={{0,32},{4,36},{8,40},{12,44},{16,48},{20,52},{24,56},{28,60},{32,0... | collective-permute-start | bytes 24584 | tf_op jit(solution)/shard_map/ppermute | solution.py:337
  60.1 4.9 %collective-permute-start.13 = (f32[8,256]{1,0:T(8,128)S(1)}, f32[8,256]{1,0:T(8,128)S(1)}, u32[]{:S(2)}, u32[]{:S(2)}) collective-permute-start(f32[8,256]{1,0:T(8,128)S(1)} %add.26), channel_id=1, source_target_pairs={{0,96},{4,100},{8,104},{12,108},{16,112},{20,116},{24,120},{28,124... | collective-permute-start | bytes 24584 | tf_op jit(solution)/shard_map/ppermute | solution.py:337

commit v4 on v3

--- a/solution.py
+++ b/solution.py
@@ -14,9 +14,8 @@
 C = 64
 HALF = 512
 NAMES = HALF + 2 * C
-STRIP = 256
+STRIP = 512
 ROUNDS = N // STRIP
-AHEAD = 3
 MIB = 1 << 20
 
 
@@ -62,16 +61,13 @@
     for copy in copies:
         copy.start()
     pay_ref[3 * C :] = jnp.zeros((8, L), F32)
-    copies[0].wait()
+    for copy in copies:
+        copy.wait()
     for s in range(2):
         ch, cl = split(coup[s])
-        copies[1 + s].wait()
         dh, dl = split(direc[s])
         pay_ref[s * C : (s + 1) * C] = dot(ch, dh) + dot(ch, dl) + dot(cl, dh)
-    copies[3].wait()
-    for s in range(2):
         pay_ref[3 * C + s : 3 * C + s + 1, 0:C] = corner[s].astype(F32)
-    copies[4].wait()
 
 
 def running_count(mask):
@@ -87,66 +83,47 @@
 def local_kernel(
     place_ref, pay_hbm, flex_hbm, direc_hbm, coup_hbm, partner_hbm,
     local_hbm, cross_hbm, near_hbm,
-    flex, direc, coup, partner, local, packed, right, left, high, low, sems, out_sems,
+    flex, direc, coup, partner, local, packed, right, high, low, sems, out_sems,
 ):
     del pay_hbm
-    strips = 2 * ROUNDS
-    flex_copies, local_copies = [], []
-    for t in range(strips):
-        s, rows = t // ROUNDS, pl.ds((t % ROUNDS) * STRIP, STRIP)
-        flex_copies.append(
-            pltpu.make_async_copy(flex_hbm.at[s, rows], flex.at[s, rows], sems.at[t])
-        )
-        local_copies.append(
-            pltpu.make_async_copy(local.at[s, rows], local_hbm.at[s, rows], out_sems.at[t])
-        )
+    direc_copy = pltpu.make_async_copy(direc_hbm, direc, sems.at[0])
+    flex_copies = [
+        pltpu.make_async_copy(flex_hbm.at[s], flex.at[s], sems.at[1 + s]) for s in range(2)
+    ]
     others = [
-        pltpu.make_async_copy(direc_hbm.at[0], direc.at[0], sems.at[strips]),
-        pltpu.make_async_copy(direc_hbm.at[1], direc.at[1], sems.at[strips + 1]),
-        pltpu.make_async_copy(coup_hbm, coup, sems.at[strips + 2]),
-        pltpu.make_async_copy(partner_hbm, partner, sems.at[strips + 3]),
+        pltpu.make_async_copy(coup_hbm, coup, sems.at[3]),
+        pltpu.make_async_copy(partner_hbm, partner, sems.at[4]),
     ]
-    others[0].start()
-    flex_copies[0].start()
-    others[1].start()
-    for t in range(1, AHEAD):
-        flex_copies[t].start()
-    others[2].start()
-    others[3].start()
+    out_copies = [
+        pltpu.make_async_copy(local.at[s], local_hbm.at[s], out_sems.at[s]) for s in range(2)
+    ]
+    direc_copy.start()
+    for copy in flex_copies + others:
+        copy.start()
     me = place_ref[0]
     odd = lax.rem(me, 2)
-    for s in range(2):
-        others[s].wait()
+    direc_copy.wait()
+    for s in range(2):
         dh, dl = split(direc[s])
         right[s, 0:N] = dh
         right[s, N:] = dl
-    waited = False
-    for t in range(strips + 1):
-        if t < strips:
-            s, start = t // ROUNDS, (t % ROUNDS) * STRIP
-            flex_copies[t].wait()
-            if t + AHEAD < strips:
-                flex_copies[t + AHEAD].start()
-            ah, al = split(flex[s, start : start + STRIP])
-            left[t % 2, :, 0:N] = ah
-            left[t % 2, :, N:] = al
-        if t == 0:
-            continue
-        u = t - 1
-        s, start = u // ROUNDS, (u % ROUNDS) * STRIP
-        upper = left[u % 2, :, 0:N]
-        out = dot(upper, right[s, 0:N]) + dot(upper, right[s, N:]) + dot(left[u % 2, :, N:], right[s, 0:N])
-        local[s, start : start + STRIP] = out
-        oh, ol = split(out)
-        high[s, start : start + STRIP] = oh
-        low[s, start : start + STRIP] = ol
-        local_copies[u].start()
-        if start + STRIP < N:
-            continue
-        if not waited:
-            others[2].wait()
-            others[3].wait()
-            waited = True
+    flex_copies[0].wait()
+    for s in range(2):
+        if s == 1:
+            out_copies[0].start()
+            flex_copies[1].wait()
+            for copy in others:
+                copy.wait()
+        for r in range(ROUNDS):
+            rows = slice(r * STRIP, (r + 1) * STRIP)
+            ah, al = split(flex[s, rows])
+            out = dot(ah, right[s, 0:N]) + dot(ah, right[s, N:]) + dot(al, right[s, 0:N])
+            local[s, rows] = out
+            oh, ol = split(out)
+            high[s, rows] = oh
+            low[s, rows] = ol
+    out_copies[1].start()
+    for s in range(2):
         target = partner[s] - (2 * me - 1) * N
         match = (target >= 3 * N) if s else (target < N)
         key = jnp.where(match, running_count(match) - 1, -1)
@@ -169,11 +146,11 @@
             packed[s, NAMES + c : NAMES + c + 1] = (
                 extra[2 * C : 2 * C + 1] * 32.0 + extra[2 * C + 1 : 2 * C + 2]
             )
-    cross_copy = pltpu.make_async_copy(packed.at[odd], cross_hbm, out_sems.at[strips])
-    near_copy = pltpu.make_async_copy(packed.at[1 - odd], near_hbm, out_sems.at[strips + 1])
+    cross_copy = pltpu.make_async_copy(packed.at[odd], cross_hbm, out_sems.at[2])
+    near_copy = pltpu.make_async_copy(packed.at[1 - odd], near_hbm, out_sems.at[3])
     cross_copy.start()
     near_copy.start()
-    for copy in local_copies:
+    for copy in out_copies:
         copy.wait()
     cross_copy.wait()
     near_copy.wait()
@@ -378,11 +355,10 @@
             pltpu.VMEM((2, N, L), F32),
             pltpu.VMEM((2, NAMES + 8, L), F32),
             pltpu.VMEM((2, 2 * N, L), BF16),
-            pltpu.VMEM((2, STRIP, 2 * N), BF16),
             pltpu.VMEM((2, N, L), BF16),
             pltpu.VMEM((2, N, L), BF16),
-            pltpu.SemaphoreType.DMA((2 * ROUNDS + 4,)),
-            pltpu.SemaphoreType.DMA((2 * ROUNDS + 2,)),
+            pltpu.SemaphoreType.DMA((5,)),
+            pltpu.SemaphoreType.DMA((4,)),
         ],
         name="local",
         compiler_params=pltpu.CompilerParams(vmem_limit_bytes=58 * MIB),
@@ -437,11 +413,11 @@
     )(place, part, got_cross, got_near, got_cross_pick, got_near_pick, scale, sums)
 
     total = total + exchange(total, "sub", chain, beside)
-    for m in (1, 3):
-        total = total + exchange(total, "grp", 4, lambda i, m=m: i ^ m)
-    for bit in (2, 8):
-        for m in (1, 3):
-            total = total + exchange(total, "sub", chain, lambda i, m=m, bit=bit: i ^ (m * bit))
+    both = ("sub", "grp")
+    size = 4 * chain
+    for near_bit, far_bit in (((4 * 8, 1)), ((3 * 4 * 8, 3)), ((4 * 2, 3 * 4 * 2))):
+        flips = (near_bit, far_bit, near_bit ^ far_bit)
+        total = total + sum(exchange(total, both, size, lambda i, m=m: i ^ m) for m in flips)
 
     lam_next, resid_next, direc_next, ratio = pl.pallas_call(
         final_kernel,

time: 68.9 us -> 62.5 us (0.907)
  Pallas kernels: 26.5 us -> 22.5 us
  waiting for transfers between devices: 12.5 us -> 10.9 us
    pallas_call x1, Pallas kernels: 13.2 us -> 9.32 us  [per_device(): pl.pallas_call(local_kernel, out_shape=(jax.ShapeDtypeStruct((2, N, L), F...]
    ppermute x14 -> x17, waiting for transfers between devices: 12.5 us -> 10.9 us  [exchange(): return lax.ppermute(x, axes, pairs)]
    ppermute x14 -> x17, starting transfers between devices: 28.5 us -> 28 us  [exchange(): return lax.ppermute(x, axes, pairs)]
  transfers between devices with their start and end apart: 14 -> 17, of which waited for: 7 -> 8; matrix products, arithmetic and copies ran while one was open for 0% -> 0% of each run, Pallas kernels for 26% -> 22%
where the time goes in v4:
time: 62.5 us; the launch traced here: 62.4 us
  starting transfers between devices  28 us (45%)
  Pallas kernels  22.5 us (36%)
  waiting for transfers between devices  10.9 us (17%)
  between operations  0.99 us (2%)
    ppermute x17, starting transfers between devices, exchange(): return lax.ppermute(x, axes, pairs)  28 us
    ppermute x17, waiting for transfers between devices, exchange(): return lax.ppermute(x, axes, pairs)  10.9 us
    pallas_call x1, Pallas kernels, per_device(): pl.pallas_call(local_kernel, out_shape=(jax.ShapeDtypeStruct((2, N, L), F...  9.32 us
    pallas_call x1, Pallas kernels, per_device(): pl.pallas_call(final_kernel, out_shape=(whole, whole, whole, jax.ShapeDty...  3.48 us
    pallas_call x1, Pallas kernels, per_device(): pl.pallas_call(inner_kernel, out_shape=(whole, jax.ShapeDtypeStruct((3, 8...  3.41 us
    pallas_call x1, Pallas kernels, per_device(): pl.pallas_call(primal_kernel, out_shape=jax.ShapeDtypeStruct((3 * C + 8,...  3.17 us
    pallas_call x1, Pallas kernels, per_device(): pl.pallas_call(outer_kernel, out_shape=(whole, jax.ShapeDtypeStruct((8, L...  1.83 us
    pallas_call x1, Pallas kernels, per_device(): pl.pallas_call(coarse_kernel, out_shape=(piece, piece), in_specs=[smem()]...  1.27 us
  transfers between devices with their start and end apart: 17, of which 8 were waited for; matrix products, arithmetic and copies ran while one was open for 0% of the time, Pallas kernels for 22%

profile of v4, /device:TPU:0, one launch (start us, length us, event | category | flops | bytes accessed | tf_op | source)
XLA Modules:
  0.0 62.4 jit_solution(1530343173922182581)
XLA Ops:
  0.6 3.2 %primal.1.pay_hbm.pay_ref = f32[200,256]{1,0:T(8,128)} custom-call(f32[2,1024,256]{2,1,0:T(8,128)} %bitcast.17, f32[2,64,1024]{2,1,0:T(8,128)} %bitcast.24, s32[2,1,64]{2,1,0:T(1,128)} %map_hbm.1, f32[64,256]{1,0:T(8,128)} %bitcast.27), custom_call_target="tpu_custom_call" | custom-call | flops 200000000 | bytes 3145728 | tf_op jit(solution)/shard_map/primal/pallas_call | solution.py:327
  3.8 3.2 %collective-permute-start.2 = (f32[200,256]{1,0:T(8,128)}, f32[200,256]{1,0:T(8,128)S(1)}, u32[]{:S(2)}, u32[]{:S(2)}) collective-permute-start(f32[200,256]{1,0:T(8,128)} %primal.1.pay_hbm.pay_ref), channel_id=1, source_target_pairs={{0,2},{1,3},{2,0},{3,1},{4,6},{5,7},{6,4},{7,5},{8,10},{9,11},{10,... | collective-permute-start | bytes 614408 | tf_op jit(solution)/shard_map/ppermute | solution.py:314
  7.0 1.1 %collective-permute-start.1 = (f32[200,256]{1,0:T(8,128)}, f32[200,256]{1,0:T(8,128)S(1)}, u32[]{:S(2)}, u32[]{:S(2)}) collective-permute-start(f32[200,256]{1,0:T(8,128)} %primal.1.pay_hbm.pay_ref), channel_id=1, source_target_pairs={{0,3},{1,2},{2,1},{3,0},{4,7},{5,6},{6,5},{7,4},{8,11},{9,10},{10,... | collective-permute-start | bytes 614408 | tf_op jit(solution)/shard_map/ppermute | solution.py:314
  8.1 0.0 collective-permute-start
  8.1 9.3 %local.1 = (f32[2,1024,256]{2,1,0:T(8,128)}, f32[648,256]{1,0:T(8,128)}, f32[648,256]{1,0:T(8,128)}) custom-call(s32[1]{0:T(128)} %bitcast.place_ref, f32[200,256]{1,0:T(8,128)} %primal.1.pay_hbm.pay_ref, f32[2,1024,1024]{2,1,0:T(8,128)} %bitcast.28, f32[2,1024,256]{2,1,0:T(8,128)} %bitcast.18, f32[2,64,1024]{2,1,0:T(8,128)} %bitcast.25, ...), custom_call_target="tpu_custom_call" | custom-call | flops 4000000000 | bytes 12582912 | tf_op jit(solution)/shard_map/local/pallas_call | solution.py:345
  17.5 0.7 %collective-permute-start.3 = (f32[648,256]{1,0:T(8,128)}, f32[648,256]{1,0:T(8,128)S(1)}, u32[]{:S(2)}, u32[]{:S(2)}) collective-permute-start(f32[648,256]{1,0:T(8,128)} %get-tuple-element.21), channel_id=1, source_target_pairs={{4,8},{8,4},{12,16},{16,12},{20,24},{24,20},{28,32},{32,28},{36,40... | collective-permute-start | bytes 1990664 | tf_op jit(solution)/shard_map/ppermute | solution.py:314
  18.2 0.0 copy-start
  18.2 0.0 copy-start.1
  18.2 0.0 copy-start.3
  18.2 0.0 copy-start.5
  18.2 0.0 copy-start.6
  18.2 0.0 copy-start.7
  18.3 3.3 %collective-permute-start.4 = (f32[648,256]{1,0:T(8,128)}, f32[648,256]{1,0:T(8,128)S(1)}, u32[]{:S(2)}, u32[]{:S(2)}) collective-permute-start(f32[648,256]{1,0:T(8,128)} %get-tuple-element.22), channel_id=1, source_target_pairs={{0,4},{4,0},{8,12},{12,8},{16,20},{20,16},{24,28},{28,24},{32,36},... | collective-permute-start | bytes 1990664 | tf_op jit(solution)/shard_map/ppermute | solution.py:314
  21.6 0.0 collective-permute-done.2.three_ref
  21.6 0.0 collective-permute-done.1.two_ref
  21.6 0.0 collective-permute-done.one_ref
  21.6 1.3 %coarse.1 = (f32[64,256]{1,0:T(8,128)S(1)}, f32[64,256]{1,0:T(8,128)S(1)}) custom-call(s32[1]{0:T(128)} %bitcast.place_ref, f32[200,256]{1,0:T(8,128)S(1)} %copy-done.4, f32[200,256]{1,0:T(8,128)S(1)} %collective-permute-done.one_ref, f32[200,256]{1,0:T(8,128)S(1)} %collective-permute-done.1.two_ref, f32[200,256]{1,0:T(8,128)S(1)} %collective-permute-done.2.three_ref), custom_call_target="tpu_custom_call" | custom-call | flops 30000001024 | bytes 1048576 | tf_op jit(solution)/shard_map/coarse/pallas_call | solution.py:379
  22.9 0.7 %collective-permute-start.5 = (f32[64,256]{1,0:T(8,128)S(1)}, f32[64,256]{1,0:T(8,128)S(1)}, u32[]{:S(2)}, u32[]{:S(2)}) collective-permute-start(f32[64,256]{1,0:T(8,128)S(1)} %get-tuple-element.18.cross_ref), channel_id=1, source_target_pairs={{4,8},{8,4},{12,16},{16,12},{20,24},{24,20},{28,32},{32,28},{36,40... | collective-permute-start | bytes 196616 | tf_op jit(solution)/shard_map/ppermute | solution.py:314
  23.6 3.5 %collective-permute-start.6 = (f32[64,256]{1,0:T(8,128)S(1)}, f32[64,256]{1,0:T(8,128)S(1)}, u32[]{:S(2)}, u32[]{:S(2)}) collective-permute-start(f32[64,256]{1,0:T(8,128)S(1)} %get-tuple-element.19.near_ref), channel_id=1, source_target_pairs={{0,4},{4,0},{8,12},{12,8},{16,20},{20,16},{24,28},{28,24},{32,36},... | collective-permute-start | bytes 196616 | tf_op jit(solution)/shard_map/ppermute | solution.py:314
  27.1 0.0 copy-done.3
  27.1 3.4 %inner.1 = (f32[2,1024,256]{2,1,0:T(8,128)S(1)}, f32[3,8,256]{2,1,0:T(8,128)S(1)}) custom-call(s32[1]{0:T(128)} %bitcast.place_ref, f32[2,1024,256]{2,1,0:T(8,128)S(1)} %copy-done.7, f32[64,256]{1,0:T(8,128)S(1)} %get-tuple-element.18.cross_ref, f32[64,256]{1,0:T(8,128)S(1)} %get-tuple-element.19.near_ref, f32[2,64,1024]{2,1,0:T(8,128)S(1)} %bitcast.26, ...), custom_call_target="tpu_custom_call" | custom-call | flops 2500000000 | bytes 8388608 | tf_op jit(solution)/shard_map/inner/pallas_call | solution.py:391
  30.5 0.0 copy-start.2
  30.5 0.0 collective-permute-done.5.cross_pick_ref
  30.6 0.0 collective-permute-done.6.near_pick_ref
  30.6 0.0 collective-permute-done.3.cross_ref
  30.6 0.0 collective-permute-done.4.near_ref
  30.6 1.8 %outer.1 = (f32[2,1024,256]{2,1,0:T(8,128)S(1)}, f32[8,256]{1,0:T(8,128)S(1)}) custom-call(s32[1]{0:T(128)} %bitcast.place_ref, f32[2,1024,256]{2,1,0:T(8,128)S(1)} %get-tuple-element.20.part_ref, f32[648,256]{1,0:T(8,128)S(1)} %collective-permute-done.3.cross_ref, f32[648,256]{1,0:T(8,128)S(1)} %collective-permute-done.4.near_ref, ...), custom_call_target="tpu_custom_call" | custom-call | tf_op jit(solution)/shard_map/outer/pallas_call | solution.py:406
  32.4 0.2 collective-permute-start.7
  32.6 1.1 %collective-permute-done.7 = f32[8,256]{1,0:T(8,128)S(1)} collective-permute-done((f32[8,256]{1,0:T(8,128)S(1)}, f32[8,256]{1,0:T(8,128)S(1)}, u32[]{:S(2)}, u32[]{:S(2)}) %collective-permute-start.7) | collective-permute-done | bytes 8224 | tf_op jit(solution)/shard_map/ppermute | solution.py:314
  33.7 4.9 %collective-permute-start.10 = (f32[8,256]{1,0:T(8,128)S(1)}, f32[8,256]{1,0:T(8,128)S(1)}, u32[]{:S(2)}, u32[]{:S(2)}) collective-permute-start(f32[8,256]{1,0:T(8,128)S(1)} %add.30), channel_id=1, source_target_pairs={{0,33},{1,32},{2,35},{3,34},{4,37},{5,36},{6,39},{7,38},{8,41},{9,... | collective-permute-start | bytes 24584 | tf_op jit(solution)/shard_map/ppermute | solution.py:314
  38.6 0.0 collective-permute-start.9
  38.6 0.6 collective-permute-start.8
  39.2 1.1 %collective-permute-done.10 = f32[8,256]{1,0:T(8,128)S(1)} collective-permute-done((f32[8,256]{1,0:T(8,128)S(1)}, f32[8,256]{1,0:T(8,128)S(1)}, u32[]{:S(2)}, u32[]{:S(2)}) %collective-permute-start.10) | collective-permute-done | bytes 8224 | tf_op jit(solution)/shard_map/ppermute | solution.py:314
  40.2 2.0 %collective-permute-done.9 = f32[8,256]{1,0:T(8,128)S(1)} collective-permute-done((f32[8,256]{1,0:T(8,128)S(1)}, f32[8,256]{1,0:T(8,128)S(1)}, u32[]{:S(2)}, u32[]{:S(2)}) %collective-permute-start.9) | collective-permute-done | bytes 8224 | tf_op jit(solution)/shard_map/ppermute | solution.py:314
  42.3 0.0 collective-permute-done.8
  42.3 3.8 %collective-permute-start.13 = (f32[8,256]{1,0:T(8,128)S(1)}, f32[8,256]{1,0:T(8,128)S(1)}, u32[]{:S(2)}, u32[]{:S(2)}) collective-permute-start(f32[8,256]{1,0:T(8,128)S(1)} %add_add_fusion.2), channel_id=1, source_target_pairs={{0,99},{1,98},{2,97},{3,96},{4,103},{5,102},{6,101},{7,100},{8,107... | collective-permute-start | bytes 24584 | tf_op jit(solution)/shard_map/ppermute | solution.py:314
  46.1 1.1 %collective-permute-start.12 = (f32[8,256]{1,0:T(8,128)S(1)}, f32[8,256]{1,0:T(8,128)S(1)}, u32[]{:S(2)}, u32[]{:S(2)}) collective-permute-start(f32[8,256]{1,0:T(8,128)S(1)} %add_add_fusion.2), channel_id=1, source_target_pairs={{0,3},{1,2},{2,1},{3,0},{4,7},{5,6},{6,5},{7,4},{8,11},{9,10},{10,... | collective-permute-start | bytes 24584 | tf_op jit(solution)/shard_map/ppermute | solution.py:314
  47.2 1.1 %collective-permute-start.11 = (f32[8,256]{1,0:T(8,128)S(1)}, f32[8,256]{1,0:T(8,128)S(1)}, u32[]{:S(2)}, u32[]{:S(2)}) collective-permute-start(f32[8,256]{1,0:T(8,128)S(1)} %add_add_fusion.2), channel_id=1, source_target_pairs={{0,96},{1,97},{2,98},{3,99},{4,100},{5,101},{6,102},{7,103},{8,104... | collective-permute-start | bytes 24584 | tf_op jit(solution)/shard_map/ppermute | solution.py:314
  48.3 1.1 %collective-permute-done.13 = f32[8,256]{1,0:T(8,128)S(1)} collective-permute-done((f32[8,256]{1,0:T(8,128)S(1)}, f32[8,256]{1,0:T(8,128)S(1)}, u32[]{:S(2)}, u32[]{:S(2)}) %collective-permute-start.13) | collective-permute-done | bytes 8224 | tf_op jit(solution)/shard_map/ppermute | solution.py:314
  49.3 1.6 %collective-permute-done.12 = f32[8,256]{1,0:T(8,128)S(1)} collective-permute-done((f32[8,256]{1,0:T(8,128)S(1)}, f32[8,256]{1,0:T(8,128)S(1)}, u32[]{:S(2)}, u32[]{:S(2)}) %collective-permute-start.12) | collective-permute-done | bytes 8224 | tf_op jit(solution)/shard_map/ppermute | solution.py:314
  50.9 1.1 %collective-permute-done.11 = f32[8,256]{1,0:T(8,128)S(1)} collective-permute-done((f32[8,256]{1,0:T(8,128)S(1)}, f32[8,256]{1,0:T(8,128)S(1)}, u32[]{:S(2)}, u32[]{:S(2)}) %collective-permute-start.11) | collective-permute-done | bytes 8224 | tf_op jit(solution)/shard_map/ppermute | solution.py:314
  52.1 1.8 %collective-permute-start.16 = (f32[8,256]{1,0:T(8,128)S(1)}, f32[8,256]{1,0:T(8,128)S(1)}, u32[]{:S(2)}, u32[]{:S(2)}) collective-permute-start(f32[8,256]{1,0:T(8,128)S(1)} %add_add_fusion.1), channel_id=1, source_target_pairs={{0,16},{1,17},{2,18},{3,19},{4,20},{5,21},{6,22},{7,23},{8,24},{9,... | collective-permute-start | bytes 24584 | tf_op jit(solution)/shard_map/ppermute | solution.py:314
  53.9 1.2 %collective-permute-start.15 = (f32[8,256]{1,0:T(8,128)S(1)}, f32[8,256]{1,0:T(8,128)S(1)}, u32[]{:S(2)}, u32[]{:S(2)}) collective-permute-start(f32[8,256]{1,0:T(8,128)S(1)} %add_add_fusion.1), channel_id=1, source_target_pairs={{0,24},{1,25},{2,26},{3,27},{4,28},{5,29},{6,30},{7,31},{8,16},{9,... | collective-permute-start | bytes 24584 | tf_op jit(solution)/shard_map/ppermute | solution.py:314
  55.1 0.8 %collective-permute-start.14 = (f32[8,256]{1,0:T(8,128)S(1)}, f32[8,256]{1,0:T(8,128)S(1)}, u32[]{:S(2)}, u32[]{:S(2)}) collective-permute-start(f32[8,256]{1,0:T(8,128)S(1)} %add_add_fusion.1), channel_id=1, source_target_pairs={{0,8},{1,9},{2,10},{3,11},{4,12},{5,13},{6,14},{7,15},{8,0},{9,1},... | collective-permute-start | bytes 24584 | tf_op jit(solution)/shard_map/ppermute | solution.py:314
  55.8 1.4 %collective-permute-done.16 = f32[8,256]{1,0:T(8,128)S(1)} collective-permute-done((f32[8,256]{1,0:T(8,128)S(1)}, f32[8,256]{1,0:T(8,128)S(1)}, u32[]{:S(2)}, u32[]{:S(2)}) %collective-permute-start.16) | collective-permute-done | bytes 8224 | tf_op jit(solution)/shard_map/ppermute | solution.py:314
  57.2 1.5 %collective-permute-done.15 = f32[8,256]{1,0:T(8,128)S(1)} collective-permute-done((f32[8,256]{1,0:T(8,128)S(1)}, f32[8,256]{1,0:T(8,128)S(1)}, u32[]{:S(2)}, u32[]{:S(2)}) %collective-permute-start.15) | collective-permute-done | bytes 8224 | tf_op jit(solution)/shard_map/ppermute | solution.py:314
  58.7 0.0 collective-permute-done.14
  58.7 3.5 %final.1 = (f32[2,1024,256]{2,1,0:T(8,128)}, f32[2,1024,256]{2,1,0:T(8,128)}, f32[2,1024,256]{2,1,0:T(8,128)}, f32[1,256]{1,0:T(1,128)}) custom-call(f32[8,256]{1,0:T(8,128)S(1)} %add_add_fusion.total_ref, f32[2,1,1024]{2,1,0:T(1,128)S(1)} %copy-done.5, f32[2,1024,256]{2,1,0:T(8,128)S(1)} %bitcast.23, f32[2,1024,256]{2,1,0:T(8,128)S(1)} %bitcast.22, ...), custom_call_target="tpu_custom_call" | custom-call | tf_op jit(solution)/shard_map/final/pallas_call | solution.py:422
  (12 shorter events, 0.0 us)
Async XLA Ops:
  3.8 17.8 %collective-permute-start.2 = (f32[200,256]{1,0:T(8,128)}, f32[200,256]{1,0:T(8,128)S(1)}, u32[]{:S(2)}, u32[]{:S(2)}) collective-permute-start(f32[200,256]{1,0:T(8,128)} %primal.1.pay_hbm.pay_ref), channel_id=1, source_target_pairs={{0,2},{1,3},{2,0},{3,1},{4,6},{5,7},{6,4},{7,5},{8,10},{9,11},{10,... | collective-permute-start | bytes 614408 | tf_op jit(solution)/shard_map/ppermute | solution.py:314
  7.0 14.6 %collective-permute-start.1 = (f32[200,256]{1,0:T(8,128)}, f32[200,256]{1,0:T(8,128)S(1)}, u32[]{:S(2)}, u32[]{:S(2)}) collective-permute-start(f32[200,256]{1,0:T(8,128)} %primal.1.pay_hbm.pay_ref), channel_id=1, source_target_pairs={{0,3},{1,2},{2,1},{3,0},{4,7},{5,6},{6,5},{7,4},{8,11},{9,10},{10,... | collective-permute-start | bytes 614408 | tf_op jit(solution)/shard_map/ppermute | solution.py:314
  8.1 13.5 %collective-permute-start = (f32[200,256]{1,0:T(8,128)}, f32[200,256]{1,0:T(8,128)S(1)}, u32[]{:S(2)}, u32[]{:S(2)}) collective-permute-start(f32[200,256]{1,0:T(8,128)} %primal.1.pay_hbm.pay_ref), channel_id=1, source_target_pairs={{0,1},{1,0},{2,3},{3,2},{4,5},{5,4},{6,7},{7,6},{8,9},{9,8},{10,11... | collective-permute-start | bytes 614408 | tf_op jit(solution)/shard_map/ppermute | solution.py:314
  8.1 13.5 %copy-start.4 = (f32[200,256]{1,0:T(8,128)S(1)}, f32[200,256]{1,0:T(8,128)}, u32[]{:S(2)}) copy-start(f32[200,256]{1,0:T(8,128)} %primal.1.pay_hbm.pay_ref) | copy-start | bytes 614404
  17.5 13.1 %collective-permute-start.3 = (f32[648,256]{1,0:T(8,128)}, f32[648,256]{1,0:T(8,128)S(1)}, u32[]{:S(2)}, u32[]{:S(2)}) collective-permute-start(f32[648,256]{1,0:T(8,128)} %get-tuple-element.21), channel_id=1, source_target_pairs={{4,8},{8,4},{12,16},{16,12},{20,24},{24,20},{28,32},{32,28},{36,40... | collective-permute-start | bytes 1990664 | tf_op jit(solution)/shard_map/ppermute | solution.py:314
  18.2 8.9 %copy-start = (f32[2,1,1024,256]{3,2,1,0:T(8,128)S(1)}, f32[2,1,1024,256]{3,2,1,0:T(8,128)}, u32[]{:S(2)}) copy-start(f32[2,1,1024,256]{3,2,1,0:T(8,128)} %param.18) | copy-start | bytes 6291460
  18.2 8.9 %copy-start.1 = (f32[2,1,1024,256]{3,2,1,0:T(8,128)S(1)}, f32[2,1,1024,256]{3,2,1,0:T(8,128)}, u32[]{:S(2)}) copy-start(f32[2,1,1024,256]{3,2,1,0:T(8,128)} %param.17) | copy-start | bytes 6291460
  18.2 8.9 %copy-start.3 = (f32[2,1,64,1024]{3,2,1,0:T(8,128)S(1)}, f32[2,1,64,1024]{3,2,1,0:T(8,128)}, u32[]{:S(2)}) copy-start(f32[2,1,64,1024]{3,2,1,0:T(8,128)} %param.11) | copy-start | bytes 1572868
  18.2 8.9 %copy-start.5 = (f32[2,1,1024]{2,1,0:T(1,128)S(1)}, f32[2,1,1024]{2,1,0:T(1,128)}, u32[]{:S(2)}) copy-start(f32[2,1,1024]{2,1,0:T(1,128)} %weight_ref.5) | copy-start | bytes 24580
  18.2 8.9 %copy-start.6 = (s32[2,1,1024]{2,1,0:T(1,128)S(1)}, s32[2,1,1024]{2,1,0:T(1,128)}, u32[]{:S(2)}) copy-start(s32[2,1,1024]{2,1,0:T(1,128)} %partner_ref.1) | copy-start | bytes 24580
  18.2 8.9 %copy-start.7 = (f32[2,1024,256]{2,1,0:T(8,128)S(1)}, f32[2,1024,256]{2,1,0:T(8,128)}, u32[]{:S(2)}) copy-start(f32[2,1024,256]{2,1,0:T(8,128)} %get-tuple-element.17.local_ref) | copy-start | bytes 6291460
  18.3 12.3 %collective-permute-start.4 = (f32[648,256]{1,0:T(8,128)}, f32[648,256]{1,0:T(8,128)S(1)}, u32[]{:S(2)}, u32[]{:S(2)}) collective-permute-start(f32[648,256]{1,0:T(8,128)} %get-tuple-element.22), channel_id=1, source_target_pairs={{0,4},{4,0},{8,12},{12,8},{16,20},{20,16},{24,28},{28,24},{32,36},... | collective-permute-start | bytes 1990664 | tf_op jit(solution)/shard_map/ppermute | solution.py:314
  22.9 7.7 %collective-permute-start.5 = (f32[64,256]{1,0:T(8,128)S(1)}, f32[64,256]{1,0:T(8,128)S(1)}, u32[]{:S(2)}, u32[]{:S(2)}) collective-permute-start(f32[64,256]{1,0:T(8,128)S(1)} %get-tuple-element.18.cross_ref), channel_id=1, source_target_pairs={{4,8},{8,4},{12,16},{16,12},{20,24},{24,20},{28,32},{32,28},{36,40... | collective-permute-start | bytes 196616 | tf_op jit(solution)/shard_map/ppermute | solution.py:314
  23.6 7.0 %collective-permute-start.6 = (f32[64,256]{1,0:T(8,128)S(1)}, f32[64,256]{1,0:T(8,128)S(1)}, u32[]{:S(2)}, u32[]{:S(2)}) collective-permute-start(f32[64,256]{1,0:T(8,128)S(1)} %get-tuple-element.19.near_ref), channel_id=1, source_target_pairs={{0,4},{4,0},{8,12},{12,8},{16,20},{20,16},{24,28},{28,24},{32,36},... | collective-permute-start | bytes 196616 | tf_op jit(solution)/shard_map/ppermute | solution.py:314
  30.5 28.2 %copy-start.2 = (f32[2,1,1024,256]{3,2,1,0:T(8,128)S(1)}, f32[2,1,1024,256]{3,2,1,0:T(8,128)}, u32[]{:S(2)}) copy-start(f32[2,1,1024,256]{3,2,1,0:T(8,128)} %param.16) | copy-start | bytes 6291460
  32.4 1.3 %collective-permute-start.7 = (f32[8,256]{1,0:T(8,128)S(1)}, f32[8,256]{1,0:T(8,128)S(1)}, u32[]{:S(2)}, u32[]{:S(2)}) collective-permute-start(f32[8,256]{1,0:T(8,128)S(1)} %get-tuple-element.24), channel_id=1, source_target_pairs={{0,4},{4,0},{8,12},{12,8},{16,20},{20,16},{24,28},{28,24},{32,36},... | collective-permute-start | bytes 24584 | tf_op jit(solution)/shard_map/ppermute | solution.py:314
  33.7 6.6 %collective-permute-start.10 = (f32[8,256]{1,0:T(8,128)S(1)}, f32[8,256]{1,0:T(8,128)S(1)}, u32[]{:S(2)}, u32[]{:S(2)}) collective-permute-start(f32[8,256]{1,0:T(8,128)S(1)} %add.30), channel_id=1, source_target_pairs={{0,33},{1,32},{2,35},{3,34},{4,37},{5,36},{6,39},{7,38},{8,41},{9,... | collective-permute-start | bytes 24584 | tf_op jit(solution)/shard_map/ppermute | solution.py:314
  38.6 3.7 %collective-permute-start.9 = (f32[8,256]{1,0:T(8,128)S(1)}, f32[8,256]{1,0:T(8,128)S(1)}, u32[]{:S(2)}, u32[]{:S(2)}) collective-permute-start(f32[8,256]{1,0:T(8,128)S(1)} %add.30), channel_id=1, source_target_pairs={{0,1},{1,0},{2,3},{3,2},{4,5},{5,4},{6,7},{7,6},{8,9},{9,8},{10,11... | collective-permute-start | bytes 24584 | tf_op jit(solution)/shard_map/ppermute | solution.py:314
  38.6 3.7 %collective-permute-start.8 = (f32[8,256]{1,0:T(8,128)S(1)}, f32[8,256]{1,0:T(8,128)S(1)}, u32[]{:S(2)}, u32[]{:S(2)}) collective-permute-start(f32[8,256]{1,0:T(8,128)S(1)} %add.30), channel_id=1, source_target_pairs={{0,32},{1,33},{2,34},{3,35},{4,36},{5,37},{6,38},{7,39},{8,40},{9,... | collective-permute-start | bytes 24584 | tf_op jit(solution)/shard_map/ppermute | solution.py:314
  42.3 7.0 %collective-permute-start.13 = (f32[8,256]{1,0:T(8,128)S(1)}, f32[8,256]{1,0:T(8,128)S(1)}, u32[]{:S(2)}, u32[]{:S(2)}) collective-permute-start(f32[8,256]{1,0:T(8,128)S(1)} %add_add_fusion.2), channel_id=1, source_target_pairs={{0,99},{1,98},{2,97},{3,96},{4,103},{5,102},{6,101},{7,100},{8,107... | collective-permute-start | bytes 24584 | tf_op jit(solution)/shard_map/ppermute | solution.py:314
  46.1 4.9 %collective-permute-start.12 = (f32[8,256]{1,0:T(8,128)S(1)}, f32[8,256]{1,0:T(8,128)S(1)}, u32[]{:S(2)}, u32[]{:S(2)}) collective-permute-start(f32[8,256]{1,0:T(8,128)S(1)} %add_add_fusion.2), channel_id=1, source_target_pairs={{0,3},{1,2},{2,1},{3,0},{4,7},{5,6},{6,5},{7,4},{8,11},{9,10},{10,... | collective-permute-start | bytes 24584 | tf_op jit(solution)/shard_map/ppermute | solution.py:314
  47.2 4.9 %collective-permute-start.11 = (f32[8,256]{1,0:T(8,128)S(1)}, f32[8,256]{1,0:T(8,128)S(1)}, u32[]{:S(2)}, u32[]{:S(2)}) collective-permute-start(f32[8,256]{1,0:T(8,128)S(1)} %add_add_fusion.2), channel_id=1, source_target_pairs={{0,96},{1,97},{2,98},{3,99},{4,100},{5,101},{6,102},{7,103},{8,104... | collective-permute-start | bytes 24584 | tf_op jit(solution)/shard_map/ppermute | solution.py:314
  52.1 5.2 %collective-permute-start.16 = (f32[8,256]{1,0:T(8,128)S(1)}, f32[8,256]{1,0:T(8,128)S(1)}, u32[]{:S(2)}, u32[]{:S(2)}) collective-permute-start(f32[8,256]{1,0:T(8,128)S(1)} %add_add_fusion.1), channel_id=1, source_target_pairs={{0,16},{1,17},{2,18},{3,19},{4,20},{5,21},{6,22},{7,23},{8,24},{9,... | collective-permute-start | bytes 24584 | tf_op jit(solution)/shard_map/ppermute | solution.py:314
  53.9 4.9 %collective-permute-start.15 = (f32[8,256]{1,0:T(8,128)S(1)}, f32[8,256]{1,0:T(8,128)S(1)}, u32[]{:S(2)}, u32[]{:S(2)}) collective-permute-start(f32[8,256]{1,0:T(8,128)S(1)} %add_add_fusion.1), channel_id=1, source_target_pairs={{0,24},{1,25},{2,26},{3,27},{4,28},{5,29},{6,30},{7,31},{8,16},{9,... | collective-permute-start | bytes 24584 | tf_op jit(solution)/shard_map/ppermute | solution.py:314
  55.1 3.7 %collective-permute-start.14 = (f32[8,256]{1,0:T(8,128)S(1)}, f32[8,256]{1,0:T(8,128)S(1)}, u32[]{:S(2)}, u32[]{:S(2)}) collective-permute-start(f32[8,256]{1,0:T(8,128)S(1)} %add_add_fusion.1), channel_id=1, source_target_pairs={{0,8},{1,9},{2,10},{3,11},{4,12},{5,13},{6,14},{7,15},{8,0},{9,1},... | collective-permute-start | bytes 24584 | tf_op jit(solution)/shard_map/ppermute | solution.py:314

commit v5 on v4

--- a/solution.py
+++ b/solution.py
@@ -50,26 +50,6 @@
     return jnp.concatenate([tall, tall], axis=1)
 
 
-def primal_kernel(direc_hbm, coup_hbm, map_hbm, factor_hbm, pay_ref, direc, coup, corner, sems):
-    copies = [
-        pltpu.make_async_copy(coup_hbm, coup, sems.at[0]),
-        pltpu.make_async_copy(direc_hbm.at[0], direc.at[0], sems.at[1]),
-        pltpu.make_async_copy(direc_hbm.at[1], direc.at[1], sems.at[2]),
-        pltpu.make_async_copy(map_hbm, corner, sems.at[3]),
-        pltpu.make_async_copy(factor_hbm, pay_ref.at[pl.ds(2 * C, C)], sems.at[4]),
-    ]
-    for copy in copies:
-        copy.start()
-    pay_ref[3 * C :] = jnp.zeros((8, L), F32)
-    for copy in copies:
-        copy.wait()
-    for s in range(2):
-        ch, cl = split(coup[s])
-        dh, dl = split(direc[s])
-        pay_ref[s * C : (s + 1) * C] = dot(ch, dh) + dot(ch, dl) + dot(cl, dh)
-        pay_ref[3 * C + s : 3 * C + s + 1, 0:C] = corner[s].astype(F32)
-
-
 def running_count(mask):
     total = mask.astype(jnp.int32)
     lane = iota(total.shape, 1)
@@ -81,39 +61,44 @@
 
 
 def local_kernel(
-    place_ref, pay_hbm, flex_hbm, direc_hbm, coup_hbm, partner_hbm,
-    local_hbm, cross_hbm, near_hbm,
-    flex, direc, coup, partner, local, packed, right, high, low, sems, out_sems,
+    place_ref, flex_hbm, direc_hbm, coup_hbm, partner_hbm, map_hbm, factor_hbm,
+    pay_hbm, local_hbm, cross_hbm, near_hbm,
+    flex, direc, coup, partner, corner, pay, local, packed, right, high, low, sems, out_sems,
 ):
-    del pay_hbm
-    direc_copy = pltpu.make_async_copy(direc_hbm, direc, sems.at[0])
+    first = [
+        pltpu.make_async_copy(direc_hbm, direc, sems.at[0]),
+        pltpu.make_async_copy(coup_hbm, coup, sems.at[1]),
+        pltpu.make_async_copy(map_hbm, corner, sems.at[2]),
+        pltpu.make_async_copy(factor_hbm, pay.at[pl.ds(2 * C, C)], sems.at[3]),
+        pltpu.make_async_copy(partner_hbm, partner, sems.at[4]),
+    ]
     flex_copies = [
-        pltpu.make_async_copy(flex_hbm.at[s], flex.at[s], sems.at[1 + s]) for s in range(2)
-    ]
-    others = [
-        pltpu.make_async_copy(coup_hbm, coup, sems.at[3]),
-        pltpu.make_async_copy(partner_hbm, partner, sems.at[4]),
+        pltpu.make_async_copy(flex_hbm.at[s], flex.at[s], sems.at[5 + s]) for s in range(2)
     ]
     out_copies = [
         pltpu.make_async_copy(local.at[s], local_hbm.at[s], out_sems.at[s]) for s in range(2)
     ]
-    direc_copy.start()
-    for copy in flex_copies + others:
+    pay_copy = pltpu.make_async_copy(pay, pay_hbm, out_sems.at[4])
+    for copy in first + flex_copies:
         copy.start()
     me = place_ref[0]
     odd = lax.rem(me, 2)
-    direc_copy.wait()
+    pay[3 * C :] = jnp.zeros((8, L), F32)
+    for copy in first:
+        copy.wait()
     for s in range(2):
         dh, dl = split(direc[s])
         right[s, 0:N] = dh
         right[s, N:] = dl
+        ch, cl = split(coup[s])
+        pay[s * C : (s + 1) * C] = dot(ch, dh) + dot(ch, dl) + dot(cl, dh)
+        pay[3 * C + s : 3 * C + s + 1, 0:C] = corner[s].astype(F32)
+    pay_copy.start()
     flex_copies[0].wait()
     for s in range(2):
         if s == 1:
             out_copies[0].start()
             flex_copies[1].wait()
-            for copy in others:
-                copy.wait()
         for r in range(ROUNDS):
             rows = slice(r * STRIP, (r + 1) * STRIP)
             ah, al = split(flex[s, rows])
@@ -122,7 +107,6 @@
             oh, ol = split(out)
             high[s, rows] = oh
             low[s, rows] = ol
-    out_copies[1].start()
     for s in range(2):
         target = partner[s] - (2 * me - 1) * N
         match = (target >= 3 * N) if s else (target < N)
@@ -150,8 +134,10 @@
     near_copy = pltpu.make_async_copy(packed.at[1 - odd], near_hbm, out_sems.at[3])
     cross_copy.start()
     near_copy.start()
+    out_copies[1].start()
     for copy in out_copies:
         copy.wait()
+    pay_copy.wait()
     cross_copy.wait()
     near_copy.wait()
 
@@ -163,7 +149,8 @@
     return one_hot(iota((L, 2 * C), 0) == both)
 
 
-def coarse_kernel(place_ref, pay_ref, one_ref, two_ref, three_ref, cross_ref, near_ref):
+def coarse_kernel(place_ref, pay_ref, one_ref, two_ref, three_ref, mix_hbm, cross_ref, near_ref):
+    del mix_hbm
     odd = lax.rem(place_ref[0], 2)
     members = (pay_ref, one_ref, two_ref, three_ref)
     sels, parts = [], []
@@ -194,72 +181,77 @@
         cross_ref[...] = picked[C:]
 
 
-def inner_kernel(
-    place_ref, local_ref, cross_ref, near_ref, coup_ref, direc_ref, resid_ref, weight_ref, partner_ref,
-    jump_ref, sums_ref, image_ref, high, low,
-):
+def inner_kernel(place_ref, local_ref, coup_ref, partner_ref, part_ref, mix_ref, high, low):
     me = place_ref[0]
-    odd = lax.rem(me, 2) == 1
-    old = jnp.zeros((8, L), F32)
-    curve = jnp.zeros((8, L), F32)
-    mixed = jnp.zeros((8, L), F32)
+    stacks = []
     for s in range(2):
         ch, cl = split(coup_ref[s])
-        qh, ql = split(jnp.where(odd == (s == 1), cross_ref[...], near_ref[...]))
-        left = jnp.concatenate([ch, ch, cl], axis=0)
-        right = jnp.concatenate([qh, ql, qh], axis=0)
+        stacks.append(jnp.concatenate([ch, cl], axis=0))
         for r in range(0, N, L):
-            image = local_ref[s, r : r + L] + dot_t(left[:, r : r + L], right)
-            image_ref[s, r : r + L] = image
-            ih, il = split(image)
-            high[s, r : r + L] = ih
-            low[s, r : r + L] = il
+            lh, ll = split(local_ref[s, r : r + L])
+            high[s, r : r + L] = lh
+            low[s, r : r + L] = ll
     for s in range(2):
         other = 1 - s
         theirs = partner_ref[other] - (2 * me + s) * N
         mine = partner_ref[s]
         awake = jnp.where(lax.shift_right_arithmetic(mine, 10) != 2 * me + s, 1.0, 0.0)
+        mix_ref[s, 0:C] = coup_ref[s] * awake
         for r in range(0, N, L):
             rows = slice(r, r + L)
             place = one_hot(iota((L, N), 0) + r == theirs)
             opposite = dot(place, high[other]) + dot(place, low[other])
-            image = image_ref[s, rows]
-            jump_ref[s, rows] = column(awake[:, rows]) * image - opposite
-            scaled = column(weight_ref[s][:, rows]) * resid_ref[s, rows]
-            old = old + fold(scaled * resid_ref[s, rows])
-            curve = curve + fold(direc_ref[s, rows] * image)
-            mixed = mixed + fold(scaled * image)
-    sums_ref[0] = old
-    sums_ref[1] = curve
-    sums_ref[2] = mixed
+            part_ref[s, rows] = column(awake[:, rows]) * local_ref[s, rows] - opposite
+            moved = lax.dot_general(
+                stacks[other], place, (((1,), (1,)), ((), ())), preferred_element_type=F32
+            )
+            mix_ref[s, C:, rows] = -(moved[0:C] + moved[C:])
+
+
+def triple(x, first):
+    high, low = split(x)
+    return jnp.concatenate([high, high, low] if first else [high, low, high], axis=0)
 
 
 def outer_kernel(
-    place_ref, part_ref, cross_ref, near_ref, cross_pick_ref, near_pick_ref, weight_ref, sums_ref,
-    jump_ref, total_ref,
+    place_ref, part_ref, mix_ref, cross_ref, near_ref, cross_pick_ref, near_pick_ref,
+    own_cross_ref, own_near_ref, weight_ref, resid_ref, direc_ref,
+    jump_ref, total_ref, images, rows_ref,
 ):
-    odd = lax.rem(place_ref[0], 2)
-    square = jnp.zeros((8, L), F32)
-    for ref, pick_ref, s in ((cross_ref, cross_pick_ref, odd), (near_ref, near_pick_ref, 1 - odd)):
-        qh, ql = split(pick_ref[...])
-        right = jnp.concatenate([qh, ql, qh], axis=0)
-        highs, lows = [], []
+    is_odd = lax.rem(place_ref[0], 2) == 1
+    for k, (ref, pick_ref) in enumerate(((cross_ref, cross_pick_ref), (near_ref, near_pick_ref))):
+        right = triple(pick_ref[...], False)
         for c in range(2):
-            ch, cl = split(ref[HALF + c * C : HALF + (c + 1) * C])
-            left = jnp.concatenate([ch, ch, cl], axis=0)
+            left = triple(ref[HALF + c * C : HALF + (c + 1) * C], True)
             image_high, image_low = split(ref[c * L : (c + 1) * L] + dot_t(left, right))
-            highs.append(image_high)
-            lows.append(image_low)
-        stacked = jnp.concatenate(highs + lows, axis=0)
-        names = [ref[NAMES + c : NAMES + c + 1].astype(jnp.int32) for c in range(2)]
+            images[k, c * L : (c + 1) * L] = image_high
+            images[k, HALF + c * L : HALF + (c + 1) * L] = image_low
+            rows_ref[k, c : c + 1] = ref[NAMES + c : NAMES + c + 1].astype(jnp.int32)
+    flip = is_odd.astype(jnp.int32)
+    picks = (
+        jnp.where(is_odd, own_near_ref[...], own_cross_ref[...]),
+        jnp.where(is_odd, own_cross_ref[...], own_near_ref[...]),
+    )
+    sums = [jnp.zeros((8, L), F32)] * 4
+    for s in range(2):
+        k = flip if s == 0 else 1 - flip
+        stacked = images[k]
+        names = [rows_ref[k, c : c + 1] for c in range(2)]
+        right = triple(jnp.concatenate([picks[s], picks[1 - s]], axis=0), False)
+        left = triple(mix_ref[s], True)
         for r in range(0, N, L):
+            rows = slice(r, r + L)
             places = [one_hot(iota((L, L), 0) + (r + 1) == name) for name in names]
             opposite = dot(jnp.concatenate(places + places, axis=1), stacked)
-            jump = part_ref[s, r : r + L] - opposite
-            jump_ref[s, r : r + L] = jump
-            square = square + fold(column(weight_ref[s][:, r : r + L]) * jump * jump)
-    rows = [jnp.sum(x, axis=0, keepdims=True) for x in (sums_ref[0], sums_ref[1], sums_ref[2], square)]
-    total_ref[...] = jnp.concatenate(rows + [jnp.zeros((4, L), F32)], axis=0)
+            jump = part_ref[s, rows] + dot_t(left[:, rows], right) - opposite
+            jump_ref[s, rows] = jump
+            resid = resid_ref[s, rows]
+            scale = column(weight_ref[s][:, rows])
+            scaled = scale * resid
+            terms = (scaled * resid, direc_ref[s, rows] * jump, scaled * jump, scale * jump * jump)
+            sums = [total + fold(term) for total, term in zip(sums, terms)]
+    lines = [jnp.sum(x, axis=0, keepdims=True) for x in sums]
+    total_ref[...] = jnp.concatenate(lines + [jnp.zeros((4, L), F32)], axis=0)
 
 
 def final_kernel(
@@ -267,8 +259,8 @@
     lam_hbm, resid_hbm, direc_hbm, ratio_ref, lam_out, resid_out, direc_out, sems,
 ):
     old = total_ref[0:1]
-    alpha = old / (2.0 * total_ref[1:2])
-    new = old + alpha * (alpha * total_ref[3:4] - 4.0 * total_ref[2:3])
+    alpha = old / total_ref[1:2]
+    new = old + alpha * (alpha * total_ref[3:4] - 2.0 * total_ref[2:3])
     ratio = new / old
     ratio_ref[...] = ratio
     copies = []
@@ -324,46 +316,33 @@
     place = lax.axis_index("sub").astype(jnp.int32).reshape(1)
 
     whole = jax.ShapeDtypeStruct((2, N, L), F32)
-    pay = pl.pallas_call(
-        primal_kernel,
-        out_shape=jax.ShapeDtypeStruct((3 * C + 8, L), F32),
-        in_specs=[hbm()] * 4,
-        out_specs=vmem(),
-        scratch_shapes=[
-            pltpu.VMEM((2, N, L), F32),
-            pltpu.VMEM((2, C, N), F32),
-            pltpu.VMEM((2, 1, C), jnp.int32),
-            pltpu.SemaphoreType.DMA((5,)),
-        ],
-        name="primal",
-        compiler_params=pltpu.CompilerParams(vmem_limit_bytes=58 * MIB),
-        cost_estimate=pl.CostEstimate(flops=200_000_000, bytes_accessed=3 * MIB, transcendentals=0),
-    )(direc2, links, corner_map, coarse_factor[0])
-    others = [exchange(pay, "grp", 4, lambda i, m=m: i ^ m) for m in (1, 3, 2)]
-
     packed = jax.ShapeDtypeStruct((NAMES + 8, L), F32)
-    local, cross, near = pl.pallas_call(
+    pay_shape = jax.ShapeDtypeStruct((3 * C + 8, L), F32)
+    pay, local, cross, near = pl.pallas_call(
         local_kernel,
-        out_shape=(jax.ShapeDtypeStruct((2, N, L), F32), packed, packed),
-        in_specs=[smem()] + [hbm()] * 5,
-        out_specs=(hbm(), hbm(), hbm()),
+        out_shape=(pay_shape, whole, packed, packed),
+        in_specs=[smem()] + [hbm()] * 6,
+        out_specs=(hbm(), hbm(), hbm(), hbm()),
         scratch_shapes=[
             pltpu.VMEM((2, N, N), F32),
             pltpu.VMEM((2, N, L), F32),
             pltpu.VMEM((2, C, N), F32),
             pltpu.VMEM((2, 1, N), jnp.int32),
+            pltpu.VMEM((2, 1, C), jnp.int32),
+            pltpu.VMEM((3 * C + 8, L), F32),
             pltpu.VMEM((2, N, L), F32),
             pltpu.VMEM((2, NAMES + 8, L), F32),
             pltpu.VMEM((2, 2 * N, L), BF16),
             pltpu.VMEM((2, N, L), BF16),
             pltpu.VMEM((2, N, L), BF16),
+            pltpu.SemaphoreType.DMA((7,)),
             pltpu.SemaphoreType.DMA((5,)),
-            pltpu.SemaphoreType.DMA((4,)),
         ],
         name="local",
         compiler_params=pltpu.CompilerParams(vmem_limit_bytes=58 * MIB),
         cost_estimate=pl.CostEstimate(flops=4_000_000_000, bytes_accessed=12 * MIB, transcendentals=0),
-    )(place, pay, blocks, direc2, links, partner)
+    )(place, blocks, direc2, links, partner, corner_map, coarse_factor[0])
+    others = [exchange(pay, "grp", 4, lambda i, m=m: i ^ m) for m in (1, 3, 2)]
 
     def across(i):
         j = i + 1 if i % 2 else i - 1
@@ -374,43 +353,44 @@
 
     got_cross = exchange(cross, "sub", chain, across)
     got_near = exchange(near, "sub", chain, beside)
+
+    part, mix = pl.pallas_call(
+        inner_kernel,
+        out_shape=(whole, jax.ShapeDtypeStruct((2, 2 * C, N), F32)),
+        in_specs=[smem()] + [vmem()] * 3,
+        out_specs=(vmem(), vmem()),
+        scratch_shapes=[pltpu.VMEM((2, N, L), BF16)] * 2,
+        name="inner",
+        compiler_params=pltpu.CompilerParams(vmem_limit_bytes=16 * MIB),
+        cost_estimate=pl.CostEstimate(flops=3_500_000_000, bytes_accessed=8 * MIB, transcendentals=0),
+    )(place, local, links, partner)
 
     piece = jax.ShapeDtypeStruct((C, L), F32)
     cross_pick, near_pick = pl.pallas_call(
         coarse_kernel,
         out_shape=(piece, piece),
-        in_specs=[smem()] + [vmem()] * 4,
+        in_specs=[smem()] + [vmem()] * 4 + [hbm()],
         out_specs=(vmem(), vmem()),
         name="coarse",
         compiler_params=pltpu.CompilerParams(vmem_limit_bytes=16 * MIB),
         cost_estimate=pl.CostEstimate(flops=30_000_000_000, bytes_accessed=MIB, transcendentals=0),
-    )(place, pay, *others)
+    )(place, pay, *others, mix)
     got_cross_pick = exchange(cross_pick, "sub", chain, across)
     got_near_pick = exchange(near_pick, "sub", chain, beside)
-
-    part, sums = pl.pallas_call(
-        inner_kernel,
-        out_shape=(whole, jax.ShapeDtypeStruct((3, 8, L), F32)),
-        in_specs=[smem()] + [vmem()] * 8,
-        out_specs=(vmem(), vmem()),
-        scratch_shapes=[
-            pltpu.VMEM((2, N, L), F32),
-            pltpu.VMEM((2, N, L), BF16),
-            pltpu.VMEM((2, N, L), BF16),
-        ],
-        name="inner",
-        compiler_params=pltpu.CompilerParams(vmem_limit_bytes=24 * MIB),
-        cost_estimate=pl.CostEstimate(flops=2_500_000_000, bytes_accessed=8 * MIB, transcendentals=0),
-    )(place, local, cross_pick, near_pick, links, direc2, resid2, scale, partner)
 
     jump, total = pl.pallas_call(
         outer_kernel,
         out_shape=(whole, jax.ShapeDtypeStruct((8, L), F32)),
-        in_specs=[smem()] + [vmem()] * 7,
+        in_specs=[smem()] + [vmem()] * 11,
         out_specs=(vmem(), vmem()),
+        scratch_shapes=[pltpu.VMEM((2, N, L), BF16), pltpu.VMEM((2, 8, L), jnp.int32)],
         name="outer",
-        compiler_params=pltpu.CompilerParams(vmem_limit_bytes=24 * MIB),
-    )(place, part, got_cross, got_near, got_cross_pick, got_near_pick, scale, sums)
+        compiler_params=pltpu.CompilerParams(vmem_limit_bytes=16 * MIB),
+        cost_estimate=pl.CostEstimate(flops=2_000_000_000, bytes_accessed=8 * MIB, transcendentals=0),
+    )(
+        place, part, mix, got_cross, got_near, got_cross_pick, got_near_pick,
+        cross_pick, near_pick, scale, resid2, direc2,
+    )
 
     total = total + exchange(total, "sub", chain, beside)
     both = ("sub", "grp")

time: 62.5 us -> 64.3 us (1.029)
  Pallas kernels: 22.5 us -> 20.7 us
  local copies, waits for them, and re-layouts: 0.05 us -> 1.63 us
  starting transfers between devices: 28 us -> 29.1 us
  waiting for transfers between devices: 10.9 us -> 11.7 us
    pallas_call x3 -> x2, Pallas kernels: 15.9 us -> 13.4 us  [the longest x1 9.94 us: per_device(): pl.pallas_call(local_kernel, out_shape=(pay_shape, whole, packed, packed)...]
    unnamed x16, local copies, waits for them, and re-layouts: 0.05 us -> 1.63 us
    ppermute x17, starting transfers between devices: 28 us -> 29.1 us  [exchange(): return lax.ppermute(x, axes, pairs)]
    ppermute x17, waiting for transfers between devices: 10.9 us -> 11.7 us  [exchange(): return lax.ppermute(x, axes, pairs)]
    pallas_call x1, Pallas kernels: 1.83 us -> 2.59 us  [per_device(): pl.pallas_call(outer_kernel, out_shape=(whole, jax.ShapeDtypeStruct((8, L...]
  transfers between devices with their start and end apart: 17 -> 17, of which waited for: 8 -> 11; matrix products, arithmetic and copies ran while one was open for 0% -> 0% of each run, Pallas kernels for 22% -> 7%
where the time goes in v5:
time: 64.3 us; the launch traced here: 64.1 us
  starting transfers between devices  29.1 us (45%)
  Pallas kernels  20.7 us (32%)
  waiting for transfers between devices  11.7 us (18%)
  local copies, waits for them, and re-layouts  1.63 us (3%)
  between operations  0.96 us (1%)
    ppermute x17, starting transfers between devices, exchange(): return lax.ppermute(x, axes, pairs)  29.1 us
    ppermute x17, waiting for transfers between devices, exchange(): return lax.ppermute(x, axes, pairs)  11.7 us
    pallas_call x1, Pallas kernels, per_device(): pl.pallas_call(local_kernel, out_shape=(pay_shape, whole, packed, packed)...  9.94 us
    pallas_call x1, Pallas kernels, per_device(): pl.pallas_call(final_kernel, out_shape=(whole, whole, whole, jax.ShapeDty...  3.47 us
    pallas_call x1, Pallas kernels, per_device(): pl.pallas_call(inner_kernel, out_shape=(whole, jax.ShapeDtypeStruct((2, 2...  3.45 us
    pallas_call x1, Pallas kernels, per_device(): pl.pallas_call(outer_kernel, out_shape=(whole, jax.ShapeDtypeStruct((8, L...  2.59 us
    unnamed x16, local copies, waits for them, and re-layouts  1.63 us
  transfers between devices with their start and end apart: 17, of which 11 were waited for; matrix products, arithmetic and copies ran while one was open for 0% of the time, Pallas kernels for 7%

profile of v5, /device:TPU:0, one launch (start us, length us, event | category | flops | bytes accessed | tf_op | source)
XLA Modules:
  0.0 64.1 jit_solution(17356531092776602846)
XLA Ops:
  0.6 0.0 copy-start.4
  0.6 0.0 copy-start.6
  0.7 9.9 %local.1 = (f32[200,256]{1,0:T(8,128)}, f32[2,1024,256]{2,1,0:T(8,128)}, f32[648,256]{1,0:T(8,128)}, f32[648,256]{1,0:T(8,128)}) custom-call(s32[1]{0:T(128)} %bitcast.place_ref, f32[2,1024,1024]{2,1,0:T(8,128)} %bitcast.25, f32[2,1024,256]{2,1,0:T(8,128)} %bitcast.17, f32[2,64,1024]{2,1,0:T(8,128)} %bitcast.23, s32[2,1,1024]{2,1,0:T(1,128)} %partner_ref.1, ...), custom_call_target="tpu_custom_call" | custom-call | flops 4000000000 | bytes 12582912 | tf_op jit(solution)/shard_map/local/pallas_call | solution.py:321
  10.6 3.2 %collective-permute-start.4 = (f32[200,256]{1,0:T(8,128)}, f32[200,256]{1,0:T(8,128)S(1)}, u32[]{:S(2)}, u32[]{:S(2)}) collective-permute-start(f32[200,256]{1,0:T(8,128)} %get-tuple-element.23.pay_ref), channel_id=1, source_target_pairs={{0,2},{1,3},{2,0},{3,1},{4,6},{5,7},{6,4},{7,5},{8,10},{9,11},{10,... | collective-permute-start | bytes 614408 | tf_op jit(solution)/shard_map/ppermute | solution.py:306
  13.8 1.1 %collective-permute-start.3 = (f32[200,256]{1,0:T(8,128)}, f32[200,256]{1,0:T(8,128)S(1)}, u32[]{:S(2)}, u32[]{:S(2)}) collective-permute-start(f32[200,256]{1,0:T(8,128)} %get-tuple-element.23.pay_ref), channel_id=1, source_target_pairs={{0,3},{1,2},{2,1},{3,0},{4,7},{5,6},{6,5},{7,4},{8,11},{9,10},{10,... | collective-permute-start | bytes 614408 | tf_op jit(solution)/shard_map/ppermute | solution.py:306
  14.9 0.0 collective-permute-start.2
  14.9 0.7 %collective-permute-start = (f32[648,256]{1,0:T(8,128)}, f32[648,256]{1,0:T(8,128)S(1)}, u32[]{:S(2)}, u32[]{:S(2)}) collective-permute-start(f32[648,256]{1,0:T(8,128)} %get-tuple-element.21), channel_id=1, source_target_pairs={{4,8},{8,4},{12,16},{16,12},{20,24},{24,20},{28,32},{32,28},{36,40... | collective-permute-start | bytes 1990664 | tf_op jit(solution)/shard_map/ppermute | solution.py:306
  15.6 3.3 %collective-permute-start.1 = (f32[648,256]{1,0:T(8,128)}, f32[648,256]{1,0:T(8,128)S(1)}, u32[]{:S(2)}, u32[]{:S(2)}) collective-permute-start(f32[648,256]{1,0:T(8,128)} %get-tuple-element.22), channel_id=1, source_target_pairs={{0,4},{4,0},{8,12},{12,8},{16,20},{20,16},{24,28},{28,24},{32,36},... | collective-permute-start | bytes 1990664 | tf_op jit(solution)/shard_map/ppermute | solution.py:306
  19.0 0.0 copy-done.4
  19.0 0.0 copy-done.6
  19.0 1.6 %copy-done.7 = f32[2,1024,256]{2,1,0:T(8,128)S(1)} copy-done((f32[2,1024,256]{2,1,0:T(8,128)S(1)}, f32[2,1024,256]{2,1,0:T(8,128)}, u32[]{:S(2)}) %copy-start.7) | copy-done | bytes 2097176
  20.6 3.5 %inner.1 = (f32[2,1024,256]{2,1,0:T(8,128)S(1)}, f32[2,128,1024]{2,1,0:T(8,128)S(1)}) custom-call(s32[1]{0:T(128)} %bitcast.place_ref, f32[2,1024,256]{2,1,0:T(8,128)S(1)} %copy-done.7, f32[2,64,1024]{2,1,0:T(8,128)S(1)} %bitcast.24, s32[2,1,1024]{2,1,0:T(1,128)S(1)} %copy-done.6), custom_call_target="tpu_custom_call" | custom-call | flops 3500000000 | bytes 8388608 | tf_op jit(solution)/shard_map/inner/pallas_call | solution.py:357
  24.0 0.0 collective-permute-done.4.three_ref
  24.0 0.0 collective-permute-done.3.two_ref
  24.0 0.0 collective-permute-done.2.one_ref
  24.1 0.0 copy-start
  24.1 0.0 copy-start.1
  24.1 0.0 copy-start.3
  24.1 1.3 %coarse.1 = (f32[64,256]{1,0:T(8,128)S(1)}, f32[64,256]{1,0:T(8,128)S(1)}) custom-call(s32[1]{0:T(128)} %bitcast.place_ref, f32[200,256]{1,0:T(8,128)S(1)} %copy-done.5, f32[200,256]{1,0:T(8,128)S(1)} %collective-permute-done.2.one_ref, f32[200,256]{1,0:T(8,128)S(1)} %collective-permute-done.3.two_ref, f32[200,256]{1,0:T(8,128)S(1)} %collective-permute-done.4.three_ref, ...), custom_call_target="tpu_custom_call" | custom-call | flops 30000001024 | bytes 1048576 | tf_op jit(solution)/shard_map/coarse/pallas_call | solution.py:369
  25.4 0.7 %collective-permute-start.5 = (f32[64,256]{1,0:T(8,128)S(1)}, f32[64,256]{1,0:T(8,128)S(1)}, u32[]{:S(2)}, u32[]{:S(2)}) collective-permute-start(f32[64,256]{1,0:T(8,128)S(1)} %get-tuple-element.24.own_cross_ref), channel_id=1, source_target_pairs={{4,8},{8,4},{12,16},{16,12},{20,24},{24,20},{28,32},{32,28},{36,40... | collective-permute-start | bytes 196616 | tf_op jit(solution)/shard_map/ppermute | solution.py:306
  26.0 3.5 %collective-permute-start.6 = (f32[64,256]{1,0:T(8,128)S(1)}, f32[64,256]{1,0:T(8,128)S(1)}, u32[]{:S(2)}, u32[]{:S(2)}) collective-permute-start(f32[64,256]{1,0:T(8,128)S(1)} %get-tuple-element.25.own_near_ref), channel_id=1, source_target_pairs={{0,4},{4,0},{8,12},{12,8},{16,20},{20,16},{24,28},{28,24},{32,36},... | collective-permute-start | bytes 196616 | tf_op jit(solution)/shard_map/ppermute | solution.py:306
  29.6 0.0 collective-permute-done.5.cross_pick_ref
  29.6 0.9 %collective-permute-done.6.near_pick_ref = f32[64,256]{1,0:T(8,128)S(1)} collective-permute-done((f32[64,256]{1,0:T(8,128)S(1)}, f32[64,256]{1,0:T(8,128)S(1)}, u32[]{:S(2)}, u32[]{:S(2)}) %collective-permute-start.6) | collective-permute-done | bytes 65568 | tf_op jit(solution)/shard_map/ppermute | solution.py:306
  30.5 0.0 collective-permute-done.cross_ref
  30.5 0.0 collective-permute-done.1.near_ref
  30.5 0.0 copy-start.2
  30.5 2.6 %outer.1 = (f32[2,1024,256]{2,1,0:T(8,128)S(1)}, f32[8,256]{1,0:T(8,128)S(1)}) custom-call(s32[1]{0:T(128)} %bitcast.place_ref, f32[2,1024,256]{2,1,0:T(8,128)S(1)} %get-tuple-element.19.part_ref, f32[2,128,1024]{2,1,0:T(8,128)S(1)} %get-tuple-element.20.mix_hbm.mix_ref, f32[648,256]{1,0:T(8,128)S(1)} %collective-permute-done.cross_ref, ...), custom_call_target="tpu_custom_call" | custom-call | flops 2000000000 | bytes 8388608 | tf_op jit(solution)/shard_map/outer/pallas_call | solution.py:381
  33.1 0.9 %collective-permute-start.7 = (f32[8,256]{1,0:T(8,128)S(1)}, f32[8,256]{1,0:T(8,128)S(1)}, u32[]{:S(2)}, u32[]{:S(2)}) collective-permute-start(f32[8,256]{1,0:T(8,128)S(1)} %get-tuple-element.26), channel_id=1, source_target_pairs={{0,4},{4,0},{8,12},{12,8},{16,20},{20,16},{24,28},{28,24},{32,36},... | collective-permute-start | bytes 24584 | tf_op jit(solution)/shard_map/ppermute | solution.py:306
  34.0 0.8 %collective-permute-done.7 = f32[8,256]{1,0:T(8,128)S(1)} collective-permute-done((f32[8,256]{1,0:T(8,128)S(1)}, f32[8,256]{1,0:T(8,128)S(1)}, u32[]{:S(2)}, u32[]{:S(2)}) %collective-permute-start.7) | collective-permute-done | bytes 8224 | tf_op jit(solution)/shard_map/ppermute | solution.py:306
  34.8 5.7 %collective-permute-start.10 = (f32[8,256]{1,0:T(8,128)S(1)}, f32[8,256]{1,0:T(8,128)S(1)}, u32[]{:S(2)}, u32[]{:S(2)}) collective-permute-start(f32[8,256]{1,0:T(8,128)S(1)} %add.30), channel_id=1, source_target_pairs={{0,33},{1,32},{2,35},{3,34},{4,37},{5,36},{6,39},{7,38},{8,41},{9,... | collective-permute-start | bytes 24584 | tf_op jit(solution)/shard_map/ppermute | solution.py:306
  40.5 0.3 collective-permute-start.9
  40.8 0.3 collective-permute-start.8
  41.1 1.1 %collective-permute-done.10 = f32[8,256]{1,0:T(8,128)S(1)} collective-permute-done((f32[8,256]{1,0:T(8,128)S(1)}, f32[8,256]{1,0:T(8,128)S(1)}, u32[]{:S(2)}, u32[]{:S(2)}) %collective-permute-start.10) | collective-permute-done | bytes 8224 | tf_op jit(solution)/shard_map/ppermute | solution.py:306
  42.2 2.0 %collective-permute-done.9 = f32[8,256]{1,0:T(8,128)S(1)} collective-permute-done((f32[8,256]{1,0:T(8,128)S(1)}, f32[8,256]{1,0:T(8,128)S(1)}, u32[]{:S(2)}, u32[]{:S(2)}) %collective-permute-start.9) | collective-permute-done | bytes 8224 | tf_op jit(solution)/shard_map/ppermute | solution.py:306
  44.2 0.3 collective-permute-done.8
  44.5 3.7 %collective-permute-start.13 = (f32[8,256]{1,0:T(8,128)S(1)}, f32[8,256]{1,0:T(8,128)S(1)}, u32[]{:S(2)}, u32[]{:S(2)}) collective-permute-start(f32[8,256]{1,0:T(8,128)S(1)} %add_add_fusion.2), channel_id=1, source_target_pairs={{0,99},{1,98},{2,97},{3,96},{4,103},{5,102},{6,101},{7,100},{8,107... | collective-permute-start | bytes 24584 | tf_op jit(solution)/shard_map/ppermute | solution.py:306
  48.2 1.1 %collective-permute-start.12 = (f32[8,256]{1,0:T(8,128)S(1)}, f32[8,256]{1,0:T(8,128)S(1)}, u32[]{:S(2)}, u32[]{:S(2)}) collective-permute-start(f32[8,256]{1,0:T(8,128)S(1)} %add_add_fusion.2), channel_id=1, source_target_pairs={{0,3},{1,2},{2,1},{3,0},{4,7},{5,6},{6,5},{7,4},{8,11},{9,10},{10,... | collective-permute-start | bytes 24584 | tf_op jit(solution)/shard_map/ppermute | solution.py:306
  49.3 1.1 %collective-permute-start.11 = (f32[8,256]{1,0:T(8,128)S(1)}, f32[8,256]{1,0:T(8,128)S(1)}, u32[]{:S(2)}, u32[]{:S(2)}) collective-permute-start(f32[8,256]{1,0:T(8,128)S(1)} %add_add_fusion.2), channel_id=1, source_target_pairs={{0,96},{1,97},{2,98},{3,99},{4,100},{5,101},{6,102},{7,103},{8,104... | collective-permute-start | bytes 24584 | tf_op jit(solution)/shard_map/ppermute | solution.py:306
  50.4 1.1 %collective-permute-done.13 = f32[8,256]{1,0:T(8,128)S(1)} collective-permute-done((f32[8,256]{1,0:T(8,128)S(1)}, f32[8,256]{1,0:T(8,128)S(1)}, u32[]{:S(2)}, u32[]{:S(2)}) %collective-permute-start.13) | collective-permute-done | bytes 8224 | tf_op jit(solution)/shard_map/ppermute | solution.py:306
  51.5 1.6 %collective-permute-done.12 = f32[8,256]{1,0:T(8,128)S(1)} collective-permute-done((f32[8,256]{1,0:T(8,128)S(1)}, f32[8,256]{1,0:T(8,128)S(1)}, u32[]{:S(2)}, u32[]{:S(2)}) %collective-permute-start.12) | collective-permute-done | bytes 8224 | tf_op jit(solution)/shard_map/ppermute | solution.py:306
  53.1 1.1 %collective-permute-done.11 = f32[8,256]{1,0:T(8,128)S(1)} collective-permute-done((f32[8,256]{1,0:T(8,128)S(1)}, f32[8,256]{1,0:T(8,128)S(1)}, u32[]{:S(2)}, u32[]{:S(2)}) %collective-permute-start.11) | collective-permute-done | bytes 8224 | tf_op jit(solution)/shard_map/ppermute | solution.py:306
  54.2 0.8 %collective-permute-start.16 = (f32[8,256]{1,0:T(8,128)S(1)}, f32[8,256]{1,0:T(8,128)S(1)}, u32[]{:S(2)}, u32[]{:S(2)}) collective-permute-start(f32[8,256]{1,0:T(8,128)S(1)} %add_add_fusion.1), channel_id=1, source_target_pairs={{0,16},{1,17},{2,18},{3,19},{4,20},{5,21},{6,22},{7,23},{8,24},{9,... | collective-permute-start | bytes 24584 | tf_op jit(solution)/shard_map/ppermute | solution.py:306
  55.0 1.9 %collective-permute-start.15 = (f32[8,256]{1,0:T(8,128)S(1)}, f32[8,256]{1,0:T(8,128)S(1)}, u32[]{:S(2)}, u32[]{:S(2)}) collective-permute-start(f32[8,256]{1,0:T(8,128)S(1)} %add_add_fusion.1), channel_id=1, source_target_pairs={{0,24},{1,25},{2,26},{3,27},{4,28},{5,29},{6,30},{7,31},{8,16},{9,... | collective-permute-start | bytes 24584 | tf_op jit(solution)/shard_map/ppermute | solution.py:306
  56.8 0.9 %collective-permute-start.14 = (f32[8,256]{1,0:T(8,128)S(1)}, f32[8,256]{1,0:T(8,128)S(1)}, u32[]{:S(2)}, u32[]{:S(2)}) collective-permute-start(f32[8,256]{1,0:T(8,128)S(1)} %add_add_fusion.1), channel_id=1, source_target_pairs={{0,8},{1,9},{2,10},{3,11},{4,12},{5,13},{6,14},{7,15},{8,0},{9,1},... | collective-permute-start | bytes 24584 | tf_op jit(solution)/shard_map/ppermute | solution.py:306
  57.7 1.7 %collective-permute-done.16 = f32[8,256]{1,0:T(8,128)S(1)} collective-permute-done((f32[8,256]{1,0:T(8,128)S(1)}, f32[8,256]{1,0:T(8,128)S(1)}, u32[]{:S(2)}, u32[]{:S(2)}) %collective-permute-start.16) | collective-permute-done | bytes 8224 | tf_op jit(solution)/shard_map/ppermute | solution.py:306
  59.4 0.5 collective-permute-done.15
  59.8 0.7 %collective-permute-done.14 = f32[8,256]{1,0:T(8,128)S(1)} collective-permute-done((f32[8,256]{1,0:T(8,128)S(1)}, f32[8,256]{1,0:T(8,128)S(1)}, u32[]{:S(2)}, u32[]{:S(2)}) %collective-permute-start.14) | collective-permute-done | bytes 8224 | tf_op jit(solution)/shard_map/ppermute | solution.py:306
  60.5 3.5 %final.1 = (f32[2,1024,256]{2,1,0:T(8,128)}, f32[2,1024,256]{2,1,0:T(8,128)}, f32[2,1024,256]{2,1,0:T(8,128)}, f32[1,256]{1,0:T(1,128)}) custom-call(f32[8,256]{1,0:T(8,128)S(1)} %add_add_fusion.total_ref, f32[2,1,1024]{2,1,0:T(1,128)S(1)} %copy-done.3, f32[2,1024,256]{2,1,0:T(8,128)S(1)} %bitcast.22, f32[2,1024,256]{2,1,0:T(8,128)S(1)} %bitcast.21, ...), custom_call_target="tpu_custom_call" | custom-call | tf_op jit(solution)/shard_map/final/pallas_call | solution.py:402
  (11 shorter events, 0.0 us)
Async XLA Ops:
  0.6 18.3 %copy-start.4 = (f32[2,1,64,1024]{3,2,1,0:T(8,128)S(1)}, f32[2,1,64,1024]{3,2,1,0:T(8,128)}, u32[]{:S(2)}) copy-start(f32[2,1,64,1024]{3,2,1,0:T(8,128)} %param.11) | copy-start | bytes 1572868
  0.6 18.3 %copy-start.6 = (s32[2,1,1024]{2,1,0:T(1,128)S(1)}, s32[2,1,1024]{2,1,0:T(1,128)}, u32[]{:S(2)}) copy-start(s32[2,1,1024]{2,1,0:T(1,128)} %partner_ref.1) | copy-start | bytes 24580
  10.6 13.4 %collective-permute-start.4 = (f32[200,256]{1,0:T(8,128)}, f32[200,256]{1,0:T(8,128)S(1)}, u32[]{:S(2)}, u32[]{:S(2)}) collective-permute-start(f32[200,256]{1,0:T(8,128)} %get-tuple-element.23.pay_ref), channel_id=1, source_target_pairs={{0,2},{1,3},{2,0},{3,1},{4,6},{5,7},{6,4},{7,5},{8,10},{9,11},{10,... | collective-permute-start | bytes 614408 | tf_op jit(solution)/shard_map/ppermute | solution.py:306
  13.8 10.2 %collective-permute-start.3 = (f32[200,256]{1,0:T(8,128)}, f32[200,256]{1,0:T(8,128)S(1)}, u32[]{:S(2)}, u32[]{:S(2)}) collective-permute-start(f32[200,256]{1,0:T(8,128)} %get-tuple-element.23.pay_ref), channel_id=1, source_target_pairs={{0,3},{1,2},{2,1},{3,0},{4,7},{5,6},{6,5},{7,4},{8,11},{9,10},{10,... | collective-permute-start | bytes 614408 | tf_op jit(solution)/shard_map/ppermute | solution.py:306
  14.9 9.1 %collective-permute-start.2 = (f32[200,256]{1,0:T(8,128)}, f32[200,256]{1,0:T(8,128)S(1)}, u32[]{:S(2)}, u32[]{:S(2)}) collective-permute-start(f32[200,256]{1,0:T(8,128)} %get-tuple-element.23.pay_ref), channel_id=1, source_target_pairs={{0,1},{1,0},{2,3},{3,2},{4,5},{5,4},{6,7},{7,6},{8,9},{9,8},{10,11... | collective-permute-start | bytes 614408 | tf_op jit(solution)/shard_map/ppermute | solution.py:306
  14.9 15.5 %collective-permute-start = (f32[648,256]{1,0:T(8,128)}, f32[648,256]{1,0:T(8,128)S(1)}, u32[]{:S(2)}, u32[]{:S(2)}) collective-permute-start(f32[648,256]{1,0:T(8,128)} %get-tuple-element.21), channel_id=1, source_target_pairs={{4,8},{8,4},{12,16},{16,12},{20,24},{24,20},{28,32},{32,28},{36,40... | collective-permute-start | bytes 1990664 | tf_op jit(solution)/shard_map/ppermute | solution.py:306
  15.6 14.9 %collective-permute-start.1 = (f32[648,256]{1,0:T(8,128)}, f32[648,256]{1,0:T(8,128)S(1)}, u32[]{:S(2)}, u32[]{:S(2)}) collective-permute-start(f32[648,256]{1,0:T(8,128)} %get-tuple-element.22), channel_id=1, source_target_pairs={{0,4},{4,0},{8,12},{12,8},{16,20},{20,16},{24,28},{28,24},{32,36},... | collective-permute-start | bytes 1990664 | tf_op jit(solution)/shard_map/ppermute | solution.py:306
  19.0 1.6 %copy-start.7 = (f32[2,1024,256]{2,1,0:T(8,128)S(1)}, f32[2,1024,256]{2,1,0:T(8,128)}, u32[]{:S(2)}) copy-start(f32[2,1024,256]{2,1,0:T(8,128)} %get-tuple-element.18.local_ref) | copy-start | bytes 6291460
  20.6 3.5 %copy-start.5 = (f32[200,256]{1,0:T(8,128)S(1)}, f32[200,256]{1,0:T(8,128)}, u32[]{:S(2)}) copy-start(f32[200,256]{1,0:T(8,128)} %get-tuple-element.23.pay_ref) | copy-start | bytes 614404
  24.1 6.4 %copy-start = (f32[2,1,1024,256]{3,2,1,0:T(8,128)S(1)}, f32[2,1,1024,256]{3,2,1,0:T(8,128)}, u32[]{:S(2)}) copy-start(f32[2,1,1024,256]{3,2,1,0:T(8,128)} %param.18) | copy-start | bytes 6291460
  24.1 6.4 %copy-start.1 = (f32[2,1,1024,256]{3,2,1,0:T(8,128)S(1)}, f32[2,1,1024,256]{3,2,1,0:T(8,128)}, u32[]{:S(2)}) copy-start(f32[2,1,1024,256]{3,2,1,0:T(8,128)} %param.17) | copy-start | bytes 6291460
  24.1 6.4 %copy-start.3 = (f32[2,1,1024]{2,1,0:T(1,128)S(1)}, f32[2,1,1024]{2,1,0:T(1,128)}, u32[]{:S(2)}) copy-start(f32[2,1,1024]{2,1,0:T(1,128)} %weight_ref.3) | copy-start | bytes 24580
  25.4 4.2 %collective-permute-start.5 = (f32[64,256]{1,0:T(8,128)S(1)}, f32[64,256]{1,0:T(8,128)S(1)}, u32[]{:S(2)}, u32[]{:S(2)}) collective-permute-start(f32[64,256]{1,0:T(8,128)S(1)} %get-tuple-element.24.own_cross_ref), channel_id=1, source_target_pairs={{4,8},{8,4},{12,16},{16,12},{20,24},{24,20},{28,32},{32,28},{36,40... | collective-permute-start | bytes 196616 | tf_op jit(solution)/shard_map/ppermute | solution.py:306
  26.0 4.4 %collective-permute-start.6 = (f32[64,256]{1,0:T(8,128)S(1)}, f32[64,256]{1,0:T(8,128)S(1)}, u32[]{:S(2)}, u32[]{:S(2)}) collective-permute-start(f32[64,256]{1,0:T(8,128)S(1)} %get-tuple-element.25.own_near_ref), channel_id=1, source_target_pairs={{0,4},{4,0},{8,12},{12,8},{16,20},{20,16},{24,28},{28,24},{32,36},... | collective-permute-start | bytes 196616 | tf_op jit(solution)/shard_map/ppermute | solution.py:306
  30.5 30.0 %copy-start.2 = (f32[2,1,1024,256]{3,2,1,0:T(8,128)S(1)}, f32[2,1,1024,256]{3,2,1,0:T(8,128)}, u32[]{:S(2)}) copy-start(f32[2,1,1024,256]{3,2,1,0:T(8,128)} %param.16) | copy-start | bytes 6291460
  33.1 1.7 %collective-permute-start.7 = (f32[8,256]{1,0:T(8,128)S(1)}, f32[8,256]{1,0:T(8,128)S(1)}, u32[]{:S(2)}, u32[]{:S(2)}) collective-permute-start(f32[8,256]{1,0:T(8,128)S(1)} %get-tuple-element.26), channel_id=1, source_target_pairs={{0,4},{4,0},{8,12},{12,8},{16,20},{20,16},{24,28},{28,24},{32,36},... | collective-permute-start | bytes 24584 | tf_op jit(solution)/shard_map/ppermute | solution.py:306
  34.8 7.3 %collective-permute-start.10 = (f32[8,256]{1,0:T(8,128)S(1)}, f32[8,256]{1,0:T(8,128)S(1)}, u32[]{:S(2)}, u32[]{:S(2)}) collective-permute-start(f32[8,256]{1,0:T(8,128)S(1)} %add.30), channel_id=1, source_target_pairs={{0,33},{1,32},{2,35},{3,34},{4,37},{5,36},{6,39},{7,38},{8,41},{9,... | collective-permute-start | bytes 24584 | tf_op jit(solution)/shard_map/ppermute | solution.py:306
  40.5 3.7 %collective-permute-start.9 = (f32[8,256]{1,0:T(8,128)S(1)}, f32[8,256]{1,0:T(8,128)S(1)}, u32[]{:S(2)}, u32[]{:S(2)}) collective-permute-start(f32[8,256]{1,0:T(8,128)S(1)} %add.30), channel_id=1, source_target_pairs={{0,1},{1,0},{2,3},{3,2},{4,5},{5,4},{6,7},{7,6},{8,9},{9,8},{10,11... | collective-permute-start | bytes 24584 | tf_op jit(solution)/shard_map/ppermute | solution.py:306
  40.8 3.7 %collective-permute-start.8 = (f32[8,256]{1,0:T(8,128)S(1)}, f32[8,256]{1,0:T(8,128)S(1)}, u32[]{:S(2)}, u32[]{:S(2)}) collective-permute-start(f32[8,256]{1,0:T(8,128)S(1)} %add.30), channel_id=1, source_target_pairs={{0,32},{1,33},{2,34},{3,35},{4,36},{5,37},{6,38},{7,39},{8,40},{9,... | collective-permute-start | bytes 24584 | tf_op jit(solution)/shard_map/ppermute | solution.py:306
  44.5 7.0 %collective-permute-start.13 = (f32[8,256]{1,0:T(8,128)S(1)}, f32[8,256]{1,0:T(8,128)S(1)}, u32[]{:S(2)}, u32[]{:S(2)}) collective-permute-start(f32[8,256]{1,0:T(8,128)S(1)} %add_add_fusion.2), channel_id=1, source_target_pairs={{0,99},{1,98},{2,97},{3,96},{4,103},{5,102},{6,101},{7,100},{8,107... | collective-permute-start | bytes 24584 | tf_op jit(solution)/shard_map/ppermute | solution.py:306
  48.2 4.9 %collective-permute-start.12 = (f32[8,256]{1,0:T(8,128)S(1)}, f32[8,256]{1,0:T(8,128)S(1)}, u32[]{:S(2)}, u32[]{:S(2)}) collective-permute-start(f32[8,256]{1,0:T(8,128)S(1)} %add_add_fusion.2), channel_id=1, source_target_pairs={{0,3},{1,2},{2,1},{3,0},{4,7},{5,6},{6,5},{7,4},{8,11},{9,10},{10,... | collective-permute-start | bytes 24584 | tf_op jit(solution)/shard_map/ppermute | solution.py:306
  49.3 4.9 %collective-permute-start.11 = (f32[8,256]{1,0:T(8,128)S(1)}, f32[8,256]{1,0:T(8,128)S(1)}, u32[]{:S(2)}, u32[]{:S(2)}) collective-permute-start(f32[8,256]{1,0:T(8,128)S(1)} %add_add_fusion.2), channel_id=1, source_target_pairs={{0,96},{1,97},{2,98},{3,99},{4,100},{5,101},{6,102},{7,103},{8,104... | collective-permute-start | bytes 24584 | tf_op jit(solution)/shard_map/ppermute | solution.py:306
  54.2 5.2 %collective-permute-start.16 = (f32[8,256]{1,0:T(8,128)S(1)}, f32[8,256]{1,0:T(8,128)S(1)}, u32[]{:S(2)}, u32[]{:S(2)}) collective-permute-start(f32[8,256]{1,0:T(8,128)S(1)} %add_add_fusion.1), channel_id=1, source_target_pairs={{0,16},{1,17},{2,18},{3,19},{4,20},{5,21},{6,22},{7,23},{8,24},{9,... | collective-permute-start | bytes 24584 | tf_op jit(solution)/shard_map/ppermute | solution.py:306
  55.0 4.9 %collective-permute-start.15 = (f32[8,256]{1,0:T(8,128)S(1)}, f32[8,256]{1,0:T(8,128)S(1)}, u32[]{:S(2)}, u32[]{:S(2)}) collective-permute-start(f32[8,256]{1,0:T(8,128)S(1)} %add_add_fusion.1), channel_id=1, source_target_pairs={{0,24},{1,25},{2,26},{3,27},{4,28},{5,29},{6,30},{7,31},{8,16},{9,... | collective-permute-start | bytes 24584 | tf_op jit(solution)/shard_map/ppermute | solution.py:306
  56.8 3.7 %collective-permute-start.14 = (f32[8,256]{1,0:T(8,128)S(1)}, f32[8,256]{1,0:T(8,128)S(1)}, u32[]{:S(2)}, u32[]{:S(2)}) collective-permute-start(f32[8,256]{1,0:T(8,128)S(1)} %add_add_fusion.1), channel_id=1, source_target_pairs={{0,8},{1,9},{2,10},{3,11},{4,12},{5,13},{6,14},{7,15},{8,0},{9,1},... | collective-permute-start | bytes 24584 | tf_op jit(solution)/shard_map/ppermute | solution.py:306

commit v6 on v4

--- a/solution.py
+++ b/solution.py
@@ -83,7 +83,7 @@
 def local_kernel(
     place_ref, pay_hbm, flex_hbm, direc_hbm, coup_hbm, partner_hbm,
     local_hbm, cross_hbm, near_hbm,
-    flex, direc, coup, partner, local, packed, right, high, low, sems, out_sems,
+    flex, direc, coup, partner, local, packed, places, right, high, low, sems, out_sems,
 ):
     del pay_hbm
     direc_copy = pltpu.make_async_copy(direc_hbm, direc, sems.at[0])
@@ -97,32 +97,14 @@
     out_copies = [
         pltpu.make_async_copy(local.at[s], local_hbm.at[s], out_sems.at[s]) for s in range(2)
     ]
+    for copy in others:
+        copy.start()
     direc_copy.start()
-    for copy in flex_copies + others:
-        copy.start()
+    flex_copies[0].start()
     me = place_ref[0]
     odd = lax.rem(me, 2)
-    direc_copy.wait()
-    for s in range(2):
-        dh, dl = split(direc[s])
-        right[s, 0:N] = dh
-        right[s, N:] = dl
-    flex_copies[0].wait()
-    for s in range(2):
-        if s == 1:
-            out_copies[0].start()
-            flex_copies[1].wait()
-            for copy in others:
-                copy.wait()
-        for r in range(ROUNDS):
-            rows = slice(r * STRIP, (r + 1) * STRIP)
-            ah, al = split(flex[s, rows])
-            out = dot(ah, right[s, 0:N]) + dot(ah, right[s, N:]) + dot(al, right[s, 0:N])
-            local[s, rows] = out
-            oh, ol = split(out)
-            high[s, rows] = oh
-            low[s, rows] = ol
-    out_copies[1].start()
+    for copy in others:
+        copy.wait()
     for s in range(2):
         target = partner[s] - (2 * me - 1) * N
         match = (target >= 3 * N) if s else (target < N)
@@ -138,7 +120,7 @@
         packed[s, NAMES:] = jnp.zeros((8, L), F32)
         for c in range(2):
             place = one_hot(iota((L, N), 0) + c * L == key)
-            packed[s, c * L : (c + 1) * L] = dot(place, high[s]) + dot(place, low[s])
+            places[s, c * L : (c + 1) * L] = place
             extra = lax.dot_general(
                 stack, place, (((1,), (1,)), ((), ())), preferred_element_type=F32
             )
@@ -146,10 +128,32 @@
             packed[s, NAMES + c : NAMES + c + 1] = (
                 extra[2 * C : 2 * C + 1] * 32.0 + extra[2 * C + 1 : 2 * C + 2]
             )
+    direc_copy.wait()
+    flex_copies[1].start()
+    for s in range(2):
+        dh, dl = split(direc[s])
+        right[s, 0:N] = dh
+        right[s, N:] = dl
+    flex_copies[0].wait()
+    for s in range(2):
+        if s == 1:
+            out_copies[0].start()
+            flex_copies[1].wait()
+        for r in range(ROUNDS):
+            rows = slice(r * STRIP, (r + 1) * STRIP)
+            ah, al = split(flex[s, rows])
+            out = dot(ah, right[s, 0:N]) + dot(ah, right[s, N:]) + dot(al, right[s, 0:N])
+            local[s, rows] = out
+            oh, ol = split(out)
+            high[s, rows] = oh
+            low[s, rows] = ol
+    for s in range(2):
+        packed[s, 0:HALF] = dot(places[s], high[s]) + dot(places[s], low[s])
     cross_copy = pltpu.make_async_copy(packed.at[odd], cross_hbm, out_sems.at[2])
     near_copy = pltpu.make_async_copy(packed.at[1 - odd], near_hbm, out_sems.at[3])
     cross_copy.start()
     near_copy.start()
+    out_copies[1].start()
     for copy in out_copies:
         copy.wait()
     cross_copy.wait()
@@ -354,6 +358,7 @@
             pltpu.VMEM((2, 1, N), jnp.int32),
             pltpu.VMEM((2, N, L), F32),
             pltpu.VMEM((2, NAMES + 8, L), F32),
+            pltpu.VMEM((2, HALF, N), BF16),
             pltpu.VMEM((2, 2 * N, L), BF16),
             pltpu.VMEM((2, N, L), BF16),
             pltpu.VMEM((2, N, L), BF16),

time: 62.5 us -> 62.7 us (level)
  transfers between devices with their start and end apart: 17 -> 17, of which waited for: 8 -> 8; matrix products, arithmetic and copies ran while one was open for 0% -> 0% of each run, Pallas kernels for 22% -> 23%
where the time goes in v6:
time: 62.7 us; the launch traced here: 62.5 us
  starting transfers between devices  28 us (45%)
  Pallas kernels  22.6 us (36%)
  waiting for transfers between devices  10.9 us (17%)
  between operations  0.99 us (2%)
    ppermute x17, starting transfers between devices, exchange(): return lax.ppermute(x, axes, pairs)  28 us
    ppermute x17, waiting for transfers between devices, exchange(): return lax.ppermute(x, axes, pairs)  10.9 us
    pallas_call x1, Pallas kernels, per_device(): pl.pallas_call(local_kernel, out_shape=(jax.ShapeDtypeStruct((2, N, L), F...  9.42 us
    pallas_call x1, Pallas kernels, per_device(): pl.pallas_call(final_kernel, out_shape=(whole, whole, whole, jax.ShapeDty...  3.48 us
    pallas_call x1, Pallas kernels, per_device(): pl.pallas_call(inner_kernel, out_shape=(whole, jax.ShapeDtypeStruct((3, 8...  3.41 us
    pallas_call x1, Pallas kernels, per_device(): pl.pallas_call(primal_kernel, out_shape=jax.ShapeDtypeStruct((3 * C + 8,...  3.17 us
    pallas_call x1, Pallas kernels, per_device(): pl.pallas_call(outer_kernel, out_shape=(whole, jax.ShapeDtypeStruct((8, L...  1.83 us
    pallas_call x1, Pallas kernels, per_device(): pl.pallas_call(coarse_kernel, out_shape=(piece, piece), in_specs=[smem()]...  1.27 us
  transfers between devices with their start and end apart: 17, of which 8 were waited for; matrix products, arithmetic and copies ran while one was open for 0% of the time, Pallas kernels for 23%

profile of v6, /device:TPU:0, one launch (start us, length us, event | category | flops | bytes accessed | tf_op | source)
XLA Modules:
  0.0 62.5 jit_solution(8291079097928833442)
XLA Ops:
  0.6 3.2 %primal.1.pay_hbm.pay_ref = f32[200,256]{1,0:T(8,128)} custom-call(f32[2,1024,256]{2,1,0:T(8,128)} %bitcast.17, f32[2,64,1024]{2,1,0:T(8,128)} %bitcast.24, s32[2,1,64]{2,1,0:T(1,128)} %map_hbm.1, f32[64,256]{1,0:T(8,128)} %bitcast.27), custom_call_target="tpu_custom_call" | custom-call | flops 200000000 | bytes 3145728 | tf_op jit(solution)/shard_map/primal/pallas_call | solution.py:331
  3.8 3.2 %collective-permute-start.2 = (f32[200,256]{1,0:T(8,128)}, f32[200,256]{1,0:T(8,128)S(1)}, u32[]{:S(2)}, u32[]{:S(2)}) collective-permute-start(f32[200,256]{1,0:T(8,128)} %primal.1.pay_hbm.pay_ref), channel_id=1, source_target_pairs={{0,2},{1,3},{2,0},{3,1},{4,6},{5,7},{6,4},{7,5},{8,10},{9,11},{10,... | collective-permute-start | bytes 614408 | tf_op jit(solution)/shard_map/ppermute | solution.py:318
  7.0 1.1 %collective-permute-start.1 = (f32[200,256]{1,0:T(8,128)}, f32[200,256]{1,0:T(8,128)S(1)}, u32[]{:S(2)}, u32[]{:S(2)}) collective-permute-start(f32[200,256]{1,0:T(8,128)} %primal.1.pay_hbm.pay_ref), channel_id=1, source_target_pairs={{0,3},{1,2},{2,1},{3,0},{4,7},{5,6},{6,5},{7,4},{8,11},{9,10},{10,... | collective-permute-start | bytes 614408 | tf_op jit(solution)/shard_map/ppermute | solution.py:318
  8.1 0.0 collective-permute-start
  8.1 9.4 %local.1 = (f32[2,1024,256]{2,1,0:T(8,128)}, f32[648,256]{1,0:T(8,128)}, f32[648,256]{1,0:T(8,128)}) custom-call(s32[1]{0:T(128)} %bitcast.place_ref, f32[200,256]{1,0:T(8,128)} %primal.1.pay_hbm.pay_ref, f32[2,1024,1024]{2,1,0:T(8,128)} %bitcast.28, f32[2,1024,256]{2,1,0:T(8,128)} %bitcast.18, f32[2,64,1024]{2,1,0:T(8,128)} %bitcast.25, ...), custom_call_target="tpu_custom_call" | custom-call | flops 4000000000 | bytes 12582912 | tf_op jit(solution)/shard_map/local/pallas_call | solution.py:349
  17.6 0.7 %collective-permute-start.3 = (f32[648,256]{1,0:T(8,128)}, f32[648,256]{1,0:T(8,128)S(1)}, u32[]{:S(2)}, u32[]{:S(2)}) collective-permute-start(f32[648,256]{1,0:T(8,128)} %get-tuple-element.21), channel_id=1, source_target_pairs={{4,8},{8,4},{12,16},{16,12},{20,24},{24,20},{28,32},{32,28},{36,40... | collective-permute-start | bytes 1990664 | tf_op jit(solution)/shard_map/ppermute | solution.py:318
  18.3 0.0 copy-start
  18.3 0.0 copy-start.1
  18.3 0.0 copy-start.3
  18.3 0.0 copy-start.5
  18.3 0.0 copy-start.6
  18.3 0.0 copy-start.7
  18.3 3.3 %collective-permute-start.4 = (f32[648,256]{1,0:T(8,128)}, f32[648,256]{1,0:T(8,128)S(1)}, u32[]{:S(2)}, u32[]{:S(2)}) collective-permute-start(f32[648,256]{1,0:T(8,128)} %get-tuple-element.22), channel_id=1, source_target_pairs={{0,4},{4,0},{8,12},{12,8},{16,20},{20,16},{24,28},{28,24},{32,36},... | collective-permute-start | bytes 1990664 | tf_op jit(solution)/shard_map/ppermute | solution.py:318
  21.7 0.0 collective-permute-done.2.three_ref
  21.7 0.0 collective-permute-done.1.two_ref
  21.7 0.0 collective-permute-done.one_ref
  21.7 0.0 copy-done.4
  21.7 1.3 %coarse.1 = (f32[64,256]{1,0:T(8,128)S(1)}, f32[64,256]{1,0:T(8,128)S(1)}) custom-call(s32[1]{0:T(128)} %bitcast.place_ref, f32[200,256]{1,0:T(8,128)S(1)} %copy-done.4, f32[200,256]{1,0:T(8,128)S(1)} %collective-permute-done.one_ref, f32[200,256]{1,0:T(8,128)S(1)} %collective-permute-done.1.two_ref, f32[200,256]{1,0:T(8,128)S(1)} %collective-permute-done.2.three_ref), custom_call_target="tpu_custom_call" | custom-call | flops 30000001024 | bytes 1048576 | tf_op jit(solution)/shard_map/coarse/pallas_call | solution.py:384
  23.0 0.7 %collective-permute-start.5 = (f32[64,256]{1,0:T(8,128)S(1)}, f32[64,256]{1,0:T(8,128)S(1)}, u32[]{:S(2)}, u32[]{:S(2)}) collective-permute-start(f32[64,256]{1,0:T(8,128)S(1)} %get-tuple-element.18.cross_ref), channel_id=1, source_target_pairs={{4,8},{8,4},{12,16},{16,12},{20,24},{24,20},{28,32},{32,28},{36,40... | collective-permute-start | bytes 196616 | tf_op jit(solution)/shard_map/ppermute | solution.py:318
  23.6 3.5 %collective-permute-start.6 = (f32[64,256]{1,0:T(8,128)S(1)}, f32[64,256]{1,0:T(8,128)S(1)}, u32[]{:S(2)}, u32[]{:S(2)}) collective-permute-start(f32[64,256]{1,0:T(8,128)S(1)} %get-tuple-element.19.near_ref), channel_id=1, source_target_pairs={{0,4},{4,0},{8,12},{12,8},{16,20},{20,16},{24,28},{28,24},{32,36},... | collective-permute-start | bytes 196616 | tf_op jit(solution)/shard_map/ppermute | solution.py:318
  27.2 3.4 %inner.1 = (f32[2,1024,256]{2,1,0:T(8,128)S(1)}, f32[3,8,256]{2,1,0:T(8,128)S(1)}) custom-call(s32[1]{0:T(128)} %bitcast.place_ref, f32[2,1024,256]{2,1,0:T(8,128)S(1)} %copy-done.7, f32[64,256]{1,0:T(8,128)S(1)} %get-tuple-element.18.cross_ref, f32[64,256]{1,0:T(8,128)S(1)} %get-tuple-element.19.near_ref, f32[2,64,1024]{2,1,0:T(8,128)S(1)} %bitcast.26, ...), custom_call_target="tpu_custom_call" | custom-call | flops 2500000000 | bytes 8388608 | tf_op jit(solution)/shard_map/inner/pallas_call | solution.py:396
  30.6 0.0 copy-start.2
  30.6 0.0 collective-permute-done.5.cross_pick_ref
  30.7 0.0 collective-permute-done.6.near_pick_ref
  30.7 0.0 collective-permute-done.3.cross_ref
  30.7 0.0 collective-permute-done.4.near_ref
  30.7 1.8 %outer.1 = (f32[2,1024,256]{2,1,0:T(8,128)S(1)}, f32[8,256]{1,0:T(8,128)S(1)}) custom-call(s32[1]{0:T(128)} %bitcast.place_ref, f32[2,1024,256]{2,1,0:T(8,128)S(1)} %get-tuple-element.20.part_ref, f32[648,256]{1,0:T(8,128)S(1)} %collective-permute-done.3.cross_ref, f32[648,256]{1,0:T(8,128)S(1)} %collective-permute-done.4.near_ref, ...), custom_call_target="tpu_custom_call" | custom-call | tf_op jit(solution)/shard_map/outer/pallas_call | solution.py:411
  32.5 0.2 collective-permute-start.7
  32.7 1.1 %collective-permute-done.7 = f32[8,256]{1,0:T(8,128)S(1)} collective-permute-done((f32[8,256]{1,0:T(8,128)S(1)}, f32[8,256]{1,0:T(8,128)S(1)}, u32[]{:S(2)}, u32[]{:S(2)}) %collective-permute-start.7) | collective-permute-done | bytes 8224 | tf_op jit(solution)/shard_map/ppermute | solution.py:318
  33.8 4.9 %collective-permute-start.10 = (f32[8,256]{1,0:T(8,128)S(1)}, f32[8,256]{1,0:T(8,128)S(1)}, u32[]{:S(2)}, u32[]{:S(2)}) collective-permute-start(f32[8,256]{1,0:T(8,128)S(1)} %add.30), channel_id=1, source_target_pairs={{0,33},{1,32},{2,35},{3,34},{4,37},{5,36},{6,39},{7,38},{8,41},{9,... | collective-permute-start | bytes 24584 | tf_op jit(solution)/shard_map/ppermute | solution.py:318
  38.7 0.0 collective-permute-start.9
  38.7 0.6 collective-permute-start.8
  39.3 1.1 %collective-permute-done.10 = f32[8,256]{1,0:T(8,128)S(1)} collective-permute-done((f32[8,256]{1,0:T(8,128)S(1)}, f32[8,256]{1,0:T(8,128)S(1)}, u32[]{:S(2)}, u32[]{:S(2)}) %collective-permute-start.10) | collective-permute-done | bytes 8224 | tf_op jit(solution)/shard_map/ppermute | solution.py:318
  40.3 2.0 %collective-permute-done.9 = f32[8,256]{1,0:T(8,128)S(1)} collective-permute-done((f32[8,256]{1,0:T(8,128)S(1)}, f32[8,256]{1,0:T(8,128)S(1)}, u32[]{:S(2)}, u32[]{:S(2)}) %collective-permute-start.9) | collective-permute-done | bytes 8224 | tf_op jit(solution)/shard_map/ppermute | solution.py:318
  42.4 0.0 collective-permute-done.8
  42.4 3.8 %collective-permute-start.13 = (f32[8,256]{1,0:T(8,128)S(1)}, f32[8,256]{1,0:T(8,128)S(1)}, u32[]{:S(2)}, u32[]{:S(2)}) collective-permute-start(f32[8,256]{1,0:T(8,128)S(1)} %add_add_fusion.2), channel_id=1, source_target_pairs={{0,99},{1,98},{2,97},{3,96},{4,103},{5,102},{6,101},{7,100},{8,107... | collective-permute-start | bytes 24584 | tf_op jit(solution)/shard_map/ppermute | solution.py:318
  46.2 1.1 %collective-permute-start.12 = (f32[8,256]{1,0:T(8,128)S(1)}, f32[8,256]{1,0:T(8,128)S(1)}, u32[]{:S(2)}, u32[]{:S(2)}) collective-permute-start(f32[8,256]{1,0:T(8,128)S(1)} %add_add_fusion.2), channel_id=1, source_target_pairs={{0,3},{1,2},{2,1},{3,0},{4,7},{5,6},{6,5},{7,4},{8,11},{9,10},{10,... | collective-permute-start | bytes 24584 | tf_op jit(solution)/shard_map/ppermute | solution.py:318
  47.3 1.1 %collective-permute-start.11 = (f32[8,256]{1,0:T(8,128)S(1)}, f32[8,256]{1,0:T(8,128)S(1)}, u32[]{:S(2)}, u32[]{:S(2)}) collective-permute-start(f32[8,256]{1,0:T(8,128)S(1)} %add_add_fusion.2), channel_id=1, source_target_pairs={{0,96},{1,97},{2,98},{3,99},{4,100},{5,101},{6,102},{7,103},{8,104... | collective-permute-start | bytes 24584 | tf_op jit(solution)/shard_map/ppermute | solution.py:318
  48.4 1.1 %collective-permute-done.13 = f32[8,256]{1,0:T(8,128)S(1)} collective-permute-done((f32[8,256]{1,0:T(8,128)S(1)}, f32[8,256]{1,0:T(8,128)S(1)}, u32[]{:S(2)}, u32[]{:S(2)}) %collective-permute-start.13) | collective-permute-done | bytes 8224 | tf_op jit(solution)/shard_map/ppermute | solution.py:318
  49.4 1.6 %collective-permute-done.12 = f32[8,256]{1,0:T(8,128)S(1)} collective-permute-done((f32[8,256]{1,0:T(8,128)S(1)}, f32[8,256]{1,0:T(8,128)S(1)}, u32[]{:S(2)}, u32[]{:S(2)}) %collective-permute-start.12) | collective-permute-done | bytes 8224 | tf_op jit(solution)/shard_map/ppermute | solution.py:318
  51.0 1.1 %collective-permute-done.11 = f32[8,256]{1,0:T(8,128)S(1)} collective-permute-done((f32[8,256]{1,0:T(8,128)S(1)}, f32[8,256]{1,0:T(8,128)S(1)}, u32[]{:S(2)}, u32[]{:S(2)}) %collective-permute-start.11) | collective-permute-done | bytes 8224 | tf_op jit(solution)/shard_map/ppermute | solution.py:318
  52.2 1.8 %collective-permute-start.16 = (f32[8,256]{1,0:T(8,128)S(1)}, f32[8,256]{1,0:T(8,128)S(1)}, u32[]{:S(2)}, u32[]{:S(2)}) collective-permute-start(f32[8,256]{1,0:T(8,128)S(1)} %add_add_fusion.1), channel_id=1, source_target_pairs={{0,16},{1,17},{2,18},{3,19},{4,20},{5,21},{6,22},{7,23},{8,24},{9,... | collective-permute-start | bytes 24584 | tf_op jit(solution)/shard_map/ppermute | solution.py:318
  54.0 1.2 %collective-permute-start.15 = (f32[8,256]{1,0:T(8,128)S(1)}, f32[8,256]{1,0:T(8,128)S(1)}, u32[]{:S(2)}, u32[]{:S(2)}) collective-permute-start(f32[8,256]{1,0:T(8,128)S(1)} %add_add_fusion.1), channel_id=1, source_target_pairs={{0,24},{1,25},{2,26},{3,27},{4,28},{5,29},{6,30},{7,31},{8,16},{9,... | collective-permute-start | bytes 24584 | tf_op jit(solution)/shard_map/ppermute | solution.py:318
  55.1 0.8 %collective-permute-start.14 = (f32[8,256]{1,0:T(8,128)S(1)}, f32[8,256]{1,0:T(8,128)S(1)}, u32[]{:S(2)}, u32[]{:S(2)}) collective-permute-start(f32[8,256]{1,0:T(8,128)S(1)} %add_add_fusion.1), channel_id=1, source_target_pairs={{0,8},{1,9},{2,10},{3,11},{4,12},{5,13},{6,14},{7,15},{8,0},{9,1},... | collective-permute-start | bytes 24584 | tf_op jit(solution)/shard_map/ppermute | solution.py:318
  55.9 1.4 %collective-permute-done.16 = f32[8,256]{1,0:T(8,128)S(1)} collective-permute-done((f32[8,256]{1,0:T(8,128)S(1)}, f32[8,256]{1,0:T(8,128)S(1)}, u32[]{:S(2)}, u32[]{:S(2)}) %collective-permute-start.16) | collective-permute-done | bytes 8224 | tf_op jit(solution)/shard_map/ppermute | solution.py:318
  57.3 1.5 %collective-permute-done.15 = f32[8,256]{1,0:T(8,128)S(1)} collective-permute-done((f32[8,256]{1,0:T(8,128)S(1)}, f32[8,256]{1,0:T(8,128)S(1)}, u32[]{:S(2)}, u32[]{:S(2)}) %collective-permute-start.15) | collective-permute-done | bytes 8224 | tf_op jit(solution)/shard_map/ppermute | solution.py:318
  58.8 0.0 collective-permute-done.14
  58.8 3.5 %final.1 = (f32[2,1024,256]{2,1,0:T(8,128)}, f32[2,1024,256]{2,1,0:T(8,128)}, f32[2,1024,256]{2,1,0:T(8,128)}, f32[1,256]{1,0:T(1,128)}) custom-call(f32[8,256]{1,0:T(8,128)S(1)} %add_add_fusion.total_ref, f32[2,1,1024]{2,1,0:T(1,128)S(1)} %copy-done.5, f32[2,1024,256]{2,1,0:T(8,128)S(1)} %bitcast.23, f32[2,1024,256]{2,1,0:T(8,128)S(1)} %bitcast.22, ...), custom_call_target="tpu_custom_call" | custom-call | tf_op jit(solution)/shard_map/final/pallas_call | solution.py:427
  (12 shorter events, 0.0 us)
Async XLA Ops:
  3.8 17.9 %collective-permute-start.2 = (f32[200,256]{1,0:T(8,128)}, f32[200,256]{1,0:T(8,128)S(1)}, u32[]{:S(2)}, u32[]{:S(2)}) collective-permute-start(f32[200,256]{1,0:T(8,128)} %primal.1.pay_hbm.pay_ref), channel_id=1, source_target_pairs={{0,2},{1,3},{2,0},{3,1},{4,6},{5,7},{6,4},{7,5},{8,10},{9,11},{10,... | collective-permute-start | bytes 614408 | tf_op jit(solution)/shard_map/ppermute | solution.py:318
  7.0 14.7 %collective-permute-start.1 = (f32[200,256]{1,0:T(8,128)}, f32[200,256]{1,0:T(8,128)S(1)}, u32[]{:S(2)}, u32[]{:S(2)}) collective-permute-start(f32[200,256]{1,0:T(8,128)} %primal.1.pay_hbm.pay_ref), channel_id=1, source_target_pairs={{0,3},{1,2},{2,1},{3,0},{4,7},{5,6},{6,5},{7,4},{8,11},{9,10},{10,... | collective-permute-start | bytes 614408 | tf_op jit(solution)/shard_map/ppermute | solution.py:318
  8.1 13.5 %collective-permute-start = (f32[200,256]{1,0:T(8,128)}, f32[200,256]{1,0:T(8,128)S(1)}, u32[]{:S(2)}, u32[]{:S(2)}) collective-permute-start(f32[200,256]{1,0:T(8,128)} %primal.1.pay_hbm.pay_ref), channel_id=1, source_target_pairs={{0,1},{1,0},{2,3},{3,2},{4,5},{5,4},{6,7},{7,6},{8,9},{9,8},{10,11... | collective-permute-start | bytes 614408 | tf_op jit(solution)/shard_map/ppermute | solution.py:318
  8.1 13.5 %copy-start.4 = (f32[200,256]{1,0:T(8,128)S(1)}, f32[200,256]{1,0:T(8,128)}, u32[]{:S(2)}) copy-start(f32[200,256]{1,0:T(8,128)} %primal.1.pay_hbm.pay_ref) | copy-start | bytes 614404
  17.6 13.1 %collective-permute-start.3 = (f32[648,256]{1,0:T(8,128)}, f32[648,256]{1,0:T(8,128)S(1)}, u32[]{:S(2)}, u32[]{:S(2)}) collective-permute-start(f32[648,256]{1,0:T(8,128)} %get-tuple-element.21), channel_id=1, source_target_pairs={{4,8},{8,4},{12,16},{16,12},{20,24},{24,20},{28,32},{32,28},{36,40... | collective-permute-start | bytes 1990664 | tf_op jit(solution)/shard_map/ppermute | solution.py:318
  18.3 8.9 %copy-start = (f32[2,1,1024,256]{3,2,1,0:T(8,128)S(1)}, f32[2,1,1024,256]{3,2,1,0:T(8,128)}, u32[]{:S(2)}) copy-start(f32[2,1,1024,256]{3,2,1,0:T(8,128)} %param.18) | copy-start | bytes 6291460
  18.3 8.9 %copy-start.1 = (f32[2,1,1024,256]{3,2,1,0:T(8,128)S(1)}, f32[2,1,1024,256]{3,2,1,0:T(8,128)}, u32[]{:S(2)}) copy-start(f32[2,1,1024,256]{3,2,1,0:T(8,128)} %param.17) | copy-start | bytes 6291460
  18.3 8.9 %copy-start.3 = (f32[2,1,64,1024]{3,2,1,0:T(8,128)S(1)}, f32[2,1,64,1024]{3,2,1,0:T(8,128)}, u32[]{:S(2)}) copy-start(f32[2,1,64,1024]{3,2,1,0:T(8,128)} %param.11) | copy-start | bytes 1572868
  18.3 8.9 %copy-start.5 = (f32[2,1,1024]{2,1,0:T(1,128)S(1)}, f32[2,1,1024]{2,1,0:T(1,128)}, u32[]{:S(2)}) copy-start(f32[2,1,1024]{2,1,0:T(1,128)} %weight_ref.5) | copy-start | bytes 24580
  18.3 8.9 %copy-start.6 = (s32[2,1,1024]{2,1,0:T(1,128)S(1)}, s32[2,1,1024]{2,1,0:T(1,128)}, u32[]{:S(2)}) copy-start(s32[2,1,1024]{2,1,0:T(1,128)} %partner_ref.1) | copy-start | bytes 24580
  18.3 8.9 %copy-start.7 = (f32[2,1024,256]{2,1,0:T(8,128)S(1)}, f32[2,1024,256]{2,1,0:T(8,128)}, u32[]{:S(2)}) copy-start(f32[2,1024,256]{2,1,0:T(8,128)} %get-tuple-element.17.local_ref) | copy-start | bytes 6291460
  18.3 12.3 %collective-permute-start.4 = (f32[648,256]{1,0:T(8,128)}, f32[648,256]{1,0:T(8,128)S(1)}, u32[]{:S(2)}, u32[]{:S(2)}) collective-permute-start(f32[648,256]{1,0:T(8,128)} %get-tuple-element.22), channel_id=1, source_target_pairs={{0,4},{4,0},{8,12},{12,8},{16,20},{20,16},{24,28},{28,24},{32,36},... | collective-permute-start | bytes 1990664 | tf_op jit(solution)/shard_map/ppermute | solution.py:318
  23.0 7.7 %collective-permute-start.5 = (f32[64,256]{1,0:T(8,128)S(1)}, f32[64,256]{1,0:T(8,128)S(1)}, u32[]{:S(2)}, u32[]{:S(2)}) collective-permute-start(f32[64,256]{1,0:T(8,128)S(1)} %get-tuple-element.18.cross_ref), channel_id=1, source_target_pairs={{4,8},{8,4},{12,16},{16,12},{20,24},{24,20},{28,32},{32,28},{36,40... | collective-permute-start | bytes 196616 | tf_op jit(solution)/shard_map/ppermute | solution.py:318
  23.6 7.0 %collective-permute-start.6 = (f32[64,256]{1,0:T(8,128)S(1)}, f32[64,256]{1,0:T(8,128)S(1)}, u32[]{:S(2)}, u32[]{:S(2)}) collective-permute-start(f32[64,256]{1,0:T(8,128)S(1)} %get-tuple-element.19.near_ref), channel_id=1, source_target_pairs={{0,4},{4,0},{8,12},{12,8},{16,20},{20,16},{24,28},{28,24},{32,36},... | collective-permute-start | bytes 196616 | tf_op jit(solution)/shard_map/ppermute | solution.py:318
  30.6 28.2 %copy-start.2 = (f32[2,1,1024,256]{3,2,1,0:T(8,128)S(1)}, f32[2,1,1024,256]{3,2,1,0:T(8,128)}, u32[]{:S(2)}) copy-start(f32[2,1,1024,256]{3,2,1,0:T(8,128)} %param.16) | copy-start | bytes 6291460
  32.5 1.3 %collective-permute-start.7 = (f32[8,256]{1,0:T(8,128)S(1)}, f32[8,256]{1,0:T(8,128)S(1)}, u32[]{:S(2)}, u32[]{:S(2)}) collective-permute-start(f32[8,256]{1,0:T(8,128)S(1)} %get-tuple-element.24), channel_id=1, source_target_pairs={{0,4},{4,0},{8,12},{12,8},{16,20},{20,16},{24,28},{28,24},{32,36},... | collective-permute-start | bytes 24584 | tf_op jit(solution)/shard_map/ppermute | solution.py:318
  33.8 6.6 %collective-permute-start.10 = (f32[8,256]{1,0:T(8,128)S(1)}, f32[8,256]{1,0:T(8,128)S(1)}, u32[]{:S(2)}, u32[]{:S(2)}) collective-permute-start(f32[8,256]{1,0:T(8,128)S(1)} %add.30), channel_id=1, source_target_pairs={{0,33},{1,32},{2,35},{3,34},{4,37},{5,36},{6,39},{7,38},{8,41},{9,... | collective-permute-start | bytes 24584 | tf_op jit(solution)/shard_map/ppermute | solution.py:318
  38.7 3.7 %collective-permute-start.9 = (f32[8,256]{1,0:T(8,128)S(1)}, f32[8,256]{1,0:T(8,128)S(1)}, u32[]{:S(2)}, u32[]{:S(2)}) collective-permute-start(f32[8,256]{1,0:T(8,128)S(1)} %add.30), channel_id=1, source_target_pairs={{0,1},{1,0},{2,3},{3,2},{4,5},{5,4},{6,7},{7,6},{8,9},{9,8},{10,11... | collective-permute-start | bytes 24584 | tf_op jit(solution)/shard_map/ppermute | solution.py:318
  38.7 3.7 %collective-permute-start.8 = (f32[8,256]{1,0:T(8,128)S(1)}, f32[8,256]{1,0:T(8,128)S(1)}, u32[]{:S(2)}, u32[]{:S(2)}) collective-permute-start(f32[8,256]{1,0:T(8,128)S(1)} %add.30), channel_id=1, source_target_pairs={{0,32},{1,33},{2,34},{3,35},{4,36},{5,37},{6,38},{7,39},{8,40},{9,... | collective-permute-start | bytes 24584 | tf_op jit(solution)/shard_map/ppermute | solution.py:318
  42.4 7.0 %collective-permute-start.13 = (f32[8,256]{1,0:T(8,128)S(1)}, f32[8,256]{1,0:T(8,128)S(1)}, u32[]{:S(2)}, u32[]{:S(2)}) collective-permute-start(f32[8,256]{1,0:T(8,128)S(1)} %add_add_fusion.2), channel_id=1, source_target_pairs={{0,99},{1,98},{2,97},{3,96},{4,103},{5,102},{6,101},{7,100},{8,107... | collective-permute-start | bytes 24584 | tf_op jit(solution)/shard_map/ppermute | solution.py:318
  46.2 4.9 %collective-permute-start.12 = (f32[8,256]{1,0:T(8,128)S(1)}, f32[8,256]{1,0:T(8,128)S(1)}, u32[]{:S(2)}, u32[]{:S(2)}) collective-permute-start(f32[8,256]{1,0:T(8,128)S(1)} %add_add_fusion.2), channel_id=1, source_target_pairs={{0,3},{1,2},{2,1},{3,0},{4,7},{5,6},{6,5},{7,4},{8,11},{9,10},{10,... | collective-permute-start | bytes 24584 | tf_op jit(solution)/shard_map/ppermute | solution.py:318
  47.3 4.9 %collective-permute-start.11 = (f32[8,256]{1,0:T(8,128)S(1)}, f32[8,256]{1,0:T(8,128)S(1)}, u32[]{:S(2)}, u32[]{:S(2)}) collective-permute-start(f32[8,256]{1,0:T(8,128)S(1)} %add_add_fusion.2), channel_id=1, source_target_pairs={{0,96},{1,97},{2,98},{3,99},{4,100},{5,101},{6,102},{7,103},{8,104... | collective-permute-start | bytes 24584 | tf_op jit(solution)/shard_map/ppermute | solution.py:318
  52.2 5.2 %collective-permute-start.16 = (f32[8,256]{1,0:T(8,128)S(1)}, f32[8,256]{1,0:T(8,128)S(1)}, u32[]{:S(2)}, u32[]{:S(2)}) collective-permute-start(f32[8,256]{1,0:T(8,128)S(1)} %add_add_fusion.1), channel_id=1, source_target_pairs={{0,16},{1,17},{2,18},{3,19},{4,20},{5,21},{6,22},{7,23},{8,24},{9,... | collective-permute-start | bytes 24584 | tf_op jit(solution)/shard_map/ppermute | solution.py:318
  54.0 4.9 %collective-permute-start.15 = (f32[8,256]{1,0:T(8,128)S(1)}, f32[8,256]{1,0:T(8,128)S(1)}, u32[]{:S(2)}, u32[]{:S(2)}) collective-permute-start(f32[8,256]{1,0:T(8,128)S(1)} %add_add_fusion.1), channel_id=1, source_target_pairs={{0,24},{1,25},{2,26},{3,27},{4,28},{5,29},{6,30},{7,31},{8,16},{9,... | collective-permute-start | bytes 24584 | tf_op jit(solution)/shard_map/ppermute | solution.py:318
  55.1 3.7 %collective-permute-start.14 = (f32[8,256]{1,0:T(8,128)S(1)}, f32[8,256]{1,0:T(8,128)S(1)}, u32[]{:S(2)}, u32[]{:S(2)}) collective-permute-start(f32[8,256]{1,0:T(8,128)S(1)} %add_add_fusion.1), channel_id=1, source_target_pairs={{0,8},{1,9},{2,10},{3,11},{4,12},{5,13},{6,14},{7,15},{8,0},{9,1},... | collective-permute-start | bytes 24584 | tf_op jit(solution)/shard_map/ppermute | solution.py:318

commit v7 on v6

--- a/solution.py
+++ b/solution.py
@@ -17,6 +17,7 @@
 STRIP = 512
 ROUNDS = N // STRIP
 MIB = 1 << 20
+LIMIT = 46 * MIB
 
 
 def dot(a, b):
@@ -50,7 +51,10 @@
     return jnp.concatenate([tall, tall], axis=1)
 
 
-def primal_kernel(direc_hbm, coup_hbm, map_hbm, factor_hbm, pay_ref, direc, coup, corner, sems):
+def primal_kernel(
+    place_ref, direc_hbm, coup_hbm, map_hbm, factor_hbm, pay_ref, token_ref, direc, coup, corner, sems
+):
+    token_ref[0] = place_ref[0]
     copies = [
         pltpu.make_async_copy(coup_hbm, coup, sems.at[0]),
         pltpu.make_async_copy(direc_hbm.at[0], direc.at[0], sems.at[1]),
@@ -81,30 +85,17 @@
 
 
 def local_kernel(
-    place_ref, pay_hbm, flex_hbm, direc_hbm, coup_hbm, partner_hbm,
-    local_hbm, cross_hbm, near_hbm,
-    flex, direc, coup, partner, local, packed, places, right, high, low, sems, out_sems,
-):
-    del pay_hbm
-    direc_copy = pltpu.make_async_copy(direc_hbm, direc, sems.at[0])
+    place_ref, flex_hbm, direc, coup, partner,
+    local, cross_hbm, near_hbm,
+    flex, packed, places, right, high, low, sems, out_sems,
+):
     flex_copies = [
-        pltpu.make_async_copy(flex_hbm.at[s], flex.at[s], sems.at[1 + s]) for s in range(2)
+        pltpu.make_async_copy(flex_hbm.at[s], flex.at[s], sems.at[s]) for s in range(2)
     ]
-    others = [
-        pltpu.make_async_copy(coup_hbm, coup, sems.at[3]),
-        pltpu.make_async_copy(partner_hbm, partner, sems.at[4]),
-    ]
-    out_copies = [
-        pltpu.make_async_copy(local.at[s], local_hbm.at[s], out_sems.at[s]) for s in range(2)
-    ]
-    for copy in others:
+    for copy in flex_copies:
         copy.start()
-    direc_copy.start()
-    flex_copies[0].start()
     me = place_ref[0]
     odd = lax.rem(me, 2)
-    for copy in others:
-        copy.wait()
     for s in range(2):
         target = partner[s] - (2 * me - 1) * N
         match = (target >= 3 * N) if s else (target < N)
@@ -128,8 +119,6 @@
             packed[s, NAMES + c : NAMES + c + 1] = (
                 extra[2 * C : 2 * C + 1] * 32.0 + extra[2 * C + 1 : 2 * C + 2]
             )
-    direc_copy.wait()
-    flex_copies[1].start()
     for s in range(2):
         dh, dl = split(direc[s])
         right[s, 0:N] = dh
@@ -137,7 +126,6 @@
     flex_copies[0].wait()
     for s in range(2):
         if s == 1:
-            out_copies[0].start()
             flex_copies[1].wait()
         for r in range(ROUNDS):
             rows = slice(r * STRIP, (r + 1) * STRIP)
@@ -149,13 +137,10 @@
             low[s, rows] = ol
     for s in range(2):
         packed[s, 0:HALF] = dot(places[s], high[s]) + dot(places[s], low[s])
-    cross_copy = pltpu.make_async_copy(packed.at[odd], cross_hbm, out_sems.at[2])
-    near_copy = pltpu.make_async_copy(packed.at[1 - odd], near_hbm, out_sems.at[3])
+    cross_copy = pltpu.make_async_copy(packed.at[odd], cross_hbm, out_sems.at[0])
+    near_copy = pltpu.make_async_copy(packed.at[1 - odd], near_hbm, out_sems.at[1])
     cross_copy.start()
     near_copy.start()
-    out_copies[1].start()
-    for copy in out_copies:
-        copy.wait()
     cross_copy.wait()
     near_copy.wait()
 
@@ -328,11 +313,14 @@
     place = lax.axis_index("sub").astype(jnp.int32).reshape(1)
 
     whole = jax.ShapeDtypeStruct((2, N, L), F32)
-    pay = pl.pallas_call(
+    pay, token = pl.pallas_call(
         primal_kernel,
-        out_shape=jax.ShapeDtypeStruct((3 * C + 8, L), F32),
-        in_specs=[hbm()] * 4,
-        out_specs=vmem(),
+        out_shape=(
+            jax.ShapeDtypeStruct((3 * C + 8, L), F32),
+            jax.ShapeDtypeStruct((1,), jnp.int32),
+        ),
+        in_specs=[smem()] + [hbm()] * 4,
+        out_specs=(vmem(), smem()),
         scratch_shapes=[
             pltpu.VMEM((2, N, L), F32),
             pltpu.VMEM((2, C, N), F32),
@@ -342,33 +330,29 @@
         name="primal",
         compiler_params=pltpu.CompilerParams(vmem_limit_bytes=58 * MIB),
         cost_estimate=pl.CostEstimate(flops=200_000_000, bytes_accessed=3 * MIB, transcendentals=0),
-    )(direc2, links, corner_map, coarse_factor[0])
+    )(place, direc2, links, corner_map, coarse_factor[0])
     others = [exchange(pay, "grp", 4, lambda i, m=m: i ^ m) for m in (1, 3, 2)]
 
     packed = jax.ShapeDtypeStruct((NAMES + 8, L), F32)
     local, cross, near = pl.pallas_call(
         local_kernel,
         out_shape=(jax.ShapeDtypeStruct((2, N, L), F32), packed, packed),
-        in_specs=[smem()] + [hbm()] * 5,
-        out_specs=(hbm(), hbm(), hbm()),
+        in_specs=[smem(), hbm()] + [vmem()] * 3,
+        out_specs=(vmem(), hbm(), hbm()),
         scratch_shapes=[
             pltpu.VMEM((2, N, N), F32),
-            pltpu.VMEM((2, N, L), F32),
-            pltpu.VMEM((2, C, N), F32),
-            pltpu.VMEM((2, 1, N), jnp.int32),
-            pltpu.VMEM((2, N, L), F32),
             pltpu.VMEM((2, NAMES + 8, L), F32),
             pltpu.VMEM((2, HALF, N), BF16),
             pltpu.VMEM((2, 2 * N, L), BF16),
             pltpu.VMEM((2, N, L), BF16),
             pltpu.VMEM((2, N, L), BF16),
-            pltpu.SemaphoreType.DMA((5,)),
-            pltpu.SemaphoreType.DMA((4,)),
+            pltpu.SemaphoreType.DMA((2,)),
+            pltpu.SemaphoreType.DMA((2,)),
         ],
         name="local",
-        compiler_params=pltpu.CompilerParams(vmem_limit_bytes=58 * MIB),
+        compiler_params=pltpu.CompilerParams(vmem_limit_bytes=LIMIT),
         cost_estimate=pl.CostEstimate(flops=4_000_000_000, bytes_accessed=12 * MIB, transcendentals=0),
-    )(place, pay, blocks, direc2, links, partner)
+    )(token, blocks, direc2, links, partner)
 
     def across(i):
         j = i + 1 if i % 2 else i - 1

time: 62.7 us -> 62.8 us (level)
  no operation moved by 1% of the time
where the time goes in v7:
time: 62.8 us; the launch traced here: 62.6 us
  starting transfers between devices  27.8 us (44%)
  Pallas kernels  22.9 us (36%)
  waiting for transfers between devices  10.9 us (17%)
  between operations  0.98 us (2%)
    ppermute x17, starting transfers between devices, exchange(): return lax.ppermute(x, axes, pairs)  27.8 us
    ppermute x17, waiting for transfers between devices, exchange(): return lax.ppermute(x, axes, pairs)  10.9 us
    pallas_call x1, Pallas kernels, per_device(): pl.pallas_call(local_kernel, out_shape=(jax.ShapeDtypeStruct((2, N, L), F...  9.61 us
    pallas_call x1, Pallas kernels, per_device(): pl.pallas_call(final_kernel, out_shape=(whole, whole, whole, jax.ShapeDty...  3.49 us
    pallas_call x1, Pallas kernels, per_device(): pl.pallas_call(inner_kernel, out_shape=(whole, jax.ShapeDtypeStruct((3, 8...  3.36 us
    pallas_call x1, Pallas kernels, per_device(): pl.pallas_call(primal_kernel, out_shape=(jax.ShapeDtypeStruct((3 * C + 8,...  3.31 us
    pallas_call x1, Pallas kernels, per_device(): pl.pallas_call(outer_kernel, out_shape=(whole, jax.ShapeDtypeStruct((8, L...  1.82 us
    pallas_call x1, Pallas kernels, per_device(): pl.pallas_call(coarse_kernel, out_shape=(piece, piece), in_specs=[smem()]...  1.27 us
  transfers between devices with their start and end apart: 17, of which 8 were waited for; matrix products, arithmetic and copies ran while one was open for 0% of the time, Pallas kernels for 23%

profile of v7, /device:TPU:0, one launch (start us, length us, event | category | flops | bytes accessed | tf_op | source)
XLA Modules:
  0.0 62.6 jit_solution(4144252737223761841)
XLA Ops:
  0.6 0.0 copy-start
  0.7 3.3 %primal.1 = (f32[200,256]{1,0:T(8,128)}, s32[1]{0:T(128)}) custom-call(s32[1]{0:T(128)} %bitcast.place_ref, f32[2,1024,256]{2,1,0:T(8,128)} %bitcast.17, f32[2,64,1024]{2,1,0:T(8,128)} %bitcast.24, s32[2,1,64]{2,1,0:T(1,128)} %map_hbm.1, f32[64,256]{1,0:T(8,128)} %bitcast.27), custom_call_target="tpu_custom_call" | custom-call | flops 200000000 | bytes 3145728 | tf_op jit(solution)/shard_map/primal/pallas_call | solution.py:316
  4.0 3.2 %collective-permute-start.2 = (f32[200,256]{1,0:T(8,128)}, f32[200,256]{1,0:T(8,128)S(1)}, u32[]{:S(2)}, u32[]{:S(2)}) collective-permute-start(f32[200,256]{1,0:T(8,128)} %get-tuple-element.21.pay_ref), channel_id=1, source_target_pairs={{0,2},{1,3},{2,0},{3,1},{4,6},{5,7},{6,4},{7,5},{8,10},{9,11},{10,... | collective-permute-start | bytes 614408 | tf_op jit(solution)/shard_map/ppermute | solution.py:303
  7.2 1.1 %collective-permute-start.1 = (f32[200,256]{1,0:T(8,128)}, f32[200,256]{1,0:T(8,128)S(1)}, u32[]{:S(2)}, u32[]{:S(2)}) collective-permute-start(f32[200,256]{1,0:T(8,128)} %get-tuple-element.21.pay_ref), channel_id=1, source_target_pairs={{0,3},{1,2},{2,1},{3,0},{4,7},{5,6},{6,5},{7,4},{8,11},{9,10},{10,... | collective-permute-start | bytes 614408 | tf_op jit(solution)/shard_map/ppermute | solution.py:303
  8.3 0.0 collective-permute-start
  8.3 0.0 copy-done.6
  8.3 0.0 copy-start.5
  8.3 9.6 %local.1 = (f32[2,1024,256]{2,1,0:T(8,128)S(1)}, f32[648,256]{1,0:T(8,128)S(1)}, f32[648,256]{1,0:T(8,128)S(1)}) custom-call(s32[1]{0:T(128)} %get-tuple-element.19.place_ref, f32[2,1024,1024]{2,1,0:T(8,128)} %bitcast.28, f32[2,1024,256]{2,1,0:T(8,128)S(1)} %bitcast.18, f32[2,64,1024]{2,1,0:T(8,128)S(1)} %bitcast.25, s32[2,1,1024]{2,1,0:T(1,128)S(1)} %copy-done.6), custom_call_target="tpu_custom_call" | custom-call | flops 4000000000 | bytes 12582912 | tf_op jit(solution)/shard_map/local/pallas_call | solution.py:337
  18.0 0.7 %collective-permute-start.3 = (f32[648,256]{1,0:T(8,128)S(1)}, f32[648,256]{1,0:T(8,128)S(1)}, u32[]{:S(2)}, u32[]{:S(2)}) collective-permute-start(f32[648,256]{1,0:T(8,128)S(1)} %get-tuple-element.25), channel_id=1, source_target_pairs={{4,8},{8,4},{12,16},{16,12},{20,24},{24,20},{28,32},{32,28},{36,40... | collective-permute-start | bytes 1990664 | tf_op jit(solution)/shard_map/ppermute | solution.py:303
  18.7 0.0 copy-start.1
  18.7 0.0 copy-start.4
  18.7 3.3 %collective-permute-start.4 = (f32[648,256]{1,0:T(8,128)S(1)}, f32[648,256]{1,0:T(8,128)S(1)}, u32[]{:S(2)}, u32[]{:S(2)}) collective-permute-start(f32[648,256]{1,0:T(8,128)S(1)} %get-tuple-element.26), channel_id=1, source_target_pairs={{0,4},{4,0},{8,12},{12,8},{16,20},{20,16},{24,28},{28,24},{32,36},... | collective-permute-start | bytes 1990664 | tf_op jit(solution)/shard_map/ppermute | solution.py:303
  22.0 0.0 collective-permute-done.2.three_ref
  22.0 0.0 collective-permute-done.1.two_ref
  22.0 0.0 collective-permute-done.one_ref
  22.0 0.0 copy-done.5
  22.0 1.3 %coarse.1 = (f32[64,256]{1,0:T(8,128)S(1)}, f32[64,256]{1,0:T(8,128)S(1)}) custom-call(s32[1]{0:T(128)} %bitcast.place_ref, f32[200,256]{1,0:T(8,128)S(1)} %copy-done.5, f32[200,256]{1,0:T(8,128)S(1)} %collective-permute-done.one_ref, f32[200,256]{1,0:T(8,128)S(1)} %collective-permute-done.1.two_ref, f32[200,256]{1,0:T(8,128)S(1)} %collective-permute-done.2.three_ref), custom_call_target="tpu_custom_call" | custom-call | flops 30000001024 | bytes 1048576 | tf_op jit(solution)/shard_map/coarse/pallas_call | solution.py:368
  23.3 0.7 %collective-permute-start.5 = (f32[64,256]{1,0:T(8,128)S(1)}, f32[64,256]{1,0:T(8,128)S(1)}, u32[]{:S(2)}, u32[]{:S(2)}) collective-permute-start(f32[64,256]{1,0:T(8,128)S(1)} %get-tuple-element.22.cross_ref), channel_id=1, source_target_pairs={{4,8},{8,4},{12,16},{16,12},{20,24},{24,20},{28,32},{32,28},{36,40... | collective-permute-start | bytes 196616 | tf_op jit(solution)/shard_map/ppermute | solution.py:303
  24.0 3.5 %collective-permute-start.6 = (f32[64,256]{1,0:T(8,128)S(1)}, f32[64,256]{1,0:T(8,128)S(1)}, u32[]{:S(2)}, u32[]{:S(2)}) collective-permute-start(f32[64,256]{1,0:T(8,128)S(1)} %get-tuple-element.23.near_ref), channel_id=1, source_target_pairs={{0,4},{4,0},{8,12},{12,8},{16,20},{20,16},{24,28},{28,24},{32,36},... | collective-permute-start | bytes 196616 | tf_op jit(solution)/shard_map/ppermute | solution.py:303
  27.5 0.0 copy-done.1
  27.5 3.4 %inner.1 = (f32[2,1024,256]{2,1,0:T(8,128)S(1)}, f32[3,8,256]{2,1,0:T(8,128)S(1)}) custom-call(s32[1]{0:T(128)} %bitcast.place_ref, f32[2,1024,256]{2,1,0:T(8,128)S(1)} %get-tuple-element.20.local_ref, f32[64,256]{1,0:T(8,128)S(1)} %get-tuple-element.22.cross_ref, f32[64,256]{1,0:T(8,128)S(1)} %get-tuple-element.23.near_ref, f32[2,64,1024]{2,1,0:T(8,128)S(1)} %bitcast.26, ...), custom_call_target="tpu_custom_call" | custom-call | flops 2500000000 | bytes 8388608 | tf_op jit(solution)/shard_map/inner/pallas_call | solution.py:380
  30.9 0.0 copy-start.2
  30.9 0.0 collective-permute-done.5.cross_pick_ref
  30.9 0.0 collective-permute-done.6.near_pick_ref
  30.9 0.0 collective-permute-done.3.cross_ref
  31.0 0.0 collective-permute-done.4.near_ref
  31.0 1.8 %outer.1 = (f32[2,1024,256]{2,1,0:T(8,128)S(1)}, f32[8,256]{1,0:T(8,128)S(1)}) custom-call(s32[1]{0:T(128)} %bitcast.place_ref, f32[2,1024,256]{2,1,0:T(8,128)S(1)} %get-tuple-element.24.part_ref, f32[648,256]{1,0:T(8,128)S(1)} %collective-permute-done.3.cross_ref, f32[648,256]{1,0:T(8,128)S(1)} %collective-permute-done.4.near_ref, ...), custom_call_target="tpu_custom_call" | custom-call | tf_op jit(solution)/shard_map/outer/pallas_call | solution.py:395
  32.8 0.1 collective-permute-start.7
  32.9 1.1 %collective-permute-done.7 = f32[8,256]{1,0:T(8,128)S(1)} collective-permute-done((f32[8,256]{1,0:T(8,128)S(1)}, f32[8,256]{1,0:T(8,128)S(1)}, u32[]{:S(2)}, u32[]{:S(2)}) %collective-permute-start.7) | collective-permute-done | bytes 8224 | tf_op jit(solution)/shard_map/ppermute | solution.py:303
  34.0 4.8 %collective-permute-start.10 = (f32[8,256]{1,0:T(8,128)S(1)}, f32[8,256]{1,0:T(8,128)S(1)}, u32[]{:S(2)}, u32[]{:S(2)}) collective-permute-start(f32[8,256]{1,0:T(8,128)S(1)} %add.30), channel_id=1, source_target_pairs={{0,33},{1,32},{2,35},{3,34},{4,37},{5,36},{6,39},{7,38},{8,41},{9,... | collective-permute-start | bytes 24584 | tf_op jit(solution)/shard_map/ppermute | solution.py:303
  38.9 0.0 collective-permute-start.9
  38.9 0.5 collective-permute-start.8
  39.5 1.1 %collective-permute-done.10 = f32[8,256]{1,0:T(8,128)S(1)} collective-permute-done((f32[8,256]{1,0:T(8,128)S(1)}, f32[8,256]{1,0:T(8,128)S(1)}, u32[]{:S(2)}, u32[]{:S(2)}) %collective-permute-start.10) | collective-permute-done | bytes 8224 | tf_op jit(solution)/shard_map/ppermute | solution.py:303
  40.5 2.0 %collective-permute-done.9 = f32[8,256]{1,0:T(8,128)S(1)} collective-permute-done((f32[8,256]{1,0:T(8,128)S(1)}, f32[8,256]{1,0:T(8,128)S(1)}, u32[]{:S(2)}, u32[]{:S(2)}) %collective-permute-start.9) | collective-permute-done | bytes 8224 | tf_op jit(solution)/shard_map/ppermute | solution.py:303
  42.5 0.0 collective-permute-done.8
  42.6 3.8 %collective-permute-start.13 = (f32[8,256]{1,0:T(8,128)S(1)}, f32[8,256]{1,0:T(8,128)S(1)}, u32[]{:S(2)}, u32[]{:S(2)}) collective-permute-start(f32[8,256]{1,0:T(8,128)S(1)} %add_add_fusion.2), channel_id=1, source_target_pairs={{0,99},{1,98},{2,97},{3,96},{4,103},{5,102},{6,101},{7,100},{8,107... | collective-permute-start | bytes 24584 | tf_op jit(solution)/shard_map/ppermute | solution.py:303
  46.3 1.1 %collective-permute-start.12 = (f32[8,256]{1,0:T(8,128)S(1)}, f32[8,256]{1,0:T(8,128)S(1)}, u32[]{:S(2)}, u32[]{:S(2)}) collective-permute-start(f32[8,256]{1,0:T(8,128)S(1)} %add_add_fusion.2), channel_id=1, source_target_pairs={{0,3},{1,2},{2,1},{3,0},{4,7},{5,6},{6,5},{7,4},{8,11},{9,10},{10,... | collective-permute-start | bytes 24584 | tf_op jit(solution)/shard_map/ppermute | solution.py:303
  47.5 1.1 %collective-permute-start.11 = (f32[8,256]{1,0:T(8,128)S(1)}, f32[8,256]{1,0:T(8,128)S(1)}, u32[]{:S(2)}, u32[]{:S(2)}) collective-permute-start(f32[8,256]{1,0:T(8,128)S(1)} %add_add_fusion.2), channel_id=1, source_target_pairs={{0,96},{1,97},{2,98},{3,99},{4,100},{5,101},{6,102},{7,103},{8,104... | collective-permute-start | bytes 24584 | tf_op jit(solution)/shard_map/ppermute | solution.py:303
  48.5 1.1 %collective-permute-done.13 = f32[8,256]{1,0:T(8,128)S(1)} collective-permute-done((f32[8,256]{1,0:T(8,128)S(1)}, f32[8,256]{1,0:T(8,128)S(1)}, u32[]{:S(2)}, u32[]{:S(2)}) %collective-permute-start.13) | collective-permute-done | bytes 8224 | tf_op jit(solution)/shard_map/ppermute | solution.py:303
  49.6 1.6 %collective-permute-done.12 = f32[8,256]{1,0:T(8,128)S(1)} collective-permute-done((f32[8,256]{1,0:T(8,128)S(1)}, f32[8,256]{1,0:T(8,128)S(1)}, u32[]{:S(2)}, u32[]{:S(2)}) %collective-permute-start.12) | collective-permute-done | bytes 8224 | tf_op jit(solution)/shard_map/ppermute | solution.py:303
  51.2 1.1 %collective-permute-done.11 = f32[8,256]{1,0:T(8,128)S(1)} collective-permute-done((f32[8,256]{1,0:T(8,128)S(1)}, f32[8,256]{1,0:T(8,128)S(1)}, u32[]{:S(2)}, u32[]{:S(2)}) %collective-permute-start.11) | collective-permute-done | bytes 8224 | tf_op jit(solution)/shard_map/ppermute | solution.py:303
  52.4 1.8 %collective-permute-start.16 = (f32[8,256]{1,0:T(8,128)S(1)}, f32[8,256]{1,0:T(8,128)S(1)}, u32[]{:S(2)}, u32[]{:S(2)}) collective-permute-start(f32[8,256]{1,0:T(8,128)S(1)} %add_add_fusion.1), channel_id=1, source_target_pairs={{0,16},{1,17},{2,18},{3,19},{4,20},{5,21},{6,22},{7,23},{8,24},{9,... | collective-permute-start | bytes 24584 | tf_op jit(solution)/shard_map/ppermute | solution.py:303
  54.1 1.2 %collective-permute-start.15 = (f32[8,256]{1,0:T(8,128)S(1)}, f32[8,256]{1,0:T(8,128)S(1)}, u32[]{:S(2)}, u32[]{:S(2)}) collective-permute-start(f32[8,256]{1,0:T(8,128)S(1)} %add_add_fusion.1), channel_id=1, source_target_pairs={{0,24},{1,25},{2,26},{3,27},{4,28},{5,29},{6,30},{7,31},{8,16},{9,... | collective-permute-start | bytes 24584 | tf_op jit(solution)/shard_map/ppermute | solution.py:303
  55.3 0.8 %collective-permute-start.14 = (f32[8,256]{1,0:T(8,128)S(1)}, f32[8,256]{1,0:T(8,128)S(1)}, u32[]{:S(2)}, u32[]{:S(2)}) collective-permute-start(f32[8,256]{1,0:T(8,128)S(1)} %add_add_fusion.1), channel_id=1, source_target_pairs={{0,8},{1,9},{2,10},{3,11},{4,12},{5,13},{6,14},{7,15},{8,0},{9,1},... | collective-permute-start | bytes 24584 | tf_op jit(solution)/shard_map/ppermute | solution.py:303
  56.1 1.4 %collective-permute-done.16 = f32[8,256]{1,0:T(8,128)S(1)} collective-permute-done((f32[8,256]{1,0:T(8,128)S(1)}, f32[8,256]{1,0:T(8,128)S(1)}, u32[]{:S(2)}, u32[]{:S(2)}) %collective-permute-start.16) | collective-permute-done | bytes 8224 | tf_op jit(solution)/shard_map/ppermute | solution.py:303
  57.5 1.5 %collective-permute-done.15 = f32[8,256]{1,0:T(8,128)S(1)} collective-permute-done((f32[8,256]{1,0:T(8,128)S(1)}, f32[8,256]{1,0:T(8,128)S(1)}, u32[]{:S(2)}, u32[]{:S(2)}) %collective-permute-start.15) | collective-permute-done | bytes 8224 | tf_op jit(solution)/shard_map/ppermute | solution.py:303
  59.0 0.0 collective-permute-done.14
  59.0 3.5 %final.1 = (f32[2,1024,256]{2,1,0:T(8,128)}, f32[2,1024,256]{2,1,0:T(8,128)}, f32[2,1024,256]{2,1,0:T(8,128)}, f32[1,256]{1,0:T(1,128)}) custom-call(f32[8,256]{1,0:T(8,128)S(1)} %add_add_fusion.total_ref, f32[2,1,1024]{2,1,0:T(1,128)S(1)} %copy-done.4, f32[2,1024,256]{2,1,0:T(8,128)S(1)} %bitcast.23, f32[2,1024,256]{2,1,0:T(8,128)S(1)} %bitcast.22, ...), custom_call_target="tpu_custom_call" | custom-call | tf_op jit(solution)/shard_map/final/pallas_call | solution.py:411
  (10 shorter events, 0.0 us)
Async XLA Ops:
  0.6 7.7 %copy-start = (f32[2,1,1024,256]{3,2,1,0:T(8,128)S(1)}, f32[2,1,1024,256]{3,2,1,0:T(8,128)}, u32[]{:S(2)}) copy-start(f32[2,1,1024,256]{3,2,1,0:T(8,128)} %param.18) | copy-start | bytes 6291460
  0.6 7.7 %copy-start.3 = (f32[2,1,64,1024]{3,2,1,0:T(8,128)S(1)}, f32[2,1,64,1024]{3,2,1,0:T(8,128)}, u32[]{:S(2)}) copy-start(f32[2,1,64,1024]{3,2,1,0:T(8,128)} %param.11) | copy-start | bytes 1572868
  0.7 7.7 %copy-start.6 = (s32[2,1,1024]{2,1,0:T(1,128)S(1)}, s32[2,1,1024]{2,1,0:T(1,128)}, u32[]{:S(2)}) copy-start(s32[2,1,1024]{2,1,0:T(1,128)} %partner_ref.1) | copy-start | bytes 24580
  4.0 18.0 %collective-permute-start.2 = (f32[200,256]{1,0:T(8,128)}, f32[200,256]{1,0:T(8,128)S(1)}, u32[]{:S(2)}, u32[]{:S(2)}) collective-permute-start(f32[200,256]{1,0:T(8,128)} %get-tuple-element.21.pay_ref), channel_id=1, source_target_pairs={{0,2},{1,3},{2,0},{3,1},{4,6},{5,7},{6,4},{7,5},{8,10},{9,11},{10,... | collective-permute-start | bytes 614408 | tf_op jit(solution)/shard_map/ppermute | solution.py:303
  7.2 14.8 %collective-permute-start.1 = (f32[200,256]{1,0:T(8,128)}, f32[200,256]{1,0:T(8,128)S(1)}, u32[]{:S(2)}, u32[]{:S(2)}) collective-permute-start(f32[200,256]{1,0:T(8,128)} %get-tuple-element.21.pay_ref), channel_id=1, source_target_pairs={{0,3},{1,2},{2,1},{3,0},{4,7},{5,6},{6,5},{7,4},{8,11},{9,10},{10,... | collective-permute-start | bytes 614408 | tf_op jit(solution)/shard_map/ppermute | solution.py:303
  8.3 13.7 %collective-permute-start = (f32[200,256]{1,0:T(8,128)}, f32[200,256]{1,0:T(8,128)S(1)}, u32[]{:S(2)}, u32[]{:S(2)}) collective-permute-start(f32[200,256]{1,0:T(8,128)} %get-tuple-element.21.pay_ref), channel_id=1, source_target_pairs={{0,1},{1,0},{2,3},{3,2},{4,5},{5,4},{6,7},{7,6},{8,9},{9,8},{10,11... | collective-permute-start | bytes 614408 | tf_op jit(solution)/shard_map/ppermute | solution.py:303
  8.3 13.7 %copy-start.5 = (f32[200,256]{1,0:T(8,128)S(1)}, f32[200,256]{1,0:T(8,128)}, u32[]{:S(2)}) copy-start(f32[200,256]{1,0:T(8,128)} %get-tuple-element.21.pay_ref) | copy-start | bytes 614404
  18.0 13.0 %collective-permute-start.3 = (f32[648,256]{1,0:T(8,128)S(1)}, f32[648,256]{1,0:T(8,128)S(1)}, u32[]{:S(2)}, u32[]{:S(2)}) collective-permute-start(f32[648,256]{1,0:T(8,128)S(1)} %get-tuple-element.25), channel_id=1, source_target_pairs={{4,8},{8,4},{12,16},{16,12},{20,24},{24,20},{28,32},{32,28},{36,40... | collective-permute-start | bytes 1990664 | tf_op jit(solution)/shard_map/ppermute | solution.py:303
  18.7 8.9 %copy-start.1 = (f32[2,1,1024,256]{3,2,1,0:T(8,128)S(1)}, f32[2,1,1024,256]{3,2,1,0:T(8,128)}, u32[]{:S(2)}) copy-start(f32[2,1,1024,256]{3,2,1,0:T(8,128)} %param.17) | copy-start | bytes 6291460
  18.7 8.9 %copy-start.4 = (f32[2,1,1024]{2,1,0:T(1,128)S(1)}, f32[2,1,1024]{2,1,0:T(1,128)}, u32[]{:S(2)}) copy-start(f32[2,1,1024]{2,1,0:T(1,128)} %weight_ref.5) | copy-start | bytes 24580
  18.7 12.3 %collective-permute-start.4 = (f32[648,256]{1,0:T(8,128)S(1)}, f32[648,256]{1,0:T(8,128)S(1)}, u32[]{:S(2)}, u32[]{:S(2)}) collective-permute-start(f32[648,256]{1,0:T(8,128)S(1)} %get-tuple-element.26), channel_id=1, source_target_pairs={{0,4},{4,0},{8,12},{12,8},{16,20},{20,16},{24,28},{28,24},{32,36},... | collective-permute-start | bytes 1990664 | tf_op jit(solution)/shard_map/ppermute | solution.py:303
  23.3 7.6 %collective-permute-start.5 = (f32[64,256]{1,0:T(8,128)S(1)}, f32[64,256]{1,0:T(8,128)S(1)}, u32[]{:S(2)}, u32[]{:S(2)}) collective-permute-start(f32[64,256]{1,0:T(8,128)S(1)} %get-tuple-element.22.cross_ref), channel_id=1, source_target_pairs={{4,8},{8,4},{12,16},{16,12},{20,24},{24,20},{28,32},{32,28},{36,40... | collective-permute-start | bytes 196616 | tf_op jit(solution)/shard_map/ppermute | solution.py:303
  24.0 6.9 %collective-permute-start.6 = (f32[64,256]{1,0:T(8,128)S(1)}, f32[64,256]{1,0:T(8,128)S(1)}, u32[]{:S(2)}, u32[]{:S(2)}) collective-permute-start(f32[64,256]{1,0:T(8,128)S(1)} %get-tuple-element.23.near_ref), channel_id=1, source_target_pairs={{0,4},{4,0},{8,12},{12,8},{16,20},{20,16},{24,28},{28,24},{32,36},... | collective-permute-start | bytes 196616 | tf_op jit(solution)/shard_map/ppermute | solution.py:303
  30.9 28.1 %copy-start.2 = (f32[2,1,1024,256]{3,2,1,0:T(8,128)S(1)}, f32[2,1,1024,256]{3,2,1,0:T(8,128)}, u32[]{:S(2)}) copy-start(f32[2,1,1024,256]{3,2,1,0:T(8,128)} %param.16) | copy-start | bytes 6291460
  32.8 1.3 %collective-permute-start.7 = (f32[8,256]{1,0:T(8,128)S(1)}, f32[8,256]{1,0:T(8,128)S(1)}, u32[]{:S(2)}, u32[]{:S(2)}) collective-permute-start(f32[8,256]{1,0:T(8,128)S(1)} %get-tuple-element.28), channel_id=1, source_target_pairs={{0,4},{4,0},{8,12},{12,8},{16,20},{20,16},{24,28},{28,24},{32,36},... | collective-permute-start | bytes 24584 | tf_op jit(solution)/shard_map/ppermute | solution.py:303
  34.0 6.5 %collective-permute-start.10 = (f32[8,256]{1,0:T(8,128)S(1)}, f32[8,256]{1,0:T(8,128)S(1)}, u32[]{:S(2)}, u32[]{:S(2)}) collective-permute-start(f32[8,256]{1,0:T(8,128)S(1)} %add.30), channel_id=1, source_target_pairs={{0,33},{1,32},{2,35},{3,34},{4,37},{5,36},{6,39},{7,38},{8,41},{9,... | collective-permute-start | bytes 24584 | tf_op jit(solution)/shard_map/ppermute | solution.py:303
  38.9 3.7 %collective-permute-start.9 = (f32[8,256]{1,0:T(8,128)S(1)}, f32[8,256]{1,0:T(8,128)S(1)}, u32[]{:S(2)}, u32[]{:S(2)}) collective-permute-start(f32[8,256]{1,0:T(8,128)S(1)} %add.30), channel_id=1, source_target_pairs={{0,1},{1,0},{2,3},{3,2},{4,5},{5,4},{6,7},{7,6},{8,9},{9,8},{10,11... | collective-permute-start | bytes 24584 | tf_op jit(solution)/shard_map/ppermute | solution.py:303
  38.9 3.7 %collective-permute-start.8 = (f32[8,256]{1,0:T(8,128)S(1)}, f32[8,256]{1,0:T(8,128)S(1)}, u32[]{:S(2)}, u32[]{:S(2)}) collective-permute-start(f32[8,256]{1,0:T(8,128)S(1)} %add.30), channel_id=1, source_target_pairs={{0,32},{1,33},{2,34},{3,35},{4,36},{5,37},{6,38},{7,39},{8,40},{9,... | collective-permute-start | bytes 24584 | tf_op jit(solution)/shard_map/ppermute | solution.py:303
  42.6 7.0 %collective-permute-start.13 = (f32[8,256]{1,0:T(8,128)S(1)}, f32[8,256]{1,0:T(8,128)S(1)}, u32[]{:S(2)}, u32[]{:S(2)}) collective-permute-start(f32[8,256]{1,0:T(8,128)S(1)} %add_add_fusion.2), channel_id=1, source_target_pairs={{0,99},{1,98},{2,97},{3,96},{4,103},{5,102},{6,101},{7,100},{8,107... | collective-permute-start | bytes 24584 | tf_op jit(solution)/shard_map/ppermute | solution.py:303
  46.3 4.9 %collective-permute-start.12 = (f32[8,256]{1,0:T(8,128)S(1)}, f32[8,256]{1,0:T(8,128)S(1)}, u32[]{:S(2)}, u32[]{:S(2)}) collective-permute-start(f32[8,256]{1,0:T(8,128)S(1)} %add_add_fusion.2), channel_id=1, source_target_pairs={{0,3},{1,2},{2,1},{3,0},{4,7},{5,6},{6,5},{7,4},{8,11},{9,10},{10,... | collective-permute-start | bytes 24584 | tf_op jit(solution)/shard_map/ppermute | solution.py:303
  47.5 4.9 %collective-permute-start.11 = (f32[8,256]{1,0:T(8,128)S(1)}, f32[8,256]{1,0:T(8,128)S(1)}, u32[]{:S(2)}, u32[]{:S(2)}) collective-permute-start(f32[8,256]{1,0:T(8,128)S(1)} %add_add_fusion.2), channel_id=1, source_target_pairs={{0,96},{1,97},{2,98},{3,99},{4,100},{5,101},{6,102},{7,103},{8,104... | collective-permute-start | bytes 24584 | tf_op jit(solution)/shard_map/ppermute | solution.py:303
  52.4 5.2 %collective-permute-start.16 = (f32[8,256]{1,0:T(8,128)S(1)}, f32[8,256]{1,0:T(8,128)S(1)}, u32[]{:S(2)}, u32[]{:S(2)}) collective-permute-start(f32[8,256]{1,0:T(8,128)S(1)} %add_add_fusion.1), channel_id=1, source_target_pairs={{0,16},{1,17},{2,18},{3,19},{4,20},{5,21},{6,22},{7,23},{8,24},{9,... | collective-permute-start | bytes 24584 | tf_op jit(solution)/shard_map/ppermute | solution.py:303
  54.1 4.9 %collective-permute-start.15 = (f32[8,256]{1,0:T(8,128)S(1)}, f32[8,256]{1,0:T(8,128)S(1)}, u32[]{:S(2)}, u32[]{:S(2)}) collective-permute-start(f32[8,256]{1,0:T(8,128)S(1)} %add_add_fusion.1), channel_id=1, source_target_pairs={{0,24},{1,25},{2,26},{3,27},{4,28},{5,29},{6,30},{7,31},{8,16},{9,... | collective-permute-start | bytes 24584 | tf_op jit(solution)/shard_map/ppermute | solution.py:303
  55.3 3.7 %collective-permute-start.14 = (f32[8,256]{1,0:T(8,128)S(1)}, f32[8,256]{1,0:T(8,128)S(1)}, u32[]{:S(2)}, u32[]{:S(2)}) collective-permute-start(f32[8,256]{1,0:T(8,128)S(1)} %add_add_fusion.1), channel_id=1, source_target_pairs={{0,8},{1,9},{2,10},{3,11},{4,12},{5,13},{6,14},{7,15},{8,0},{9,1},... | collective-permute-start | bytes 24584 | tf_op jit(solution)/shard_map/ppermute | solution.py:303

commit v8 on v7

--- a/solution.py
+++ b/solution.py
@@ -92,8 +92,7 @@
     flex_copies = [
         pltpu.make_async_copy(flex_hbm.at[s], flex.at[s], sems.at[s]) for s in range(2)
     ]
-    for copy in flex_copies:
-        copy.start()
+    flex_copies[0].start()
     me = place_ref[0]
     odd = lax.rem(me, 2)
     for s in range(2):
@@ -119,6 +118,7 @@
             packed[s, NAMES + c : NAMES + c + 1] = (
                 extra[2 * C : 2 * C + 1] * 32.0 + extra[2 * C + 1 : 2 * C + 2]
             )
+    flex_copies[1].start()
     for s in range(2):
         dh, dl = split(direc[s])
         right[s, 0:N] = dh

time: 62.8 us -> 62.8 us (level)
  no operation moved by 1% of the time
where the time goes in v8:
time: 62.8 us; the launch traced here: 62.6 us
  starting transfers between devices  27.8 us (44%)
  Pallas kernels  22.9 us (36%)
  waiting for transfers between devices  10.9 us (17%)
  between operations  0.98 us (2%)
    ppermute x17, starting transfers between devices, exchange(): return lax.ppermute(x, axes, pairs)  27.8 us
    ppermute x17, waiting for transfers between devices, exchange(): return lax.ppermute(x, axes, pairs)  10.9 us
    pallas_call x1, Pallas kernels, per_device(): pl.pallas_call(local_kernel, out_shape=(jax.ShapeDtypeStruct((2, N, L), F...  9.61 us
    pallas_call x1, Pallas kernels, per_device(): pl.pallas_call(final_kernel, out_shape=(whole, whole, whole, jax.ShapeDty...  3.49 us
    pallas_call x1, Pallas kernels, per_device(): pl.pallas_call(inner_kernel, out_shape=(whole, jax.ShapeDtypeStruct((3, 8...  3.36 us
    pallas_call x1, Pallas kernels, per_device(): pl.pallas_call(primal_kernel, out_shape=(jax.ShapeDtypeStruct((3 * C + 8,...  3.31 us
    pallas_call x1, Pallas kernels, per_device(): pl.pallas_call(outer_kernel, out_shape=(whole, jax.ShapeDtypeStruct((8, L...  1.82 us
    pallas_call x1, Pallas kernels, per_device(): pl.pallas_call(coarse_kernel, out_shape=(piece, piece), in_specs=[smem()]...  1.27 us
  transfers between devices with their start and end apart: 17, of which 8 were waited for; matrix products, arithmetic and copies ran while one was open for 0% of the time, Pallas kernels for 23%

profile of v8, /device:TPU:0, one launch (start us, length us, event | category | flops | bytes accessed | tf_op | source)
XLA Modules:
  0.0 62.6 jit_solution(4144252737223761841)
XLA Ops:
  0.6 0.0 copy-start
  0.7 3.3 %primal.1 = (f32[200,256]{1,0:T(8,128)}, s32[1]{0:T(128)}) custom-call(s32[1]{0:T(128)} %bitcast.place_ref, f32[2,1024,256]{2,1,0:T(8,128)} %bitcast.17, f32[2,64,1024]{2,1,0:T(8,128)} %bitcast.24, s32[2,1,64]{2,1,0:T(1,128)} %map_hbm.1, f32[64,256]{1,0:T(8,128)} %bitcast.27), custom_call_target="tpu_custom_call" | custom-call | flops 200000000 | bytes 3145728 | tf_op jit(solution)/shard_map/primal/pallas_call | solution.py:316
  4.0 3.2 %collective-permute-start.2 = (f32[200,256]{1,0:T(8,128)}, f32[200,256]{1,0:T(8,128)S(1)}, u32[]{:S(2)}, u32[]{:S(2)}) collective-permute-start(f32[200,256]{1,0:T(8,128)} %get-tuple-element.21.pay_ref), channel_id=1, source_target_pairs={{0,2},{1,3},{2,0},{3,1},{4,6},{5,7},{6,4},{7,5},{8,10},{9,11},{10,... | collective-permute-start | bytes 614408 | tf_op jit(solution)/shard_map/ppermute | solution.py:303
  7.2 1.1 %collective-permute-start.1 = (f32[200,256]{1,0:T(8,128)}, f32[200,256]{1,0:T(8,128)S(1)}, u32[]{:S(2)}, u32[]{:S(2)}) collective-permute-start(f32[200,256]{1,0:T(8,128)} %get-tuple-element.21.pay_ref), channel_id=1, source_target_pairs={{0,3},{1,2},{2,1},{3,0},{4,7},{5,6},{6,5},{7,4},{8,11},{9,10},{10,... | collective-permute-start | bytes 614408 | tf_op jit(solution)/shard_map/ppermute | solution.py:303
  8.3 0.0 collective-permute-start
  8.3 0.0 copy-done.6
  8.3 0.0 copy-start.5
  8.3 9.6 %local.1 = (f32[2,1024,256]{2,1,0:T(8,128)S(1)}, f32[648,256]{1,0:T(8,128)S(1)}, f32[648,256]{1,0:T(8,128)S(1)}) custom-call(s32[1]{0:T(128)} %get-tuple-element.19.place_ref, f32[2,1024,1024]{2,1,0:T(8,128)} %bitcast.28, f32[2,1024,256]{2,1,0:T(8,128)S(1)} %bitcast.18, f32[2,64,1024]{2,1,0:T(8,128)S(1)} %bitcast.25, s32[2,1,1024]{2,1,0:T(1,128)S(1)} %copy-done.6), custom_call_target="tpu_custom_call" | custom-call | flops 4000000000 | bytes 12582912 | tf_op jit(solution)/shard_map/local/pallas_call | solution.py:337
  18.0 0.7 %collective-permute-start.3 = (f32[648,256]{1,0:T(8,128)S(1)}, f32[648,256]{1,0:T(8,128)S(1)}, u32[]{:S(2)}, u32[]{:S(2)}) collective-permute-start(f32[648,256]{1,0:T(8,128)S(1)} %get-tuple-element.25), channel_id=1, source_target_pairs={{4,8},{8,4},{12,16},{16,12},{20,24},{24,20},{28,32},{32,28},{36,40... | collective-permute-start | bytes 1990664 | tf_op jit(solution)/shard_map/ppermute | solution.py:303
  18.7 0.0 copy-start.1
  18.7 0.0 copy-start.4
  18.7 3.3 %collective-permute-start.4 = (f32[648,256]{1,0:T(8,128)S(1)}, f32[648,256]{1,0:T(8,128)S(1)}, u32[]{:S(2)}, u32[]{:S(2)}) collective-permute-start(f32[648,256]{1,0:T(8,128)S(1)} %get-tuple-element.26), channel_id=1, source_target_pairs={{0,4},{4,0},{8,12},{12,8},{16,20},{20,16},{24,28},{28,24},{32,36},... | collective-permute-start | bytes 1990664 | tf_op jit(solution)/shard_map/ppermute | solution.py:303
  22.0 0.0 collective-permute-done.2.three_ref
  22.0 0.0 collective-permute-done.1.two_ref
  22.0 0.0 collective-permute-done.one_ref
  22.0 0.0 copy-done.5
  22.0 1.3 %coarse.1 = (f32[64,256]{1,0:T(8,128)S(1)}, f32[64,256]{1,0:T(8,128)S(1)}) custom-call(s32[1]{0:T(128)} %bitcast.place_ref, f32[200,256]{1,0:T(8,128)S(1)} %copy-done.5, f32[200,256]{1,0:T(8,128)S(1)} %collective-permute-done.one_ref, f32[200,256]{1,0:T(8,128)S(1)} %collective-permute-done.1.two_ref, f32[200,256]{1,0:T(8,128)S(1)} %collective-permute-done.2.three_ref), custom_call_target="tpu_custom_call" | custom-call | flops 30000001024 | bytes 1048576 | tf_op jit(solution)/shard_map/coarse/pallas_call | solution.py:368
  23.3 0.7 %collective-permute-start.5 = (f32[64,256]{1,0:T(8,128)S(1)}, f32[64,256]{1,0:T(8,128)S(1)}, u32[]{:S(2)}, u32[]{:S(2)}) collective-permute-start(f32[64,256]{1,0:T(8,128)S(1)} %get-tuple-element.22.cross_ref), channel_id=1, source_target_pairs={{4,8},{8,4},{12,16},{16,12},{20,24},{24,20},{28,32},{32,28},{36,40... | collective-permute-start | bytes 196616 | tf_op jit(solution)/shard_map/ppermute | solution.py:303
  24.0 3.5 %collective-permute-start.6 = (f32[64,256]{1,0:T(8,128)S(1)}, f32[64,256]{1,0:T(8,128)S(1)}, u32[]{:S(2)}, u32[]{:S(2)}) collective-permute-start(f32[64,256]{1,0:T(8,128)S(1)} %get-tuple-element.23.near_ref), channel_id=1, source_target_pairs={{0,4},{4,0},{8,12},{12,8},{16,20},{20,16},{24,28},{28,24},{32,36},... | collective-permute-start | bytes 196616 | tf_op jit(solution)/shard_map/ppermute | solution.py:303
  27.5 0.0 copy-done.1
  27.5 3.4 %inner.1 = (f32[2,1024,256]{2,1,0:T(8,128)S(1)}, f32[3,8,256]{2,1,0:T(8,128)S(1)}) custom-call(s32[1]{0:T(128)} %bitcast.place_ref, f32[2,1024,256]{2,1,0:T(8,128)S(1)} %get-tuple-element.20.local_ref, f32[64,256]{1,0:T(8,128)S(1)} %get-tuple-element.22.cross_ref, f32[64,256]{1,0:T(8,128)S(1)} %get-tuple-element.23.near_ref, f32[2,64,1024]{2,1,0:T(8,128)S(1)} %bitcast.26, ...), custom_call_target="tpu_custom_call" | custom-call | flops 2500000000 | bytes 8388608 | tf_op jit(solution)/shard_map/inner/pallas_call | solution.py:380
  30.9 0.0 copy-start.2
  30.9 0.0 collective-permute-done.5.cross_pick_ref
  30.9 0.0 collective-permute-done.6.near_pick_ref
  30.9 0.0 collective-permute-done.3.cross_ref
  31.0 0.0 collective-permute-done.4.near_ref
  31.0 1.8 %outer.1 = (f32[2,1024,256]{2,1,0:T(8,128)S(1)}, f32[8,256]{1,0:T(8,128)S(1)}) custom-call(s32[1]{0:T(128)} %bitcast.place_ref, f32[2,1024,256]{2,1,0:T(8,128)S(1)} %get-tuple-element.24.part_ref, f32[648,256]{1,0:T(8,128)S(1)} %collective-permute-done.3.cross_ref, f32[648,256]{1,0:T(8,128)S(1)} %collective-permute-done.4.near_ref, ...), custom_call_target="tpu_custom_call" | custom-call | tf_op jit(solution)/shard_map/outer/pallas_call | solution.py:395
  32.8 0.1 collective-permute-start.7
  32.9 1.1 %collective-permute-done.7 = f32[8,256]{1,0:T(8,128)S(1)} collective-permute-done((f32[8,256]{1,0:T(8,128)S(1)}, f32[8,256]{1,0:T(8,128)S(1)}, u32[]{:S(2)}, u32[]{:S(2)}) %collective-permute-start.7) | collective-permute-done | bytes 8224 | tf_op jit(solution)/shard_map/ppermute | solution.py:303
  34.0 4.8 %collective-permute-start.10 = (f32[8,256]{1,0:T(8,128)S(1)}, f32[8,256]{1,0:T(8,128)S(1)}, u32[]{:S(2)}, u32[]{:S(2)}) collective-permute-start(f32[8,256]{1,0:T(8,128)S(1)} %add.30), channel_id=1, source_target_pairs={{0,33},{1,32},{2,35},{3,34},{4,37},{5,36},{6,39},{7,38},{8,41},{9,... | collective-permute-start | bytes 24584 | tf_op jit(solution)/shard_map/ppermute | solution.py:303
  38.9 0.0 collective-permute-start.9
  38.9 0.5 collective-permute-start.8
  39.5 1.1 %collective-permute-done.10 = f32[8,256]{1,0:T(8,128)S(1)} collective-permute-done((f32[8,256]{1,0:T(8,128)S(1)}, f32[8,256]{1,0:T(8,128)S(1)}, u32[]{:S(2)}, u32[]{:S(2)}) %collective-permute-start.10) | collective-permute-done | bytes 8224 | tf_op jit(solution)/shard_map/ppermute | solution.py:303
  40.5 2.0 %collective-permute-done.9 = f32[8,256]{1,0:T(8,128)S(1)} collective-permute-done((f32[8,256]{1,0:T(8,128)S(1)}, f32[8,256]{1,0:T(8,128)S(1)}, u32[]{:S(2)}, u32[]{:S(2)}) %collective-permute-start.9) | collective-permute-done | bytes 8224 | tf_op jit(solution)/shard_map/ppermute | solution.py:303
  42.5 0.0 collective-permute-done.8
  42.6 3.8 %collective-permute-start.13 = (f32[8,256]{1,0:T(8,128)S(1)}, f32[8,256]{1,0:T(8,128)S(1)}, u32[]{:S(2)}, u32[]{:S(2)}) collective-permute-start(f32[8,256]{1,0:T(8,128)S(1)} %add_add_fusion.2), channel_id=1, source_target_pairs={{0,99},{1,98},{2,97},{3,96},{4,103},{5,102},{6,101},{7,100},{8,107... | collective-permute-start | bytes 24584 | tf_op jit(solution)/shard_map/ppermute | solution.py:303
  46.3 1.1 %collective-permute-start.12 = (f32[8,256]{1,0:T(8,128)S(1)}, f32[8,256]{1,0:T(8,128)S(1)}, u32[]{:S(2)}, u32[]{:S(2)}) collective-permute-start(f32[8,256]{1,0:T(8,128)S(1)} %add_add_fusion.2), channel_id=1, source_target_pairs={{0,3},{1,2},{2,1},{3,0},{4,7},{5,6},{6,5},{7,4},{8,11},{9,10},{10,... | collective-permute-start | bytes 24584 | tf_op jit(solution)/shard_map/ppermute | solution.py:303
  47.5 1.1 %collective-permute-start.11 = (f32[8,256]{1,0:T(8,128)S(1)}, f32[8,256]{1,0:T(8,128)S(1)}, u32[]{:S(2)}, u32[]{:S(2)}) collective-permute-start(f32[8,256]{1,0:T(8,128)S(1)} %add_add_fusion.2), channel_id=1, source_target_pairs={{0,96},{1,97},{2,98},{3,99},{4,100},{5,101},{6,102},{7,103},{8,104... | collective-permute-start | bytes 24584 | tf_op jit(solution)/shard_map/ppermute | solution.py:303
  48.5 1.1 %collective-permute-done.13 = f32[8,256]{1,0:T(8,128)S(1)} collective-permute-done((f32[8,256]{1,0:T(8,128)S(1)}, f32[8,256]{1,0:T(8,128)S(1)}, u32[]{:S(2)}, u32[]{:S(2)}) %collective-permute-start.13) | collective-permute-done | bytes 8224 | tf_op jit(solution)/shard_map/ppermute | solution.py:303
  49.6 1.6 %collective-permute-done.12 = f32[8,256]{1,0:T(8,128)S(1)} collective-permute-done((f32[8,256]{1,0:T(8,128)S(1)}, f32[8,256]{1,0:T(8,128)S(1)}, u32[]{:S(2)}, u32[]{:S(2)}) %collective-permute-start.12) | collective-permute-done | bytes 8224 | tf_op jit(solution)/shard_map/ppermute | solution.py:303
  51.2 1.1 %collective-permute-done.11 = f32[8,256]{1,0:T(8,128)S(1)} collective-permute-done((f32[8,256]{1,0:T(8,128)S(1)}, f32[8,256]{1,0:T(8,128)S(1)}, u32[]{:S(2)}, u32[]{:S(2)}) %collective-permute-start.11) | collective-permute-done | bytes 8224 | tf_op jit(solution)/shard_map/ppermute | solution.py:303
  52.4 1.8 %collective-permute-start.16 = (f32[8,256]{1,0:T(8,128)S(1)}, f32[8,256]{1,0:T(8,128)S(1)}, u32[]{:S(2)}, u32[]{:S(2)}) collective-permute-start(f32[8,256]{1,0:T(8,128)S(1)} %add_add_fusion.1), channel_id=1, source_target_pairs={{0,16},{1,17},{2,18},{3,19},{4,20},{5,21},{6,22},{7,23},{8,24},{9,... | collective-permute-start | bytes 24584 | tf_op jit(solution)/shard_map/ppermute | solution.py:303
  54.1 1.2 %collective-permute-start.15 = (f32[8,256]{1,0:T(8,128)S(1)}, f32[8,256]{1,0:T(8,128)S(1)}, u32[]{:S(2)}, u32[]{:S(2)}) collective-permute-start(f32[8,256]{1,0:T(8,128)S(1)} %add_add_fusion.1), channel_id=1, source_target_pairs={{0,24},{1,25},{2,26},{3,27},{4,28},{5,29},{6,30},{7,31},{8,16},{9,... | collective-permute-start | bytes 24584 | tf_op jit(solution)/shard_map/ppermute | solution.py:303
  55.3 0.8 %collective-permute-start.14 = (f32[8,256]{1,0:T(8,128)S(1)}, f32[8,256]{1,0:T(8,128)S(1)}, u32[]{:S(2)}, u32[]{:S(2)}) collective-permute-start(f32[8,256]{1,0:T(8,128)S(1)} %add_add_fusion.1), channel_id=1, source_target_pairs={{0,8},{1,9},{2,10},{3,11},{4,12},{5,13},{6,14},{7,15},{8,0},{9,1},... | collective-permute-start | bytes 24584 | tf_op jit(solution)/shard_map/ppermute | solution.py:303
  56.1 1.4 %collective-permute-done.16 = f32[8,256]{1,0:T(8,128)S(1)} collective-permute-done((f32[8,256]{1,0:T(8,128)S(1)}, f32[8,256]{1,0:T(8,128)S(1)}, u32[]{:S(2)}, u32[]{:S(2)}) %collective-permute-start.16) | collective-permute-done | bytes 8224 | tf_op jit(solution)/shard_map/ppermute | solution.py:303
  57.5 1.5 %collective-permute-done.15 = f32[8,256]{1,0:T(8,128)S(1)} collective-permute-done((f32[8,256]{1,0:T(8,128)S(1)}, f32[8,256]{1,0:T(8,128)S(1)}, u32[]{:S(2)}, u32[]{:S(2)}) %collective-permute-start.15) | collective-permute-done | bytes 8224 | tf_op jit(solution)/shard_map/ppermute | solution.py:303
  59.0 0.0 collective-permute-done.14
  59.0 3.5 %final.1 = (f32[2,1024,256]{2,1,0:T(8,128)}, f32[2,1024,256]{2,1,0:T(8,128)}, f32[2,1024,256]{2,1,0:T(8,128)}, f32[1,256]{1,0:T(1,128)}) custom-call(f32[8,256]{1,0:T(8,128)S(1)} %add_add_fusion.total_ref, f32[2,1,1024]{2,1,0:T(1,128)S(1)} %copy-done.4, f32[2,1024,256]{2,1,0:T(8,128)S(1)} %bitcast.23, f32[2,1024,256]{2,1,0:T(8,128)S(1)} %bitcast.22, ...), custom_call_target="tpu_custom_call" | custom-call | tf_op jit(solution)/shard_map/final/pallas_call | solution.py:411
  (10 shorter events, 0.0 us)
Async XLA Ops:
  0.6 7.7 %copy-start = (f32[2,1,1024,256]{3,2,1,0:T(8,128)S(1)}, f32[2,1,1024,256]{3,2,1,0:T(8,128)}, u32[]{:S(2)}) copy-start(f32[2,1,1024,256]{3,2,1,0:T(8,128)} %param.18) | copy-start | bytes 6291460
  0.6 7.7 %copy-start.3 = (f32[2,1,64,1024]{3,2,1,0:T(8,128)S(1)}, f32[2,1,64,1024]{3,2,1,0:T(8,128)}, u32[]{:S(2)}) copy-start(f32[2,1,64,1024]{3,2,1,0:T(8,128)} %param.11) | copy-start | bytes 1572868
  0.7 7.7 %copy-start.6 = (s32[2,1,1024]{2,1,0:T(1,128)S(1)}, s32[2,1,1024]{2,1,0:T(1,128)}, u32[]{:S(2)}) copy-start(s32[2,1,1024]{2,1,0:T(1,128)} %partner_ref.1) | copy-start | bytes 24580
  4.0 18.0 %collective-permute-start.2 = (f32[200,256]{1,0:T(8,128)}, f32[200,256]{1,0:T(8,128)S(1)}, u32[]{:S(2)}, u32[]{:S(2)}) collective-permute-start(f32[200,256]{1,0:T(8,128)} %get-tuple-element.21.pay_ref), channel_id=1, source_target_pairs={{0,2},{1,3},{2,0},{3,1},{4,6},{5,7},{6,4},{7,5},{8,10},{9,11},{10,... | collective-permute-start | bytes 614408 | tf_op jit(solution)/shard_map/ppermute | solution.py:303
  7.2 14.8 %collective-permute-start.1 = (f32[200,256]{1,0:T(8,128)}, f32[200,256]{1,0:T(8,128)S(1)}, u32[]{:S(2)}, u32[]{:S(2)}) collective-permute-start(f32[200,256]{1,0:T(8,128)} %get-tuple-element.21.pay_ref), channel_id=1, source_target_pairs={{0,3},{1,2},{2,1},{3,0},{4,7},{5,6},{6,5},{7,4},{8,11},{9,10},{10,... | collective-permute-start | bytes 614408 | tf_op jit(solution)/shard_map/ppermute | solution.py:303
  8.3 13.7 %collective-permute-start = (f32[200,256]{1,0:T(8,128)}, f32[200,256]{1,0:T(8,128)S(1)}, u32[]{:S(2)}, u32[]{:S(2)}) collective-permute-start(f32[200,256]{1,0:T(8,128)} %get-tuple-element.21.pay_ref), channel_id=1, source_target_pairs={{0,1},{1,0},{2,3},{3,2},{4,5},{5,4},{6,7},{7,6},{8,9},{9,8},{10,11... | collective-permute-start | bytes 614408 | tf_op jit(solution)/shard_map/ppermute | solution.py:303
  8.3 13.7 %copy-start.5 = (f32[200,256]{1,0:T(8,128)S(1)}, f32[200,256]{1,0:T(8,128)}, u32[]{:S(2)}) copy-start(f32[200,256]{1,0:T(8,128)} %get-tuple-element.21.pay_ref) | copy-start | bytes 614404
  18.0 13.0 %collective-permute-start.3 = (f32[648,256]{1,0:T(8,128)S(1)}, f32[648,256]{1,0:T(8,128)S(1)}, u32[]{:S(2)}, u32[]{:S(2)}) collective-permute-start(f32[648,256]{1,0:T(8,128)S(1)} %get-tuple-element.25), channel_id=1, source_target_pairs={{4,8},{8,4},{12,16},{16,12},{20,24},{24,20},{28,32},{32,28},{36,40... | collective-permute-start | bytes 1990664 | tf_op jit(solution)/shard_map/ppermute | solution.py:303
  18.7 8.9 %copy-start.1 = (f32[2,1,1024,256]{3,2,1,0:T(8,128)S(1)}, f32[2,1,1024,256]{3,2,1,0:T(8,128)}, u32[]{:S(2)}) copy-start(f32[2,1,1024,256]{3,2,1,0:T(8,128)} %param.17) | copy-start | bytes 6291460
  18.7 8.9 %copy-start.4 = (f32[2,1,1024]{2,1,0:T(1,128)S(1)}, f32[2,1,1024]{2,1,0:T(1,128)}, u32[]{:S(2)}) copy-start(f32[2,1,1024]{2,1,0:T(1,128)} %weight_ref.5) | copy-start | bytes 24580
  18.7 12.3 %collective-permute-start.4 = (f32[648,256]{1,0:T(8,128)S(1)}, f32[648,256]{1,0:T(8,128)S(1)}, u32[]{:S(2)}, u32[]{:S(2)}) collective-permute-start(f32[648,256]{1,0:T(8,128)S(1)} %get-tuple-element.26), channel_id=1, source_target_pairs={{0,4},{4,0},{8,12},{12,8},{16,20},{20,16},{24,28},{28,24},{32,36},... | collective-permute-start | bytes 1990664 | tf_op jit(solution)/shard_map/ppermute | solution.py:303
  23.3 7.6 %collective-permute-start.5 = (f32[64,256]{1,0:T(8,128)S(1)}, f32[64,256]{1,0:T(8,128)S(1)}, u32[]{:S(2)}, u32[]{:S(2)}) collective-permute-start(f32[64,256]{1,0:T(8,128)S(1)} %get-tuple-element.22.cross_ref), channel_id=1, source_target_pairs={{4,8},{8,4},{12,16},{16,12},{20,24},{24,20},{28,32},{32,28},{36,40... | collective-permute-start | bytes 196616 | tf_op jit(solution)/shard_map/ppermute | solution.py:303
  24.0 6.9 %collective-permute-start.6 = (f32[64,256]{1,0:T(8,128)S(1)}, f32[64,256]{1,0:T(8,128)S(1)}, u32[]{:S(2)}, u32[]{:S(2)}) collective-permute-start(f32[64,256]{1,0:T(8,128)S(1)} %get-tuple-element.23.near_ref), channel_id=1, source_target_pairs={{0,4},{4,0},{8,12},{12,8},{16,20},{20,16},{24,28},{28,24},{32,36},... | collective-permute-start | bytes 196616 | tf_op jit(solution)/shard_map/ppermute | solution.py:303
  30.9 28.1 %copy-start.2 = (f32[2,1,1024,256]{3,2,1,0:T(8,128)S(1)}, f32[2,1,1024,256]{3,2,1,0:T(8,128)}, u32[]{:S(2)}) copy-start(f32[2,1,1024,256]{3,2,1,0:T(8,128)} %param.16) | copy-start | bytes 6291460
  32.8 1.3 %collective-permute-start.7 = (f32[8,256]{1,0:T(8,128)S(1)}, f32[8,256]{1,0:T(8,128)S(1)}, u32[]{:S(2)}, u32[]{:S(2)}) collective-permute-start(f32[8,256]{1,0:T(8,128)S(1)} %get-tuple-element.28), channel_id=1, source_target_pairs={{0,4},{4,0},{8,12},{12,8},{16,20},{20,16},{24,28},{28,24},{32,36},... | collective-permute-start | bytes 24584 | tf_op jit(solution)/shard_map/ppermute | solution.py:303
  34.0 6.5 %collective-permute-start.10 = (f32[8,256]{1,0:T(8,128)S(1)}, f32[8,256]{1,0:T(8,128)S(1)}, u32[]{:S(2)}, u32[]{:S(2)}) collective-permute-start(f32[8,256]{1,0:T(8,128)S(1)} %add.30), channel_id=1, source_target_pairs={{0,33},{1,32},{2,35},{3,34},{4,37},{5,36},{6,39},{7,38},{8,41},{9,... | collective-permute-start | bytes 24584 | tf_op jit(solution)/shard_map/ppermute | solution.py:303
  38.9 3.7 %collective-permute-start.9 = (f32[8,256]{1,0:T(8,128)S(1)}, f32[8,256]{1,0:T(8,128)S(1)}, u32[]{:S(2)}, u32[]{:S(2)}) collective-permute-start(f32[8,256]{1,0:T(8,128)S(1)} %add.30), channel_id=1, source_target_pairs={{0,1},{1,0},{2,3},{3,2},{4,5},{5,4},{6,7},{7,6},{8,9},{9,8},{10,11... | collective-permute-start | bytes 24584 | tf_op jit(solution)/shard_map/ppermute | solution.py:303
  38.9 3.7 %collective-permute-start.8 = (f32[8,256]{1,0:T(8,128)S(1)}, f32[8,256]{1,0:T(8,128)S(1)}, u32[]{:S(2)}, u32[]{:S(2)}) collective-permute-start(f32[8,256]{1,0:T(8,128)S(1)} %add.30), channel_id=1, source_target_pairs={{0,32},{1,33},{2,34},{3,35},{4,36},{5,37},{6,38},{7,39},{8,40},{9,... | collective-permute-start | bytes 24584 | tf_op jit(solution)/shard_map/ppermute | solution.py:303
  42.6 7.0 %collective-permute-start.13 = (f32[8,256]{1,0:T(8,128)S(1)}, f32[8,256]{1,0:T(8,128)S(1)}, u32[]{:S(2)}, u32[]{:S(2)}) collective-permute-start(f32[8,256]{1,0:T(8,128)S(1)} %add_add_fusion.2), channel_id=1, source_target_pairs={{0,99},{1,98},{2,97},{3,96},{4,103},{5,102},{6,101},{7,100},{8,107... | collective-permute-start | bytes 24584 | tf_op jit(solution)/shard_map/ppermute | solution.py:303
  46.3 4.9 %collective-permute-start.12 = (f32[8,256]{1,0:T(8,128)S(1)}, f32[8,256]{1,0:T(8,128)S(1)}, u32[]{:S(2)}, u32[]{:S(2)}) collective-permute-start(f32[8,256]{1,0:T(8,128)S(1)} %add_add_fusion.2), channel_id=1, source_target_pairs={{0,3},{1,2},{2,1},{3,0},{4,7},{5,6},{6,5},{7,4},{8,11},{9,10},{10,... | collective-permute-start | bytes 24584 | tf_op jit(solution)/shard_map/ppermute | solution.py:303
  47.5 4.9 %collective-permute-start.11 = (f32[8,256]{1,0:T(8,128)S(1)}, f32[8,256]{1,0:T(8,128)S(1)}, u32[]{:S(2)}, u32[]{:S(2)}) collective-permute-start(f32[8,256]{1,0:T(8,128)S(1)} %add_add_fusion.2), channel_id=1, source_target_pairs={{0,96},{1,97},{2,98},{3,99},{4,100},{5,101},{6,102},{7,103},{8,104... | collective-permute-start | bytes 24584 | tf_op jit(solution)/shard_map/ppermute | solution.py:303
  52.4 5.2 %collective-permute-start.16 = (f32[8,256]{1,0:T(8,128)S(1)}, f32[8,256]{1,0:T(8,128)S(1)}, u32[]{:S(2)}, u32[]{:S(2)}) collective-permute-start(f32[8,256]{1,0:T(8,128)S(1)} %add_add_fusion.1), channel_id=1, source_target_pairs={{0,16},{1,17},{2,18},{3,19},{4,20},{5,21},{6,22},{7,23},{8,24},{9,... | collective-permute-start | bytes 24584 | tf_op jit(solution)/shard_map/ppermute | solution.py:303
  54.1 4.9 %collective-permute-start.15 = (f32[8,256]{1,0:T(8,128)S(1)}, f32[8,256]{1,0:T(8,128)S(1)}, u32[]{:S(2)}, u32[]{:S(2)}) collective-permute-start(f32[8,256]{1,0:T(8,128)S(1)} %add_add_fusion.1), channel_id=1, source_target_pairs={{0,24},{1,25},{2,26},{3,27},{4,28},{5,29},{6,30},{7,31},{8,16},{9,... | collective-permute-start | bytes 24584 | tf_op jit(solution)/shard_map/ppermute | solution.py:303
  55.3 3.7 %collective-permute-start.14 = (f32[8,256]{1,0:T(8,128)S(1)}, f32[8,256]{1,0:T(8,128)S(1)}, u32[]{:S(2)}, u32[]{:S(2)}) collective-permute-start(f32[8,256]{1,0:T(8,128)S(1)} %add_add_fusion.1), channel_id=1, source_target_pairs={{0,8},{1,9},{2,10},{3,11},{4,12},{5,13},{6,14},{7,15},{8,0},{9,1},... | collective-permute-start | bytes 24584 | tf_op jit(solution)/shard_map/ppermute | solution.py:303

commit v9 on v4

--- a/solution.py
+++ b/solution.py
@@ -136,15 +136,16 @@
         ch, cl = split(coup[s])
         stack = jnp.concatenate([ch, cl, digits], axis=0)
         packed[s, NAMES:] = jnp.zeros((8, L), F32)
+        place = one_hot(iota((HALF, N), 0) == key)
+        packed[s, 0:HALF] = dot(place, high[s]) + dot(place, low[s])
+        extra = lax.dot_general(
+            stack, place, (((1,), (1,)), ((), ())), preferred_element_type=F32
+        )
         for c in range(2):
-            place = one_hot(iota((L, N), 0) + c * L == key)
-            packed[s, c * L : (c + 1) * L] = dot(place, high[s]) + dot(place, low[s])
-            extra = lax.dot_general(
-                stack, place, (((1,), (1,)), ((), ())), preferred_element_type=F32
-            )
-            packed[s, HALF + c * C : HALF + (c + 1) * C] = extra[0:C] + extra[C : 2 * C]
+            part = extra[:, c * L : (c + 1) * L]
+            packed[s, HALF + c * C : HALF + (c + 1) * C] = part[0:C] + part[C : 2 * C]
             packed[s, NAMES + c : NAMES + c + 1] = (
-                extra[2 * C : 2 * C + 1] * 32.0 + extra[2 * C + 1 : 2 * C + 2]
+                part[2 * C : 2 * C + 1] * 32.0 + part[2 * C + 1 : 2 * C + 2]
             )
     cross_copy = pltpu.make_async_copy(packed.at[odd], cross_hbm, out_sems.at[2])
     near_copy = pltpu.make_async_copy(packed.at[1 - odd], near_hbm, out_sems.at[3])
@@ -219,9 +220,9 @@
         theirs = partner_ref[other] - (2 * me + s) * N
         mine = partner_ref[s]
         awake = jnp.where(lax.shift_right_arithmetic(mine, 10) != 2 * me + s, 1.0, 0.0)
-        for r in range(0, N, L):
-            rows = slice(r, r + L)
-            place = one_hot(iota((L, N), 0) + r == theirs)
+        for r in range(0, N, STRIP):
+            rows = slice(r, r + STRIP)
+            place = one_hot(iota((STRIP, N), 0) + r == theirs)
             opposite = dot(place, high[other]) + dot(place, low[other])
             image = image_ref[s, rows]
             jump_ref[s, rows] = column(awake[:, rows]) * image - opposite
@@ -252,12 +253,12 @@
             lows.append(image_low)
         stacked = jnp.concatenate(highs + lows, axis=0)
         names = [ref[NAMES + c : NAMES + c + 1].astype(jnp.int32) for c in range(2)]
-        for r in range(0, N, L):
-            places = [one_hot(iota((L, L), 0) + (r + 1) == name) for name in names]
+        for r in range(0, N, STRIP):
+            places = [one_hot(iota((STRIP, L), 0) + (r + 1) == name) for name in names]
             opposite = dot(jnp.concatenate(places + places, axis=1), stacked)
-            jump = part_ref[s, r : r + L] - opposite
-            jump_ref[s, r : r + L] = jump
-            square = square + fold(column(weight_ref[s][:, r : r + L]) * jump * jump)
+            jump = part_ref[s, r : r + STRIP] - opposite
+            jump_ref[s, r : r + STRIP] = jump
+            square = square + fold(column(weight_ref[s][:, r : r + STRIP]) * jump * jump)
     rows = [jnp.sum(x, axis=0, keepdims=True) for x in (sums_ref[0], sums_ref[1], sums_ref[2], square)]
     total_ref[...] = jnp.concatenate(rows + [jnp.zeros((4, L), F32)], axis=0)
 

time: 62.5 us -> 62.5 us (level)
  transfers between devices with their start and end apart: 17 -> 17, of which waited for: 8 -> 8; matrix products, arithmetic and copies ran while one was open for 0% -> 0% of each run, Pallas kernels for 22% -> 23%
where the time goes in v9:
time: 62.5 us; the launch traced here: 62.3 us
  starting transfers between devices  27.9 us (45%)
  Pallas kernels  22.5 us (36%)
  waiting for transfers between devices  10.9 us (17%)
  between operations  0.99 us (2%)
    ppermute x17, starting transfers between devices, exchange(): return lax.ppermute(x, axes, pairs)  27.9 us
    ppermute x17, waiting for transfers between devices, exchange(): return lax.ppermute(x, axes, pairs)  10.9 us
    pallas_call x1, Pallas kernels, per_device(): pl.pallas_call(local_kernel, out_shape=(jax.ShapeDtypeStruct((2, N, L), F...  9.36 us
    pallas_call x1, Pallas kernels, per_device(): pl.pallas_call(final_kernel, out_shape=(whole, whole, whole, jax.ShapeDty...  3.48 us
    pallas_call x1, Pallas kernels, per_device(): pl.pallas_call(inner_kernel, out_shape=(whole, jax.ShapeDtypeStruct((3, 8...  3.45 us
    pallas_call x1, Pallas kernels, per_device(): pl.pallas_call(primal_kernel, out_shape=jax.ShapeDtypeStruct((3 * C + 8,...  3.17 us
    pallas_call x1, Pallas kernels, per_device(): pl.pallas_call(outer_kernel, out_shape=(whole, jax.ShapeDtypeStruct((8, L...  1.74 us
    pallas_call x1, Pallas kernels, per_device(): pl.pallas_call(coarse_kernel, out_shape=(piece, piece), in_specs=[smem()]...  1.27 us
  transfers between devices with their start and end apart: 17, of which 8 were waited for; matrix products, arithmetic and copies ran while one was open for 0% of the time, Pallas kernels for 23%

profile of v9, /device:TPU:0, one launch (start us, length us, event | category | flops | bytes accessed | tf_op | source)
XLA Modules:
  0.0 62.3 jit_solution(4422670898836283635)
XLA Ops:
  0.6 3.2 %primal.1.pay_hbm.pay_ref = f32[200,256]{1,0:T(8,128)} custom-call(f32[2,1024,256]{2,1,0:T(8,128)} %bitcast.17, f32[2,64,1024]{2,1,0:T(8,128)} %bitcast.24, s32[2,1,64]{2,1,0:T(1,128)} %map_hbm.1, f32[64,256]{1,0:T(8,128)} %bitcast.27), custom_call_target="tpu_custom_call" | custom-call | flops 200000000 | bytes 3145728 | tf_op jit(solution)/shard_map/primal/pallas_call | solution.py:328
  3.8 3.2 %collective-permute-start.2 = (f32[200,256]{1,0:T(8,128)}, f32[200,256]{1,0:T(8,128)S(1)}, u32[]{:S(2)}, u32[]{:S(2)}) collective-permute-start(f32[200,256]{1,0:T(8,128)} %primal.1.pay_hbm.pay_ref), channel_id=1, source_target_pairs={{0,2},{1,3},{2,0},{3,1},{4,6},{5,7},{6,4},{7,5},{8,10},{9,11},{10,... | collective-permute-start | bytes 614408 | tf_op jit(solution)/shard_map/ppermute | solution.py:315
  7.0 1.1 %collective-permute-start.1 = (f32[200,256]{1,0:T(8,128)}, f32[200,256]{1,0:T(8,128)S(1)}, u32[]{:S(2)}, u32[]{:S(2)}) collective-permute-start(f32[200,256]{1,0:T(8,128)} %primal.1.pay_hbm.pay_ref), channel_id=1, source_target_pairs={{0,3},{1,2},{2,1},{3,0},{4,7},{5,6},{6,5},{7,4},{8,11},{9,10},{10,... | collective-permute-start | bytes 614408 | tf_op jit(solution)/shard_map/ppermute | solution.py:315
  8.1 0.0 collective-permute-start
  8.1 9.4 %local.1 = (f32[2,1024,256]{2,1,0:T(8,128)}, f32[648,256]{1,0:T(8,128)}, f32[648,256]{1,0:T(8,128)}) custom-call(s32[1]{0:T(128)} %bitcast.place_ref, f32[200,256]{1,0:T(8,128)} %primal.1.pay_hbm.pay_ref, f32[2,1024,1024]{2,1,0:T(8,128)} %bitcast.28, f32[2,1024,256]{2,1,0:T(8,128)} %bitcast.18, f32[2,64,1024]{2,1,0:T(8,128)} %bitcast.25, ...), custom_call_target="tpu_custom_call" | custom-call | flops 4000000000 | bytes 12582912 | tf_op jit(solution)/shard_map/local/pallas_call | solution.py:346
  17.5 0.7 %collective-permute-start.3 = (f32[648,256]{1,0:T(8,128)}, f32[648,256]{1,0:T(8,128)S(1)}, u32[]{:S(2)}, u32[]{:S(2)}) collective-permute-start(f32[648,256]{1,0:T(8,128)} %get-tuple-element.21), channel_id=1, source_target_pairs={{4,8},{8,4},{12,16},{16,12},{20,24},{24,20},{28,32},{32,28},{36,40... | collective-permute-start | bytes 1990664 | tf_op jit(solution)/shard_map/ppermute | solution.py:315
  18.2 0.0 copy-start
  18.2 0.0 copy-start.1
  18.2 0.0 copy-start.3
  18.2 0.0 copy-start.5
  18.3 0.0 copy-start.6
  18.3 0.0 copy-start.7
  18.3 3.3 %collective-permute-start.4 = (f32[648,256]{1,0:T(8,128)}, f32[648,256]{1,0:T(8,128)S(1)}, u32[]{:S(2)}, u32[]{:S(2)}) collective-permute-start(f32[648,256]{1,0:T(8,128)} %get-tuple-element.22), channel_id=1, source_target_pairs={{0,4},{4,0},{8,12},{12,8},{16,20},{20,16},{24,28},{28,24},{32,36},... | collective-permute-start | bytes 1990664 | tf_op jit(solution)/shard_map/ppermute | solution.py:315
  21.6 0.0 collective-permute-done.2.three_ref
  21.6 0.0 collective-permute-done.1.two_ref
  21.6 0.0 collective-permute-done.one_ref
  21.6 0.0 copy-done.4
  21.6 1.3 %coarse.1 = (f32[64,256]{1,0:T(8,128)S(1)}, f32[64,256]{1,0:T(8,128)S(1)}) custom-call(s32[1]{0:T(128)} %bitcast.place_ref, f32[200,256]{1,0:T(8,128)S(1)} %copy-done.4, f32[200,256]{1,0:T(8,128)S(1)} %collective-permute-done.one_ref, f32[200,256]{1,0:T(8,128)S(1)} %collective-permute-done.1.two_ref, f32[200,256]{1,0:T(8,128)S(1)} %collective-permute-done.2.three_ref), custom_call_target="tpu_custom_call" | custom-call | flops 30000001024 | bytes 1048576 | tf_op jit(solution)/shard_map/coarse/pallas_call | solution.py:380
  22.9 0.7 %collective-permute-start.5 = (f32[64,256]{1,0:T(8,128)S(1)}, f32[64,256]{1,0:T(8,128)S(1)}, u32[]{:S(2)}, u32[]{:S(2)}) collective-permute-start(f32[64,256]{1,0:T(8,128)S(1)} %get-tuple-element.18.cross_ref), channel_id=1, source_target_pairs={{4,8},{8,4},{12,16},{16,12},{20,24},{24,20},{28,32},{32,28},{36,40... | collective-permute-start | bytes 196616 | tf_op jit(solution)/shard_map/ppermute | solution.py:315
  23.6 3.5 %collective-permute-start.6 = (f32[64,256]{1,0:T(8,128)S(1)}, f32[64,256]{1,0:T(8,128)S(1)}, u32[]{:S(2)}, u32[]{:S(2)}) collective-permute-start(f32[64,256]{1,0:T(8,128)S(1)} %get-tuple-element.19.near_ref), channel_id=1, source_target_pairs={{0,4},{4,0},{8,12},{12,8},{16,20},{20,16},{24,28},{28,24},{32,36},... | collective-permute-start | bytes 196616 | tf_op jit(solution)/shard_map/ppermute | solution.py:315
  27.1 3.5 %inner.1 = (f32[2,1024,256]{2,1,0:T(8,128)S(1)}, f32[3,8,256]{2,1,0:T(8,128)S(1)}) custom-call(s32[1]{0:T(128)} %bitcast.place_ref, f32[2,1024,256]{2,1,0:T(8,128)S(1)} %copy-done.7, f32[64,256]{1,0:T(8,128)S(1)} %get-tuple-element.18.cross_ref, f32[64,256]{1,0:T(8,128)S(1)} %get-tuple-element.19.near_ref, f32[2,64,1024]{2,1,0:T(8,128)S(1)} %bitcast.26, ...), custom_call_target="tpu_custom_call" | custom-call | flops 2500000000 | bytes 8388608 | tf_op jit(solution)/shard_map/inner/pallas_call | solution.py:392
  30.6 0.0 copy-start.2
  30.6 0.0 collective-permute-done.5.cross_pick_ref
  30.6 0.0 collective-permute-done.6.near_pick_ref
  30.6 0.0 collective-permute-done.3.cross_ref
  30.7 0.0 collective-permute-done.4.near_ref
  30.7 1.7 %outer.1 = (f32[2,1024,256]{2,1,0:T(8,128)S(1)}, f32[8,256]{1,0:T(8,128)S(1)}) custom-call(s32[1]{0:T(128)} %bitcast.place_ref, f32[2,1024,256]{2,1,0:T(8,128)S(1)} %get-tuple-element.20.part_ref, f32[648,256]{1,0:T(8,128)S(1)} %collective-permute-done.3.cross_ref, f32[648,256]{1,0:T(8,128)S(1)} %collective-permute-done.4.near_ref, ...), custom_call_target="tpu_custom_call" | custom-call | tf_op jit(solution)/shard_map/outer/pallas_call | solution.py:407
  32.4 0.1 collective-permute-start.7
  32.6 1.1 %collective-permute-done.7 = f32[8,256]{1,0:T(8,128)S(1)} collective-permute-done((f32[8,256]{1,0:T(8,128)S(1)}, f32[8,256]{1,0:T(8,128)S(1)}, u32[]{:S(2)}, u32[]{:S(2)}) %collective-permute-start.7) | collective-permute-done | bytes 8224 | tf_op jit(solution)/shard_map/ppermute | solution.py:315
  33.7 4.9 %collective-permute-start.10 = (f32[8,256]{1,0:T(8,128)S(1)}, f32[8,256]{1,0:T(8,128)S(1)}, u32[]{:S(2)}, u32[]{:S(2)}) collective-permute-start(f32[8,256]{1,0:T(8,128)S(1)} %add.30), channel_id=1, source_target_pairs={{0,33},{1,32},{2,35},{3,34},{4,37},{5,36},{6,39},{7,38},{8,41},{9,... | collective-permute-start | bytes 24584 | tf_op jit(solution)/shard_map/ppermute | solution.py:315
  38.6 0.0 collective-permute-start.9
  38.6 0.6 collective-permute-start.8
  39.1 1.1 %collective-permute-done.10 = f32[8,256]{1,0:T(8,128)S(1)} collective-permute-done((f32[8,256]{1,0:T(8,128)S(1)}, f32[8,256]{1,0:T(8,128)S(1)}, u32[]{:S(2)}, u32[]{:S(2)}) %collective-permute-start.10) | collective-permute-done | bytes 8224 | tf_op jit(solution)/shard_map/ppermute | solution.py:315
  40.2 2.0 %collective-permute-done.9 = f32[8,256]{1,0:T(8,128)S(1)} collective-permute-done((f32[8,256]{1,0:T(8,128)S(1)}, f32[8,256]{1,0:T(8,128)S(1)}, u32[]{:S(2)}, u32[]{:S(2)}) %collective-permute-start.9) | collective-permute-done | bytes 8224 | tf_op jit(solution)/shard_map/ppermute | solution.py:315
  42.2 0.0 collective-permute-done.8
  42.2 3.8 %collective-permute-start.13 = (f32[8,256]{1,0:T(8,128)S(1)}, f32[8,256]{1,0:T(8,128)S(1)}, u32[]{:S(2)}, u32[]{:S(2)}) collective-permute-start(f32[8,256]{1,0:T(8,128)S(1)} %add_add_fusion.2), channel_id=1, source_target_pairs={{0,99},{1,98},{2,97},{3,96},{4,103},{5,102},{6,101},{7,100},{8,107... | collective-permute-start | bytes 24584 | tf_op jit(solution)/shard_map/ppermute | solution.py:315
  46.0 1.1 %collective-permute-start.12 = (f32[8,256]{1,0:T(8,128)S(1)}, f32[8,256]{1,0:T(8,128)S(1)}, u32[]{:S(2)}, u32[]{:S(2)}) collective-permute-start(f32[8,256]{1,0:T(8,128)S(1)} %add_add_fusion.2), channel_id=1, source_target_pairs={{0,3},{1,2},{2,1},{3,0},{4,7},{5,6},{6,5},{7,4},{8,11},{9,10},{10,... | collective-permute-start | bytes 24584 | tf_op jit(solution)/shard_map/ppermute | solution.py:315
  47.2 1.1 %collective-permute-start.11 = (f32[8,256]{1,0:T(8,128)S(1)}, f32[8,256]{1,0:T(8,128)S(1)}, u32[]{:S(2)}, u32[]{:S(2)}) collective-permute-start(f32[8,256]{1,0:T(8,128)S(1)} %add_add_fusion.2), channel_id=1, source_target_pairs={{0,96},{1,97},{2,98},{3,99},{4,100},{5,101},{6,102},{7,103},{8,104... | collective-permute-start | bytes 24584 | tf_op jit(solution)/shard_map/ppermute | solution.py:315
  48.2 1.1 %collective-permute-done.13 = f32[8,256]{1,0:T(8,128)S(1)} collective-permute-done((f32[8,256]{1,0:T(8,128)S(1)}, f32[8,256]{1,0:T(8,128)S(1)}, u32[]{:S(2)}, u32[]{:S(2)}) %collective-permute-start.13) | collective-permute-done | bytes 8224 | tf_op jit(solution)/shard_map/ppermute | solution.py:315
  49.3 1.6 %collective-permute-done.12 = f32[8,256]{1,0:T(8,128)S(1)} collective-permute-done((f32[8,256]{1,0:T(8,128)S(1)}, f32[8,256]{1,0:T(8,128)S(1)}, u32[]{:S(2)}, u32[]{:S(2)}) %collective-permute-start.12) | collective-permute-done | bytes 8224 | tf_op jit(solution)/shard_map/ppermute | solution.py:315
  50.9 1.1 %collective-permute-done.11 = f32[8,256]{1,0:T(8,128)S(1)} collective-permute-done((f32[8,256]{1,0:T(8,128)S(1)}, f32[8,256]{1,0:T(8,128)S(1)}, u32[]{:S(2)}, u32[]{:S(2)}) %collective-permute-start.11) | collective-permute-done | bytes 8224 | tf_op jit(solution)/shard_map/ppermute | solution.py:315
  52.0 1.8 %collective-permute-start.16 = (f32[8,256]{1,0:T(8,128)S(1)}, f32[8,256]{1,0:T(8,128)S(1)}, u32[]{:S(2)}, u32[]{:S(2)}) collective-permute-start(f32[8,256]{1,0:T(8,128)S(1)} %add_add_fusion.1), channel_id=1, source_target_pairs={{0,16},{1,17},{2,18},{3,19},{4,20},{5,21},{6,22},{7,23},{8,24},{9,... | collective-permute-start | bytes 24584 | tf_op jit(solution)/shard_map/ppermute | solution.py:315
  53.8 1.2 %collective-permute-start.15 = (f32[8,256]{1,0:T(8,128)S(1)}, f32[8,256]{1,0:T(8,128)S(1)}, u32[]{:S(2)}, u32[]{:S(2)}) collective-permute-start(f32[8,256]{1,0:T(8,128)S(1)} %add_add_fusion.1), channel_id=1, source_target_pairs={{0,24},{1,25},{2,26},{3,27},{4,28},{5,29},{6,30},{7,31},{8,16},{9,... | collective-permute-start | bytes 24584 | tf_op jit(solution)/shard_map/ppermute | solution.py:315
  55.0 0.8 %collective-permute-start.14 = (f32[8,256]{1,0:T(8,128)S(1)}, f32[8,256]{1,0:T(8,128)S(1)}, u32[]{:S(2)}, u32[]{:S(2)}) collective-permute-start(f32[8,256]{1,0:T(8,128)S(1)} %add_add_fusion.1), channel_id=1, source_target_pairs={{0,8},{1,9},{2,10},{3,11},{4,12},{5,13},{6,14},{7,15},{8,0},{9,1},... | collective-permute-start | bytes 24584 | tf_op jit(solution)/shard_map/ppermute | solution.py:315
  55.8 1.4 %collective-permute-done.16 = f32[8,256]{1,0:T(8,128)S(1)} collective-permute-done((f32[8,256]{1,0:T(8,128)S(1)}, f32[8,256]{1,0:T(8,128)S(1)}, u32[]{:S(2)}, u32[]{:S(2)}) %collective-permute-start.16) | collective-permute-done | bytes 8224 | tf_op jit(solution)/shard_map/ppermute | solution.py:315
  57.2 1.5 %collective-permute-done.15 = f32[8,256]{1,0:T(8,128)S(1)} collective-permute-done((f32[8,256]{1,0:T(8,128)S(1)}, f32[8,256]{1,0:T(8,128)S(1)}, u32[]{:S(2)}, u32[]{:S(2)}) %collective-permute-start.15) | collective-permute-done | bytes 8224 | tf_op jit(solution)/shard_map/ppermute | solution.py:315
  58.7 0.0 collective-permute-done.14
  58.7 3.5 %final.1 = (f32[2,1024,256]{2,1,0:T(8,128)}, f32[2,1024,256]{2,1,0:T(8,128)}, f32[2,1024,256]{2,1,0:T(8,128)}, f32[1,256]{1,0:T(1,128)}) custom-call(f32[8,256]{1,0:T(8,128)S(1)} %add_add_fusion.total_ref, f32[2,1,1024]{2,1,0:T(1,128)S(1)} %copy-done.5, f32[2,1024,256]{2,1,0:T(8,128)S(1)} %bitcast.23, f32[2,1024,256]{2,1,0:T(8,128)S(1)} %bitcast.22, ...), custom_call_target="tpu_custom_call" | custom-call | tf_op jit(solution)/shard_map/final/pallas_call | solution.py:423
  (12 shorter events, 0.0 us)
Async XLA Ops:
  3.8 17.8 %collective-permute-start.2 = (f32[200,256]{1,0:T(8,128)}, f32[200,256]{1,0:T(8,128)S(1)}, u32[]{:S(2)}, u32[]{:S(2)}) collective-permute-start(f32[200,256]{1,0:T(8,128)} %primal.1.pay_hbm.pay_ref), channel_id=1, source_target_pairs={{0,2},{1,3},{2,0},{3,1},{4,6},{5,7},{6,4},{7,5},{8,10},{9,11},{10,... | collective-permute-start | bytes 614408 | tf_op jit(solution)/shard_map/ppermute | solution.py:315
  7.0 14.6 %collective-permute-start.1 = (f32[200,256]{1,0:T(8,128)}, f32[200,256]{1,0:T(8,128)S(1)}, u32[]{:S(2)}, u32[]{:S(2)}) collective-permute-start(f32[200,256]{1,0:T(8,128)} %primal.1.pay_hbm.pay_ref), channel_id=1, source_target_pairs={{0,3},{1,2},{2,1},{3,0},{4,7},{5,6},{6,5},{7,4},{8,11},{9,10},{10,... | collective-permute-start | bytes 614408 | tf_op jit(solution)/shard_map/ppermute | solution.py:315
  8.1 13.5 %collective-permute-start = (f32[200,256]{1,0:T(8,128)}, f32[200,256]{1,0:T(8,128)S(1)}, u32[]{:S(2)}, u32[]{:S(2)}) collective-permute-start(f32[200,256]{1,0:T(8,128)} %primal.1.pay_hbm.pay_ref), channel_id=1, source_target_pairs={{0,1},{1,0},{2,3},{3,2},{4,5},{5,4},{6,7},{7,6},{8,9},{9,8},{10,11... | collective-permute-start | bytes 614408 | tf_op jit(solution)/shard_map/ppermute | solution.py:315
  8.1 13.5 %copy-start.4 = (f32[200,256]{1,0:T(8,128)S(1)}, f32[200,256]{1,0:T(8,128)}, u32[]{:S(2)}) copy-start(f32[200,256]{1,0:T(8,128)} %primal.1.pay_hbm.pay_ref) | copy-start | bytes 614404
  17.5 13.1 %collective-permute-start.3 = (f32[648,256]{1,0:T(8,128)}, f32[648,256]{1,0:T(8,128)S(1)}, u32[]{:S(2)}, u32[]{:S(2)}) collective-permute-start(f32[648,256]{1,0:T(8,128)} %get-tuple-element.21), channel_id=1, source_target_pairs={{4,8},{8,4},{12,16},{16,12},{20,24},{24,20},{28,32},{32,28},{36,40... | collective-permute-start | bytes 1990664 | tf_op jit(solution)/shard_map/ppermute | solution.py:315
  18.2 8.9 %copy-start = (f32[2,1,1024,256]{3,2,1,0:T(8,128)S(1)}, f32[2,1,1024,256]{3,2,1,0:T(8,128)}, u32[]{:S(2)}) copy-start(f32[2,1,1024,256]{3,2,1,0:T(8,128)} %param.18) | copy-start | bytes 6291460
  18.2 8.9 %copy-start.1 = (f32[2,1,1024,256]{3,2,1,0:T(8,128)S(1)}, f32[2,1,1024,256]{3,2,1,0:T(8,128)}, u32[]{:S(2)}) copy-start(f32[2,1,1024,256]{3,2,1,0:T(8,128)} %param.17) | copy-start | bytes 6291460
  18.2 8.9 %copy-start.3 = (f32[2,1,64,1024]{3,2,1,0:T(8,128)S(1)}, f32[2,1,64,1024]{3,2,1,0:T(8,128)}, u32[]{:S(2)}) copy-start(f32[2,1,64,1024]{3,2,1,0:T(8,128)} %param.11) | copy-start | bytes 1572868
  18.2 8.9 %copy-start.5 = (f32[2,1,1024]{2,1,0:T(1,128)S(1)}, f32[2,1,1024]{2,1,0:T(1,128)}, u32[]{:S(2)}) copy-start(f32[2,1,1024]{2,1,0:T(1,128)} %weight_ref.5) | copy-start | bytes 24580
  18.3 8.9 %copy-start.6 = (s32[2,1,1024]{2,1,0:T(1,128)S(1)}, s32[2,1,1024]{2,1,0:T(1,128)}, u32[]{:S(2)}) copy-start(s32[2,1,1024]{2,1,0:T(1,128)} %partner_ref.1) | copy-start | bytes 24580
  18.3 8.9 %copy-start.7 = (f32[2,1024,256]{2,1,0:T(8,128)S(1)}, f32[2,1024,256]{2,1,0:T(8,128)}, u32[]{:S(2)}) copy-start(f32[2,1024,256]{2,1,0:T(8,128)} %get-tuple-element.17.local_ref) | copy-start | bytes 6291460
  18.3 12.4 %collective-permute-start.4 = (f32[648,256]{1,0:T(8,128)}, f32[648,256]{1,0:T(8,128)S(1)}, u32[]{:S(2)}, u32[]{:S(2)}) collective-permute-start(f32[648,256]{1,0:T(8,128)} %get-tuple-element.22), channel_id=1, source_target_pairs={{0,4},{4,0},{8,12},{12,8},{16,20},{20,16},{24,28},{28,24},{32,36},... | collective-permute-start | bytes 1990664 | tf_op jit(solution)/shard_map/ppermute | solution.py:315
  22.9 7.7 %collective-permute-start.5 = (f32[64,256]{1,0:T(8,128)S(1)}, f32[64,256]{1,0:T(8,128)S(1)}, u32[]{:S(2)}, u32[]{:S(2)}) collective-permute-start(f32[64,256]{1,0:T(8,128)S(1)} %get-tuple-element.18.cross_ref), channel_id=1, source_target_pairs={{4,8},{8,4},{12,16},{16,12},{20,24},{24,20},{28,32},{32,28},{36,40... | collective-permute-start | bytes 196616 | tf_op jit(solution)/shard_map/ppermute | solution.py:315
  23.6 7.1 %collective-permute-start.6 = (f32[64,256]{1,0:T(8,128)S(1)}, f32[64,256]{1,0:T(8,128)S(1)}, u32[]{:S(2)}, u32[]{:S(2)}) collective-permute-start(f32[64,256]{1,0:T(8,128)S(1)} %get-tuple-element.19.near_ref), channel_id=1, source_target_pairs={{0,4},{4,0},{8,12},{12,8},{16,20},{20,16},{24,28},{28,24},{32,36},... | collective-permute-start | bytes 196616 | tf_op jit(solution)/shard_map/ppermute | solution.py:315
  30.6 28.1 %copy-start.2 = (f32[2,1,1024,256]{3,2,1,0:T(8,128)S(1)}, f32[2,1,1024,256]{3,2,1,0:T(8,128)}, u32[]{:S(2)}) copy-start(f32[2,1,1024,256]{3,2,1,0:T(8,128)} %param.16) | copy-start | bytes 6291460
  32.4 1.3 %collective-permute-start.7 = (f32[8,256]{1,0:T(8,128)S(1)}, f32[8,256]{1,0:T(8,128)S(1)}, u32[]{:S(2)}, u32[]{:S(2)}) collective-permute-start(f32[8,256]{1,0:T(8,128)S(1)} %get-tuple-element.24), channel_id=1, source_target_pairs={{0,4},{4,0},{8,12},{12,8},{16,20},{20,16},{24,28},{28,24},{32,36},... | collective-permute-start | bytes 24584 | tf_op jit(solution)/shard_map/ppermute | solution.py:315
  33.7 6.5 %collective-permute-start.10 = (f32[8,256]{1,0:T(8,128)S(1)}, f32[8,256]{1,0:T(8,128)S(1)}, u32[]{:S(2)}, u32[]{:S(2)}) collective-permute-start(f32[8,256]{1,0:T(8,128)S(1)} %add.30), channel_id=1, source_target_pairs={{0,33},{1,32},{2,35},{3,34},{4,37},{5,36},{6,39},{7,38},{8,41},{9,... | collective-permute-start | bytes 24584 | tf_op jit(solution)/shard_map/ppermute | solution.py:315
  38.6 3.7 %collective-permute-start.9 = (f32[8,256]{1,0:T(8,128)S(1)}, f32[8,256]{1,0:T(8,128)S(1)}, u32[]{:S(2)}, u32[]{:S(2)}) collective-permute-start(f32[8,256]{1,0:T(8,128)S(1)} %add.30), channel_id=1, source_target_pairs={{0,1},{1,0},{2,3},{3,2},{4,5},{5,4},{6,7},{7,6},{8,9},{9,8},{10,11... | collective-permute-start | bytes 24584 | tf_op jit(solution)/shard_map/ppermute | solution.py:315
  38.6 3.7 %collective-permute-start.8 = (f32[8,256]{1,0:T(8,128)S(1)}, f32[8,256]{1,0:T(8,128)S(1)}, u32[]{:S(2)}, u32[]{:S(2)}) collective-permute-start(f32[8,256]{1,0:T(8,128)S(1)} %add.30), channel_id=1, source_target_pairs={{0,32},{1,33},{2,34},{3,35},{4,36},{5,37},{6,38},{7,39},{8,40},{9,... | collective-permute-start | bytes 24584 | tf_op jit(solution)/shard_map/ppermute | solution.py:315
  42.2 7.0 %collective-permute-start.13 = (f32[8,256]{1,0:T(8,128)S(1)}, f32[8,256]{1,0:T(8,128)S(1)}, u32[]{:S(2)}, u32[]{:S(2)}) collective-permute-start(f32[8,256]{1,0:T(8,128)S(1)} %add_add_fusion.2), channel_id=1, source_target_pairs={{0,99},{1,98},{2,97},{3,96},{4,103},{5,102},{6,101},{7,100},{8,107... | collective-permute-start | bytes 24584 | tf_op jit(solution)/shard_map/ppermute | solution.py:315
  46.0 4.9 %collective-permute-start.12 = (f32[8,256]{1,0:T(8,128)S(1)}, f32[8,256]{1,0:T(8,128)S(1)}, u32[]{:S(2)}, u32[]{:S(2)}) collective-permute-start(f32[8,256]{1,0:T(8,128)S(1)} %add_add_fusion.2), channel_id=1, source_target_pairs={{0,3},{1,2},{2,1},{3,0},{4,7},{5,6},{6,5},{7,4},{8,11},{9,10},{10,... | collective-permute-start | bytes 24584 | tf_op jit(solution)/shard_map/ppermute | solution.py:315
  47.2 4.9 %collective-permute-start.11 = (f32[8,256]{1,0:T(8,128)S(1)}, f32[8,256]{1,0:T(8,128)S(1)}, u32[]{:S(2)}, u32[]{:S(2)}) collective-permute-start(f32[8,256]{1,0:T(8,128)S(1)} %add_add_fusion.2), channel_id=1, source_target_pairs={{0,96},{1,97},{2,98},{3,99},{4,100},{5,101},{6,102},{7,103},{8,104... | collective-permute-start | bytes 24584 | tf_op jit(solution)/shard_map/ppermute | solution.py:315
  52.0 5.2 %collective-permute-start.16 = (f32[8,256]{1,0:T(8,128)S(1)}, f32[8,256]{1,0:T(8,128)S(1)}, u32[]{:S(2)}, u32[]{:S(2)}) collective-permute-start(f32[8,256]{1,0:T(8,128)S(1)} %add_add_fusion.1), channel_id=1, source_target_pairs={{0,16},{1,17},{2,18},{3,19},{4,20},{5,21},{6,22},{7,23},{8,24},{9,... | collective-permute-start | bytes 24584 | tf_op jit(solution)/shard_map/ppermute | solution.py:315
  53.8 4.9 %collective-permute-start.15 = (f32[8,256]{1,0:T(8,128)S(1)}, f32[8,256]{1,0:T(8,128)S(1)}, u32[]{:S(2)}, u32[]{:S(2)}) collective-permute-start(f32[8,256]{1,0:T(8,128)S(1)} %add_add_fusion.1), channel_id=1, source_target_pairs={{0,24},{1,25},{2,26},{3,27},{4,28},{5,29},{6,30},{7,31},{8,16},{9,... | collective-permute-start | bytes 24584 | tf_op jit(solution)/shard_map/ppermute | solution.py:315
  55.0 3.7 %collective-permute-start.14 = (f32[8,256]{1,0:T(8,128)S(1)}, f32[8,256]{1,0:T(8,128)S(1)}, u32[]{:S(2)}, u32[]{:S(2)}) collective-permute-start(f32[8,256]{1,0:T(8,128)S(1)} %add_add_fusion.1), channel_id=1, source_target_pairs={{0,8},{1,9},{2,10},{3,11},{4,12},{5,13},{6,14},{7,15},{8,0},{9,1},... | collective-permute-start | bytes 24584 | tf_op jit(solution)/shard_map/ppermute | solution.py:315

commit v10 on v9

--- a/solution.py
+++ b/solution.py
@@ -66,7 +66,8 @@
     for s in range(2):
         ch, cl = split(coup[s])
         dh, dl = split(direc[s])
-        pay_ref[s * C : (s + 1) * C] = dot(ch, dh) + dot(ch, dl) + dot(cl, dh)
+        both = dot(jnp.concatenate([ch, cl], axis=0), dh)
+        pay_ref[s * C : (s + 1) * C] = both[0:C] + both[C:] + dot(ch, dl)
         pay_ref[3 * C + s : 3 * C + s + 1, 0:C] = corner[s].astype(F32)
 
 
@@ -117,7 +118,8 @@
         for r in range(ROUNDS):
             rows = slice(r * STRIP, (r + 1) * STRIP)
             ah, al = split(flex[s, rows])
-            out = dot(ah, right[s, 0:N]) + dot(ah, right[s, N:]) + dot(al, right[s, 0:N])
+            both = dot(jnp.concatenate([ah, al], axis=0), right[s, 0:N])
+            out = both[0:STRIP] + both[STRIP:] + dot(ah, right[s, N:])
             local[s, rows] = out
             oh, ol = split(out)
             high[s, rows] = oh

time: 62.5 us -> 62.3 us (level)
  no operation moved by 1% of the time
where the time goes in v10:
time: 62.3 us; the launch traced here: 62.2 us
  starting transfers between devices  27.9 us (45%)
  Pallas kernels  22.3 us (36%)
  waiting for transfers between devices  10.9 us (17%)
  between operations  0.99 us (2%)
    ppermute x17, starting transfers between devices, exchange(): return lax.ppermute(x, axes, pairs)  27.9 us
    ppermute x17, waiting for transfers between devices, exchange(): return lax.ppermute(x, axes, pairs)  10.9 us
    pallas_call x1, Pallas kernels, per_device(): pl.pallas_call(local_kernel, out_shape=(jax.ShapeDtypeStruct((2, N, L), F...  9.34 us
    pallas_call x1, Pallas kernels, per_device(): pl.pallas_call(final_kernel, out_shape=(whole, whole, whole, jax.ShapeDty...  3.48 us
    pallas_call x1, Pallas kernels, per_device(): pl.pallas_call(inner_kernel, out_shape=(whole, jax.ShapeDtypeStruct((3, 8...  3.45 us
    pallas_call x1, Pallas kernels, per_device(): pl.pallas_call(primal_kernel, out_shape=jax.ShapeDtypeStruct((3 * C + 8,...  3.01 us
    pallas_call x1, Pallas kernels, per_device(): pl.pallas_call(outer_kernel, out_shape=(whole, jax.ShapeDtypeStruct((8, L...  1.75 us
    pallas_call x1, Pallas kernels, per_device(): pl.pallas_call(coarse_kernel, out_shape=(piece, piece), in_specs=[smem()]...  1.27 us
  transfers between devices with their start and end apart: 17, of which 8 were waited for; matrix products, arithmetic and copies ran while one was open for 0% of the time, Pallas kernels for 23%

profile of v10, /device:TPU:0, one launch (start us, length us, event | category | flops | bytes accessed | tf_op | source)
XLA Modules:
  0.0 62.2 jit_solution(4725980543373008970)
XLA Ops:
  0.6 3.0 %primal.1.pay_hbm.pay_ref = f32[200,256]{1,0:T(8,128)} custom-call(f32[2,1024,256]{2,1,0:T(8,128)} %bitcast.17, f32[2,64,1024]{2,1,0:T(8,128)} %bitcast.24, s32[2,1,64]{2,1,0:T(1,128)} %map_hbm.1, f32[64,256]{1,0:T(8,128)} %bitcast.27), custom_call_target="tpu_custom_call" | custom-call | flops 200000000 | bytes 3145728 | tf_op jit(solution)/shard_map/primal/pallas_call | solution.py:330
  3.7 3.2 %collective-permute-start.2 = (f32[200,256]{1,0:T(8,128)}, f32[200,256]{1,0:T(8,128)S(1)}, u32[]{:S(2)}, u32[]{:S(2)}) collective-permute-start(f32[200,256]{1,0:T(8,128)} %primal.1.pay_hbm.pay_ref), channel_id=1, source_target_pairs={{0,2},{1,3},{2,0},{3,1},{4,6},{5,7},{6,4},{7,5},{8,10},{9,11},{10,... | collective-permute-start | bytes 614408 | tf_op jit(solution)/shard_map/ppermute | solution.py:317
  6.8 1.1 %collective-permute-start.1 = (f32[200,256]{1,0:T(8,128)}, f32[200,256]{1,0:T(8,128)S(1)}, u32[]{:S(2)}, u32[]{:S(2)}) collective-permute-start(f32[200,256]{1,0:T(8,128)} %primal.1.pay_hbm.pay_ref), channel_id=1, source_target_pairs={{0,3},{1,2},{2,1},{3,0},{4,7},{5,6},{6,5},{7,4},{8,11},{9,10},{10,... | collective-permute-start | bytes 614408 | tf_op jit(solution)/shard_map/ppermute | solution.py:317
  8.0 0.0 collective-permute-start
  8.0 9.3 %local.1 = (f32[2,1024,256]{2,1,0:T(8,128)}, f32[648,256]{1,0:T(8,128)}, f32[648,256]{1,0:T(8,128)}) custom-call(s32[1]{0:T(128)} %bitcast.place_ref, f32[200,256]{1,0:T(8,128)} %primal.1.pay_hbm.pay_ref, f32[2,1024,1024]{2,1,0:T(8,128)} %bitcast.28, f32[2,1024,256]{2,1,0:T(8,128)} %bitcast.18, f32[2,64,1024]{2,1,0:T(8,128)} %bitcast.25, ...), custom_call_target="tpu_custom_call" | custom-call | flops 4000000000 | bytes 12582912 | tf_op jit(solution)/shard_map/local/pallas_call | solution.py:348
  17.3 0.7 %collective-permute-start.3 = (f32[648,256]{1,0:T(8,128)}, f32[648,256]{1,0:T(8,128)S(1)}, u32[]{:S(2)}, u32[]{:S(2)}) collective-permute-start(f32[648,256]{1,0:T(8,128)} %get-tuple-element.21), channel_id=1, source_target_pairs={{4,8},{8,4},{12,16},{16,12},{20,24},{24,20},{28,32},{32,28},{36,40... | collective-permute-start | bytes 1990664 | tf_op jit(solution)/shard_map/ppermute | solution.py:317
  18.0 0.0 copy-start
  18.1 0.0 copy-start.1
  18.1 0.0 copy-start.3
  18.1 0.0 copy-start.5
  18.1 0.0 copy-start.6
  18.1 0.0 copy-start.7
  18.1 3.3 %collective-permute-start.4 = (f32[648,256]{1,0:T(8,128)}, f32[648,256]{1,0:T(8,128)S(1)}, u32[]{:S(2)}, u32[]{:S(2)}) collective-permute-start(f32[648,256]{1,0:T(8,128)} %get-tuple-element.22), channel_id=1, source_target_pairs={{0,4},{4,0},{8,12},{12,8},{16,20},{20,16},{24,28},{28,24},{32,36},... | collective-permute-start | bytes 1990664 | tf_op jit(solution)/shard_map/ppermute | solution.py:317
  21.4 0.0 collective-permute-done.2.three_ref
  21.4 0.0 collective-permute-done.1.two_ref
  21.4 0.0 collective-permute-done.one_ref
  21.4 1.3 %coarse.1 = (f32[64,256]{1,0:T(8,128)S(1)}, f32[64,256]{1,0:T(8,128)S(1)}) custom-call(s32[1]{0:T(128)} %bitcast.place_ref, f32[200,256]{1,0:T(8,128)S(1)} %copy-done.4, f32[200,256]{1,0:T(8,128)S(1)} %collective-permute-done.one_ref, f32[200,256]{1,0:T(8,128)S(1)} %collective-permute-done.1.two_ref, f32[200,256]{1,0:T(8,128)S(1)} %collective-permute-done.2.three_ref), custom_call_target="tpu_custom_call" | custom-call | flops 30000001024 | bytes 1048576 | tf_op jit(solution)/shard_map/coarse/pallas_call | solution.py:382
  22.7 0.7 %collective-permute-start.5 = (f32[64,256]{1,0:T(8,128)S(1)}, f32[64,256]{1,0:T(8,128)S(1)}, u32[]{:S(2)}, u32[]{:S(2)}) collective-permute-start(f32[64,256]{1,0:T(8,128)S(1)} %get-tuple-element.18.cross_ref), channel_id=1, source_target_pairs={{4,8},{8,4},{12,16},{16,12},{20,24},{24,20},{28,32},{32,28},{36,40... | collective-permute-start | bytes 196616 | tf_op jit(solution)/shard_map/ppermute | solution.py:317
  23.4 3.5 %collective-permute-start.6 = (f32[64,256]{1,0:T(8,128)S(1)}, f32[64,256]{1,0:T(8,128)S(1)}, u32[]{:S(2)}, u32[]{:S(2)}) collective-permute-start(f32[64,256]{1,0:T(8,128)S(1)} %get-tuple-element.19.near_ref), channel_id=1, source_target_pairs={{0,4},{4,0},{8,12},{12,8},{16,20},{20,16},{24,28},{28,24},{32,36},... | collective-permute-start | bytes 196616 | tf_op jit(solution)/shard_map/ppermute | solution.py:317
  26.9 0.0 copy-done.1
  27.0 3.5 %inner.1 = (f32[2,1024,256]{2,1,0:T(8,128)S(1)}, f32[3,8,256]{2,1,0:T(8,128)S(1)}) custom-call(s32[1]{0:T(128)} %bitcast.place_ref, f32[2,1024,256]{2,1,0:T(8,128)S(1)} %copy-done.7, f32[64,256]{1,0:T(8,128)S(1)} %get-tuple-element.18.cross_ref, f32[64,256]{1,0:T(8,128)S(1)} %get-tuple-element.19.near_ref, f32[2,64,1024]{2,1,0:T(8,128)S(1)} %bitcast.26, ...), custom_call_target="tpu_custom_call" | custom-call | flops 2500000000 | bytes 8388608 | tf_op jit(solution)/shard_map/inner/pallas_call | solution.py:394
  30.4 0.0 copy-start.2
  30.4 0.0 collective-permute-done.5.cross_pick_ref
  30.5 0.0 collective-permute-done.6.near_pick_ref
  30.5 0.0 collective-permute-done.3.cross_ref
  30.5 0.0 collective-permute-done.4.near_ref
  30.5 1.8 %outer.1 = (f32[2,1024,256]{2,1,0:T(8,128)S(1)}, f32[8,256]{1,0:T(8,128)S(1)}) custom-call(s32[1]{0:T(128)} %bitcast.place_ref, f32[2,1024,256]{2,1,0:T(8,128)S(1)} %get-tuple-element.20.part_ref, f32[648,256]{1,0:T(8,128)S(1)} %collective-permute-done.3.cross_ref, f32[648,256]{1,0:T(8,128)S(1)} %collective-permute-done.4.near_ref, ...), custom_call_target="tpu_custom_call" | custom-call | tf_op jit(solution)/shard_map/outer/pallas_call | solution.py:409
  32.2 0.1 collective-permute-start.7
  32.4 1.1 %collective-permute-done.7 = f32[8,256]{1,0:T(8,128)S(1)} collective-permute-done((f32[8,256]{1,0:T(8,128)S(1)}, f32[8,256]{1,0:T(8,128)S(1)}, u32[]{:S(2)}, u32[]{:S(2)}) %collective-permute-start.7) | collective-permute-done | bytes 8224 | tf_op jit(solution)/shard_map/ppermute | solution.py:317
  33.5 4.9 %collective-permute-start.10 = (f32[8,256]{1,0:T(8,128)S(1)}, f32[8,256]{1,0:T(8,128)S(1)}, u32[]{:S(2)}, u32[]{:S(2)}) collective-permute-start(f32[8,256]{1,0:T(8,128)S(1)} %add.30), channel_id=1, source_target_pairs={{0,33},{1,32},{2,35},{3,34},{4,37},{5,36},{6,39},{7,38},{8,41},{9,... | collective-permute-start | bytes 24584 | tf_op jit(solution)/shard_map/ppermute | solution.py:317
  38.4 0.0 collective-permute-start.9
  38.4 0.6 collective-permute-start.8
  39.0 1.1 %collective-permute-done.10 = f32[8,256]{1,0:T(8,128)S(1)} collective-permute-done((f32[8,256]{1,0:T(8,128)S(1)}, f32[8,256]{1,0:T(8,128)S(1)}, u32[]{:S(2)}, u32[]{:S(2)}) %collective-permute-start.10) | collective-permute-done | bytes 8224 | tf_op jit(solution)/shard_map/ppermute | solution.py:317
  40.0 2.0 %collective-permute-done.9 = f32[8,256]{1,0:T(8,128)S(1)} collective-permute-done((f32[8,256]{1,0:T(8,128)S(1)}, f32[8,256]{1,0:T(8,128)S(1)}, u32[]{:S(2)}, u32[]{:S(2)}) %collective-permute-start.9) | collective-permute-done | bytes 8224 | tf_op jit(solution)/shard_map/ppermute | solution.py:317
  42.0 0.0 collective-permute-done.8
  42.1 3.8 %collective-permute-start.13 = (f32[8,256]{1,0:T(8,128)S(1)}, f32[8,256]{1,0:T(8,128)S(1)}, u32[]{:S(2)}, u32[]{:S(2)}) collective-permute-start(f32[8,256]{1,0:T(8,128)S(1)} %add_add_fusion.2), channel_id=1, source_target_pairs={{0,99},{1,98},{2,97},{3,96},{4,103},{5,102},{6,101},{7,100},{8,107... | collective-permute-start | bytes 24584 | tf_op jit(solution)/shard_map/ppermute | solution.py:317
  45.9 1.1 %collective-permute-start.12 = (f32[8,256]{1,0:T(8,128)S(1)}, f32[8,256]{1,0:T(8,128)S(1)}, u32[]{:S(2)}, u32[]{:S(2)}) collective-permute-start(f32[8,256]{1,0:T(8,128)S(1)} %add_add_fusion.2), channel_id=1, source_target_pairs={{0,3},{1,2},{2,1},{3,0},{4,7},{5,6},{6,5},{7,4},{8,11},{9,10},{10,... | collective-permute-start | bytes 24584 | tf_op jit(solution)/shard_map/ppermute | solution.py:317
  47.0 1.1 %collective-permute-start.11 = (f32[8,256]{1,0:T(8,128)S(1)}, f32[8,256]{1,0:T(8,128)S(1)}, u32[]{:S(2)}, u32[]{:S(2)}) collective-permute-start(f32[8,256]{1,0:T(8,128)S(1)} %add_add_fusion.2), channel_id=1, source_target_pairs={{0,96},{1,97},{2,98},{3,99},{4,100},{5,101},{6,102},{7,103},{8,104... | collective-permute-start | bytes 24584 | tf_op jit(solution)/shard_map/ppermute | solution.py:317
  48.0 1.1 %collective-permute-done.13 = f32[8,256]{1,0:T(8,128)S(1)} collective-permute-done((f32[8,256]{1,0:T(8,128)S(1)}, f32[8,256]{1,0:T(8,128)S(1)}, u32[]{:S(2)}, u32[]{:S(2)}) %collective-permute-start.13) | collective-permute-done | bytes 8224 | tf_op jit(solution)/shard_map/ppermute | solution.py:317
  49.1 1.6 %collective-permute-done.12 = f32[8,256]{1,0:T(8,128)S(1)} collective-permute-done((f32[8,256]{1,0:T(8,128)S(1)}, f32[8,256]{1,0:T(8,128)S(1)}, u32[]{:S(2)}, u32[]{:S(2)}) %collective-permute-start.12) | collective-permute-done | bytes 8224 | tf_op jit(solution)/shard_map/ppermute | solution.py:317
  50.7 1.1 %collective-permute-done.11 = f32[8,256]{1,0:T(8,128)S(1)} collective-permute-done((f32[8,256]{1,0:T(8,128)S(1)}, f32[8,256]{1,0:T(8,128)S(1)}, u32[]{:S(2)}, u32[]{:S(2)}) %collective-permute-start.11) | collective-permute-done | bytes 8224 | tf_op jit(solution)/shard_map/ppermute | solution.py:317
  51.9 1.8 %collective-permute-start.16 = (f32[8,256]{1,0:T(8,128)S(1)}, f32[8,256]{1,0:T(8,128)S(1)}, u32[]{:S(2)}, u32[]{:S(2)}) collective-permute-start(f32[8,256]{1,0:T(8,128)S(1)} %add_add_fusion.1), channel_id=1, source_target_pairs={{0,16},{1,17},{2,18},{3,19},{4,20},{5,21},{6,22},{7,23},{8,24},{9,... | collective-permute-start | bytes 24584 | tf_op jit(solution)/shard_map/ppermute | solution.py:317
  53.6 1.2 %collective-permute-start.15 = (f32[8,256]{1,0:T(8,128)S(1)}, f32[8,256]{1,0:T(8,128)S(1)}, u32[]{:S(2)}, u32[]{:S(2)}) collective-permute-start(f32[8,256]{1,0:T(8,128)S(1)} %add_add_fusion.1), channel_id=1, source_target_pairs={{0,24},{1,25},{2,26},{3,27},{4,28},{5,29},{6,30},{7,31},{8,16},{9,... | collective-permute-start | bytes 24584 | tf_op jit(solution)/shard_map/ppermute | solution.py:317
  54.8 0.8 %collective-permute-start.14 = (f32[8,256]{1,0:T(8,128)S(1)}, f32[8,256]{1,0:T(8,128)S(1)}, u32[]{:S(2)}, u32[]{:S(2)}) collective-permute-start(f32[8,256]{1,0:T(8,128)S(1)} %add_add_fusion.1), channel_id=1, source_target_pairs={{0,8},{1,9},{2,10},{3,11},{4,12},{5,13},{6,14},{7,15},{8,0},{9,1},... | collective-permute-start | bytes 24584 | tf_op jit(solution)/shard_map/ppermute | solution.py:317
  55.6 1.4 %collective-permute-done.16 = f32[8,256]{1,0:T(8,128)S(1)} collective-permute-done((f32[8,256]{1,0:T(8,128)S(1)}, f32[8,256]{1,0:T(8,128)S(1)}, u32[]{:S(2)}, u32[]{:S(2)}) %collective-permute-start.16) | collective-permute-done | bytes 8224 | tf_op jit(solution)/shard_map/ppermute | solution.py:317
  57.0 1.5 %collective-permute-done.15 = f32[8,256]{1,0:T(8,128)S(1)} collective-permute-done((f32[8,256]{1,0:T(8,128)S(1)}, f32[8,256]{1,0:T(8,128)S(1)}, u32[]{:S(2)}, u32[]{:S(2)}) %collective-permute-start.15) | collective-permute-done | bytes 8224 | tf_op jit(solution)/shard_map/ppermute | solution.py:317
  58.5 0.0 collective-permute-done.14
  58.5 3.5 %final.1 = (f32[2,1024,256]{2,1,0:T(8,128)}, f32[2,1024,256]{2,1,0:T(8,128)}, f32[2,1024,256]{2,1,0:T(8,128)}, f32[1,256]{1,0:T(1,128)}) custom-call(f32[8,256]{1,0:T(8,128)S(1)} %add_add_fusion.total_ref, f32[2,1,1024]{2,1,0:T(1,128)S(1)} %copy-done.5, f32[2,1024,256]{2,1,0:T(8,128)S(1)} %bitcast.23, f32[2,1024,256]{2,1,0:T(8,128)S(1)} %bitcast.22, ...), custom_call_target="tpu_custom_call" | custom-call | tf_op jit(solution)/shard_map/final/pallas_call | solution.py:425
  (12 shorter events, 0.0 us)
Async XLA Ops:
  3.7 17.8 %collective-permute-start.2 = (f32[200,256]{1,0:T(8,128)}, f32[200,256]{1,0:T(8,128)S(1)}, u32[]{:S(2)}, u32[]{:S(2)}) collective-permute-start(f32[200,256]{1,0:T(8,128)} %primal.1.pay_hbm.pay_ref), channel_id=1, source_target_pairs={{0,2},{1,3},{2,0},{3,1},{4,6},{5,7},{6,4},{7,5},{8,10},{9,11},{10,... | collective-permute-start | bytes 614408 | tf_op jit(solution)/shard_map/ppermute | solution.py:317
  6.8 14.6 %collective-permute-start.1 = (f32[200,256]{1,0:T(8,128)}, f32[200,256]{1,0:T(8,128)S(1)}, u32[]{:S(2)}, u32[]{:S(2)}) collective-permute-start(f32[200,256]{1,0:T(8,128)} %primal.1.pay_hbm.pay_ref), channel_id=1, source_target_pairs={{0,3},{1,2},{2,1},{3,0},{4,7},{5,6},{6,5},{7,4},{8,11},{9,10},{10,... | collective-permute-start | bytes 614408 | tf_op jit(solution)/shard_map/ppermute | solution.py:317
  8.0 13.5 %collective-permute-start = (f32[200,256]{1,0:T(8,128)}, f32[200,256]{1,0:T(8,128)S(1)}, u32[]{:S(2)}, u32[]{:S(2)}) collective-permute-start(f32[200,256]{1,0:T(8,128)} %primal.1.pay_hbm.pay_ref), channel_id=1, source_target_pairs={{0,1},{1,0},{2,3},{3,2},{4,5},{5,4},{6,7},{7,6},{8,9},{9,8},{10,11... | collective-permute-start | bytes 614408 | tf_op jit(solution)/shard_map/ppermute | solution.py:317
  8.0 13.5 %copy-start.4 = (f32[200,256]{1,0:T(8,128)S(1)}, f32[200,256]{1,0:T(8,128)}, u32[]{:S(2)}) copy-start(f32[200,256]{1,0:T(8,128)} %primal.1.pay_hbm.pay_ref) | copy-start | bytes 614404
  17.3 13.1 %collective-permute-start.3 = (f32[648,256]{1,0:T(8,128)}, f32[648,256]{1,0:T(8,128)S(1)}, u32[]{:S(2)}, u32[]{:S(2)}) collective-permute-start(f32[648,256]{1,0:T(8,128)} %get-tuple-element.21), channel_id=1, source_target_pairs={{4,8},{8,4},{12,16},{16,12},{20,24},{24,20},{28,32},{32,28},{36,40... | collective-permute-start | bytes 1990664 | tf_op jit(solution)/shard_map/ppermute | solution.py:317
  18.0 8.9 %copy-start = (f32[2,1,1024,256]{3,2,1,0:T(8,128)S(1)}, f32[2,1,1024,256]{3,2,1,0:T(8,128)}, u32[]{:S(2)}) copy-start(f32[2,1,1024,256]{3,2,1,0:T(8,128)} %param.18) | copy-start | bytes 6291460
  18.1 8.9 %copy-start.1 = (f32[2,1,1024,256]{3,2,1,0:T(8,128)S(1)}, f32[2,1,1024,256]{3,2,1,0:T(8,128)}, u32[]{:S(2)}) copy-start(f32[2,1,1024,256]{3,2,1,0:T(8,128)} %param.17) | copy-start | bytes 6291460
  18.1 8.9 %copy-start.3 = (f32[2,1,64,1024]{3,2,1,0:T(8,128)S(1)}, f32[2,1,64,1024]{3,2,1,0:T(8,128)}, u32[]{:S(2)}) copy-start(f32[2,1,64,1024]{3,2,1,0:T(8,128)} %param.11) | copy-start | bytes 1572868
  18.1 8.9 %copy-start.5 = (f32[2,1,1024]{2,1,0:T(1,128)S(1)}, f32[2,1,1024]{2,1,0:T(1,128)}, u32[]{:S(2)}) copy-start(f32[2,1,1024]{2,1,0:T(1,128)} %weight_ref.5) | copy-start | bytes 24580
  18.1 8.9 %copy-start.6 = (s32[2,1,1024]{2,1,0:T(1,128)S(1)}, s32[2,1,1024]{2,1,0:T(1,128)}, u32[]{:S(2)}) copy-start(s32[2,1,1024]{2,1,0:T(1,128)} %partner_ref.1) | copy-start | bytes 24580
  18.1 8.9 %copy-start.7 = (f32[2,1024,256]{2,1,0:T(8,128)S(1)}, f32[2,1024,256]{2,1,0:T(8,128)}, u32[]{:S(2)}) copy-start(f32[2,1024,256]{2,1,0:T(8,128)} %get-tuple-element.17.local_ref) | copy-start | bytes 6291460
  18.1 12.4 %collective-permute-start.4 = (f32[648,256]{1,0:T(8,128)}, f32[648,256]{1,0:T(8,128)S(1)}, u32[]{:S(2)}, u32[]{:S(2)}) collective-permute-start(f32[648,256]{1,0:T(8,128)} %get-tuple-element.22), channel_id=1, source_target_pairs={{0,4},{4,0},{8,12},{12,8},{16,20},{20,16},{24,28},{28,24},{32,36},... | collective-permute-start | bytes 1990664 | tf_op jit(solution)/shard_map/ppermute | solution.py:317
  22.7 7.7 %collective-permute-start.5 = (f32[64,256]{1,0:T(8,128)S(1)}, f32[64,256]{1,0:T(8,128)S(1)}, u32[]{:S(2)}, u32[]{:S(2)}) collective-permute-start(f32[64,256]{1,0:T(8,128)S(1)} %get-tuple-element.18.cross_ref), channel_id=1, source_target_pairs={{4,8},{8,4},{12,16},{16,12},{20,24},{24,20},{28,32},{32,28},{36,40... | collective-permute-start | bytes 196616 | tf_op jit(solution)/shard_map/ppermute | solution.py:317
  23.4 7.1 %collective-permute-start.6 = (f32[64,256]{1,0:T(8,128)S(1)}, f32[64,256]{1,0:T(8,128)S(1)}, u32[]{:S(2)}, u32[]{:S(2)}) collective-permute-start(f32[64,256]{1,0:T(8,128)S(1)} %get-tuple-element.19.near_ref), channel_id=1, source_target_pairs={{0,4},{4,0},{8,12},{12,8},{16,20},{20,16},{24,28},{28,24},{32,36},... | collective-permute-start | bytes 196616 | tf_op jit(solution)/shard_map/ppermute | solution.py:317
  30.4 28.1 %copy-start.2 = (f32[2,1,1024,256]{3,2,1,0:T(8,128)S(1)}, f32[2,1,1024,256]{3,2,1,0:T(8,128)}, u32[]{:S(2)}) copy-start(f32[2,1,1024,256]{3,2,1,0:T(8,128)} %param.16) | copy-start | bytes 6291460
  32.2 1.3 %collective-permute-start.7 = (f32[8,256]{1,0:T(8,128)S(1)}, f32[8,256]{1,0:T(8,128)S(1)}, u32[]{:S(2)}, u32[]{:S(2)}) collective-permute-start(f32[8,256]{1,0:T(8,128)S(1)} %get-tuple-element.24), channel_id=1, source_target_pairs={{0,4},{4,0},{8,12},{12,8},{16,20},{20,16},{24,28},{28,24},{32,36},... | collective-permute-start | bytes 24584 | tf_op jit(solution)/shard_map/ppermute | solution.py:317
  33.5 6.5 %collective-permute-start.10 = (f32[8,256]{1,0:T(8,128)S(1)}, f32[8,256]{1,0:T(8,128)S(1)}, u32[]{:S(2)}, u32[]{:S(2)}) collective-permute-start(f32[8,256]{1,0:T(8,128)S(1)} %add.30), channel_id=1, source_target_pairs={{0,33},{1,32},{2,35},{3,34},{4,37},{5,36},{6,39},{7,38},{8,41},{9,... | collective-permute-start | bytes 24584 | tf_op jit(solution)/shard_map/ppermute | solution.py:317
  38.4 3.7 %collective-permute-start.9 = (f32[8,256]{1,0:T(8,128)S(1)}, f32[8,256]{1,0:T(8,128)S(1)}, u32[]{:S(2)}, u32[]{:S(2)}) collective-permute-start(f32[8,256]{1,0:T(8,128)S(1)} %add.30), channel_id=1, source_target_pairs={{0,1},{1,0},{2,3},{3,2},{4,5},{5,4},{6,7},{7,6},{8,9},{9,8},{10,11... | collective-permute-start | bytes 24584 | tf_op jit(solution)/shard_map/ppermute | solution.py:317
  38.4 3.7 %collective-permute-start.8 = (f32[8,256]{1,0:T(8,128)S(1)}, f32[8,256]{1,0:T(8,128)S(1)}, u32[]{:S(2)}, u32[]{:S(2)}) collective-permute-start(f32[8,256]{1,0:T(8,128)S(1)} %add.30), channel_id=1, source_target_pairs={{0,32},{1,33},{2,34},{3,35},{4,36},{5,37},{6,38},{7,39},{8,40},{9,... | collective-permute-start | bytes 24584 | tf_op jit(solution)/shard_map/ppermute | solution.py:317
  42.1 7.0 %collective-permute-start.13 = (f32[8,256]{1,0:T(8,128)S(1)}, f32[8,256]{1,0:T(8,128)S(1)}, u32[]{:S(2)}, u32[]{:S(2)}) collective-permute-start(f32[8,256]{1,0:T(8,128)S(1)} %add_add_fusion.2), channel_id=1, source_target_pairs={{0,99},{1,98},{2,97},{3,96},{4,103},{5,102},{6,101},{7,100},{8,107... | collective-permute-start | bytes 24584 | tf_op jit(solution)/shard_map/ppermute | solution.py:317
  45.9 4.9 %collective-permute-start.12 = (f32[8,256]{1,0:T(8,128)S(1)}, f32[8,256]{1,0:T(8,128)S(1)}, u32[]{:S(2)}, u32[]{:S(2)}) collective-permute-start(f32[8,256]{1,0:T(8,128)S(1)} %add_add_fusion.2), channel_id=1, source_target_pairs={{0,3},{1,2},{2,1},{3,0},{4,7},{5,6},{6,5},{7,4},{8,11},{9,10},{10,... | collective-permute-start | bytes 24584 | tf_op jit(solution)/shard_map/ppermute | solution.py:317
  47.0 4.9 %collective-permute-start.11 = (f32[8,256]{1,0:T(8,128)S(1)}, f32[8,256]{1,0:T(8,128)S(1)}, u32[]{:S(2)}, u32[]{:S(2)}) collective-permute-start(f32[8,256]{1,0:T(8,128)S(1)} %add_add_fusion.2), channel_id=1, source_target_pairs={{0,96},{1,97},{2,98},{3,99},{4,100},{5,101},{6,102},{7,103},{8,104... | collective-permute-start | bytes 24584 | tf_op jit(solution)/shard_map/ppermute | solution.py:317
  51.9 5.2 %collective-permute-start.16 = (f32[8,256]{1,0:T(8,128)S(1)}, f32[8,256]{1,0:T(8,128)S(1)}, u32[]{:S(2)}, u32[]{:S(2)}) collective-permute-start(f32[8,256]{1,0:T(8,128)S(1)} %add_add_fusion.1), channel_id=1, source_target_pairs={{0,16},{1,17},{2,18},{3,19},{4,20},{5,21},{6,22},{7,23},{8,24},{9,... | collective-permute-start | bytes 24584 | tf_op jit(solution)/shard_map/ppermute | solution.py:317
  53.6 4.9 %collective-permute-start.15 = (f32[8,256]{1,0:T(8,128)S(1)}, f32[8,256]{1,0:T(8,128)S(1)}, u32[]{:S(2)}, u32[]{:S(2)}) collective-permute-start(f32[8,256]{1,0:T(8,128)S(1)} %add_add_fusion.1), channel_id=1, source_target_pairs={{0,24},{1,25},{2,26},{3,27},{4,28},{5,29},{6,30},{7,31},{8,16},{9,... | collective-permute-start | bytes 24584 | tf_op jit(solution)/shard_map/ppermute | solution.py:317
  54.8 3.7 %collective-permute-start.14 = (f32[8,256]{1,0:T(8,128)S(1)}, f32[8,256]{1,0:T(8,128)S(1)}, u32[]{:S(2)}, u32[]{:S(2)}) collective-permute-start(f32[8,256]{1,0:T(8,128)S(1)} %add_add_fusion.1), channel_id=1, source_target_pairs={{0,8},{1,9},{2,10},{3,11},{4,12},{5,13},{6,14},{7,15},{8,0},{9,1},... | collective-permute-start | bytes 24584 | tf_op jit(solution)/shard_map/ppermute | solution.py:317

commit v11 on v10

--- a/solution.py
+++ b/solution.py
@@ -15,6 +15,7 @@
 HALF = 512
 NAMES = HALF + 2 * C
 STRIP = 512
+PIECE = 128
 ROUNDS = N // STRIP
 MIB = 1 << 20
 
@@ -276,19 +277,19 @@
     ratio_ref[...] = ratio
     copies = []
     for s in range(2):
-        for r in range(4):
-            rows = slice(r * L, (r + 1) * L)
+        for r in range(N // PIECE):
+            rows = slice(r * PIECE, (r + 1) * PIECE)
             direc = direc_ref[s, rows]
             resid = resid_ref[s, rows] - alpha * jump_ref[s, rows]
             lam_out[s, rows] = lam_ref[s, rows] + alpha * direc
             resid_out[s, rows] = resid
             direc_out[s, rows] = column(weight_ref[s][:, rows]) * resid + ratio * direc
-            piece = pl.ds(r * L, L)
+            piece = pl.ds(r * PIECE, PIECE)
             for k, (here, there) in enumerate(
                 ((lam_out, lam_hbm), (resid_out, resid_hbm), (direc_out, direc_hbm))
             ):
                 copy = pltpu.make_async_copy(
-                    here.at[s, piece], there.at[s, piece], sems.at[(s * 4 + r) * 3 + k]
+                    here.at[s, piece], there.at[s, piece], sems.at[(s * (N // PIECE) + r) * 3 + k]
                 )
                 copy.start()
                 copies.append(copy)
@@ -427,7 +428,7 @@
         out_shape=(whole, whole, whole, jax.ShapeDtypeStruct((1, L), F32)),
         in_specs=[vmem()] * 6,
         out_specs=(hbm(), hbm(), hbm(), vmem()),
-        scratch_shapes=[pltpu.VMEM((2, N, L), F32)] * 3 + [pltpu.SemaphoreType.DMA((24,))],
+        scratch_shapes=[pltpu.VMEM((2, N, L), F32)] * 3 + [pltpu.SemaphoreType.DMA((6 * N // PIECE,))],
         name="final",
         compiler_params=pltpu.CompilerParams(vmem_limit_bytes=24 * MIB),
     )(total, scale, lam2, resid2, direc2, jump)

time: 62.3 us -> 62.5 us (level)
  no operation moved by 1% of the time
where the time goes in v11:
time: 62.5 us; the launch traced here: 62.4 us
  starting transfers between devices  27.9 us (45%)
  Pallas kernels  22.5 us (36%)
  waiting for transfers between devices  10.9 us (17%)
  between operations  0.99 us (2%)
    ppermute x17, starting transfers between devices, exchange(): return lax.ppermute(x, axes, pairs)  27.9 us
    ppermute x17, waiting for transfers between devices, exchange(): return lax.ppermute(x, axes, pairs)  10.9 us
    pallas_call x1, Pallas kernels, per_device(): pl.pallas_call(local_kernel, out_shape=(jax.ShapeDtypeStruct((2, N, L), F...  9.34 us
    pallas_call x1, Pallas kernels, per_device(): pl.pallas_call(final_kernel, out_shape=(whole, whole, whole, jax.ShapeDty...  3.67 us
    pallas_call x1, Pallas kernels, per_device(): pl.pallas_call(inner_kernel, out_shape=(whole, jax.ShapeDtypeStruct((3, 8...  3.45 us
    pallas_call x1, Pallas kernels, per_device(): pl.pallas_call(primal_kernel, out_shape=jax.ShapeDtypeStruct((3 * C + 8,...  3.01 us
    pallas_call x1, Pallas kernels, per_device(): pl.pallas_call(outer_kernel, out_shape=(whole, jax.ShapeDtypeStruct((8, L...  1.75 us
    pallas_call x1, Pallas kernels, per_device(): pl.pallas_call(coarse_kernel, out_shape=(piece, piece), in_specs=[smem()]...  1.27 us
  transfers between devices with their start and end apart: 17, of which 8 were waited for; matrix products, arithmetic and copies ran while one was open for 0% of the time, Pallas kernels for 23%

profile of v11, /device:TPU:0, one launch (start us, length us, event | category | flops | bytes accessed | tf_op | source)
XLA Modules:
  0.0 62.4 jit_solution(11059611171454249874)
XLA Ops:
  0.6 3.0 %primal.1.pay_hbm.pay_ref = f32[200,256]{1,0:T(8,128)} custom-call(f32[2,1024,256]{2,1,0:T(8,128)} %bitcast.17, f32[2,64,1024]{2,1,0:T(8,128)} %bitcast.24, s32[2,1,64]{2,1,0:T(1,128)} %map_hbm.1, f32[64,256]{1,0:T(8,128)} %bitcast.27), custom_call_target="tpu_custom_call" | custom-call | flops 200000000 | bytes 3145728 | tf_op jit(solution)/shard_map/primal/pallas_call | solution.py:331
  3.7 3.2 %collective-permute-start.2 = (f32[200,256]{1,0:T(8,128)}, f32[200,256]{1,0:T(8,128)S(1)}, u32[]{:S(2)}, u32[]{:S(2)}) collective-permute-start(f32[200,256]{1,0:T(8,128)} %primal.1.pay_hbm.pay_ref), channel_id=1, source_target_pairs={{0,2},{1,3},{2,0},{3,1},{4,6},{5,7},{6,4},{7,5},{8,10},{9,11},{10,... | collective-permute-start | bytes 614408 | tf_op jit(solution)/shard_map/ppermute | solution.py:318
  6.8 1.1 %collective-permute-start.1 = (f32[200,256]{1,0:T(8,128)}, f32[200,256]{1,0:T(8,128)S(1)}, u32[]{:S(2)}, u32[]{:S(2)}) collective-permute-start(f32[200,256]{1,0:T(8,128)} %primal.1.pay_hbm.pay_ref), channel_id=1, source_target_pairs={{0,3},{1,2},{2,1},{3,0},{4,7},{5,6},{6,5},{7,4},{8,11},{9,10},{10,... | collective-permute-start | bytes 614408 | tf_op jit(solution)/shard_map/ppermute | solution.py:318
  8.0 0.0 collective-permute-start
  8.0 9.3 %local.1 = (f32[2,1024,256]{2,1,0:T(8,128)}, f32[648,256]{1,0:T(8,128)}, f32[648,256]{1,0:T(8,128)}) custom-call(s32[1]{0:T(128)} %bitcast.place_ref, f32[200,256]{1,0:T(8,128)} %primal.1.pay_hbm.pay_ref, f32[2,1024,1024]{2,1,0:T(8,128)} %bitcast.28, f32[2,1024,256]{2,1,0:T(8,128)} %bitcast.18, f32[2,64,1024]{2,1,0:T(8,128)} %bitcast.25, ...), custom_call_target="tpu_custom_call" | custom-call | flops 4000000000 | bytes 12582912 | tf_op jit(solution)/shard_map/local/pallas_call | solution.py:349
  17.3 0.7 %collective-permute-start.3 = (f32[648,256]{1,0:T(8,128)}, f32[648,256]{1,0:T(8,128)S(1)}, u32[]{:S(2)}, u32[]{:S(2)}) collective-permute-start(f32[648,256]{1,0:T(8,128)} %get-tuple-element.21), channel_id=1, source_target_pairs={{4,8},{8,4},{12,16},{16,12},{20,24},{24,20},{28,32},{32,28},{36,40... | collective-permute-start | bytes 1990664 | tf_op jit(solution)/shard_map/ppermute | solution.py:318
  18.0 0.0 copy-start
  18.1 0.0 copy-start.1
  18.1 0.0 copy-start.3
  18.1 0.0 copy-start.5
  18.1 0.0 copy-start.6
  18.1 0.0 copy-start.7
  18.1 3.3 %collective-permute-start.4 = (f32[648,256]{1,0:T(8,128)}, f32[648,256]{1,0:T(8,128)S(1)}, u32[]{:S(2)}, u32[]{:S(2)}) collective-permute-start(f32[648,256]{1,0:T(8,128)} %get-tuple-element.22), channel_id=1, source_target_pairs={{0,4},{4,0},{8,12},{12,8},{16,20},{20,16},{24,28},{28,24},{32,36},... | collective-permute-start | bytes 1990664 | tf_op jit(solution)/shard_map/ppermute | solution.py:318
  21.4 0.0 collective-permute-done.2.three_ref
  21.4 0.0 collective-permute-done.1.two_ref
  21.4 0.0 collective-permute-done.one_ref
  21.4 1.3 %coarse.1 = (f32[64,256]{1,0:T(8,128)S(1)}, f32[64,256]{1,0:T(8,128)S(1)}) custom-call(s32[1]{0:T(128)} %bitcast.place_ref, f32[200,256]{1,0:T(8,128)S(1)} %copy-done.4, f32[200,256]{1,0:T(8,128)S(1)} %collective-permute-done.one_ref, f32[200,256]{1,0:T(8,128)S(1)} %collective-permute-done.1.two_ref, f32[200,256]{1,0:T(8,128)S(1)} %collective-permute-done.2.three_ref), custom_call_target="tpu_custom_call" | custom-call | flops 30000001024 | bytes 1048576 | tf_op jit(solution)/shard_map/coarse/pallas_call | solution.py:383
  22.7 0.7 %collective-permute-start.5 = (f32[64,256]{1,0:T(8,128)S(1)}, f32[64,256]{1,0:T(8,128)S(1)}, u32[]{:S(2)}, u32[]{:S(2)}) collective-permute-start(f32[64,256]{1,0:T(8,128)S(1)} %get-tuple-element.18.cross_ref), channel_id=1, source_target_pairs={{4,8},{8,4},{12,16},{16,12},{20,24},{24,20},{28,32},{32,28},{36,40... | collective-permute-start | bytes 196616 | tf_op jit(solution)/shard_map/ppermute | solution.py:318
  23.4 3.5 %collective-permute-start.6 = (f32[64,256]{1,0:T(8,128)S(1)}, f32[64,256]{1,0:T(8,128)S(1)}, u32[]{:S(2)}, u32[]{:S(2)}) collective-permute-start(f32[64,256]{1,0:T(8,128)S(1)} %get-tuple-element.19.near_ref), channel_id=1, source_target_pairs={{0,4},{4,0},{8,12},{12,8},{16,20},{20,16},{24,28},{28,24},{32,36},... | collective-permute-start | bytes 196616 | tf_op jit(solution)/shard_map/ppermute | solution.py:318
  26.9 0.0 copy-done.1
  27.0 3.5 %inner.1 = (f32[2,1024,256]{2,1,0:T(8,128)S(1)}, f32[3,8,256]{2,1,0:T(8,128)S(1)}) custom-call(s32[1]{0:T(128)} %bitcast.place_ref, f32[2,1024,256]{2,1,0:T(8,128)S(1)} %copy-done.7, f32[64,256]{1,0:T(8,128)S(1)} %get-tuple-element.18.cross_ref, f32[64,256]{1,0:T(8,128)S(1)} %get-tuple-element.19.near_ref, f32[2,64,1024]{2,1,0:T(8,128)S(1)} %bitcast.26, ...), custom_call_target="tpu_custom_call" | custom-call | flops 2500000000 | bytes 8388608 | tf_op jit(solution)/shard_map/inner/pallas_call | solution.py:395
  30.4 0.0 copy-start.2
  30.4 0.0 collective-permute-done.5.cross_pick_ref
  30.5 0.0 collective-permute-done.6.near_pick_ref
  30.5 0.0 collective-permute-done.3.cross_ref
  30.5 0.0 collective-permute-done.4.near_ref
  30.5 1.8 %outer.1 = (f32[2,1024,256]{2,1,0:T(8,128)S(1)}, f32[8,256]{1,0:T(8,128)S(1)}) custom-call(s32[1]{0:T(128)} %bitcast.place_ref, f32[2,1024,256]{2,1,0:T(8,128)S(1)} %get-tuple-element.20.part_ref, f32[648,256]{1,0:T(8,128)S(1)} %collective-permute-done.3.cross_ref, f32[648,256]{1,0:T(8,128)S(1)} %collective-permute-done.4.near_ref, ...), custom_call_target="tpu_custom_call" | custom-call | tf_op jit(solution)/shard_map/outer/pallas_call | solution.py:410
  32.2 0.1 collective-permute-start.7
  32.4 1.1 %collective-permute-done.7 = f32[8,256]{1,0:T(8,128)S(1)} collective-permute-done((f32[8,256]{1,0:T(8,128)S(1)}, f32[8,256]{1,0:T(8,128)S(1)}, u32[]{:S(2)}, u32[]{:S(2)}) %collective-permute-start.7) | collective-permute-done | bytes 8224 | tf_op jit(solution)/shard_map/ppermute | solution.py:318
  33.5 4.9 %collective-permute-start.10 = (f32[8,256]{1,0:T(8,128)S(1)}, f32[8,256]{1,0:T(8,128)S(1)}, u32[]{:S(2)}, u32[]{:S(2)}) collective-permute-start(f32[8,256]{1,0:T(8,128)S(1)} %add.30), channel_id=1, source_target_pairs={{0,33},{1,32},{2,35},{3,34},{4,37},{5,36},{6,39},{7,38},{8,41},{9,... | collective-permute-start | bytes 24584 | tf_op jit(solution)/shard_map/ppermute | solution.py:318
  38.4 0.0 collective-permute-start.9
  38.4 0.6 collective-permute-start.8
  39.0 1.1 %collective-permute-done.10 = f32[8,256]{1,0:T(8,128)S(1)} collective-permute-done((f32[8,256]{1,0:T(8,128)S(1)}, f32[8,256]{1,0:T(8,128)S(1)}, u32[]{:S(2)}, u32[]{:S(2)}) %collective-permute-start.10) | collective-permute-done | bytes 8224 | tf_op jit(solution)/shard_map/ppermute | solution.py:318
  40.0 2.0 %collective-permute-done.9 = f32[8,256]{1,0:T(8,128)S(1)} collective-permute-done((f32[8,256]{1,0:T(8,128)S(1)}, f32[8,256]{1,0:T(8,128)S(1)}, u32[]{:S(2)}, u32[]{:S(2)}) %collective-permute-start.9) | collective-permute-done | bytes 8224 | tf_op jit(solution)/shard_map/ppermute | solution.py:318
  42.0 0.0 collective-permute-done.8
  42.1 3.8 %collective-permute-start.13 = (f32[8,256]{1,0:T(8,128)S(1)}, f32[8,256]{1,0:T(8,128)S(1)}, u32[]{:S(2)}, u32[]{:S(2)}) collective-permute-start(f32[8,256]{1,0:T(8,128)S(1)} %add_add_fusion.2), channel_id=1, source_target_pairs={{0,99},{1,98},{2,97},{3,96},{4,103},{5,102},{6,101},{7,100},{8,107... | collective-permute-start | bytes 24584 | tf_op jit(solution)/shard_map/ppermute | solution.py:318
  45.9 1.1 %collective-permute-start.12 = (f32[8,256]{1,0:T(8,128)S(1)}, f32[8,256]{1,0:T(8,128)S(1)}, u32[]{:S(2)}, u32[]{:S(2)}) collective-permute-start(f32[8,256]{1,0:T(8,128)S(1)} %add_add_fusion.2), channel_id=1, source_target_pairs={{0,3},{1,2},{2,1},{3,0},{4,7},{5,6},{6,5},{7,4},{8,11},{9,10},{10,... | collective-permute-start | bytes 24584 | tf_op jit(solution)/shard_map/ppermute | solution.py:318
  47.0 1.1 %collective-permute-start.11 = (f32[8,256]{1,0:T(8,128)S(1)}, f32[8,256]{1,0:T(8,128)S(1)}, u32[]{:S(2)}, u32[]{:S(2)}) collective-permute-start(f32[8,256]{1,0:T(8,128)S(1)} %add_add_fusion.2), channel_id=1, source_target_pairs={{0,96},{1,97},{2,98},{3,99},{4,100},{5,101},{6,102},{7,103},{8,104... | collective-permute-start | bytes 24584 | tf_op jit(solution)/shard_map/ppermute | solution.py:318
  48.0 1.1 %collective-permute-done.13 = f32[8,256]{1,0:T(8,128)S(1)} collective-permute-done((f32[8,256]{1,0:T(8,128)S(1)}, f32[8,256]{1,0:T(8,128)S(1)}, u32[]{:S(2)}, u32[]{:S(2)}) %collective-permute-start.13) | collective-permute-done | bytes 8224 | tf_op jit(solution)/shard_map/ppermute | solution.py:318
  49.1 1.6 %collective-permute-done.12 = f32[8,256]{1,0:T(8,128)S(1)} collective-permute-done((f32[8,256]{1,0:T(8,128)S(1)}, f32[8,256]{1,0:T(8,128)S(1)}, u32[]{:S(2)}, u32[]{:S(2)}) %collective-permute-start.12) | collective-permute-done | bytes 8224 | tf_op jit(solution)/shard_map/ppermute | solution.py:318
  50.7 1.1 %collective-permute-done.11 = f32[8,256]{1,0:T(8,128)S(1)} collective-permute-done((f32[8,256]{1,0:T(8,128)S(1)}, f32[8,256]{1,0:T(8,128)S(1)}, u32[]{:S(2)}, u32[]{:S(2)}) %collective-permute-start.11) | collective-permute-done | bytes 8224 | tf_op jit(solution)/shard_map/ppermute | solution.py:318
  51.9 1.8 %collective-permute-start.16 = (f32[8,256]{1,0:T(8,128)S(1)}, f32[8,256]{1,0:T(8,128)S(1)}, u32[]{:S(2)}, u32[]{:S(2)}) collective-permute-start(f32[8,256]{1,0:T(8,128)S(1)} %add_add_fusion.1), channel_id=1, source_target_pairs={{0,16},{1,17},{2,18},{3,19},{4,20},{5,21},{6,22},{7,23},{8,24},{9,... | collective-permute-start | bytes 24584 | tf_op jit(solution)/shard_map/ppermute | solution.py:318
  53.6 1.2 %collective-permute-start.15 = (f32[8,256]{1,0:T(8,128)S(1)}, f32[8,256]{1,0:T(8,128)S(1)}, u32[]{:S(2)}, u32[]{:S(2)}) collective-permute-start(f32[8,256]{1,0:T(8,128)S(1)} %add_add_fusion.1), channel_id=1, source_target_pairs={{0,24},{1,25},{2,26},{3,27},{4,28},{5,29},{6,30},{7,31},{8,16},{9,... | collective-permute-start | bytes 24584 | tf_op jit(solution)/shard_map/ppermute | solution.py:318
  54.8 0.8 %collective-permute-start.14 = (f32[8,256]{1,0:T(8,128)S(1)}, f32[8,256]{1,0:T(8,128)S(1)}, u32[]{:S(2)}, u32[]{:S(2)}) collective-permute-start(f32[8,256]{1,0:T(8,128)S(1)} %add_add_fusion.1), channel_id=1, source_target_pairs={{0,8},{1,9},{2,10},{3,11},{4,12},{5,13},{6,14},{7,15},{8,0},{9,1},... | collective-permute-start | bytes 24584 | tf_op jit(solution)/shard_map/ppermute | solution.py:318
  55.6 1.4 %collective-permute-done.16 = f32[8,256]{1,0:T(8,128)S(1)} collective-permute-done((f32[8,256]{1,0:T(8,128)S(1)}, f32[8,256]{1,0:T(8,128)S(1)}, u32[]{:S(2)}, u32[]{:S(2)}) %collective-permute-start.16) | collective-permute-done | bytes 8224 | tf_op jit(solution)/shard_map/ppermute | solution.py:318
  57.0 1.5 %collective-permute-done.15 = f32[8,256]{1,0:T(8,128)S(1)} collective-permute-done((f32[8,256]{1,0:T(8,128)S(1)}, f32[8,256]{1,0:T(8,128)S(1)}, u32[]{:S(2)}, u32[]{:S(2)}) %collective-permute-start.15) | collective-permute-done | bytes 8224 | tf_op jit(solution)/shard_map/ppermute | solution.py:318
  58.5 0.0 collective-permute-done.14
  58.5 3.7 %final.1 = (f32[2,1024,256]{2,1,0:T(8,128)}, f32[2,1024,256]{2,1,0:T(8,128)}, f32[2,1024,256]{2,1,0:T(8,128)}, f32[1,256]{1,0:T(1,128)}) custom-call(f32[8,256]{1,0:T(8,128)S(1)} %add_add_fusion.total_ref, f32[2,1,1024]{2,1,0:T(1,128)S(1)} %copy-done.5, f32[2,1024,256]{2,1,0:T(8,128)S(1)} %bitcast.23, f32[2,1024,256]{2,1,0:T(8,128)S(1)} %bitcast.22, ...), custom_call_target="tpu_custom_call" | custom-call | tf_op jit(solution)/shard_map/final/pallas_call | solution.py:426
  (12 shorter events, 0.0 us)
Async XLA Ops:
  3.7 17.8 %collective-permute-start.2 = (f32[200,256]{1,0:T(8,128)}, f32[200,256]{1,0:T(8,128)S(1)}, u32[]{:S(2)}, u32[]{:S(2)}) collective-permute-start(f32[200,256]{1,0:T(8,128)} %primal.1.pay_hbm.pay_ref), channel_id=1, source_target_pairs={{0,2},{1,3},{2,0},{3,1},{4,6},{5,7},{6,4},{7,5},{8,10},{9,11},{10,... | collective-permute-start | bytes 614408 | tf_op jit(solution)/shard_map/ppermute | solution.py:318
  6.8 14.6 %collective-permute-start.1 = (f32[200,256]{1,0:T(8,128)}, f32[200,256]{1,0:T(8,128)S(1)}, u32[]{:S(2)}, u32[]{:S(2)}) collective-permute-start(f32[200,256]{1,0:T(8,128)} %primal.1.pay_hbm.pay_ref), channel_id=1, source_target_pairs={{0,3},{1,2},{2,1},{3,0},{4,7},{5,6},{6,5},{7,4},{8,11},{9,10},{10,... | collective-permute-start | bytes 614408 | tf_op jit(solution)/shard_map/ppermute | solution.py:318
  8.0 13.5 %collective-permute-start = (f32[200,256]{1,0:T(8,128)}, f32[200,256]{1,0:T(8,128)S(1)}, u32[]{:S(2)}, u32[]{:S(2)}) collective-permute-start(f32[200,256]{1,0:T(8,128)} %primal.1.pay_hbm.pay_ref), channel_id=1, source_target_pairs={{0,1},{1,0},{2,3},{3,2},{4,5},{5,4},{6,7},{7,6},{8,9},{9,8},{10,11... | collective-permute-start | bytes 614408 | tf_op jit(solution)/shard_map/ppermute | solution.py:318
  8.0 13.5 %copy-start.4 = (f32[200,256]{1,0:T(8,128)S(1)}, f32[200,256]{1,0:T(8,128)}, u32[]{:S(2)}) copy-start(f32[200,256]{1,0:T(8,128)} %primal.1.pay_hbm.pay_ref) | copy-start | bytes 614404
  17.3 13.1 %collective-permute-start.3 = (f32[648,256]{1,0:T(8,128)}, f32[648,256]{1,0:T(8,128)S(1)}, u32[]{:S(2)}, u32[]{:S(2)}) collective-permute-start(f32[648,256]{1,0:T(8,128)} %get-tuple-element.21), channel_id=1, source_target_pairs={{4,8},{8,4},{12,16},{16,12},{20,24},{24,20},{28,32},{32,28},{36,40... | collective-permute-start | bytes 1990664 | tf_op jit(solution)/shard_map/ppermute | solution.py:318
  18.0 8.9 %copy-start = (f32[2,1,1024,256]{3,2,1,0:T(8,128)S(1)}, f32[2,1,1024,256]{3,2,1,0:T(8,128)}, u32[]{:S(2)}) copy-start(f32[2,1,1024,256]{3,2,1,0:T(8,128)} %param.18) | copy-start | bytes 6291460
  18.1 8.9 %copy-start.1 = (f32[2,1,1024,256]{3,2,1,0:T(8,128)S(1)}, f32[2,1,1024,256]{3,2,1,0:T(8,128)}, u32[]{:S(2)}) copy-start(f32[2,1,1024,256]{3,2,1,0:T(8,128)} %param.17) | copy-start | bytes 6291460
  18.1 8.9 %copy-start.3 = (f32[2,1,64,1024]{3,2,1,0:T(8,128)S(1)}, f32[2,1,64,1024]{3,2,1,0:T(8,128)}, u32[]{:S(2)}) copy-start(f32[2,1,64,1024]{3,2,1,0:T(8,128)} %param.11) | copy-start | bytes 1572868
  18.1 8.9 %copy-start.5 = (f32[2,1,1024]{2,1,0:T(1,128)S(1)}, f32[2,1,1024]{2,1,0:T(1,128)}, u32[]{:S(2)}) copy-start(f32[2,1,1024]{2,1,0:T(1,128)} %weight_ref.5) | copy-start | bytes 24580
  18.1 8.9 %copy-start.6 = (s32[2,1,1024]{2,1,0:T(1,128)S(1)}, s32[2,1,1024]{2,1,0:T(1,128)}, u32[]{:S(2)}) copy-start(s32[2,1,1024]{2,1,0:T(1,128)} %partner_ref.1) | copy-start | bytes 24580
  18.1 8.9 %copy-start.7 = (f32[2,1024,256]{2,1,0:T(8,128)S(1)}, f32[2,1024,256]{2,1,0:T(8,128)}, u32[]{:S(2)}) copy-start(f32[2,1024,256]{2,1,0:T(8,128)} %get-tuple-element.17.local_ref) | copy-start | bytes 6291460
  18.1 12.4 %collective-permute-start.4 = (f32[648,256]{1,0:T(8,128)}, f32[648,256]{1,0:T(8,128)S(1)}, u32[]{:S(2)}, u32[]{:S(2)}) collective-permute-start(f32[648,256]{1,0:T(8,128)} %get-tuple-element.22), channel_id=1, source_target_pairs={{0,4},{4,0},{8,12},{12,8},{16,20},{20,16},{24,28},{28,24},{32,36},... | collective-permute-start | bytes 1990664 | tf_op jit(solution)/shard_map/ppermute | solution.py:318
  22.7 7.7 %collective-permute-start.5 = (f32[64,256]{1,0:T(8,128)S(1)}, f32[64,256]{1,0:T(8,128)S(1)}, u32[]{:S(2)}, u32[]{:S(2)}) collective-permute-start(f32[64,256]{1,0:T(8,128)S(1)} %get-tuple-element.18.cross_ref), channel_id=1, source_target_pairs={{4,8},{8,4},{12,16},{16,12},{20,24},{24,20},{28,32},{32,28},{36,40... | collective-permute-start | bytes 196616 | tf_op jit(solution)/shard_map/ppermute | solution.py:318
  23.4 7.1 %collective-permute-start.6 = (f32[64,256]{1,0:T(8,128)S(1)}, f32[64,256]{1,0:T(8,128)S(1)}, u32[]{:S(2)}, u32[]{:S(2)}) collective-permute-start(f32[64,256]{1,0:T(8,128)S(1)} %get-tuple-element.19.near_ref), channel_id=1, source_target_pairs={{0,4},{4,0},{8,12},{12,8},{16,20},{20,16},{24,28},{28,24},{32,36},... | collective-permute-start | bytes 196616 | tf_op jit(solution)/shard_map/ppermute | solution.py:318
  30.4 28.1 %copy-start.2 = (f32[2,1,1024,256]{3,2,1,0:T(8,128)S(1)}, f32[2,1,1024,256]{3,2,1,0:T(8,128)}, u32[]{:S(2)}) copy-start(f32[2,1,1024,256]{3,2,1,0:T(8,128)} %param.16) | copy-start | bytes 6291460
  32.2 1.3 %collective-permute-start.7 = (f32[8,256]{1,0:T(8,128)S(1)}, f32[8,256]{1,0:T(8,128)S(1)}, u32[]{:S(2)}, u32[]{:S(2)}) collective-permute-start(f32[8,256]{1,0:T(8,128)S(1)} %get-tuple-element.24), channel_id=1, source_target_pairs={{0,4},{4,0},{8,12},{12,8},{16,20},{20,16},{24,28},{28,24},{32,36},... | collective-permute-start | bytes 24584 | tf_op jit(solution)/shard_map/ppermute | solution.py:318
  33.5 6.5 %collective-permute-start.10 = (f32[8,256]{1,0:T(8,128)S(1)}, f32[8,256]{1,0:T(8,128)S(1)}, u32[]{:S(2)}, u32[]{:S(2)}) collective-permute-start(f32[8,256]{1,0:T(8,128)S(1)} %add.30), channel_id=1, source_target_pairs={{0,33},{1,32},{2,35},{3,34},{4,37},{5,36},{6,39},{7,38},{8,41},{9,... | collective-permute-start | bytes 24584 | tf_op jit(solution)/shard_map/ppermute | solution.py:318
  38.4 3.7 %collective-permute-start.9 = (f32[8,256]{1,0:T(8,128)S(1)}, f32[8,256]{1,0:T(8,128)S(1)}, u32[]{:S(2)}, u32[]{:S(2)}) collective-permute-start(f32[8,256]{1,0:T(8,128)S(1)} %add.30), channel_id=1, source_target_pairs={{0,1},{1,0},{2,3},{3,2},{4,5},{5,4},{6,7},{7,6},{8,9},{9,8},{10,11... | collective-permute-start | bytes 24584 | tf_op jit(solution)/shard_map/ppermute | solution.py:318
  38.4 3.7 %collective-permute-start.8 = (f32[8,256]{1,0:T(8,128)S(1)}, f32[8,256]{1,0:T(8,128)S(1)}, u32[]{:S(2)}, u32[]{:S(2)}) collective-permute-start(f32[8,256]{1,0:T(8,128)S(1)} %add.30), channel_id=1, source_target_pairs={{0,32},{1,33},{2,34},{3,35},{4,36},{5,37},{6,38},{7,39},{8,40},{9,... | collective-permute-start | bytes 24584 | tf_op jit(solution)/shard_map/ppermute | solution.py:318
  42.1 7.0 %collective-permute-start.13 = (f32[8,256]{1,0:T(8,128)S(1)}, f32[8,256]{1,0:T(8,128)S(1)}, u32[]{:S(2)}, u32[]{:S(2)}) collective-permute-start(f32[8,256]{1,0:T(8,128)S(1)} %add_add_fusion.2), channel_id=1, source_target_pairs={{0,99},{1,98},{2,97},{3,96},{4,103},{5,102},{6,101},{7,100},{8,107... | collective-permute-start | bytes 24584 | tf_op jit(solution)/shard_map/ppermute | solution.py:318
  45.9 4.9 %collective-permute-start.12 = (f32[8,256]{1,0:T(8,128)S(1)}, f32[8,256]{1,0:T(8,128)S(1)}, u32[]{:S(2)}, u32[]{:S(2)}) collective-permute-start(f32[8,256]{1,0:T(8,128)S(1)} %add_add_fusion.2), channel_id=1, source_target_pairs={{0,3},{1,2},{2,1},{3,0},{4,7},{5,6},{6,5},{7,4},{8,11},{9,10},{10,... | collective-permute-start | bytes 24584 | tf_op jit(solution)/shard_map/ppermute | solution.py:318
  47.0 4.9 %collective-permute-start.11 = (f32[8,256]{1,0:T(8,128)S(1)}, f32[8,256]{1,0:T(8,128)S(1)}, u32[]{:S(2)}, u32[]{:S(2)}) collective-permute-start(f32[8,256]{1,0:T(8,128)S(1)} %add_add_fusion.2), channel_id=1, source_target_pairs={{0,96},{1,97},{2,98},{3,99},{4,100},{5,101},{6,102},{7,103},{8,104... | collective-permute-start | bytes 24584 | tf_op jit(solution)/shard_map/ppermute | solution.py:318
  51.9 5.2 %collective-permute-start.16 = (f32[8,256]{1,0:T(8,128)S(1)}, f32[8,256]{1,0:T(8,128)S(1)}, u32[]{:S(2)}, u32[]{:S(2)}) collective-permute-start(f32[8,256]{1,0:T(8,128)S(1)} %add_add_fusion.1), channel_id=1, source_target_pairs={{0,16},{1,17},{2,18},{3,19},{4,20},{5,21},{6,22},{7,23},{8,24},{9,... | collective-permute-start | bytes 24584 | tf_op jit(solution)/shard_map/ppermute | solution.py:318
  53.6 4.9 %collective-permute-start.15 = (f32[8,256]{1,0:T(8,128)S(1)}, f32[8,256]{1,0:T(8,128)S(1)}, u32[]{:S(2)}, u32[]{:S(2)}) collective-permute-start(f32[8,256]{1,0:T(8,128)S(1)} %add_add_fusion.1), channel_id=1, source_target_pairs={{0,24},{1,25},{2,26},{3,27},{4,28},{5,29},{6,30},{7,31},{8,16},{9,... | collective-permute-start | bytes 24584 | tf_op jit(solution)/shard_map/ppermute | solution.py:318
  54.8 3.7 %collective-permute-start.14 = (f32[8,256]{1,0:T(8,128)S(1)}, f32[8,256]{1,0:T(8,128)S(1)}, u32[]{:S(2)}, u32[]{:S(2)}) collective-permute-start(f32[8,256]{1,0:T(8,128)S(1)} %add_add_fusion.1), channel_id=1, source_target_pairs={{0,8},{1,9},{2,10},{3,11},{4,12},{5,13},{6,14},{7,15},{8,0},{9,1},... | collective-permute-start | bytes 24584 | tf_op jit(solution)/shard_map/ppermute | solution.py:318
